TPU v7x, 32 devices: a whole 2x2x4 slice. The times are simulated.
32 devices in a mesh: section: 2 (over core), group: 4 (over y, x), tensor: 4 (over z).
Axes of the slice: x: 2, y: 2, z: 4, core: 2. Of those that a mesh axis runs over, the one named last changes fastest.
Arguments:
- queries: bfloat16 [64, 3072], P(('section', 'group'), 'tensor'), may hold values from -140 to 140
- new_kv: bfloat16 [64, 2048], P(('section', 'group'), 'tensor'), may hold values from -10 to 10
- kv_cache: bfloat16 [8, 2048, 2048], P(('section', 'group'), None, 'tensor'), may hold values from -4.5 to 4.5
- cache_len: int32 [8], P(('section', 'group')), may hold values from 1 to 2048, 10240 in all
- residual: bfloat16 [64, 3072], P(('section', 'group'), 'tensor'), may hold values from -28 to 28
- norm_gain: bfloat16 [3072], P('tensor'), may hold values from 0.099609375 to 1.8984375
- router: bfloat16 [8, 3072], P(None, 'tensor'), may hold values from -0.23925781 to 0.23925781
- routes: int32 [64, 4], P(('section', 'group')), may hold values from 0 to 7, all different within a row; in each aligned block of 8 rows (0 to 7, 8 to 15, ...) at most 8 rows name the same one
- gate_w: bfloat16 [8, 6912, 3072], P(('section', 'tensor'), 'group'), may hold values from -0.109375 to 0.109375
- up_w: bfloat16 [8, 6912, 3072], P(('section', 'tensor'), 'group'), may hold values from -0.109375 to 0.109375
- down_w: bfloat16 [8, 6912, 3072], P(('section', 'tensor'), 'group'), may hold values from -0.078125 to 0.078125
Outputs:
- mixed: bfloat16 [64, 3072], P(('section', 'group'), 'tensor')
Inputs may be any that keep to these rules, and one draw needn't show every extreme that they name: `routes`: each token names 4 different experts; in each aligned block of 8 tokens (the branches of one prefix) no expert is named by more than 8 tokens, and in some block one expert is named by exactly 8. `cache_len`: the largest is 2048.
All inputs are finite; a program needn't handle non-finite values. No bound on the sum of `cache_len` on one device may be relied on, other than what follows from the above.
Results may differ from a plain program's by a relative error of at most 0.0065.
Values may be sent and summed in bfloat16 or wider, within the bound.
No kernel may reach another device: no remote copies, remote signals or barrier semaphores. Data moves between devices by JAX's collectives and lax.ppermute only.
A program may use at most 128 MiB of HBM per device.

v0:
```python
import functools

import jax
import jax.numpy as jnp
from jax import lax
from jax.experimental import pallas as pl
from jax.experimental.pallas import tpu as pltpu
from jax.sharding import PartitionSpec as P

HEAD_DIM = 128
NORM_EPS = 1e-05
LANES = 128
SLOT = 36
MASK_AT = 3 * SLOT
MIB = 1 << 20
BY_ROW = (((1,), (1,)), ((), ()))


def split_terms(value):
    high = value.astype(jnp.bfloat16).astype(jnp.float32)
    rest = value - high
    middle = rest.astype(jnp.bfloat16).astype(jnp.float32)
    return high, middle, rest - middle


def attention_kernel(
    len_ref,
    q_hbm,
    new_hbm,
    kv_hbm,
    res_hbm,
    routes_hbm,
    router_hbm,
    gain_hbm,
    out_ref,
    q_ref,
    new_ref,
    kv,
    res_ref,
    routes_ref,
    router_ref,
    gain_ref,
    scores,
    sems,
    *,
    chunks,
):
    slots = kv_hbm.shape[1]
    part = slots // chunks
    sources = [q_hbm, new_hbm] + [kv_hbm.at[0, pl.ds(c * part, part)] for c in range(chunks)]
    targets = [q_ref, new_ref] + [kv.at[pl.ds(c * part, part)] for c in range(chunks)]
    sources += [res_hbm, routes_hbm, router_hbm, gain_hbm]
    targets += [res_ref, routes_ref, router_ref, gain_ref]
    copies = [pltpu.make_async_copy(a, b, sems.at[i]) for i, (a, b) in enumerate(zip(sources, targets))]
    for copy in copies:
        copy.start()
    tokens, columns = q_ref.shape
    key_heads = new_ref.shape[1] // (2 * HEAD_DIM)
    grouped = columns // HEAD_DIM // key_heads
    rows = grouped * tokens
    scale = HEAD_DIM ** (-0.5)
    copies[0].wait()
    copies[1].wait()
    queries, selves = [], []
    for h in range(key_heads):
        first = h * grouped * HEAD_DIM
        q = jnp.concatenate(
            [
                q_ref[:, first + j * HEAD_DIM : first + (j + 1) * HEAD_DIM].astype(jnp.float32)
                for j in range(grouped)
            ],
            axis=0,
        )
        own_key = new_ref[:, 2 * h * HEAD_DIM : (2 * h + 1) * HEAD_DIM].astype(jnp.float32)
        own_key = jnp.concatenate([own_key] * grouped, axis=0)
        selves.append(jnp.sum(q * own_key, axis=1, keepdims=True) * scale)
        queries.append(q.astype(jnp.bfloat16))
    live = len_ref[0]
    for c in range(chunks):
        copies[2 + c].wait()
        for h in range(key_heads):
            keys = kv[c * part : (c + 1) * part, 2 * h * HEAD_DIM : (2 * h + 1) * HEAD_DIM]
            s = lax.dot_general(queries[h], keys, BY_ROW, preferred_element_type=jnp.float32)
            at = lax.broadcasted_iota(jnp.int32, (rows, part), 1) + c * part
            scores[h, :, c * part : (c + 1) * part] = jnp.where(at < live, s * scale, -jnp.inf)
    for copy in copies[2 + chunks :]:
        copy.wait()

    experts = router_ref.shape[0]
    routes = routes_ref[...]
    expert_at = lax.broadcasted_iota(jnp.int32, (LANES, tokens), 0) - MASK_AT
    named = jnp.zeros((LANES, tokens), jnp.float32)
    for k in range(routes.shape[0]):
        named = jnp.where(expert_at == routes[k : k + 1, :], 1.0, named)
    side = named.T

    streams = []
    for h in range(key_heads):
        s = scores[h]
        top = jnp.maximum(jnp.max(s, axis=1, keepdims=True), selves[h])
        weights = jnp.exp(s - top).astype(jnp.bfloat16)
        own = jnp.exp(selves[h] - top).astype(jnp.bfloat16).astype(jnp.float32)
        total = jnp.sum(weights.astype(jnp.float32), axis=1, keepdims=True) + own
        value_at = (2 * h + 1) * HEAD_DIM
        mixed = jnp.dot(weights, kv[:, value_at : value_at + HEAD_DIM], preferred_element_type=jnp.float32)
        own_value = new_ref[:, value_at : value_at + HEAD_DIM].astype(jnp.float32)
        mixed = (mixed + own * jnp.concatenate([own_value] * grouped, axis=0)) / total
        for j in range(grouped):
            at = (h * grouped + j) * HEAD_DIM
            got = res_ref[:, at : at + HEAD_DIM].astype(jnp.float32) + mixed[j * tokens : (j + 1) * tokens]
            got = got.astype(jnp.bfloat16)
            out_ref[:, at : at + HEAD_DIM] = got
            streams.append(got.astype(jnp.float32))

    lane = lax.broadcasted_iota(jnp.int32, (tokens, LANES), 1)
    sums = jnp.zeros((tokens, LANES), jnp.float32)

    def put(sums, at, pieces):
        total = pieces[0]
        for piece in pieces[1:]:
            total = total + piece
        return jnp.where(lane == at, jnp.sum(total, axis=1, keepdims=True), sums)

    blocks = range(len(streams))
    sums = put(sums, experts, streams)
    sums = put(sums, experts + 1, [x * x for x in streams])
    gains = [gain_ref[:, b * HEAD_DIM : (b + 1) * HEAD_DIM].astype(jnp.float32) for b in blocks]
    scaled = [x * g for x, g in zip(streams, gains)]
    for e in range(experts):
        weights = [router_ref[e : e + 1, b * HEAD_DIM : (b + 1) * HEAD_DIM].astype(jnp.float32) for b in blocks]
        sums = put(sums, e, [x * w for x, w in zip(scaled, weights)])
        plain = [jnp.broadcast_to(g * w, (tokens, HEAD_DIM)) for g, w in zip(gains, weights)]
        sums = put(sums, experts + 2 + e, plain)
    for i, term in enumerate(split_terms(sums)):
        side = side + (pltpu.roll(term, i * SLOT, 1) if i else term)
    out_ref[:, columns : columns + LANES] = side.astype(out_ref.dtype)
    gain_rows = jnp.concatenate(
        gains + [jnp.zeros((1, LANES), jnp.float32)] * (tokens - len(gains)), axis=0
    )
    out_ref[:, columns + LANES :] = gain_rows.astype(out_ref.dtype)


def attend(cache_len, queries, new_kv, kv_cache, residual, routes, router, norm_gain):
    tokens, columns = queries.shape
    slots, width = kv_cache.shape[1:]
    key_heads = new_kv.shape[1] // (2 * HEAD_DIM)
    rows = columns // HEAD_DIM // key_heads * tokens
    chunks = 4
    operands = [queries, new_kv, kv_cache, residual, routes.T, router, norm_gain.reshape(1, -1)]
    operands = [pltpu.with_memory_space_constraint(x, pltpu.HBM) for x in operands]
    kept = [pltpu.VMEM(x.shape, x.dtype) for x in operands]
    kept[2] = pltpu.VMEM((slots, width), kv_cache.dtype)
    return pl.pallas_call(
        functools.partial(attention_kernel, chunks=chunks),
        out_shape=jax.ShapeDtypeStruct((tokens, columns + 2 * LANES), jnp.bfloat16),
        in_specs=[pl.BlockSpec(memory_space=pltpu.SMEM)]
        + [pl.BlockSpec(memory_space=pl.ANY)] * len(operands),
        out_specs=pl.BlockSpec(memory_space=pltpu.VMEM),
        scratch_shapes=kept
        + [
            pltpu.VMEM((key_heads, rows, slots), jnp.float32),
            pltpu.SemaphoreType.DMA((chunks + len(operands) - 1,)),
        ],
        compiler_params=pltpu.CompilerParams(vmem_limit_bytes=8 * MIB),
        cost_estimate=pl.CostEstimate(
            flops=4 * rows * slots * HEAD_DIM * key_heads,
            bytes_accessed=slots * width * 2,
            transcendentals=rows * slots * key_heads,
        ),
        name="attention",
    )(cache_len, *operands)


def norm_kernel(place_ref, *refs, experts):
    pieces, out_ref = refs[:-1], refs[-1]
    tokens, wide = pieces[0].shape
    block = wide - 2 * LANES
    model = len(pieces) * block
    total = jnp.zeros((tokens, LANES), jnp.float32)
    for piece in pieces:
        total = total + piece[:, block : block + LANES].astype(jnp.float32)
    sums = total + pltpu.roll(total, LANES - SLOT, 1) + pltpu.roll(total, LANES - 2 * SLOT, 1)
    mean = sums[:, experts : experts + 1] / model
    variance = sums[:, experts + 1 : experts + 2] / model - mean * mean
    inv = lax.rsqrt(variance + NORM_EPS)
    plain = pltpu.roll(sums, LANES - experts - 2, 1)
    logits = (sums - mean * plain) * inv
    lane = lax.broadcasted_iota(jnp.int32, (tokens, LANES), 1)
    named = (pltpu.roll(total, LANES - MASK_AT, 1) > 0) & (lane < experts)
    raised = jnp.where(named, jnp.exp(logits), 0.0)
    share = raised / jnp.sum(raised, axis=1, keepdims=True)
    high = share.astype(jnp.bfloat16).astype(jnp.float32)
    side = high + pltpu.roll(share - high, experts, 1)
    out_ref[:, model:] = side.astype(out_ref.dtype)
    for mask, piece in enumerate(pieces):
        gain = piece[:, block + LANES :].astype(jnp.float32)
        gain = jnp.concatenate([gain[j : j + 1, :] for j in range(block // LANES)], axis=1)
        x = (piece[:, :block].astype(jnp.float32) - mean) * inv * gain
        at = pl.multiple_of(lax.bitwise_xor(place_ref[0], mask) * block, block)
        out_ref[:, pl.ds(at, block)] = x.astype(out_ref.dtype)


def norm_rows(place, blocks, experts):
    tokens, wide = blocks[0].shape
    model = (wide - 2 * LANES) * len(blocks)
    vmem = pl.BlockSpec(memory_space=pltpu.VMEM)
    return pl.pallas_call(
        functools.partial(norm_kernel, experts=experts),
        out_shape=jax.ShapeDtypeStruct((tokens, model + LANES), jnp.bfloat16),
        in_specs=[pl.BlockSpec(memory_space=pltpu.SMEM)] + [vmem] * len(blocks),
        out_specs=vmem,
        compiler_params=pltpu.CompilerParams(vmem_limit_bytes=4 * MIB),
        name="norm",
    )(place, *blocks)


def run_expert(place, near, far, gate_w, up_w, down_w, experts):
    model = gate_w.shape[2]
    rows = jnp.concatenate([near, far], axis=0)
    x, side = rows[:, :model], rows[:, model:].astype(jnp.float32)
    lane = jnp.arange(side.shape[1])[None, :]
    mine = (lane == place[1]) | (lane == place[1] + experts)
    share = jnp.sum(jnp.where(mine, side, 0.0), axis=1, keepdims=True)
    gate = lax.dot_general(x, gate_w[0], BY_ROW, preferred_element_type=jnp.float32)
    up = lax.dot_general(x, up_w[0], BY_ROW, preferred_element_type=jnp.float32)
    hidden = (jax.nn.silu(gate) * up).astype(jnp.bfloat16)
    out = jnp.dot(hidden, down_w[0], preferred_element_type=jnp.float32)
    return (out * share).astype(jnp.bfloat16)


def send(x, axis, mask):
    return lax.ppermute(x, axis, [(i, i ^ mask) for i in range(lax.axis_size(axis))])


def add(*terms):
    return sum(t.astype(jnp.float32) for t in terms)


def per_device(
    queries, new_kv, kv_cache, cache_len, residual, norm_gain, router, routes, gate_w, up_w, down_w
):
    sections, groups, tensors = (lax.axis_size(a) for a in ("section", "group", "tensor"))
    experts, block = router.shape
    tokens = queries.shape[0]
    place = lax.axis_index("tensor")
    where = jnp.stack([place, lax.axis_index("section") * tensors + place]).astype(jnp.int32)

    fresh = attend(cache_len, queries, new_kv, kv_cache, residual, routes, router, norm_gain)
    blocks = [fresh] + [send(fresh, "tensor", m) for m in range(1, tensors)]
    rows = norm_rows(where, blocks, experts)
    near = jnp.concatenate([rows] + [send(rows, "group", m) for m in range(1, groups)], axis=0)
    far = send(near, "section", 1)

    out = run_expert(where, near, far, gate_w, up_w, down_w, experts)
    half = out.shape[0] // 2
    both = add(out[:half], send(out[half:], "section", 1)).astype(jnp.bfloat16)
    both = both.reshape(groups, tokens, -1)
    got = add(both[0], *[send(both[m], "group", m) for m in range(1, groups)]).astype(jnp.bfloat16)
    parts = [lax.dynamic_slice_in_dim(got, (place ^ m) * block, block, axis=1) for m in range(tensors)]
    mixed = add(fresh[:, :block], parts[0], *[send(parts[m], "tensor", m) for m in range(1, tensors)])
    return mixed.astype(jnp.bfloat16)


def solution(mesh):
    rows = P(("section", "group"), "tensor")
    weights = P(("section", "tensor"), "group", None)
    in_specs = (
        rows,
        rows,
        P(("section", "group"), None, "tensor"),
        P(("section", "group")),
        rows,
        P("tensor"),
        P(None, "tensor"),
        P(("section", "group"), None),
        weights,
        weights,
        weights,
    )
    return jax.shard_map(per_device, mesh=mesh, in_specs=in_specs, out_specs=rows, check_vma=False)
```

profile of v0, /device:TPU:0, one launch (start us, length us, event | category | flops | bytes accessed | tf_op | source)
XLA Modules:
  0.0 60.5 jit_solution(5946224040536277352)
XLA Ops:
  0.0 1.3 %reshape.24.gain_hbm = bf16[1,768]{1,0:T(2,128)(2,1)} reshape(bf16[768]{0:T(1024)(128)(2,1)} %param.16) | data formatting | bytes 3072 | tf_op jit(solution)/shard_map/reshape | solution.py:149
  1.9 2.5 %attention.1.refs_0_ = bf16[8,1024]{1,0:T(8,128)(2,1)S(1)} custom-call(s32[1]{0:T(128)S(6)} %copy.16.len_ref, bf16[8,768]{1,0:T(8,128)(2,1)} %q_hbm.1, bf16[8,512]{1,0:T(8,128)(2,1)} %new_hbm.1, bf16[1,2048,512]{2,1,0:T(8,128)(2,1)} %kv_hbm.1, bf16[8,768]{1,0:T(8,128)(2,1)} %res_hbm.1, s32[4,8]{1,0:T(4,128)} %bitcast.20, bf16[8,768]{1,0:T(8,128)(2,1)} %router_hbm.1, ...), custom_call_target="tpu_custom_call" | custom-call | flops 50331648 | bytes 2097152 | tf_op jit(solution)/shard_map/attention/pallas_call | solution.py:153
  4.5 3.1 %collective-permute-start = (bf16[8,1024]{1,0:T(8,128)(2,1)S(1)}, bf16[8,1024]{1,0:T(8,128)(2,1)S(1)}, u32[]{:S(2)}, u32[]{:S(2)}) collective-permute-start(bf16[8,1024]{1,0:T(8,128)(2,1)S(1)} %attention.1.refs_0_), channel_id=1, source_target_pairs={{0,1},{1,0},{2,3},{3,2},{4,5},{5,4},{6,7},{7,6},{8,9},{9,8},{10,11... | collective-permute-start | bytes 49160 | tf_op jit(solution)/shard_map/ppermute | solution.py:232
  7.5 2.6 %collective-permute-start.1 = (bf16[8,1024]{1,0:T(8,128)(2,1)S(1)}, bf16[8,1024]{1,0:T(8,128)(2,1)S(1)}, u32[]{:S(2)}, u32[]{:S(2)}) collective-permute-start(bf16[8,1024]{1,0:T(8,128)(2,1)S(1)} %attention.1.refs_0_), channel_id=1, source_target_pairs={{0,2},{1,3},{2,0},{3,1},{4,6},{5,7},{6,4},{7,5},{8,10},{9,11},{10,... | collective-permute-start | bytes 49160 | tf_op jit(solution)/shard_map/ppermute | solution.py:232
  10.1 0.1 pad_add_fusion.place_ref
  10.2 2.0 %collective-permute-done.1.refs_2_ = bf16[8,1024]{1,0:T(8,128)(2,1)S(1)} collective-permute-done((bf16[8,1024]{1,0:T(8,128)(2,1)S(1)}, bf16[8,1024]{1,0:T(8,128)(2,1)S(1)}, u32[]{:S(2)}, u32[]{:S(2)}) %collective-permute-start.1) | collective-permute-done | bytes 16416 | tf_op jit(solution)/shard_map/ppermute | solution.py:232
  12.3 3.4 %collective-permute-done.2.refs_3_ = bf16[8,1024]{1,0:T(8,128)(2,1)S(1)} collective-permute-done((bf16[8,1024]{1,0:T(8,128)(2,1)S(1)}, bf16[8,1024]{1,0:T(8,128)(2,1)S(1)}, u32[]{:S(2)}, u32[]{:S(2)}) %collective-permute-start.2) | collective-permute-done | bytes 16416 | tf_op jit(solution)/shard_map/ppermute | solution.py:232
  15.7 0.9 %norm.1 = bf16[8,3200]{1,0:T(8,128)(2,1)S(1)} custom-call(s32[2]{0:T(128)S(1)} %pad_add_fusion.place_ref, bf16[8,1024]{1,0:T(8,128)(2,1)S(1)} %attention.1.refs_0_, bf16[8,1024]{1,0:T(8,128)(2,1)S(1)} %collective-permute-done.refs_1_, bf16[8,1024]{1,0:T(8,128)(2,1)S(1)} %collective-permute-done.1.refs_2_, bf16[8,1024]{1,0:T(8,128)(2,1)S(1)} %collective-permute-done.2.refs_3_), custom_call_target="tpu_custom_call" | custom-call | tf_op jit(solution)/shard_map/norm/pallas_call | solution.py:207
  16.6 1.5 %collective-permute-start.3 = (bf16[8,3200]{1,0:T(8,128)(2,1)S(1)}, bf16[8,3200]{1,0:T(8,128)(2,1)S(1)}, u32[]{:S(2)}, u32[]{:S(2)}) collective-permute-start(bf16[8,3200]{1,0:T(8,128)(2,1)S(1)} %norm.1), channel_id=1, source_target_pairs={{0,4},{4,0},{8,12},{12,8},{1,5},{5,1},{9,13},{13,9},{2,6},{6,2},{1... | collective-permute-start | bytes 153608 | tf_op jit(solution)/shard_map/ppermute | solution.py:232
  18.1 1.5 %collective-permute-start.4 = (bf16[8,3200]{1,0:T(8,128)(2,1)S(1)}, bf16[8,3200]{1,0:T(8,128)(2,1)S(1)}, u32[]{:S(2)}, u32[]{:S(2)}) collective-permute-start(bf16[8,3200]{1,0:T(8,128)(2,1)S(1)} %norm.1), channel_id=1, source_target_pairs={{0,8},{4,12},{8,0},{12,4},{1,9},{5,13},{9,1},{13,5},{2,10},{6,14},... | collective-permute-start | bytes 153608 | tf_op jit(solution)/shard_map/ppermute | solution.py:232
  19.6 0.5 collective-permute-start.5
  20.1 0.7 %collective-permute-done.3 = bf16[8,3200]{1,0:T(8,128)(2,1)S(1)} collective-permute-done((bf16[8,3200]{1,0:T(8,128)(2,1)S(1)}, bf16[8,3200]{1,0:T(8,128)(2,1)S(1)}, u32[]{:S(2)}, u32[]{:S(2)}) %collective-permute-start.3) | collective-permute-done | bytes 51232 | tf_op jit(solution)/shard_map/ppermute | solution.py:232
  20.8 1.4 %collective-permute-done.4 = bf16[8,3200]{1,0:T(8,128)(2,1)S(1)} collective-permute-done((bf16[8,3200]{1,0:T(8,128)(2,1)S(1)}, bf16[8,3200]{1,0:T(8,128)(2,1)S(1)}, u32[]{:S(2)}, u32[]{:S(2)}) %collective-permute-start.4) | collective-permute-done | bytes 51232 | tf_op jit(solution)/shard_map/ppermute | solution.py:232
  22.2 2.4 %collective-permute-done.5 = bf16[8,3200]{1,0:T(8,128)(2,1)S(1)} collective-permute-done((bf16[8,3200]{1,0:T(8,128)(2,1)S(1)}, bf16[8,3200]{1,0:T(8,128)(2,1)S(1)}, u32[]{:S(2)}, u32[]{:S(2)}) %collective-permute-start.5) | collective-permute-done | bytes 51232 | tf_op jit(solution)/shard_map/ppermute | solution.py:232
  24.6 0.1 collective-permute-start.6
  24.8 1.4 %collective-permute-done.6 = bf16[32,3200]{1,0:T(8,128)(2,1)S(1)} collective-permute-done((bf16[32,3200]{1,0:T(8,128)(2,1)S(1)}, bf16[32,3200]{1,0:T(8,128)(2,1)S(1)}, u32[]{:S(2)}, u32[]{:S(2)}) %collective-permute-start.6) | collective-permute-done | bytes 204832 | tf_op jit(solution)/shard_map/ppermute | solution.py:232
  26.2 7.3 %fusion.4 = f32[64,1728]{1,0:T(8,128)S(1)} fusion(bf16[1,1728,3072]{2,1,0:T(8,128)(2,1)} %param.19, bf16[64,3200]{1,0:T(8,128)(2,1)S(1)} %constant_dynamic-update-slice_fusion), kind=kOutput, calls=%fused_computation.4 | convolution fusion | flops 679477248 | bytes 11452416 | tf_op jit(solution)/shard_map/dot_general | solution.py:224
  33.5 0.1 select_reduce_fusion
  33.6 12.2 %fusion.9 = bf16[64,3072]{1,0:T(8,128)(2,1)S(1)} fusion(bf16[1,1728,3072]{2,1,0:T(8,128)(2,1)} %param.21, f32[64]{0:T(128)S(1)} %select_reduce_fusion, f32[64,1728]{1,0:T(8,128)S(1)} %fusion.4, bf16[1,1728,3072]{2,1,0:T(8,128)(2,1)} %param.20, bf16[64,3200]{1,0:T(8,128)(2,1)S(1)} %constant_dynamic-update-slice_fusion), kind=kOutput, calls=%fused_computation.7 | convolution fusion | flops 1360011264 | bytes 22479360 | tf_op jit(solution)/shard_map/dot_general | solution.py:227
  45.8 0.2 collective-permute-start.7
  46.0 1.3 %collective-permute-done.7 = bf16[32,3072]{1,0:T(8,128)(2,1)S(1)} collective-permute-done((bf16[32,3072]{1,0:T(8,128)(2,1)S(1)}, bf16[32,3072]{1,0:T(8,128)(2,1)S(1)}, u32[]{:S(2)}, u32[]{:S(2)}) %collective-permute-start.7) | collective-permute-done | bytes 196640 | tf_op jit(solution)/shard_map/ppermute | solution.py:232
  47.4 0.5 collective-permute-start.10
  47.9 1.5 %collective-permute-start.8 = (bf16[8,3072]{1,0:T(8,128)(2,1)S(1)}, bf16[8,3072]{1,0:T(8,128)(2,1)S(1)}, u32[]{:S(2)}, u32[]{:S(2)}) collective-permute-start(bf16[8,3072]{1,0:T(8,128)(2,1)S(1)} %get-tuple-element.5), channel_id=1, source_target_pairs={{0,4},{4,0},{8,12},{12,8},{1,5},{5,1},{9,13},{13,9},{2,6},{6,2},{1... | collective-permute-start | bytes 147464 | tf_op jit(solution)/shard_map/ppermute | solution.py:232
  49.4 1.5 %collective-permute-start.9 = (bf16[8,3072]{1,0:T(8,128)(2,1)S(1)}, bf16[8,3072]{1,0:T(8,128)(2,1)S(1)}, u32[]{:S(2)}, u32[]{:S(2)}) collective-permute-start(bf16[8,3072]{1,0:T(8,128)(2,1)S(1)} %get-tuple-element.7), channel_id=1, source_target_pairs={{0,8},{4,12},{8,0},{12,4},{1,9},{5,13},{9,1},{13,5},{2,10},{6,14},... | collective-permute-start | bytes 147464 | tf_op jit(solution)/shard_map/ppermute | solution.py:232
  50.9 1.7 %collective-permute-done.10 = bf16[8,3072]{1,0:T(8,128)(2,1)S(1)} collective-permute-done((bf16[8,3072]{1,0:T(8,128)(2,1)S(1)}, bf16[8,3072]{1,0:T(8,128)(2,1)S(1)}, u32[]{:S(2)}, u32[]{:S(2)}) %collective-permute-start.10) | collective-permute-done | bytes 49184 | tf_op jit(solution)/shard_map/ppermute | solution.py:232
  52.7 0.8 %collective-permute-done.9 = bf16[8,3072]{1,0:T(8,128)(2,1)S(1)} collective-permute-done((bf16[8,3072]{1,0:T(8,128)(2,1)S(1)}, bf16[8,3072]{1,0:T(8,128)(2,1)S(1)}, u32[]{:S(2)}, u32[]{:S(2)}) %collective-permute-start.9) | collective-permute-done | bytes 49184 | tf_op jit(solution)/shard_map/ppermute | solution.py:232
  53.6 0.1 collective-permute-start.11
  53.6 0.8 %collective-permute-start.12 = (bf16[8,768]{1,0:T(8,128)(2,1)S(1)}, bf16[8,768]{1,0:T(8,128)(2,1)S(1)}, u32[]{:S(2)}, u32[]{:S(2)}) collective-permute-start(bf16[8,768]{1,0:T(8,128)(2,1)S(1)} %get-tuple-element.10), channel_id=1, source_target_pairs={{0,2},{1,3},{2,0},{3,1},{4,6},{5,7},{6,4},{7,5},{8,10},{9,11},{10,... | collective-permute-start | bytes 36872 | tf_op jit(solution)/shard_map/ppermute | solution.py:232
  54.4 3.6 %collective-permute-start.13 = (bf16[8,768]{1,0:T(8,128)(2,1)S(1)}, bf16[8,768]{1,0:T(8,128)(2,1)S(1)}, u32[]{:S(2)}, u32[]{:S(2)}) collective-permute-start(bf16[8,768]{1,0:T(8,128)(2,1)S(1)} %get-tuple-element.9), channel_id=1, source_target_pairs={{0,3},{1,2},{2,1},{3,0},{4,7},{5,6},{6,5},{7,4},{8,11},{9,10},{10,... | collective-permute-start | bytes 36872 | tf_op jit(solution)/shard_map/ppermute | solution.py:232
  58.0 0.3 collective-permute-done.12
  58.3 1.6 %collective-permute-done.13 = bf16[8,768]{1,0:T(8,128)(2,1)S(1)} collective-permute-done((bf16[8,768]{1,0:T(8,128)(2,1)S(1)}, bf16[8,768]{1,0:T(8,128)(2,1)S(1)}, u32[]{:S(2)}, u32[]{:S(2)}) %collective-permute-start.13) | collective-permute-done | bytes 12320 | tf_op jit(solution)/shard_map/ppermute | solution.py:232
  59.9 0.6 %add_convert_fusion.2 = bf16[8,768]{1,0:T(8,128)(2,1)} fusion(bf16[8,768]{1,0:T(8,128)(2,1)S(1)} %collective-permute-done.13, bf16[8,768]{1,0:T(8,128)(2,1)S(1)} %collective-permute-done.12, bf16[8,768]{1,0:T(8,128)(2,1)S(1)} %collective-permute-done.11, bf16[8,1024]{1,0:T(8,128)(2,1)S(1)} %attention.1.refs_0_, bf16[8,3072]{1,0:T(8,128)(2,1)S(1)} %add_convert_fusion.1, ...), kind=kLoop, calls=%fused_computation.16 | loop fusion | flops 61440 | bytes 73732 | tf_op jit(solution)/shard_map/convert_element_type | solution.py:261
  (16 shorter events, 0.2 us)
Async XLA Ops:
  4.5 5.8 %collective-permute-start = (bf16[8,1024]{1,0:T(8,128)(2,1)S(1)}, bf16[8,1024]{1,0:T(8,128)(2,1)S(1)}, u32[]{:S(2)}, u32[]{:S(2)}) collective-permute-start(bf16[8,1024]{1,0:T(8,128)(2,1)S(1)} %attention.1.refs_0_), channel_id=1, source_target_pairs={{0,1},{1,0},{2,3},{3,2},{4,5},{5,4},{6,7},{7,6},{8,9},{9,8},{10,11... | collective-permute-start | bytes 49160 | tf_op jit(solution)/shard_map/ppermute | solution.py:232
  7.5 4.7 %collective-permute-start.1 = (bf16[8,1024]{1,0:T(8,128)(2,1)S(1)}, bf16[8,1024]{1,0:T(8,128)(2,1)S(1)}, u32[]{:S(2)}, u32[]{:S(2)}) collective-permute-start(bf16[8,1024]{1,0:T(8,128)(2,1)S(1)} %attention.1.refs_0_), channel_id=1, source_target_pairs={{0,2},{1,3},{2,0},{3,1},{4,6},{5,7},{6,4},{7,5},{8,10},{9,11},{10,... | collective-permute-start | bytes 49160 | tf_op jit(solution)/shard_map/ppermute | solution.py:232
  10.1 5.5 %collective-permute-start.2 = (bf16[8,1024]{1,0:T(8,128)(2,1)S(1)}, bf16[8,1024]{1,0:T(8,128)(2,1)S(1)}, u32[]{:S(2)}, u32[]{:S(2)}) collective-permute-start(bf16[8,1024]{1,0:T(8,128)(2,1)S(1)} %attention.1.refs_0_), channel_id=1, source_target_pairs={{0,3},{1,2},{2,1},{3,0},{4,7},{5,6},{6,5},{7,4},{8,11},{9,10},{10,... | collective-permute-start | bytes 49160 | tf_op jit(solution)/shard_map/ppermute | solution.py:232
  16.6 4.2 %collective-permute-start.3 = (bf16[8,3200]{1,0:T(8,128)(2,1)S(1)}, bf16[8,3200]{1,0:T(8,128)(2,1)S(1)}, u32[]{:S(2)}, u32[]{:S(2)}) collective-permute-start(bf16[8,3200]{1,0:T(8,128)(2,1)S(1)} %norm.1), channel_id=1, source_target_pairs={{0,4},{4,0},{8,12},{12,8},{1,5},{5,1},{9,13},{13,9},{2,6},{6,2},{1... | collective-permute-start | bytes 153608 | tf_op jit(solution)/shard_map/ppermute | solution.py:232
  18.1 4.1 %collective-permute-start.4 = (bf16[8,3200]{1,0:T(8,128)(2,1)S(1)}, bf16[8,3200]{1,0:T(8,128)(2,1)S(1)}, u32[]{:S(2)}, u32[]{:S(2)}) collective-permute-start(bf16[8,3200]{1,0:T(8,128)(2,1)S(1)} %norm.1), channel_id=1, source_target_pairs={{0,8},{4,12},{8,0},{12,4},{1,9},{5,13},{9,1},{13,5},{2,10},{6,14},... | collective-permute-start | bytes 153608 | tf_op jit(solution)/shard_map/ppermute | solution.py:232
  19.6 5.0 %collective-permute-start.5 = (bf16[8,3200]{1,0:T(8,128)(2,1)S(1)}, bf16[8,3200]{1,0:T(8,128)(2,1)S(1)}, u32[]{:S(2)}, u32[]{:S(2)}) collective-permute-start(bf16[8,3200]{1,0:T(8,128)(2,1)S(1)} %norm.1), channel_id=1, source_target_pairs={{0,12},{4,8},{8,4},{12,0},{1,13},{5,9},{9,5},{13,1},{2,14},{6,10},... | collective-permute-start | bytes 153608 | tf_op jit(solution)/shard_map/ppermute | solution.py:232
  24.6 1.5 %collective-permute-start.6 = (bf16[32,3200]{1,0:T(8,128)(2,1)S(1)}, bf16[32,3200]{1,0:T(8,128)(2,1)S(1)}, u32[]{:S(2)}, u32[]{:S(2)}) collective-permute-start(bf16[32,3200]{1,0:T(8,128)(2,1)S(1)} %pad_maximum_fusion), channel_id=1, source_target_pairs={{0,16},{16,0},{1,17},{17,1},{2,18},{18,2},{3,19},{19,3},{4,20},{20... | collective-permute-start | bytes 614408 | tf_op jit(solution)/shard_map/ppermute | solution.py:232
  45.8 1.5 %collective-permute-start.7 = (bf16[32,3072]{1,0:T(8,128)(2,1)S(1)}, bf16[32,3072]{1,0:T(8,128)(2,1)S(1)}, u32[]{:S(2)}, u32[]{:S(2)}) collective-permute-start(bf16[32,3072]{1,0:T(8,128)(2,1)S(1)} %slice.44), channel_id=1, source_target_pairs={{0,16},{16,0},{1,17},{17,1},{2,18},{18,2},{3,19},{19,3},{4,20},{20... | collective-permute-start | bytes 589832 | tf_op jit(solution)/shard_map/ppermute | solution.py:232
  47.4 5.3 %collective-permute-start.10 = (bf16[8,3072]{1,0:T(8,128)(2,1)S(1)}, bf16[8,3072]{1,0:T(8,128)(2,1)S(1)}, u32[]{:S(2)}, u32[]{:S(2)}) collective-permute-start(bf16[8,3072]{1,0:T(8,128)(2,1)S(1)} %get-tuple-element.6), channel_id=1, source_target_pairs={{0,12},{4,8},{8,4},{12,0},{1,13},{5,9},{9,5},{13,1},{2,14},{6,10},... | collective-permute-start | bytes 147464 | tf_op jit(solution)/shard_map/ppermute | solution.py:232
  47.9 4.7 %collective-permute-start.8 = (bf16[8,3072]{1,0:T(8,128)(2,1)S(1)}, bf16[8,3072]{1,0:T(8,128)(2,1)S(1)}, u32[]{:S(2)}, u32[]{:S(2)}) collective-permute-start(bf16[8,3072]{1,0:T(8,128)(2,1)S(1)} %get-tuple-element.5), channel_id=1, source_target_pairs={{0,4},{4,0},{8,12},{12,8},{1,5},{5,1},{9,13},{13,9},{2,6},{6,2},{1... | collective-permute-start | bytes 147464 | tf_op jit(solution)/shard_map/ppermute | solution.py:232
  49.4 4.1 %collective-permute-start.9 = (bf16[8,3072]{1,0:T(8,128)(2,1)S(1)}, bf16[8,3072]{1,0:T(8,128)(2,1)S(1)}, u32[]{:S(2)}, u32[]{:S(2)}) collective-permute-start(bf16[8,3072]{1,0:T(8,128)(2,1)S(1)} %get-tuple-element.7), channel_id=1, source_target_pairs={{0,8},{4,12},{8,0},{12,4},{1,9},{5,13},{9,1},{13,5},{2,10},{6,14},... | collective-permute-start | bytes 147464 | tf_op jit(solution)/shard_map/ppermute | solution.py:232
  53.6 4.5 %collective-permute-start.11 = (bf16[8,768]{1,0:T(8,128)(2,1)S(1)}, bf16[8,768]{1,0:T(8,128)(2,1)S(1)}, u32[]{:S(2)}, u32[]{:S(2)}) collective-permute-start(bf16[8,768]{1,0:T(8,128)(2,1)S(1)} %get-tuple-element.8), channel_id=1, source_target_pairs={{0,1},{1,0},{2,3},{3,2},{4,5},{5,4},{6,7},{7,6},{8,9},{9,8},{10,11... | collective-permute-start | bytes 36872 | tf_op jit(solution)/shard_map/ppermute | solution.py:232
  53.6 4.7 %collective-permute-start.12 = (bf16[8,768]{1,0:T(8,128)(2,1)S(1)}, bf16[8,768]{1,0:T(8,128)(2,1)S(1)}, u32[]{:S(2)}, u32[]{:S(2)}) collective-permute-start(bf16[8,768]{1,0:T(8,128)(2,1)S(1)} %get-tuple-element.10), channel_id=1, source_target_pairs={{0,2},{1,3},{2,0},{3,1},{4,6},{5,7},{6,4},{7,5},{8,10},{9,11},{10,... | collective-permute-start | bytes 36872 | tf_op jit(solution)/shard_map/ppermute | solution.py:232
  54.4 5.5 %collective-permute-start.13 = (bf16[8,768]{1,0:T(8,128)(2,1)S(1)}, bf16[8,768]{1,0:T(8,128)(2,1)S(1)}, u32[]{:S(2)}, u32[]{:S(2)}) collective-permute-start(bf16[8,768]{1,0:T(8,128)(2,1)S(1)} %get-tuple-element.9), channel_id=1, source_target_pairs={{0,3},{1,2},{2,1},{3,0},{4,7},{5,6},{6,5},{7,4},{8,11},{9,10},{10,... | collective-permute-start | bytes 36872 | tf_op jit(solution)/shard_map/ppermute | solution.py:232
where the time goes:
time: 60.8 us; the launch traced here: 60.5 us
  matrix products  19.5 us (32%)
  starting transfers between devices  17.5 us (29%)
  waiting for transfers between devices  17.1 us (28%)
  Pallas kernels  3.45 us (6%)
  local copies, waits for them, and re-layouts  1.37 us (2%)
  other arithmetic  0.9 us (1%)
  between operations  0.75 us (1%)
    ppermute x14, starting transfers between devices, send(): lax.ppermute(x, axis, [(i, i ^ mask) for i in range(lax.axis_size(axis))])  17.5 us
    ppermute x14, waiting for transfers between devices, send(): lax.ppermute(x, axis, [(i, i ^ mask) for i in range(lax.axis_size(axis))])  17.1 us
    dot_general x1, matrix products, run_expert(): out = jnp.dot(hidden, down_w[0], preferred_element_type=jnp.float32)  12.2 us
    dot_general x1, matrix products, run_expert(): lax.dot_general(x, gate_w[0], BY_ROW, preferred_element_type=jnp.float32)  7.32 us
    pallas_call x1, Pallas kernels, attend(): pl.pallas_call(functools.partial(attention_kernel, chunks=chunks), out_sh...  2.53 us
    reshape x1, local copies, waits for them, and re-layouts, attend(): norm_gain.reshape(1, -1)  1.26 us
  transfers between devices with their start and end apart: 14, of which 11 were waited for; matrix products, arithmetic and copies ran while one was open for 0% of the time, Pallas kernels for 0%

commit v1 on v0

--- a/solution.py
+++ b/solution.py
@@ -13,6 +13,7 @@
 SLOT = 36
 MASK_AT = 3 * SLOT
 MIB = 1 << 20
+CHUNKS = 6
 BY_ROW = (((1,), (1,)), ((), ()))
 
 
@@ -124,7 +125,8 @@
     blocks = range(len(streams))
     sums = put(sums, experts, streams)
     sums = put(sums, experts + 1, [x * x for x in streams])
-    gains = [gain_ref[:, b * HEAD_DIM : (b + 1) * HEAD_DIM].astype(jnp.float32) for b in blocks]
+    gain = gain_ref[...].astype(jnp.float32).reshape(1, -1)
+    gains = [gain[:, b * HEAD_DIM : (b + 1) * HEAD_DIM] for b in blocks]
     scaled = [x * g for x, g in zip(streams, gains)]
     for e in range(experts):
         weights = [router_ref[e : e + 1, b * HEAD_DIM : (b + 1) * HEAD_DIM].astype(jnp.float32) for b in blocks]
@@ -146,7 +148,7 @@
     key_heads = new_kv.shape[1] // (2 * HEAD_DIM)
     rows = columns // HEAD_DIM // key_heads * tokens
     chunks = 4
-    operands = [queries, new_kv, kv_cache, residual, routes.T, router, norm_gain.reshape(1, -1)]
+    operands = [queries, new_kv, kv_cache, residual, routes.T, router, norm_gain]
     operands = [pltpu.with_memory_space_constraint(x, pltpu.HBM) for x in operands]
     kept = [pltpu.VMEM(x.shape, x.dtype) for x in operands]
     kept[2] = pltpu.VMEM((slots, width), kv_cache.dtype)
@@ -171,7 +173,7 @@
     )(cache_len, *operands)
 
 
-def norm_kernel(place_ref, *refs, experts):
+def norm_kernel(place_ref, _, *refs, experts):
     pieces, out_ref = refs[:-1], refs[-1]
     tokens, wide = pieces[0].shape
     block = wide - 2 * LANES
@@ -200,32 +202,125 @@
         out_ref[:, pl.ds(at, block)] = x.astype(out_ref.dtype)
 
 
-def norm_rows(place, blocks, experts):
+def norm_rows(place, token, blocks, experts):
     tokens, wide = blocks[0].shape
     model = (wide - 2 * LANES) * len(blocks)
     vmem = pl.BlockSpec(memory_space=pltpu.VMEM)
     return pl.pallas_call(
         functools.partial(norm_kernel, experts=experts),
         out_shape=jax.ShapeDtypeStruct((tokens, model + LANES), jnp.bfloat16),
-        in_specs=[pl.BlockSpec(memory_space=pltpu.SMEM)] + [vmem] * len(blocks),
+        in_specs=[pl.BlockSpec(memory_space=pltpu.SMEM)] + [vmem] * (1 + len(blocks)),
         out_specs=vmem,
         compiler_params=pltpu.CompilerParams(vmem_limit_bytes=4 * MIB),
         name="norm",
-    )(place, *blocks)
-
-
-def run_expert(place, near, far, gate_w, up_w, down_w, experts):
-    model = gate_w.shape[2]
-    rows = jnp.concatenate([near, far], axis=0)
-    x, side = rows[:, :model], rows[:, model:].astype(jnp.float32)
-    lane = jnp.arange(side.shape[1])[None, :]
-    mine = (lane == place[1]) | (lane == place[1] + experts)
+    )(place, token, *blocks)
+
+
+def row_chunks(rows, most):
+    count = max(c for c in range(1, most + 1) if rows % (16 * c) == 0 or c == 1)
+    return [pl.ds(i * (rows // count), rows // count) for i in range(count)]
+
+
+def load_kernel(_, source, out_ref, token_ref, sems):
+    copies = [
+        pltpu.make_async_copy(source.at[0, part], out_ref.at[part], sems.at[i])
+        for i, part in enumerate(row_chunks(out_ref.shape[0], CHUNKS))
+    ]
+    for copy in copies:
+        copy.start()
+    token_ref[...] = jnp.zeros_like(token_ref)
+    for copy in copies:
+        copy.wait()
+
+
+def load(after, weight):
+    shape = weight.shape[1:]
+    return pl.pallas_call(
+        load_kernel,
+        out_shape=(pltpu.VMEM(shape, weight.dtype), jax.ShapeDtypeStruct((8, LANES), jnp.float32)),
+        in_specs=[pl.BlockSpec(memory_space=pl.ANY)] * 2,
+        out_specs=(pl.BlockSpec(memory_space=pltpu.VMEM),) * 2,
+        scratch_shapes=[pltpu.SemaphoreType.DMA((CHUNKS,))],
+        compiler_params=pltpu.CompilerParams(vmem_limit_bytes=MIB),
+        cost_estimate=pl.CostEstimate(flops=0, bytes_accessed=4 * shape[0] * shape[1], transcendentals=0),
+        name="load",
+    )(after, pltpu.with_memory_space_constraint(weight, pltpu.HBM))
+
+
+def stack_kernel(_, *refs):
+    pieces, out_ref = refs[:-1], refs[-1]
+    rows = 2 * pieces[0].shape[0]
+    for i in range(0, len(pieces), 2):
+        pair = [piece[...].astype(jnp.float32) for piece in pieces[i : i + 2]]
+        out_ref[i // 2 * rows : (i // 2 + 1) * rows] = jnp.concatenate(pair, axis=0).astype(out_ref.dtype)
+
+
+def stack_rows(token, pieces):
+    rows, wide = pieces[0].shape
+    vmem = pl.BlockSpec(memory_space=pltpu.VMEM)
+    return pl.pallas_call(
+        stack_kernel,
+        out_shape=jax.ShapeDtypeStruct((rows * len(pieces), wide), pieces[0].dtype),
+        in_specs=[vmem] * (1 + len(pieces)),
+        out_specs=vmem,
+        compiler_params=pltpu.CompilerParams(vmem_limit_bytes=4 * MIB),
+        name="stack",
+    )(token, *pieces)
+
+
+def expert_kernel(place_ref, near, far, gate, up, down_hbm, near_out, far_out, x, hidden, down, sems, *, experts):
+    units, model = gate.shape
+    half = near.shape[0]
+    copies = [
+        pltpu.make_async_copy(down_hbm.at[0, part], down.at[part], sems.at[i])
+        for i, part in enumerate(row_chunks(units, CHUNKS))
+    ]
+    for copy in copies:
+        copy.start()
+    x[:half] = near[:, :model]
+    x[half:] = far[:, :model]
+    side = jnp.concatenate([near[:, model:], far[:, model:]], axis=0).astype(jnp.float32)
+    lane = lax.broadcasted_iota(jnp.int32, side.shape, 1)
+    expert = place_ref[1]
+    mine = (lane == expert) | (lane == expert + experts)
     share = jnp.sum(jnp.where(mine, side, 0.0), axis=1, keepdims=True)
-    gate = lax.dot_general(x, gate_w[0], BY_ROW, preferred_element_type=jnp.float32)
-    up = lax.dot_general(x, up_w[0], BY_ROW, preferred_element_type=jnp.float32)
-    hidden = (jax.nn.silu(gate) * up).astype(jnp.bfloat16)
-    out = jnp.dot(hidden, down_w[0], preferred_element_type=jnp.float32)
-    return (out * share).astype(jnp.bfloat16)
+    for at in range(0, units, 256):
+        part = slice(at, min(at + 256, units))
+        a = lax.dot_general(x[...], gate[part], BY_ROW, preferred_element_type=jnp.float32)
+        b = lax.dot_general(x[...], up[part], BY_ROW, preferred_element_type=jnp.float32)
+        hidden[:, part] = (a / (1.0 + jnp.exp(-a)) * b).astype(hidden.dtype)
+    for copy in copies:
+        copy.wait()
+    step = model // 6
+    for at in range(0, model, step):
+        part = slice(at, at + step)
+        out = jnp.dot(hidden[...], down[:, part], preferred_element_type=jnp.float32) * share
+        near_out[:, part] = out[:half].astype(near_out.dtype)
+        far_out[:, part] = out[half:].astype(far_out.dtype)
+
+
+def run_expert(place, near, far, gate, up, down_w, experts):
+    units, model = gate.shape
+    rows = 2 * near.shape[0]
+    vmem = pl.BlockSpec(memory_space=pltpu.VMEM)
+    shape = jax.ShapeDtypeStruct((near.shape[0], model), jnp.bfloat16)
+    return pl.pallas_call(
+        functools.partial(expert_kernel, experts=experts),
+        out_shape=(shape, shape),
+        in_specs=[pl.BlockSpec(memory_space=pltpu.SMEM)] + [vmem] * 4 + [pl.BlockSpec(memory_space=pl.ANY)],
+        out_specs=(vmem, vmem),
+        scratch_shapes=[
+            pltpu.VMEM((rows, model), jnp.bfloat16),
+            pltpu.VMEM((rows, units), jnp.bfloat16),
+            pltpu.VMEM((units, model), down_w.dtype),
+            pltpu.SemaphoreType.DMA((CHUNKS,)),
+        ],
+        compiler_params=pltpu.CompilerParams(vmem_limit_bytes=20 * MIB),
+        cost_estimate=pl.CostEstimate(
+            flops=6 * rows * units * model, bytes_accessed=6 * units * model, transcendentals=rows * units
+        ),
+        name="experts",
+    )(place, near, far, gate, up, pltpu.with_memory_space_constraint(down_w, pltpu.HBM))
 
 
 def send(x, axis, mask):
@@ -247,13 +342,15 @@
 
     fresh = attend(cache_len, queries, new_kv, kv_cache, residual, routes, router, norm_gain)
     blocks = [fresh] + [send(fresh, "tensor", m) for m in range(1, tensors)]
-    rows = norm_rows(where, blocks, experts)
-    near = jnp.concatenate([rows] + [send(rows, "group", m) for m in range(1, groups)], axis=0)
+    gate, token = load(fresh, gate_w)
+    rows = norm_rows(where, token, blocks, experts)
+    arrived = [send(rows, "group", m) for m in range(1, groups)]
+    up, token = load(rows, up_w)
+    near = stack_rows(token, [rows] + arrived)
     far = send(near, "section", 1)
 
-    out = run_expert(where, near, far, gate_w, up_w, down_w, experts)
-    half = out.shape[0] // 2
-    both = add(out[:half], send(out[half:], "section", 1)).astype(jnp.bfloat16)
+    kept, other = run_expert(where, near, far, gate, up, down_w, experts)
+    both = add(kept, send(other, "section", 1)).astype(jnp.bfloat16)
     both = both.reshape(groups, tokens, -1)
     got = add(both[0], *[send(both[m], "group", m) for m in range(1, groups)]).astype(jnp.bfloat16)
     parts = [lax.dynamic_slice_in_dim(got, (place ^ m) * block, block, axis=1) for m in range(tensors)]

time: 60.8 us -> 54.3 us (0.89)
  Pallas kernels: 3.45 us -> 23.2 us
  matrix products: 19.5 us -> 0 us
  waiting for transfers between devices: 17.1 us -> 11.9 us
  local copies, waits for them, and re-layouts: 1.37 us -> 0.03 us
    pallas_call x0 -> x4, Pallas kernels: none -> 19.8 us  [the longest x1 11.5 us: run_expert(): pl.pallas_call(functools.partial(expert_kernel, experts=experts), out_sha...]
    dot_general x2 -> x0, matrix products: 19.5 us -> none  [the longest x1 12.2 us: run_expert(): out = jnp.dot(hidden, down_w[0], preferred_element_type=jnp.float32)]
    ppermute x14, waiting for transfers between devices: 17.1 us -> 11.9 us  [send(): lax.ppermute(x, axis, [(i, i ^ mask) for i in range(lax.axis_size(axis))])]
    reshape x1 -> x0, local copies, waits for them, and re-layouts: 1.26 us -> none  [attend(): norm_gain.reshape(1, -1)]
  transfers between devices with their start and end apart: 14 -> 14, of which waited for: 11 -> 9; matrix products, arithmetic and copies ran while one was open for 0% -> 0% of each run, Pallas kernels for 0% -> 15%
where the time goes in v1:
time: 54.3 us; the launch traced here: 54.1 us
  Pallas kernels  23.2 us (43%)
  starting transfers between devices  17.5 us (32%)
  waiting for transfers between devices  11.9 us (22%)
  between operations  0.77 us (1%)
  other arithmetic  0.76 us (1%)
    ppermute x14, starting transfers between devices, send(): lax.ppermute(x, axis, [(i, i ^ mask) for i in range(lax.axis_size(axis))])  17.5 us
    ppermute x14, waiting for transfers between devices, send(): lax.ppermute(x, axis, [(i, i ^ mask) for i in range(lax.axis_size(axis))])  11.9 us
    pallas_call x1, Pallas kernels, run_expert(): pl.pallas_call(functools.partial(expert_kernel, experts=experts), out_sha...  11.5 us
    pallas_call x2, Pallas kernels, load(): pl.pallas_call(load_kernel, out_shape=(pltpu.VMEM(shape, weight.dtype), j...  8.26 us
    pallas_call x1, Pallas kernels, attend(): pl.pallas_call(functools.partial(attention_kernel, chunks=chunks), out_sh...  2.53 us
  transfers between devices with their start and end apart: 14, of which 9 were waited for; matrix products, arithmetic and copies ran while one was open for 0% of the time, Pallas kernels for 15%

profile of v1, /device:TPU:0, one launch (start us, length us, event | category | flops | bytes accessed | tf_op | source)
XLA Modules:
  0.0 54.1 jit_solution(998766191669878653)
XLA Ops:
  0.7 2.5 %attention.1._.refs_0_ = bf16[8,1024]{1,0:T(8,128)(2,1)S(1)} custom-call(s32[1]{0:T(128)S(6)} %copy.12.len_ref, bf16[8,768]{1,0:T(8,128)(2,1)} %q_hbm.1, bf16[8,512]{1,0:T(8,128)(2,1)} %new_hbm.1, bf16[1,2048,512]{2,1,0:T(8,128)(2,1)} %kv_hbm.1, bf16[8,768]{1,0:T(8,128)(2,1)} %res_hbm.1, s32[4,8]{1,0:T(4,128)} %bitcast.3, bf16[8,768]{1,0:T(8,128)(2,1)} %router_hbm.1, ...), custom_call_target="tpu_custom_call" | custom-call | flops 50331648 | bytes 2097152 | tf_op jit(solution)/shard_map/attention/pallas_call | solution.py:155
  3.2 3.1 %collective-permute-start = (bf16[8,1024]{1,0:T(8,128)(2,1)S(1)}, bf16[8,1024]{1,0:T(8,128)(2,1)S(1)}, u32[]{:S(2)}, u32[]{:S(2)}) collective-permute-start(bf16[8,1024]{1,0:T(8,128)(2,1)S(1)} %attention.1._.refs_0_), channel_id=1, source_target_pairs={{0,1},{1,0},{2,3},{3,2},{4,5},{5,4},{6,7},{7,6},{8,9},{9,8},{10,11... | collective-permute-start | bytes 49160 | tf_op jit(solution)/shard_map/ppermute | solution.py:327
  6.3 2.6 %collective-permute-start.1 = (bf16[8,1024]{1,0:T(8,128)(2,1)S(1)}, bf16[8,1024]{1,0:T(8,128)(2,1)S(1)}, u32[]{:S(2)}, u32[]{:S(2)}) collective-permute-start(bf16[8,1024]{1,0:T(8,128)(2,1)S(1)} %attention.1._.refs_0_), channel_id=1, source_target_pairs={{0,2},{1,3},{2,0},{3,1},{4,6},{5,7},{6,4},{7,5},{8,10},{9,11},{10,... | collective-permute-start | bytes 49160 | tf_op jit(solution)/shard_map/ppermute | solution.py:327
  8.9 0.1 pad_add_fusion.place_ref
  8.9 4.1 %load.2 = (bf16[1728,3072]{1,0:T(8,128)(2,1)S(1)}, f32[8,128]{1,0:T(8,128)S(1)}) custom-call(bf16[8,1024]{1,0:T(8,128)(2,1)S(1)} %attention.1._.refs_0_, bf16[1,1728,3072]{2,1,0:T(8,128)(2,1)} %source.2), custom_call_target="tpu_custom_call" | custom-call | bytes 21233664 | tf_op jit(solution)/shard_map/load/pallas_call | solution.py:238
  13.1 0.0 collective-permute-done.refs_1_
  13.1 0.0 collective-permute-done.1.refs_2_
  13.1 1.3 %collective-permute-done.2.refs_3_ = bf16[8,1024]{1,0:T(8,128)(2,1)S(1)} collective-permute-done((bf16[8,1024]{1,0:T(8,128)(2,1)S(1)}, bf16[8,1024]{1,0:T(8,128)(2,1)S(1)}, u32[]{:S(2)}, u32[]{:S(2)}) %collective-permute-start.2) | collective-permute-done | bytes 16416 | tf_op jit(solution)/shard_map/ppermute | solution.py:327
  14.4 0.9 %norm.1._.refs_0_ = bf16[8,3200]{1,0:T(8,128)(2,1)S(1)} custom-call(s32[2]{0:T(128)S(1)} %pad_add_fusion.place_ref, f32[8,128]{1,0:T(8,128)S(1)} %get-tuple-element.11._, bf16[8,1024]{1,0:T(8,128)(2,1)S(1)} %attention.1._.refs_0_, bf16[8,1024]{1,0:T(8,128)(2,1)S(1)} %collective-permute-done.refs_1_, bf16[8,1024]{1,0:T(8,128)(2,1)S(1)} %collective-permute-done.1.refs_2_, ...), custom_call_target="tpu_custom_call" | custom-call | tf_op jit(solution)/shard_map/norm/pallas_call | solution.py:209
  15.3 1.5 %collective-permute-start.3 = (bf16[8,3200]{1,0:T(8,128)(2,1)S(1)}, bf16[8,3200]{1,0:T(8,128)(2,1)S(1)}, u32[]{:S(2)}, u32[]{:S(2)}) collective-permute-start(bf16[8,3200]{1,0:T(8,128)(2,1)S(1)} %norm.1._.refs_0_), channel_id=1, source_target_pairs={{0,4},{4,0},{8,12},{12,8},{1,5},{5,1},{9,13},{13,9},{2,6},{6,2},{1... | collective-permute-start | bytes 153608 | tf_op jit(solution)/shard_map/ppermute | solution.py:327
  16.8 1.5 %collective-permute-start.4 = (bf16[8,3200]{1,0:T(8,128)(2,1)S(1)}, bf16[8,3200]{1,0:T(8,128)(2,1)S(1)}, u32[]{:S(2)}, u32[]{:S(2)}) collective-permute-start(bf16[8,3200]{1,0:T(8,128)(2,1)S(1)} %norm.1._.refs_0_), channel_id=1, source_target_pairs={{0,8},{4,12},{8,0},{12,4},{1,9},{5,13},{9,1},{13,5},{2,10},{6,14},... | collective-permute-start | bytes 153608 | tf_op jit(solution)/shard_map/ppermute | solution.py:327
  18.4 0.5 collective-permute-start.5
  18.8 4.1 %load.3 = (bf16[1728,3072]{1,0:T(8,128)(2,1)S(1)}, f32[8,128]{1,0:T(8,128)S(1)}) custom-call(bf16[8,3200]{1,0:T(8,128)(2,1)S(1)} %norm.1._.refs_0_, bf16[1,1728,3072]{2,1,0:T(8,128)(2,1)} %source.3), custom_call_target="tpu_custom_call" | custom-call | bytes 21233664 | tf_op jit(solution)/shard_map/load/pallas_call | solution.py:238
  23.0 0.0 collective-permute-done.4.refs_2_
  23.0 0.4 collective-permute-done.5.refs_3_
  23.4 0.1 collective-permute-start.6
  23.5 1.4 %collective-permute-done.6.far = bf16[32,3200]{1,0:T(8,128)(2,1)S(1)} collective-permute-done((bf16[32,3200]{1,0:T(8,128)(2,1)S(1)}, bf16[32,3200]{1,0:T(8,128)(2,1)S(1)}, u32[]{:S(2)}, u32[]{:S(2)}) %collective-permute-start.6) | collective-permute-done | bytes 204832 | tf_op jit(solution)/shard_map/ppermute | solution.py:327
  24.9 11.5 %experts.1 = (bf16[32,3072]{1,0:T(8,128)(2,1)S(1)}, bf16[32,3072]{1,0:T(8,128)(2,1)S(1)}) custom-call(s32[2]{0:T(128)S(1)} %pad_add_fusion.place_ref, bf16[32,3200]{1,0:T(8,128)(2,1)S(1)} %stack.13.near, bf16[32,3200]{1,0:T(8,128)(2,1)S(1)} %collective-permute-done.6.far, bf16[1728,3072]{1,0:T(8,128)(2,1)S(1)} %get-tuple-element.13.gate, ...), custom_call_target="tpu_custom_call" | custom-call | flops 2038431744 | bytes 31850496 | tf_op jit(solution)/shard_map/experts/pallas_call | solution.py:307
  36.4 0.2 collective-permute-start.7
  36.6 1.3 %collective-permute-done.7 = bf16[32,3072]{1,0:T(8,128)(2,1)S(1)} collective-permute-done((bf16[32,3072]{1,0:T(8,128)(2,1)S(1)}, bf16[32,3072]{1,0:T(8,128)(2,1)S(1)}, u32[]{:S(2)}, u32[]{:S(2)}) %collective-permute-start.7) | collective-permute-done | bytes 196640 | tf_op jit(solution)/shard_map/ppermute | solution.py:327
  38.0 2.2 %collective-permute-start.10 = (bf16[8,3072]{1,0:T(8,128)(2,1)S(1)}, bf16[8,3072]{1,0:T(8,128)(2,1)S(1)}, u32[]{:S(2)}, u32[]{:S(2)}) collective-permute-start(bf16[8,3072]{1,0:T(8,128)(2,1)S(1)} %get-tuple-element.18), channel_id=1, source_target_pairs={{0,12},{4,8},{8,4},{12,0},{1,13},{5,9},{9,5},{13,1},{2,14},{6,10},... | collective-permute-start | bytes 147464 | tf_op jit(solution)/shard_map/ppermute | solution.py:327
  40.1 0.5 collective-permute-start.8
  40.7 0.9 %collective-permute-start.9 = (bf16[8,3072]{1,0:T(8,128)(2,1)S(1)}, bf16[8,3072]{1,0:T(8,128)(2,1)S(1)}, u32[]{:S(2)}, u32[]{:S(2)}) collective-permute-start(bf16[8,3072]{1,0:T(8,128)(2,1)S(1)} %get-tuple-element.19), channel_id=1, source_target_pairs={{0,8},{4,12},{8,0},{12,4},{1,9},{5,13},{9,1},{13,5},{2,10},{6,14},... | collective-permute-start | bytes 147464 | tf_op jit(solution)/shard_map/ppermute | solution.py:327
  41.5 2.0 %collective-permute-done.10 = bf16[8,3072]{1,0:T(8,128)(2,1)S(1)} collective-permute-done((bf16[8,3072]{1,0:T(8,128)(2,1)S(1)}, bf16[8,3072]{1,0:T(8,128)(2,1)S(1)}, u32[]{:S(2)}, u32[]{:S(2)}) %collective-permute-start.10) | collective-permute-done | bytes 49184 | tf_op jit(solution)/shard_map/ppermute | solution.py:327
  43.5 0.7 %collective-permute-done.8 = bf16[8,3072]{1,0:T(8,128)(2,1)S(1)} collective-permute-done((bf16[8,3072]{1,0:T(8,128)(2,1)S(1)}, bf16[8,3072]{1,0:T(8,128)(2,1)S(1)}, u32[]{:S(2)}, u32[]{:S(2)}) %collective-permute-start.8) | collective-permute-done | bytes 49184 | tf_op jit(solution)/shard_map/ppermute | solution.py:327
  44.2 0.5 collective-permute-done.9
  44.8 0.1 collective-permute-start.11
  44.9 3.1 %collective-permute-start.12 = (bf16[8,768]{1,0:T(8,128)(2,1)S(1)}, bf16[8,768]{1,0:T(8,128)(2,1)S(1)}, u32[]{:S(2)}, u32[]{:S(2)}) collective-permute-start(bf16[8,768]{1,0:T(8,128)(2,1)S(1)} %get-tuple-element.22), channel_id=1, source_target_pairs={{0,2},{1,3},{2,0},{3,1},{4,6},{5,7},{6,4},{7,5},{8,10},{9,11},{10,... | collective-permute-start | bytes 36872 | tf_op jit(solution)/shard_map/ppermute | solution.py:327
  48.0 1.3 %collective-permute-start.13 = (bf16[8,768]{1,0:T(8,128)(2,1)S(1)}, bf16[8,768]{1,0:T(8,128)(2,1)S(1)}, u32[]{:S(2)}, u32[]{:S(2)}) collective-permute-start(bf16[8,768]{1,0:T(8,128)(2,1)S(1)} %get-tuple-element.21), channel_id=1, source_target_pairs={{0,3},{1,2},{2,1},{3,0},{4,7},{5,6},{6,5},{7,4},{8,11},{9,10},{10,... | collective-permute-start | bytes 36872 | tf_op jit(solution)/shard_map/ppermute | solution.py:327
  49.3 0.4 collective-permute-done.12
  49.6 3.8 %collective-permute-done.13 = bf16[8,768]{1,0:T(8,128)(2,1)S(1)} collective-permute-done((bf16[8,768]{1,0:T(8,128)(2,1)S(1)}, bf16[8,768]{1,0:T(8,128)(2,1)S(1)}, u32[]{:S(2)}, u32[]{:S(2)}) %collective-permute-start.13) | collective-permute-done | bytes 12320 | tf_op jit(solution)/shard_map/ppermute | solution.py:327
  53.5 0.6 %add_convert_fusion.2 = bf16[8,768]{1,0:T(8,128)(2,1)} fusion(bf16[8,768]{1,0:T(8,128)(2,1)S(1)} %collective-permute-done.13, bf16[8,768]{1,0:T(8,128)(2,1)S(1)} %collective-permute-done.12, bf16[8,768]{1,0:T(8,128)(2,1)S(1)} %collective-permute-done.11, bf16[8,1024]{1,0:T(8,128)(2,1)S(1)} %attention.1._.refs_0_, bf16[8,3072]{1,0:T(8,128)(2,1)S(1)} %add_convert_fusion.1, ...), kind=kLoop, calls=%fused_computation.2 | loop fusion | flops 61440 | bytes 73732 | tf_op jit(solution)/shard_map/convert_element_type | solution.py:358
  (8 shorter events, 0.1 us)
Async XLA Ops:
  3.2 9.9 %collective-permute-start = (bf16[8,1024]{1,0:T(8,128)(2,1)S(1)}, bf16[8,1024]{1,0:T(8,128)(2,1)S(1)}, u32[]{:S(2)}, u32[]{:S(2)}) collective-permute-start(bf16[8,1024]{1,0:T(8,128)(2,1)S(1)} %attention.1._.refs_0_), channel_id=1, source_target_pairs={{0,1},{1,0},{2,3},{3,2},{4,5},{5,4},{6,7},{7,6},{8,9},{9,8},{10,11... | collective-permute-start | bytes 49160 | tf_op jit(solution)/shard_map/ppermute | solution.py:327
  6.3 6.8 %collective-permute-start.1 = (bf16[8,1024]{1,0:T(8,128)(2,1)S(1)}, bf16[8,1024]{1,0:T(8,128)(2,1)S(1)}, u32[]{:S(2)}, u32[]{:S(2)}) collective-permute-start(bf16[8,1024]{1,0:T(8,128)(2,1)S(1)} %attention.1._.refs_0_), channel_id=1, source_target_pairs={{0,2},{1,3},{2,0},{3,1},{4,6},{5,7},{6,4},{7,5},{8,10},{9,11},{10,... | collective-permute-start | bytes 49160 | tf_op jit(solution)/shard_map/ppermute | solution.py:327
  8.9 5.5 %collective-permute-start.2 = (bf16[8,1024]{1,0:T(8,128)(2,1)S(1)}, bf16[8,1024]{1,0:T(8,128)(2,1)S(1)}, u32[]{:S(2)}, u32[]{:S(2)}) collective-permute-start(bf16[8,1024]{1,0:T(8,128)(2,1)S(1)} %attention.1._.refs_0_), channel_id=1, source_target_pairs={{0,3},{1,2},{2,1},{3,0},{4,7},{5,6},{6,5},{7,4},{8,11},{9,10},{10,... | collective-permute-start | bytes 49160 | tf_op jit(solution)/shard_map/ppermute | solution.py:327
  15.3 7.6 %collective-permute-start.3 = (bf16[8,3200]{1,0:T(8,128)(2,1)S(1)}, bf16[8,3200]{1,0:T(8,128)(2,1)S(1)}, u32[]{:S(2)}, u32[]{:S(2)}) collective-permute-start(bf16[8,3200]{1,0:T(8,128)(2,1)S(1)} %norm.1._.refs_0_), channel_id=1, source_target_pairs={{0,4},{4,0},{8,12},{12,8},{1,5},{5,1},{9,13},{13,9},{2,6},{6,2},{1... | collective-permute-start | bytes 153608 | tf_op jit(solution)/shard_map/ppermute | solution.py:327
  16.8 6.1 %collective-permute-start.4 = (bf16[8,3200]{1,0:T(8,128)(2,1)S(1)}, bf16[8,3200]{1,0:T(8,128)(2,1)S(1)}, u32[]{:S(2)}, u32[]{:S(2)}) collective-permute-start(bf16[8,3200]{1,0:T(8,128)(2,1)S(1)} %norm.1._.refs_0_), channel_id=1, source_target_pairs={{0,8},{4,12},{8,0},{12,4},{1,9},{5,13},{9,1},{13,5},{2,10},{6,14},... | collective-permute-start | bytes 153608 | tf_op jit(solution)/shard_map/ppermute | solution.py:327
  18.4 5.0 %collective-permute-start.5 = (bf16[8,3200]{1,0:T(8,128)(2,1)S(1)}, bf16[8,3200]{1,0:T(8,128)(2,1)S(1)}, u32[]{:S(2)}, u32[]{:S(2)}) collective-permute-start(bf16[8,3200]{1,0:T(8,128)(2,1)S(1)} %norm.1._.refs_0_), channel_id=1, source_target_pairs={{0,12},{4,8},{8,4},{12,0},{1,13},{5,9},{9,5},{13,1},{2,14},{6,10},... | collective-permute-start | bytes 153608 | tf_op jit(solution)/shard_map/ppermute | solution.py:327
  23.4 1.5 %collective-permute-start.6 = (bf16[32,3200]{1,0:T(8,128)(2,1)S(1)}, bf16[32,3200]{1,0:T(8,128)(2,1)S(1)}, u32[]{:S(2)}, u32[]{:S(2)}) collective-permute-start(bf16[32,3200]{1,0:T(8,128)(2,1)S(1)} %stack.13.near), channel_id=1, source_target_pairs={{0,16},{16,0},{1,17},{17,1},{2,18},{18,2},{3,19},{19,3},{4,20},{20... | collective-permute-start | bytes 614408 | tf_op jit(solution)/shard_map/ppermute | solution.py:327
  36.4 1.5 %collective-permute-start.7 = (bf16[32,3072]{1,0:T(8,128)(2,1)S(1)}, bf16[32,3072]{1,0:T(8,128)(2,1)S(1)}, u32[]{:S(2)}, u32[]{:S(2)}) collective-permute-start(bf16[32,3072]{1,0:T(8,128)(2,1)S(1)} %get-tuple-element.16), channel_id=1, source_target_pairs={{0,16},{16,0},{1,17},{17,1},{2,18},{18,2},{3,19},{19,3},{4,20},{20... | collective-permute-start | bytes 589832 | tf_op jit(solution)/shard_map/ppermute | solution.py:327
  38.0 5.5 %collective-permute-start.10 = (bf16[8,3072]{1,0:T(8,128)(2,1)S(1)}, bf16[8,3072]{1,0:T(8,128)(2,1)S(1)}, u32[]{:S(2)}, u32[]{:S(2)}) collective-permute-start(bf16[8,3072]{1,0:T(8,128)(2,1)S(1)} %get-tuple-element.18), channel_id=1, source_target_pairs={{0,12},{4,8},{8,4},{12,0},{1,13},{5,9},{9,5},{13,1},{2,14},{6,10},... | collective-permute-start | bytes 147464 | tf_op jit(solution)/shard_map/ppermute | solution.py:327
  40.1 4.1 %collective-permute-start.8 = (bf16[8,3072]{1,0:T(8,128)(2,1)S(1)}, bf16[8,3072]{1,0:T(8,128)(2,1)S(1)}, u32[]{:S(2)}, u32[]{:S(2)}) collective-permute-start(bf16[8,3072]{1,0:T(8,128)(2,1)S(1)} %get-tuple-element.17), channel_id=1, source_target_pairs={{0,4},{4,0},{8,12},{12,8},{1,5},{5,1},{9,13},{13,9},{2,6},{6,2},{1... | collective-permute-start | bytes 147464 | tf_op jit(solution)/shard_map/ppermute | solution.py:327
  40.7 4.1 %collective-permute-start.9 = (bf16[8,3072]{1,0:T(8,128)(2,1)S(1)}, bf16[8,3072]{1,0:T(8,128)(2,1)S(1)}, u32[]{:S(2)}, u32[]{:S(2)}) collective-permute-start(bf16[8,3072]{1,0:T(8,128)(2,1)S(1)} %get-tuple-element.19), channel_id=1, source_target_pairs={{0,8},{4,12},{8,0},{12,4},{1,9},{5,13},{9,1},{13,5},{2,10},{6,14},... | collective-permute-start | bytes 147464 | tf_op jit(solution)/shard_map/ppermute | solution.py:327
  44.8 4.5 %collective-permute-start.11 = (bf16[8,768]{1,0:T(8,128)(2,1)S(1)}, bf16[8,768]{1,0:T(8,128)(2,1)S(1)}, u32[]{:S(2)}, u32[]{:S(2)}) collective-permute-start(bf16[8,768]{1,0:T(8,128)(2,1)S(1)} %get-tuple-element.20), channel_id=1, source_target_pairs={{0,1},{1,0},{2,3},{3,2},{4,5},{5,4},{6,7},{7,6},{8,9},{9,8},{10,11... | collective-permute-start | bytes 36872 | tf_op jit(solution)/shard_map/ppermute | solution.py:327
  44.9 4.8 %collective-permute-start.12 = (bf16[8,768]{1,0:T(8,128)(2,1)S(1)}, bf16[8,768]{1,0:T(8,128)(2,1)S(1)}, u32[]{:S(2)}, u32[]{:S(2)}) collective-permute-start(bf16[8,768]{1,0:T(8,128)(2,1)S(1)} %get-tuple-element.22), channel_id=1, source_target_pairs={{0,2},{1,3},{2,0},{3,1},{4,6},{5,7},{6,4},{7,5},{8,10},{9,11},{10,... | collective-permute-start | bytes 36872 | tf_op jit(solution)/shard_map/ppermute | solution.py:327
  48.0 5.5 %collective-permute-start.13 = (bf16[8,768]{1,0:T(8,128)(2,1)S(1)}, bf16[8,768]{1,0:T(8,128)(2,1)S(1)}, u32[]{:S(2)}, u32[]{:S(2)}) collective-permute-start(bf16[8,768]{1,0:T(8,128)(2,1)S(1)} %get-tuple-element.21), channel_id=1, source_target_pairs={{0,3},{1,2},{2,1},{3,0},{4,7},{5,6},{6,5},{7,4},{8,11},{9,10},{10,... | collective-permute-start | bytes 36872 | tf_op jit(solution)/shard_map/ppermute | solution.py:327

commit v2 on v0

--- a/solution.py
+++ b/solution.py
@@ -13,6 +13,8 @@
 SLOT = 36
 MASK_AT = 3 * SLOT
 MIB = 1 << 20
+CHUNKS = 4
+UNITS = 256
 BY_ROW = (((1,), (1,)), ((), ()))
 
 
@@ -124,7 +126,8 @@
     blocks = range(len(streams))
     sums = put(sums, experts, streams)
     sums = put(sums, experts + 1, [x * x for x in streams])
-    gains = [gain_ref[:, b * HEAD_DIM : (b + 1) * HEAD_DIM].astype(jnp.float32) for b in blocks]
+    gain = gain_ref[...].astype(jnp.float32).reshape(1, -1)
+    gains = [gain[:, b * HEAD_DIM : (b + 1) * HEAD_DIM] for b in blocks]
     scaled = [x * g for x, g in zip(streams, gains)]
     for e in range(experts):
         weights = [router_ref[e : e + 1, b * HEAD_DIM : (b + 1) * HEAD_DIM].astype(jnp.float32) for b in blocks]
@@ -146,7 +149,7 @@
     key_heads = new_kv.shape[1] // (2 * HEAD_DIM)
     rows = columns // HEAD_DIM // key_heads * tokens
     chunks = 4
-    operands = [queries, new_kv, kv_cache, residual, routes.T, router, norm_gain.reshape(1, -1)]
+    operands = [queries, new_kv, kv_cache, residual, routes.T, router, norm_gain]
     operands = [pltpu.with_memory_space_constraint(x, pltpu.HBM) for x in operands]
     kept = [pltpu.VMEM(x.shape, x.dtype) for x in operands]
     kept[2] = pltpu.VMEM((slots, width), kv_cache.dtype)
@@ -171,8 +174,51 @@
     )(cache_len, *operands)
 
 
-def norm_kernel(place_ref, *refs, experts):
-    pieces, out_ref = refs[:-1], refs[-1]
+def unit_parts(units):
+    first = max(UNITS, units * 3 // 4 // UNITS * UNITS)
+    if units <= 2 * UNITS:
+        first = units // 32 * 16
+    return pl.ds(0, first), pl.ds(first, units - first)
+
+
+def start_load(source, target, part, sems):
+    count = max(c for c in range(1, CHUNKS + 1) if part.size % (16 * c) == 0 or c == 1)
+    step = part.size // count
+    copies = [
+        pltpu.make_async_copy(
+            source.at[0, pl.ds(part.start + i * step, step)], target.at[pl.ds(i * step, step)], sems.at[i]
+        )
+        for i in range(count)
+    ]
+    for copy in copies:
+        copy.start()
+    return copies
+
+
+def load_kernel(_, source, out_ref, token_ref, sems, *, part):
+    copies = start_load(source, out_ref, part, sems)
+    token_ref[...] = jnp.zeros_like(token_ref)
+    for copy in copies:
+        copy.wait()
+
+
+def load(after, weight, part):
+    shape = (part.size, weight.shape[2])
+    return pl.pallas_call(
+        functools.partial(load_kernel, part=part),
+        out_shape=(pltpu.VMEM(shape, weight.dtype), jax.ShapeDtypeStruct((8, LANES), jnp.float32)),
+        in_specs=[pl.BlockSpec(memory_space=pl.ANY)] * 2,
+        out_specs=(pl.BlockSpec(memory_space=pltpu.VMEM),) * 2,
+        scratch_shapes=[pltpu.SemaphoreType.DMA((CHUNKS,))],
+        compiler_params=pltpu.CompilerParams(vmem_limit_bytes=MIB),
+        cost_estimate=pl.CostEstimate(flops=0, bytes_accessed=4 * shape[0] * shape[1], transcendentals=0),
+        name="load",
+    )(after, pltpu.with_memory_space_constraint(weight, pltpu.HBM))
+
+
+def norm_kernel(place_ref, _, source, *refs, experts, part):
+    pieces, (out_ref, rest_ref, sems) = refs[:-3], refs[-3:]
+    copies = start_load(source, rest_ref, part, sems)
     tokens, wide = pieces[0].shape
     block = wide - 2 * LANES
     model = len(pieces) * block
@@ -192,44 +238,103 @@
     high = share.astype(jnp.bfloat16).astype(jnp.float32)
     side = high + pltpu.roll(share - high, experts, 1)
     out_ref[:, model:] = side.astype(out_ref.dtype)
-    for mask, piece in enumerate(pieces):
+    for mask, piece in enumerate(reversed(pieces)):
         gain = piece[:, block + LANES :].astype(jnp.float32)
         gain = jnp.concatenate([gain[j : j + 1, :] for j in range(block // LANES)], axis=1)
         x = (piece[:, :block].astype(jnp.float32) - mean) * inv * gain
         at = pl.multiple_of(lax.bitwise_xor(place_ref[0], mask) * block, block)
         out_ref[:, pl.ds(at, block)] = x.astype(out_ref.dtype)
-
-
-def norm_rows(place, blocks, experts):
+    for copy in copies:
+        copy.wait()
+
+
+def norm_rows(place, token, weight, part, blocks, experts):
     tokens, wide = blocks[0].shape
     model = (wide - 2 * LANES) * len(blocks)
     vmem = pl.BlockSpec(memory_space=pltpu.VMEM)
     return pl.pallas_call(
-        functools.partial(norm_kernel, experts=experts),
-        out_shape=jax.ShapeDtypeStruct((tokens, model + LANES), jnp.bfloat16),
-        in_specs=[pl.BlockSpec(memory_space=pltpu.SMEM)] + [vmem] * len(blocks),
+        functools.partial(norm_kernel, experts=experts, part=part),
+        out_shape=(
+            jax.ShapeDtypeStruct((tokens, model + LANES), jnp.bfloat16),
+            pltpu.VMEM((part.size, weight.shape[2]), weight.dtype),
+        ),
+        in_specs=[pl.BlockSpec(memory_space=pltpu.SMEM), vmem, pl.BlockSpec(memory_space=pl.ANY)]
+        + [vmem] * len(blocks),
+        out_specs=(vmem, vmem),
+        scratch_shapes=[pltpu.SemaphoreType.DMA((CHUNKS,))],
+        compiler_params=pltpu.CompilerParams(vmem_limit_bytes=4 * MIB),
+        name="norm",
+    )(place, token, pltpu.with_memory_space_constraint(weight, pltpu.HBM), *blocks)
+
+
+def stack_kernel(_, *refs):
+    pieces, out_ref = refs[:-1][::-1], refs[-1]
+    rows = 2 * pieces[0].shape[0]
+    for i in range(0, len(pieces), 2):
+        pair = [piece[...].astype(jnp.float32) for piece in pieces[i : i + 2]]
+        out_ref[i // 2 * rows : (i // 2 + 1) * rows] = jnp.concatenate(pair, axis=0).astype(out_ref.dtype)
+
+
+def stack_rows(token, pieces):
+    rows, wide = pieces[0].shape
+    vmem = pl.BlockSpec(memory_space=pltpu.VMEM)
+    return pl.pallas_call(
+        stack_kernel,
+        out_shape=jax.ShapeDtypeStruct((rows * len(pieces), wide), pieces[0].dtype),
+        in_specs=[vmem] * (1 + len(pieces)),
         out_specs=vmem,
         compiler_params=pltpu.CompilerParams(vmem_limit_bytes=4 * MIB),
-        name="norm",
-    )(place, *blocks)
-
-
-def run_expert(place, near, far, gate_w, up_w, down_w, experts):
-    model = gate_w.shape[2]
-    rows = jnp.concatenate([near, far], axis=0)
-    x, side = rows[:, :model], rows[:, model:].astype(jnp.float32)
-    lane = jnp.arange(side.shape[1])[None, :]
-    mine = (lane == place[1]) | (lane == place[1] + experts)
+        name="stack",
+    )(token, *pieces)
+
+
+def hidden_kernel(place_ref, near, far, gate_a, gate_b, up_a, up_b, _, hidden, x, *, experts):
+    half = near.shape[0]
+    model = gate_a.shape[1]
+    x[:half] = near[:, :model]
+    x[half:] = far[:, :model]
+    side = jnp.concatenate([near[:, model:], far[:, model:]], axis=0).astype(jnp.float32)
+    lane = lax.broadcasted_iota(jnp.int32, side.shape, 1)
+    expert = place_ref[1]
+    mine = (lane == expert) | (lane == expert + experts)
     share = jnp.sum(jnp.where(mine, side, 0.0), axis=1, keepdims=True)
-    gate = lax.dot_general(x, gate_w[0], BY_ROW, preferred_element_type=jnp.float32)
-    up = lax.dot_general(x, up_w[0], BY_ROW, preferred_element_type=jnp.float32)
-    hidden = (jax.nn.silu(gate) * up).astype(jnp.bfloat16)
-    out = jnp.dot(hidden, down_w[0], preferred_element_type=jnp.float32)
-    return (out * share).astype(jnp.bfloat16)
+    first = 0
+    for gate, up in ((gate_a, up_a), (gate_b, up_b)):
+        units = gate.shape[0]
+        for at in range(0, units, UNITS):
+            part = slice(at, min(at + UNITS, units))
+            a = lax.dot_general(x[...], gate[part], BY_ROW, preferred_element_type=jnp.float32)
+            b = lax.dot_general(x[...], up[part], BY_ROW, preferred_element_type=jnp.float32)
+            out = a / (1.0 + jnp.exp(-a)) * b * share
+            hidden[:, first + part.start : first + part.stop] = out.astype(hidden.dtype)
+        first += units
+
+
+def run_hidden(place, near, far, weights, token, experts):
+    units = weights[0].shape[0] + weights[1].shape[0]
+    model = weights[0].shape[1]
+    rows = 2 * near.shape[0]
+    vmem = pl.BlockSpec(memory_space=pltpu.VMEM)
+    return pl.pallas_call(
+        functools.partial(hidden_kernel, experts=experts),
+        out_shape=jax.ShapeDtypeStruct((rows, units), jnp.bfloat16),
+        in_specs=[pl.BlockSpec(memory_space=pltpu.SMEM)] + [vmem] * 7,
+        out_specs=vmem,
+        scratch_shapes=[pltpu.VMEM((rows, model), jnp.bfloat16)],
+        compiler_params=pltpu.CompilerParams(vmem_limit_bytes=6 * MIB),
+        cost_estimate=pl.CostEstimate(
+            flops=4 * rows * units * model, bytes_accessed=4 * units * model, transcendentals=rows * units
+        ),
+        name="hidden",
+    )(place, near, far, *weights, token)
 
 
 def send(x, axis, mask):
     return lax.ppermute(x, axis, [(i, i ^ mask) for i in range(lax.axis_size(axis))])
+
+
+def exchange(parts, axis):
+    return [send(parts[m], axis, m) for m in reversed(range(1, lax.axis_size(axis)))]
 
 
 def add(*terms):
@@ -245,19 +350,26 @@
     place = lax.axis_index("tensor")
     where = jnp.stack([place, lax.axis_index("section") * tensors + place]).astype(jnp.int32)
 
+    early, late = unit_parts(gate_w.shape[1])
+
     fresh = attend(cache_len, queries, new_kv, kv_cache, residual, routes, router, norm_gain)
-    blocks = [fresh] + [send(fresh, "tensor", m) for m in range(1, tensors)]
-    rows = norm_rows(where, blocks, experts)
-    near = jnp.concatenate([rows] + [send(rows, "group", m) for m in range(1, groups)], axis=0)
+    blocks = exchange([fresh] * tensors, "tensor") + [fresh]
+    gate_a, token = load(fresh, gate_w, early)
+    rows, gate_b = norm_rows(where, token, gate_w, late, blocks, experts)
+    ranks = exchange([rows] * groups, "group") + [rows]
+    up_a, token = load(rows, up_w, early)
+    near = stack_rows(token, ranks)
     far = send(near, "section", 1)
-
-    out = run_expert(where, near, far, gate_w, up_w, down_w, experts)
+    up_b, token = load(near, up_w, late)
+
+    hidden = run_hidden(where, near, far, (gate_a, gate_b, up_a, up_b), token, experts)
+    out = jnp.dot(hidden, down_w[0], preferred_element_type=jnp.float32).astype(jnp.bfloat16)
     half = out.shape[0] // 2
     both = add(out[:half], send(out[half:], "section", 1)).astype(jnp.bfloat16)
     both = both.reshape(groups, tokens, -1)
-    got = add(both[0], *[send(both[m], "group", m) for m in range(1, groups)]).astype(jnp.bfloat16)
+    got = add(*exchange(both, "group"), both[0]).astype(jnp.bfloat16)
     parts = [lax.dynamic_slice_in_dim(got, (place ^ m) * block, block, axis=1) for m in range(tensors)]
-    mixed = add(fresh[:, :block], parts[0], *[send(parts[m], "tensor", m) for m in range(1, tensors)])
+    mixed = add(*exchange(parts, "tensor"), parts[0], fresh[:, :block])
     return mixed.astype(jnp.bfloat16)
 
 

time: 60.8 us -> 51.3 us (0.84)
  matrix products: 19.5 us -> 1.97 us
  Pallas kernels: 3.45 us -> 20.6 us
  waiting for transfers between devices: 17.1 us -> 8.92 us
  local copies, waits for them, and re-layouts: 1.37 us -> 0.06 us
    dot_general x2 -> x1, matrix products: 19.5 us -> 1.97 us  [per_device(): jnp.dot(hidden, down_w[0], preferred_element_type=jnp.float32)]
    pallas_call x1 -> x6, Pallas kernels: 0.92 us -> 18.1 us  [the longest x3 8.6 us: load(): pl.pallas_call(functools.partial(load_kernel, part=part), out_shape=(pltp...]
    ppermute x14, waiting for transfers between devices: 17.1 us -> 8.92 us  [send(): lax.ppermute(x, axis, [(i, i ^ mask) for i in range(lax.axis_size(axis))])]
    reshape x1 -> x0, local copies, waits for them, and re-layouts: 1.26 us -> none  [attend(): norm_gain.reshape(1, -1)]
  transfers between devices with their start and end apart: 14 -> 14, of which waited for: 11 -> 8; matrix products, arithmetic and copies ran while one was open for 0% -> 0% of each run, Pallas kernels for 0% -> 17%
where the time goes in v2:
time: 51.3 us; the launch traced here: 51.1 us
  Pallas kernels  20.6 us (40%)
  starting transfers between devices  17.9 us (35%)
  waiting for transfers between devices  8.92 us (17%)
  matrix products  1.97 us (4%)
  between operations  0.85 us (2%)
  other arithmetic  0.77 us (2%)
    ppermute x14, starting transfers between devices, send(): lax.ppermute(x, axis, [(i, i ^ mask) for i in range(lax.axis_size(axis))])  17.9 us
    ppermute x14, waiting for transfers between devices, send(): lax.ppermute(x, axis, [(i, i ^ mask) for i in range(lax.axis_size(axis))])  8.92 us
    pallas_call x3, Pallas kernels, load(): pl.pallas_call(functools.partial(load_kernel, part=part), out_shape=(pltp...  8.6 us
    pallas_call x1, Pallas kernels, run_hidden(): pl.pallas_call(functools.partial(hidden_kernel, experts=experts), out_sha...  7.12 us
    pallas_call x1, Pallas kernels, attend(): pl.pallas_call(functools.partial(attention_kernel, chunks=chunks), out_sh...  2.53 us
    pallas_call x1, Pallas kernels, norm_rows(): pl.pallas_call(functools.partial(norm_kernel, experts=experts, part=part)...  2.34 us
    dot_general x1, matrix products, per_device(): jnp.dot(hidden, down_w[0], preferred_element_type=jnp.float32)  1.97 us
  transfers between devices with their start and end apart: 14, of which 8 were waited for; matrix products, arithmetic and copies ran while one was open for 0% of the time, Pallas kernels for 17%

profile of v2, /device:TPU:0, one launch (start us, length us, event | category | flops | bytes accessed | tf_op | source)
XLA Modules:
  0.0 51.1 jit_solution(468622779070642246)
XLA Ops:
  0.7 2.5 %attention.1._.refs_3_ = bf16[8,1024]{1,0:T(8,128)(2,1)S(1)} custom-call(s32[1]{0:T(128)S(6)} %copy.12.len_ref, bf16[8,768]{1,0:T(8,128)(2,1)} %q_hbm.1, bf16[8,512]{1,0:T(8,128)(2,1)} %new_hbm.1, bf16[1,2048,512]{2,1,0:T(8,128)(2,1)} %kv_hbm.1, bf16[8,768]{1,0:T(8,128)(2,1)} %res_hbm.1, s32[4,8]{1,0:T(4,128)} %bitcast.11, bf16[8,768]{1,0:T(8,128)(2,1)} %router_hbm.1, ...), custom_call_target="tpu_custom_call" | custom-call | flops 50331648 | bytes 2097152 | tf_op jit(solution)/shard_map/attention/pallas_call | solution.py:156
  3.2 5.1 %collective-permute-start = (bf16[8,1024]{1,0:T(8,128)(2,1)S(1)}, bf16[8,1024]{1,0:T(8,128)(2,1)S(1)}, u32[]{:S(2)}, u32[]{:S(2)}) collective-permute-start(bf16[8,1024]{1,0:T(8,128)(2,1)S(1)} %attention.1._.refs_3_), channel_id=1, source_target_pairs={{0,3},{1,2},{2,1},{3,0},{4,7},{5,6},{6,5},{7,4},{8,11},{9,10},{10,... | collective-permute-start | bytes 49160 | tf_op jit(solution)/shard_map/ppermute | solution.py:333
  8.3 0.0 collective-permute-start.1
  8.3 0.6 %collective-permute-start.2 = (bf16[8,1024]{1,0:T(8,128)(2,1)S(1)}, bf16[8,1024]{1,0:T(8,128)(2,1)S(1)}, u32[]{:S(2)}, u32[]{:S(2)}) collective-permute-start(bf16[8,1024]{1,0:T(8,128)(2,1)S(1)} %attention.1._.refs_3_), channel_id=1, source_target_pairs={{0,1},{1,0},{2,3},{3,2},{4,5},{5,4},{6,7},{7,6},{8,9},{9,8},{10,11... | collective-permute-start | bytes 49160 | tf_op jit(solution)/shard_map/ppermute | solution.py:333
  8.9 0.1 pad_add_fusion.place_ref
  9.0 3.3 %load.3 = (bf16[1280,3072]{1,0:T(8,128)(2,1)S(1)}, f32[8,128]{1,0:T(8,128)S(1)}) custom-call(bf16[8,1024]{1,0:T(8,128)(2,1)S(1)} %attention.1._.refs_3_, bf16[1,1728,3072]{2,1,0:T(8,128)(2,1)} %source.5), custom_call_target="tpu_custom_call" | custom-call | bytes 15728640 | tf_op jit(solution)/shard_map/load/pallas_call | solution.py:207
  12.4 0.6 %collective-permute-done.1.refs_1_ = bf16[8,1024]{1,0:T(8,128)(2,1)S(1)} collective-permute-done((bf16[8,1024]{1,0:T(8,128)(2,1)S(1)}, bf16[8,1024]{1,0:T(8,128)(2,1)S(1)}, u32[]{:S(2)}, u32[]{:S(2)}) %collective-permute-start.1) | collective-permute-done | bytes 16416 | tf_op jit(solution)/shard_map/ppermute | solution.py:333
  12.9 2.3 %norm.1 = (bf16[8,3200]{1,0:T(8,128)(2,1)S(1)}, bf16[448,3072]{1,0:T(8,128)(2,1)S(1)}) custom-call(s32[2]{0:T(128)S(1)} %pad_add_fusion.place_ref, f32[8,128]{1,0:T(8,128)S(1)} %get-tuple-element.13._, bf16[1,1728,3072]{2,1,0:T(8,128)(2,1)} %source.5, bf16[8,1024]{1,0:T(8,128)(2,1)S(1)} %collective-permute-done.refs_0_, ...), custom_call_target="tpu_custom_call" | custom-call | tf_op jit(solution)/shard_map/norm/pallas_call | solution.py:255
  15.3 2.5 %collective-permute-start.3 = (bf16[8,3200]{1,0:T(8,128)(2,1)S(1)}, bf16[8,3200]{1,0:T(8,128)(2,1)S(1)}, u32[]{:S(2)}, u32[]{:S(2)}) collective-permute-start(bf16[8,3200]{1,0:T(8,128)(2,1)S(1)} %get-tuple-element.14._.refs_3_), channel_id=1, source_target_pairs={{0,12},{4,8},{8,4},{12,0},{1,13},{5,9},{9,5},{13,1},{2,14},{6,10},... | collective-permute-start | bytes 153608 | tf_op jit(solution)/shard_map/ppermute | solution.py:333
  17.8 0.5 collective-permute-start.4
  18.3 0.5 %collective-permute-start.5 = (bf16[8,3200]{1,0:T(8,128)(2,1)S(1)}, bf16[8,3200]{1,0:T(8,128)(2,1)S(1)}, u32[]{:S(2)}, u32[]{:S(2)}) collective-permute-start(bf16[8,3200]{1,0:T(8,128)(2,1)S(1)} %get-tuple-element.14._.refs_3_), channel_id=1, source_target_pairs={{0,4},{4,0},{8,12},{12,8},{1,5},{5,1},{9,13},{13,9},{2,6},{6,2},{1... | collective-permute-start | bytes 153608 | tf_op jit(solution)/shard_map/ppermute | solution.py:333
  18.8 3.3 %load.4 = (bf16[1280,3072]{1,0:T(8,128)(2,1)S(1)}, f32[8,128]{1,0:T(8,128)S(1)}) custom-call(bf16[8,3200]{1,0:T(8,128)(2,1)S(1)} %get-tuple-element.14._.refs_3_, bf16[1,1728,3072]{2,1,0:T(8,128)(2,1)} %source.7), custom_call_target="tpu_custom_call" | custom-call | bytes 15728640 | tf_op jit(solution)/shard_map/load/pallas_call | solution.py:207
  22.2 0.2 collective-permute-done.5.refs_2_
  22.4 0.1 collective-permute-start.6
  22.5 0.0 slice-start
  22.5 1.9 %load.5 = (bf16[448,3072]{1,0:T(8,128)(2,1)S(1)}, f32[8,128]{1,0:T(8,128)S(1)}) custom-call(bf16[32,3200]{1,0:T(8,128)(2,1)S(1)} %stack.13._.near, bf16[1,1728,3072]{2,1,0:T(8,128)(2,1)} %source.7), custom_call_target="tpu_custom_call" | custom-call | bytes 5505024 | tf_op jit(solution)/shard_map/load/pallas_call | solution.py:207
  24.5 0.0 slice-start.1
  24.5 7.1 %hidden.1 = bf16[64,1728]{1,0:T(8,128)(2,1)S(1)} custom-call(s32[2]{0:T(128)S(1)} %pad_add_fusion.place_ref, bf16[32,3200]{1,0:T(8,128)(2,1)S(1)} %stack.13._.near, bf16[32,3200]{1,0:T(8,128)(2,1)S(1)} %collective-permute-done.6.far, bf16[1280,3072]{1,0:T(8,128)(2,1)S(1)} %get-tuple-element.16.gate_a, bf16[448,3072]{1,0:T(8,128)(2,1)S(1)} %get-tuple-element.17.gate_b, ...), custom_call_target="tpu_custom_call" | custom-call | flops 1358954496 | bytes 21233664 | tf_op jit(solution)/shard_map/hidden/pallas_call | solution.py:318
  31.7 2.0 %fusion.2 = bf16[64,3072]{1,0:T(8,128)(2,1)S(1)} fusion(bf16[64,1728]{1,0:T(8,128)(2,1)S(1)} %hidden.1, bf16[1,1728,3072]{2,1,0:T(8,128)(2,1)S(1)} %bitcast.10), kind=kOutput, calls=%fused_computation.2 | convolution fusion | flops 679673856 | bytes 11231232 | tf_op jit(solution)/shard_map/dot_general | solution.py:366
  33.7 0.6 %collective-permute-start.7 = (bf16[32,3072]{1,0:T(8,128)(2,1)S(1)}, bf16[32,3072]{1,0:T(8,128)(2,1)S(1)}, u32[]{:S(2)}, u32[]{:S(2)}) collective-permute-start(bf16[32,3072]{1,0:T(8,128)(2,1)S(1)} %slice.33), channel_id=1, source_target_pairs={{0,16},{16,0},{1,17},{17,1},{2,18},{18,2},{3,19},{19,3},{4,20},{20... | collective-permute-start | bytes 589832 | tf_op jit(solution)/shard_map/ppermute | solution.py:333
  34.2 1.1 %collective-permute-done.7 = bf16[32,3072]{1,0:T(8,128)(2,1)S(1)} collective-permute-done((bf16[32,3072]{1,0:T(8,128)(2,1)S(1)}, bf16[32,3072]{1,0:T(8,128)(2,1)S(1)}, u32[]{:S(2)}, u32[]{:S(2)}) %collective-permute-start.7) | collective-permute-done | bytes 196640 | tf_op jit(solution)/shard_map/ppermute | solution.py:333
  35.3 1.4 %collective-permute-start.10 = (bf16[8,3072]{1,0:T(8,128)(2,1)S(1)}, bf16[8,3072]{1,0:T(8,128)(2,1)S(1)}, u32[]{:S(2)}, u32[]{:S(2)}) collective-permute-start(bf16[8,3072]{1,0:T(8,128)(2,1)S(1)} %get-tuple-element.22), channel_id=1, source_target_pairs={{0,4},{4,0},{8,12},{12,8},{1,5},{5,1},{9,13},{13,9},{2,6},{6,2},{1... | collective-permute-start | bytes 147464 | tf_op jit(solution)/shard_map/ppermute | solution.py:333
  36.7 1.7 %collective-permute-start.8 = (bf16[8,3072]{1,0:T(8,128)(2,1)S(1)}, bf16[8,3072]{1,0:T(8,128)(2,1)S(1)}, u32[]{:S(2)}, u32[]{:S(2)}) collective-permute-start(bf16[8,3072]{1,0:T(8,128)(2,1)S(1)} %get-tuple-element.21), channel_id=1, source_target_pairs={{0,12},{4,8},{8,4},{12,0},{1,13},{5,9},{9,5},{13,1},{2,14},{6,10},... | collective-permute-start | bytes 147464 | tf_op jit(solution)/shard_map/ppermute | solution.py:333
  38.4 0.5 collective-permute-start.9
  38.9 0.6 %collective-permute-done.10 = bf16[8,3072]{1,0:T(8,128)(2,1)S(1)} collective-permute-done((bf16[8,3072]{1,0:T(8,128)(2,1)S(1)}, bf16[8,3072]{1,0:T(8,128)(2,1)S(1)}, u32[]{:S(2)}, u32[]{:S(2)}) %collective-permute-start.10) | collective-permute-done | bytes 49184 | tf_op jit(solution)/shard_map/ppermute | solution.py:333
  39.5 2.3 %collective-permute-done.8 = bf16[8,3072]{1,0:T(8,128)(2,1)S(1)} collective-permute-done((bf16[8,3072]{1,0:T(8,128)(2,1)S(1)}, bf16[8,3072]{1,0:T(8,128)(2,1)S(1)}, u32[]{:S(2)}, u32[]{:S(2)}) %collective-permute-start.8) | collective-permute-done | bytes 49184 | tf_op jit(solution)/shard_map/ppermute | solution.py:333
  41.8 0.8 %collective-permute-done.9 = bf16[8,3072]{1,0:T(8,128)(2,1)S(1)} collective-permute-done((bf16[8,3072]{1,0:T(8,128)(2,1)S(1)}, bf16[8,3072]{1,0:T(8,128)(2,1)S(1)}, u32[]{:S(2)}, u32[]{:S(2)}) %collective-permute-start.9) | collective-permute-done | bytes 49184 | tf_op jit(solution)/shard_map/ppermute | solution.py:333
  42.6 3.3 %collective-permute-start.11 = (bf16[8,768]{1,0:T(8,128)(2,1)S(1)}, bf16[8,768]{1,0:T(8,128)(2,1)S(1)}, u32[]{:S(2)}, u32[]{:S(2)}) collective-permute-start(bf16[8,768]{1,0:T(8,128)(2,1)S(1)} %get-tuple-element.24), channel_id=1, source_target_pairs={{0,3},{1,2},{2,1},{3,0},{4,7},{5,6},{6,5},{7,4},{8,11},{9,10},{10,... | collective-permute-start | bytes 36872 | tf_op jit(solution)/shard_map/ppermute | solution.py:333
  45.9 1.2 %collective-permute-start.13 = (bf16[8,768]{1,0:T(8,128)(2,1)S(1)}, bf16[8,768]{1,0:T(8,128)(2,1)S(1)}, u32[]{:S(2)}, u32[]{:S(2)}) collective-permute-start(bf16[8,768]{1,0:T(8,128)(2,1)S(1)} %get-tuple-element.25), channel_id=1, source_target_pairs={{0,1},{1,0},{2,3},{3,2},{4,5},{5,4},{6,7},{7,6},{8,9},{9,8},{10,11... | collective-permute-start | bytes 36872 | tf_op jit(solution)/shard_map/ppermute | solution.py:333
  47.1 1.1 %collective-permute-done.11 = bf16[8,768]{1,0:T(8,128)(2,1)S(1)} collective-permute-done((bf16[8,768]{1,0:T(8,128)(2,1)S(1)}, bf16[8,768]{1,0:T(8,128)(2,1)S(1)}, u32[]{:S(2)}, u32[]{:S(2)}) %collective-permute-start.11) | collective-permute-done | bytes 12320 | tf_op jit(solution)/shard_map/ppermute | solution.py:333
  48.2 2.3 %collective-permute-done.12 = bf16[8,768]{1,0:T(8,128)(2,1)S(1)} collective-permute-done((bf16[8,768]{1,0:T(8,128)(2,1)S(1)}, bf16[8,768]{1,0:T(8,128)(2,1)S(1)}, u32[]{:S(2)}, u32[]{:S(2)}) %collective-permute-start.12) | collective-permute-done | bytes 12320 | tf_op jit(solution)/shard_map/ppermute | solution.py:333
  50.5 0.6 %add_convert_fusion.2 = bf16[8,768]{1,0:T(8,128)(2,1)} fusion(bf16[8,768]{1,0:T(8,128)(2,1)S(1)} %collective-permute-done.13, bf16[8,768]{1,0:T(8,128)(2,1)S(1)} %collective-permute-done.12, bf16[8,768]{1,0:T(8,128)(2,1)S(1)} %collective-permute-done.11, bf16[8,1024]{1,0:T(8,128)(2,1)S(1)} %attention.1._.refs_3_, bf16[8,3072]{1,0:T(8,128)(2,1)S(1)} %add_convert_fusion.1, ...), kind=kLoop, calls=%fused_computation.5 | loop fusion | flops 61440 | bytes 73732 | tf_op jit(solution)/shard_map/convert_element_type | solution.py:373
  (18 shorter events, 0.2 us)
Async XLA Ops:
  3.2 9.2 %collective-permute-start = (bf16[8,1024]{1,0:T(8,128)(2,1)S(1)}, bf16[8,1024]{1,0:T(8,128)(2,1)S(1)}, u32[]{:S(2)}, u32[]{:S(2)}) collective-permute-start(bf16[8,1024]{1,0:T(8,128)(2,1)S(1)} %attention.1._.refs_3_), channel_id=1, source_target_pairs={{0,3},{1,2},{2,1},{3,0},{4,7},{5,6},{6,5},{7,4},{8,11},{9,10},{10,... | collective-permute-start | bytes 49160 | tf_op jit(solution)/shard_map/ppermute | solution.py:333
  8.3 4.6 %collective-permute-start.1 = (bf16[8,1024]{1,0:T(8,128)(2,1)S(1)}, bf16[8,1024]{1,0:T(8,128)(2,1)S(1)}, u32[]{:S(2)}, u32[]{:S(2)}) collective-permute-start(bf16[8,1024]{1,0:T(8,128)(2,1)S(1)} %attention.1._.refs_3_), channel_id=1, source_target_pairs={{0,2},{1,3},{2,0},{3,1},{4,6},{5,7},{6,4},{7,5},{8,10},{9,11},{10,... | collective-permute-start | bytes 49160 | tf_op jit(solution)/shard_map/ppermute | solution.py:333
  8.3 4.6 %collective-permute-start.2 = (bf16[8,1024]{1,0:T(8,128)(2,1)S(1)}, bf16[8,1024]{1,0:T(8,128)(2,1)S(1)}, u32[]{:S(2)}, u32[]{:S(2)}) collective-permute-start(bf16[8,1024]{1,0:T(8,128)(2,1)S(1)} %attention.1._.refs_3_), channel_id=1, source_target_pairs={{0,1},{1,0},{2,3},{3,2},{4,5},{5,4},{6,7},{7,6},{8,9},{9,8},{10,11... | collective-permute-start | bytes 49160 | tf_op jit(solution)/shard_map/ppermute | solution.py:333
  15.3 6.9 %collective-permute-start.3 = (bf16[8,3200]{1,0:T(8,128)(2,1)S(1)}, bf16[8,3200]{1,0:T(8,128)(2,1)S(1)}, u32[]{:S(2)}, u32[]{:S(2)}) collective-permute-start(bf16[8,3200]{1,0:T(8,128)(2,1)S(1)} %get-tuple-element.14._.refs_3_), channel_id=1, source_target_pairs={{0,12},{4,8},{8,4},{12,0},{1,13},{5,9},{9,5},{13,1},{2,14},{6,10},... | collective-permute-start | bytes 153608 | tf_op jit(solution)/shard_map/ppermute | solution.py:333
  17.8 4.4 %collective-permute-start.4 = (bf16[8,3200]{1,0:T(8,128)(2,1)S(1)}, bf16[8,3200]{1,0:T(8,128)(2,1)S(1)}, u32[]{:S(2)}, u32[]{:S(2)}) collective-permute-start(bf16[8,3200]{1,0:T(8,128)(2,1)S(1)} %get-tuple-element.14._.refs_3_), channel_id=1, source_target_pairs={{0,8},{4,12},{8,0},{12,4},{1,9},{5,13},{9,1},{13,5},{2,10},{6,14},... | collective-permute-start | bytes 153608 | tf_op jit(solution)/shard_map/ppermute | solution.py:333
  18.3 4.1 %collective-permute-start.5 = (bf16[8,3200]{1,0:T(8,128)(2,1)S(1)}, bf16[8,3200]{1,0:T(8,128)(2,1)S(1)}, u32[]{:S(2)}, u32[]{:S(2)}) collective-permute-start(bf16[8,3200]{1,0:T(8,128)(2,1)S(1)} %get-tuple-element.14._.refs_3_), channel_id=1, source_target_pairs={{0,4},{4,0},{8,12},{12,8},{1,5},{5,1},{9,13},{13,9},{2,6},{6,2},{1... | collective-permute-start | bytes 153608 | tf_op jit(solution)/shard_map/ppermute | solution.py:333
  22.4 2.0 %collective-permute-start.6 = (bf16[32,3200]{1,0:T(8,128)(2,1)S(1)}, bf16[32,3200]{1,0:T(8,128)(2,1)S(1)}, u32[]{:S(2)}, u32[]{:S(2)}) collective-permute-start(bf16[32,3200]{1,0:T(8,128)(2,1)S(1)} %stack.13._.near), channel_id=1, source_target_pairs={{0,16},{16,0},{1,17},{17,1},{2,18},{18,2},{3,19},{19,3},{4,20},{20... | collective-permute-start | bytes 614408 | tf_op jit(solution)/shard_map/ppermute | solution.py:333
  22.5 9.1 %slice-start = ((s8[10616832]{0:T(1024)(128)(4,1)}), s8[4194304]{0:T(1024)(128)(4,1)S(1)}, s32[]{:S(2)}) async-start(s8[10616832]{0:T(1024)(128)(4,1)} %bitcast.9), calls=%async_computation | async-start | bytes 8388608
  24.5 7.2 %slice-start.1 = ((s8[10616832]{0:T(1024)(128)(4,1)}), s8[4194304]{0:T(1024)(128)(4,1)S(1)}, s32[]{:S(2)}) async-start(s8[10616832]{0:T(1024)(128)(4,1)} %bitcast.9), calls=%async_computation.1 | async-start | bytes 8388608
  24.5 7.2 %slice-start.2 = ((s8[10616832]{0:T(1024)(128)(4,1)}), s8[2228224]{0:T(1024)(128)(4,1)S(1)}, s32[]{:S(2)}) async-start(s8[10616832]{0:T(1024)(128)(4,1)} %bitcast.9), calls=%async_computation.2 | async-start | bytes 4456448
  33.7 1.6 %collective-permute-start.7 = (bf16[32,3072]{1,0:T(8,128)(2,1)S(1)}, bf16[32,3072]{1,0:T(8,128)(2,1)S(1)}, u32[]{:S(2)}, u32[]{:S(2)}) collective-permute-start(bf16[32,3072]{1,0:T(8,128)(2,1)S(1)} %slice.33), channel_id=1, source_target_pairs={{0,16},{16,0},{1,17},{17,1},{2,18},{18,2},{3,19},{19,3},{4,20},{20... | collective-permute-start | bytes 589832 | tf_op jit(solution)/shard_map/ppermute | solution.py:333
  35.3 4.2 %collective-permute-start.10 = (bf16[8,3072]{1,0:T(8,128)(2,1)S(1)}, bf16[8,3072]{1,0:T(8,128)(2,1)S(1)}, u32[]{:S(2)}, u32[]{:S(2)}) collective-permute-start(bf16[8,3072]{1,0:T(8,128)(2,1)S(1)} %get-tuple-element.22), channel_id=1, source_target_pairs={{0,4},{4,0},{8,12},{12,8},{1,5},{5,1},{9,13},{13,9},{2,6},{6,2},{1... | collective-permute-start | bytes 147464 | tf_op jit(solution)/shard_map/ppermute | solution.py:333
  36.7 5.0 %collective-permute-start.8 = (bf16[8,3072]{1,0:T(8,128)(2,1)S(1)}, bf16[8,3072]{1,0:T(8,128)(2,1)S(1)}, u32[]{:S(2)}, u32[]{:S(2)}) collective-permute-start(bf16[8,3072]{1,0:T(8,128)(2,1)S(1)} %get-tuple-element.21), channel_id=1, source_target_pairs={{0,12},{4,8},{8,4},{12,0},{1,13},{5,9},{9,5},{13,1},{2,14},{6,10},... | collective-permute-start | bytes 147464 | tf_op jit(solution)/shard_map/ppermute | solution.py:333
  38.4 4.2 %collective-permute-start.9 = (bf16[8,3072]{1,0:T(8,128)(2,1)S(1)}, bf16[8,3072]{1,0:T(8,128)(2,1)S(1)}, u32[]{:S(2)}, u32[]{:S(2)}) collective-permute-start(bf16[8,3072]{1,0:T(8,128)(2,1)S(1)} %get-tuple-element.23), channel_id=1, source_target_pairs={{0,8},{4,12},{8,0},{12,4},{1,9},{5,13},{9,1},{13,5},{2,10},{6,14},... | collective-permute-start | bytes 147464 | tf_op jit(solution)/shard_map/ppermute | solution.py:333
  42.6 5.6 %collective-permute-start.11 = (bf16[8,768]{1,0:T(8,128)(2,1)S(1)}, bf16[8,768]{1,0:T(8,128)(2,1)S(1)}, u32[]{:S(2)}, u32[]{:S(2)}) collective-permute-start(bf16[8,768]{1,0:T(8,128)(2,1)S(1)} %get-tuple-element.24), channel_id=1, source_target_pairs={{0,3},{1,2},{2,1},{3,0},{4,7},{5,6},{6,5},{7,4},{8,11},{9,10},{10,... | collective-permute-start | bytes 36872 | tf_op jit(solution)/shard_map/ppermute | solution.py:333
  45.9 4.6 %collective-permute-start.12 = (bf16[8,768]{1,0:T(8,128)(2,1)S(1)}, bf16[8,768]{1,0:T(8,128)(2,1)S(1)}, u32[]{:S(2)}, u32[]{:S(2)}) collective-permute-start(bf16[8,768]{1,0:T(8,128)(2,1)S(1)} %get-tuple-element.26), channel_id=1, source_target_pairs={{0,2},{1,3},{2,0},{3,1},{4,6},{5,7},{6,4},{7,5},{8,10},{9,11},{10,... | collective-permute-start | bytes 36872 | tf_op jit(solution)/shard_map/ppermute | solution.py:333
  45.9 4.6 %collective-permute-start.13 = (bf16[8,768]{1,0:T(8,128)(2,1)S(1)}, bf16[8,768]{1,0:T(8,128)(2,1)S(1)}, u32[]{:S(2)}, u32[]{:S(2)}) collective-permute-start(bf16[8,768]{1,0:T(8,128)(2,1)S(1)} %get-tuple-element.25), channel_id=1, source_target_pairs={{0,1},{1,0},{2,3},{3,2},{4,5},{5,4},{6,7},{7,6},{8,9},{9,8},{10,11... | collective-permute-start | bytes 36872 | tf_op jit(solution)/shard_map/ppermute | solution.py:333

commit v3 on v2

--- a/solution.py
+++ b/solution.py
@@ -25,6 +25,27 @@
     return high, middle, rest - middle
 
 
+def unit_parts(units):
+    first = max(UNITS, units * 3 // 4 // UNITS * UNITS)
+    if units <= 2 * UNITS:
+        first = units // 32 * 16
+    return pl.ds(0, first), pl.ds(first, units - first)
+
+
+def start_load(source, target, part, sems):
+    count = max(c for c in range(1, CHUNKS + 1) if part.size % (16 * c) == 0 or c == 1)
+    step = part.size // count
+    copies = [
+        pltpu.make_async_copy(
+            source.at[0, pl.ds(part.start + i * step, step)], target.at[pl.ds(i * step, step)], sems.at[i]
+        )
+        for i in range(count)
+    ]
+    for copy in copies:
+        copy.start()
+    return copies
+
+
 def attention_kernel(
     len_ref,
     q_hbm,
@@ -34,7 +55,9 @@
     routes_hbm,
     router_hbm,
     gain_hbm,
+    weight_hbm,
     out_ref,
+    weight_ref,
     q_ref,
     new_ref,
     kv,
@@ -44,8 +67,10 @@
     gain_ref,
     scores,
     sems,
+    weight_sems,
     *,
     chunks,
+    rest,
 ):
     slots = kv_hbm.shape[1]
     part = slots // chunks
@@ -56,6 +81,7 @@
     copies = [pltpu.make_async_copy(a, b, sems.at[i]) for i, (a, b) in enumerate(zip(sources, targets))]
     for copy in copies:
         copy.start()
+    loads = start_load(weight_hbm, weight_ref, rest, weight_sems)
     tokens, columns = q_ref.shape
     key_heads = new_ref.shape[1] // (2 * HEAD_DIM)
     grouped = columns // HEAD_DIM // key_heads
@@ -141,28 +167,34 @@
         gains + [jnp.zeros((1, LANES), jnp.float32)] * (tokens - len(gains)), axis=0
     )
     out_ref[:, columns + LANES :] = gain_rows.astype(out_ref.dtype)
-
-
-def attend(cache_len, queries, new_kv, kv_cache, residual, routes, router, norm_gain):
+    for copy in loads:
+        copy.wait()
+
+
+def attend(cache_len, queries, new_kv, kv_cache, residual, routes, router, norm_gain, weight, rest):
     tokens, columns = queries.shape
     slots, width = kv_cache.shape[1:]
     key_heads = new_kv.shape[1] // (2 * HEAD_DIM)
     rows = columns // HEAD_DIM // key_heads * tokens
     chunks = 4
-    operands = [queries, new_kv, kv_cache, residual, routes.T, router, norm_gain]
+    operands = [queries, new_kv, kv_cache, residual, routes.T, router, norm_gain, weight]
     operands = [pltpu.with_memory_space_constraint(x, pltpu.HBM) for x in operands]
-    kept = [pltpu.VMEM(x.shape, x.dtype) for x in operands]
+    kept = [pltpu.VMEM(x.shape, x.dtype) for x in operands[:-1]]
     kept[2] = pltpu.VMEM((slots, width), kv_cache.dtype)
     return pl.pallas_call(
-        functools.partial(attention_kernel, chunks=chunks),
-        out_shape=jax.ShapeDtypeStruct((tokens, columns + 2 * LANES), jnp.bfloat16),
+        functools.partial(attention_kernel, chunks=chunks, rest=rest),
+        out_shape=(
+            jax.ShapeDtypeStruct((tokens, columns + 2 * LANES), jnp.bfloat16),
+            pltpu.VMEM((rest.size, weight.shape[2]), weight.dtype),
+        ),
         in_specs=[pl.BlockSpec(memory_space=pltpu.SMEM)]
         + [pl.BlockSpec(memory_space=pl.ANY)] * len(operands),
-        out_specs=pl.BlockSpec(memory_space=pltpu.VMEM),
+        out_specs=(pl.BlockSpec(memory_space=pltpu.VMEM),) * 2,
         scratch_shapes=kept
         + [
             pltpu.VMEM((key_heads, rows, slots), jnp.float32),
-            pltpu.SemaphoreType.DMA((chunks + len(operands) - 1,)),
+            pltpu.SemaphoreType.DMA((chunks + len(operands) - 2,)),
+            pltpu.SemaphoreType.DMA((CHUNKS,)),
         ],
         compiler_params=pltpu.CompilerParams(vmem_limit_bytes=8 * MIB),
         cost_estimate=pl.CostEstimate(
@@ -172,27 +204,6 @@
         ),
         name="attention",
     )(cache_len, *operands)
-
-
-def unit_parts(units):
-    first = max(UNITS, units * 3 // 4 // UNITS * UNITS)
-    if units <= 2 * UNITS:
-        first = units // 32 * 16
-    return pl.ds(0, first), pl.ds(first, units - first)
-
-
-def start_load(source, target, part, sems):
-    count = max(c for c in range(1, CHUNKS + 1) if part.size % (16 * c) == 0 or c == 1)
-    step = part.size // count
-    copies = [
-        pltpu.make_async_copy(
-            source.at[0, pl.ds(part.start + i * step, step)], target.at[pl.ds(i * step, step)], sems.at[i]
-        )
-        for i in range(count)
-    ]
-    for copy in copies:
-        copy.start()
-    return copies
 
 
 def load_kernel(_, source, out_ref, token_ref, sems, *, part):
@@ -216,9 +227,8 @@
     )(after, pltpu.with_memory_space_constraint(weight, pltpu.HBM))
 
 
-def norm_kernel(place_ref, _, source, *refs, experts, part):
-    pieces, (out_ref, rest_ref, sems) = refs[:-3], refs[-3:]
-    copies = start_load(source, rest_ref, part, sems)
+def norm_kernel(place_ref, _, *refs, experts):
+    pieces, out_ref = refs[:-1], refs[-1]
     tokens, wide = pieces[0].shape
     block = wide - 2 * LANES
     model = len(pieces) * block
@@ -244,27 +254,20 @@
         x = (piece[:, :block].astype(jnp.float32) - mean) * inv * gain
         at = pl.multiple_of(lax.bitwise_xor(place_ref[0], mask) * block, block)
         out_ref[:, pl.ds(at, block)] = x.astype(out_ref.dtype)
-    for copy in copies:
-        copy.wait()
-
-
-def norm_rows(place, token, weight, part, blocks, experts):
+
+
+def norm_rows(place, token, blocks, experts):
     tokens, wide = blocks[0].shape
     model = (wide - 2 * LANES) * len(blocks)
     vmem = pl.BlockSpec(memory_space=pltpu.VMEM)
     return pl.pallas_call(
-        functools.partial(norm_kernel, experts=experts, part=part),
-        out_shape=(
-            jax.ShapeDtypeStruct((tokens, model + LANES), jnp.bfloat16),
-            pltpu.VMEM((part.size, weight.shape[2]), weight.dtype),
-        ),
-        in_specs=[pl.BlockSpec(memory_space=pltpu.SMEM), vmem, pl.BlockSpec(memory_space=pl.ANY)]
-        + [vmem] * len(blocks),
-        out_specs=(vmem, vmem),
-        scratch_shapes=[pltpu.SemaphoreType.DMA((CHUNKS,))],
+        functools.partial(norm_kernel, experts=experts),
+        out_shape=jax.ShapeDtypeStruct((tokens, model + LANES), jnp.bfloat16),
+        in_specs=[pl.BlockSpec(memory_space=pltpu.SMEM)] + [vmem] * (1 + len(blocks)),
+        out_specs=vmem,
         compiler_params=pltpu.CompilerParams(vmem_limit_bytes=4 * MIB),
         name="norm",
-    )(place, token, pltpu.with_memory_space_constraint(weight, pltpu.HBM), *blocks)
+    )(place, token, *blocks)
 
 
 def stack_kernel(_, *refs):
@@ -288,45 +291,53 @@
     )(token, *pieces)
 
 
-def hidden_kernel(place_ref, near, far, gate_a, gate_b, up_a, up_b, _, hidden, x, *, experts):
-    half = near.shape[0]
+def hidden_kernel(place_ref, near, far, gate_a, gate_b, up_a, up_hbm, hidden, x, up_b, sems, *, experts, rest):
+    loads = start_load(up_hbm, up_b, rest, sems)
     model = gate_a.shape[1]
-    x[:half] = near[:, :model]
-    x[half:] = far[:, :model]
-    side = jnp.concatenate([near[:, model:], far[:, model:]], axis=0).astype(jnp.float32)
-    lane = lax.broadcasted_iota(jnp.int32, side.shape, 1)
+    step = 2 * LANES
+    for at in range(0, model, step):
+        both = [ref[:, at : at + step].astype(jnp.float32) for ref in (near, far)]
+        x[at : at + step] = jnp.concatenate(both, axis=0).T.astype(x.dtype)
+    side = jnp.concatenate([ref[:, model:].astype(jnp.float32) for ref in (near, far)], axis=0).T
+    at = lax.broadcasted_iota(jnp.int32, side.shape, 0)
     expert = place_ref[1]
-    mine = (lane == expert) | (lane == expert + experts)
-    share = jnp.sum(jnp.where(mine, side, 0.0), axis=1, keepdims=True)
+    mine = (at == expert) | (at == expert + experts)
+    share = jnp.sum(jnp.where(mine, side, 0.0), axis=0, keepdims=True)
     first = 0
     for gate, up in ((gate_a, up_a), (gate_b, up_b)):
+        if first:
+            for copy in loads:
+                copy.wait()
         units = gate.shape[0]
         for at in range(0, units, UNITS):
             part = slice(at, min(at + UNITS, units))
-            a = lax.dot_general(x[...], gate[part], BY_ROW, preferred_element_type=jnp.float32)
-            b = lax.dot_general(x[...], up[part], BY_ROW, preferred_element_type=jnp.float32)
+            a = jnp.dot(gate[part], x[...], preferred_element_type=jnp.float32)
+            b = jnp.dot(up[part], x[...], preferred_element_type=jnp.float32)
             out = a / (1.0 + jnp.exp(-a)) * b * share
-            hidden[:, first + part.start : first + part.stop] = out.astype(hidden.dtype)
+            hidden[:, first + part.start : first + part.stop] = out.T.astype(hidden.dtype)
         first += units
 
 
-def run_hidden(place, near, far, weights, token, experts):
-    units = weights[0].shape[0] + weights[1].shape[0]
-    model = weights[0].shape[1]
+def run_hidden(place, near, far, gate_a, gate_b, up_a, up_w, rest, experts):
+    units, model = up_w.shape[1:]
     rows = 2 * near.shape[0]
     vmem = pl.BlockSpec(memory_space=pltpu.VMEM)
     return pl.pallas_call(
-        functools.partial(hidden_kernel, experts=experts),
+        functools.partial(hidden_kernel, experts=experts, rest=rest),
         out_shape=jax.ShapeDtypeStruct((rows, units), jnp.bfloat16),
-        in_specs=[pl.BlockSpec(memory_space=pltpu.SMEM)] + [vmem] * 7,
+        in_specs=[pl.BlockSpec(memory_space=pltpu.SMEM)] + [vmem] * 5 + [pl.BlockSpec(memory_space=pl.ANY)],
         out_specs=vmem,
-        scratch_shapes=[pltpu.VMEM((rows, model), jnp.bfloat16)],
-        compiler_params=pltpu.CompilerParams(vmem_limit_bytes=6 * MIB),
+        scratch_shapes=[
+            pltpu.VMEM((model, rows), jnp.bfloat16),
+            pltpu.VMEM((rest.size, model), up_w.dtype),
+            pltpu.SemaphoreType.DMA((CHUNKS,)),
+        ],
+        compiler_params=pltpu.CompilerParams(vmem_limit_bytes=(8 if rows <= 64 else 24) * MIB),
         cost_estimate=pl.CostEstimate(
             flops=4 * rows * units * model, bytes_accessed=4 * units * model, transcendentals=rows * units
         ),
         name="hidden",
-    )(place, near, far, *weights, token)
+    )(place, near, far, gate_a, gate_b, up_a, pltpu.with_memory_space_constraint(up_w, pltpu.HBM))
 
 
 def send(x, axis, mask):
@@ -352,17 +363,18 @@
 
     early, late = unit_parts(gate_w.shape[1])
 
-    fresh = attend(cache_len, queries, new_kv, kv_cache, residual, routes, router, norm_gain)
+    fresh, gate_b = attend(
+        cache_len, queries, new_kv, kv_cache, residual, routes, router, norm_gain, gate_w, late
+    )
     blocks = exchange([fresh] * tensors, "tensor") + [fresh]
     gate_a, token = load(fresh, gate_w, early)
-    rows, gate_b = norm_rows(where, token, gate_w, late, blocks, experts)
+    rows = norm_rows(where, token, blocks, experts)
     ranks = exchange([rows] * groups, "group") + [rows]
     up_a, token = load(rows, up_w, early)
     near = stack_rows(token, ranks)
     far = send(near, "section", 1)
-    up_b, token = load(near, up_w, late)
-
-    hidden = run_hidden(where, near, far, (gate_a, gate_b, up_a, up_b), token, experts)
+
+    hidden = run_hidden(where, near, far, gate_a, gate_b, up_a, up_w, late, experts)
     out = jnp.dot(hidden, down_w[0], preferred_element_type=jnp.float32).astype(jnp.bfloat16)
     half = out.shape[0] // 2
     both = add(out[:half], send(out[half:], "section", 1)).astype(jnp.bfloat16)

time: 51.3 us -> 48.9 us (0.953)
  Pallas kernels: 20.6 us -> 17.2 us
  waiting for transfers between devices: 8.92 us -> 10.4 us
    pallas_call x3 -> x2, Pallas kernels: 8.6 us -> 6.83 us  [load(): pl.pallas_call(functools.partial(load_kernel, part=part), out_shape=(pltp...]
    pallas_call x3, Pallas kernels: 12 us -> 10.3 us  [the longest x1 6.73 us: run_hidden(): pl.pallas_call(functools.partial(hidden_kernel, experts=experts, rest=res...]
    ppermute x14, waiting for transfers between devices: 8.92 us -> 10.4 us  [send(): lax.ppermute(x, axis, [(i, i ^ mask) for i in range(lax.axis_size(axis))])]
  transfers between devices with their start and end apart: 14 -> 14, of which waited for: 8 -> 9; matrix products, arithmetic and copies ran while one was open for 0% -> 0% of each run, Pallas kernels for 17% -> 14%
where the time goes in v3:
time: 48.9 us; the launch traced here: 48.7 us
  starting transfers between devices  17.5 us (36%)
  Pallas kernels  17.2 us (35%)
  waiting for transfers between devices  10.4 us (21%)
  matrix products  1.97 us (4%)
  between operations  0.8 us (2%)
  other arithmetic  0.77 us (2%)
    ppermute x14, starting transfers between devices, send(): lax.ppermute(x, axis, [(i, i ^ mask) for i in range(lax.axis_size(axis))])  17.5 us
    ppermute x14, waiting for transfers between devices, send(): lax.ppermute(x, axis, [(i, i ^ mask) for i in range(lax.axis_size(axis))])  10.4 us
    pallas_call x2, Pallas kernels, load(): pl.pallas_call(functools.partial(load_kernel, part=part), out_shape=(pltp...  6.83 us
    pallas_call x1, Pallas kernels, run_hidden(): pl.pallas_call(functools.partial(hidden_kernel, experts=experts, rest=res...  6.73 us
    pallas_call x1, Pallas kernels, attend(): pl.pallas_call(functools.partial(attention_kernel, chunks=chunks, rest=re...  2.68 us
    dot_general x1, matrix products, per_device(): jnp.dot(hidden, down_w[0], preferred_element_type=jnp.float32)  1.97 us
  transfers between devices with their start and end apart: 14, of which 9 were waited for; matrix products, arithmetic and copies ran while one was open for 0% of the time, Pallas kernels for 14%

profile of v3, /device:TPU:0, one launch (start us, length us, event | category | flops | bytes accessed | tf_op | source)
XLA Modules:
  0.0 48.7 jit_solution(6706269791393376226)
XLA Ops:
  0.7 2.7 %attention.1 = (bf16[8,1024]{1,0:T(8,128)(2,1)S(1)}, bf16[448,3072]{1,0:T(8,128)(2,1)S(1)}) custom-call(s32[1]{0:T(128)S(6)} %copy.12.len_ref, bf16[8,768]{1,0:T(8,128)(2,1)} %q_hbm.1, bf16[8,512]{1,0:T(8,128)(2,1)} %new_hbm.1, bf16[1,2048,512]{2,1,0:T(8,128)(2,1)} %kv_hbm.1, bf16[8,768]{1,0:T(8,128)(2,1)} %res_hbm.1, s32[4,8]{1,0:T(4,128)} %bitcast.11, ...), custom_call_target="tpu_custom_call" | custom-call | flops 50331648 | bytes 2097152 | tf_op jit(solution)/shard_map/attention/pallas_call | solution.py:184
  3.3 5.1 %collective-permute-start = (bf16[8,1024]{1,0:T(8,128)(2,1)S(1)}, bf16[8,1024]{1,0:T(8,128)(2,1)S(1)}, u32[]{:S(2)}, u32[]{:S(2)}) collective-permute-start(bf16[8,1024]{1,0:T(8,128)(2,1)S(1)} %get-tuple-element.11._.refs_3_), channel_id=1, source_target_pairs={{0,3},{1,2},{2,1},{3,0},{4,7},{5,6},{6,5},{7,4},{8,11},{9,10},{10,... | collective-permute-start | bytes 49160 | tf_op jit(solution)/shard_map/ppermute | solution.py:344
  8.5 0.0 collective-permute-start.1
  8.5 0.6 %collective-permute-start.2 = (bf16[8,1024]{1,0:T(8,128)(2,1)S(1)}, bf16[8,1024]{1,0:T(8,128)(2,1)S(1)}, u32[]{:S(2)}, u32[]{:S(2)}) collective-permute-start(bf16[8,1024]{1,0:T(8,128)(2,1)S(1)} %get-tuple-element.11._.refs_3_), channel_id=1, source_target_pairs={{0,1},{1,0},{2,3},{3,2},{4,5},{5,4},{6,7},{7,6},{8,9},{9,8},{10,11... | collective-permute-start | bytes 49160 | tf_op jit(solution)/shard_map/ppermute | solution.py:344
  9.1 0.1 pad_add_fusion.place_ref
  9.2 3.3 %load.2 = (bf16[1280,3072]{1,0:T(8,128)(2,1)S(1)}, f32[8,128]{1,0:T(8,128)S(1)}) custom-call(bf16[8,1024]{1,0:T(8,128)(2,1)S(1)} %get-tuple-element.11._.refs_3_, bf16[1,1728,3072]{2,1,0:T(8,128)(2,1)} %source.2), custom_call_target="tpu_custom_call" | custom-call | bytes 15728640 | tf_op jit(solution)/shard_map/load/pallas_call | solution.py:218
  12.5 0.0 collective-permute-done.refs_0_
  12.5 0.6 %collective-permute-done.1.refs_1_ = bf16[8,1024]{1,0:T(8,128)(2,1)S(1)} collective-permute-done((bf16[8,1024]{1,0:T(8,128)(2,1)S(1)}, bf16[8,1024]{1,0:T(8,128)(2,1)S(1)}, u32[]{:S(2)}, u32[]{:S(2)}) %collective-permute-start.1) | collective-permute-done | bytes 16416 | tf_op jit(solution)/shard_map/ppermute | solution.py:344
  13.1 0.9 %norm.1._.refs_3_ = bf16[8,3200]{1,0:T(8,128)(2,1)S(1)} custom-call(s32[2]{0:T(128)S(1)} %pad_add_fusion.place_ref, f32[8,128]{1,0:T(8,128)S(1)} %get-tuple-element.12._, bf16[8,1024]{1,0:T(8,128)(2,1)S(1)} %collective-permute-done.refs_0_, bf16[8,1024]{1,0:T(8,128)(2,1)S(1)} %collective-permute-done.1.refs_1_, ...), custom_call_target="tpu_custom_call" | custom-call | tf_op jit(solution)/shard_map/norm/pallas_call | solution.py:263
  14.0 2.5 %collective-permute-start.3 = (bf16[8,3200]{1,0:T(8,128)(2,1)S(1)}, bf16[8,3200]{1,0:T(8,128)(2,1)S(1)}, u32[]{:S(2)}, u32[]{:S(2)}) collective-permute-start(bf16[8,3200]{1,0:T(8,128)(2,1)S(1)} %norm.1._.refs_3_), channel_id=1, source_target_pairs={{0,12},{4,8},{8,4},{12,0},{1,13},{5,9},{9,5},{13,1},{2,14},{6,10},... | collective-permute-start | bytes 153608 | tf_op jit(solution)/shard_map/ppermute | solution.py:344
  16.5 0.5 %collective-permute-start.4 = (bf16[8,3200]{1,0:T(8,128)(2,1)S(1)}, bf16[8,3200]{1,0:T(8,128)(2,1)S(1)}, u32[]{:S(2)}, u32[]{:S(2)}) collective-permute-start(bf16[8,3200]{1,0:T(8,128)(2,1)S(1)} %norm.1._.refs_3_), channel_id=1, source_target_pairs={{0,8},{4,12},{8,0},{12,4},{1,9},{5,13},{9,1},{13,5},{2,10},{6,14},... | collective-permute-start | bytes 153608 | tf_op jit(solution)/shard_map/ppermute | solution.py:344
  17.0 0.5 %collective-permute-start.5 = (bf16[8,3200]{1,0:T(8,128)(2,1)S(1)}, bf16[8,3200]{1,0:T(8,128)(2,1)S(1)}, u32[]{:S(2)}, u32[]{:S(2)}) collective-permute-start(bf16[8,3200]{1,0:T(8,128)(2,1)S(1)} %norm.1._.refs_3_), channel_id=1, source_target_pairs={{0,4},{4,0},{8,12},{12,8},{1,5},{5,1},{9,13},{13,9},{2,6},{6,2},{1... | collective-permute-start | bytes 153608 | tf_op jit(solution)/shard_map/ppermute | solution.py:344
  17.5 3.5 %load.3 = (bf16[1280,3072]{1,0:T(8,128)(2,1)S(1)}, f32[8,128]{1,0:T(8,128)S(1)}) custom-call(bf16[8,3200]{1,0:T(8,128)(2,1)S(1)} %norm.1._.refs_3_, bf16[1,1728,3072]{2,1,0:T(8,128)(2,1)} %up_hbm.1), custom_call_target="tpu_custom_call" | custom-call | bytes 15728640 | tf_op jit(solution)/shard_map/load/pallas_call | solution.py:218
  21.0 0.1 collective-permute-done.5.refs_2_
  21.1 0.1 collective-permute-start.6
  21.2 1.4 %collective-permute-done.6.far = bf16[32,3200]{1,0:T(8,128)(2,1)S(1)} collective-permute-done((bf16[32,3200]{1,0:T(8,128)(2,1)S(1)}, bf16[32,3200]{1,0:T(8,128)(2,1)S(1)}, u32[]{:S(2)}, u32[]{:S(2)}) %collective-permute-start.6) | collective-permute-done | bytes 204832 | tf_op jit(solution)/shard_map/ppermute | solution.py:344
  22.6 6.7 %hidden.1 = bf16[64,1728]{1,0:T(8,128)(2,1)S(1)} custom-call(s32[2]{0:T(128)S(1)} %pad_add_fusion.place_ref, bf16[32,3200]{1,0:T(8,128)(2,1)S(1)} %stack.13.near, bf16[32,3200]{1,0:T(8,128)(2,1)S(1)} %collective-permute-done.6.far, bf16[1280,3072]{1,0:T(8,128)(2,1)S(1)} %get-tuple-element.14.gate_a, bf16[448,3072]{1,0:T(8,128)(2,1)S(1)} %get-tuple-element.15.gate_b, ...), custom_call_target="tpu_custom_call" | custom-call | flops 1358954496 | bytes 21233664 | tf_op jit(solution)/shard_map/hidden/pallas_call | solution.py:325
  29.4 2.0 %fusion.2 = bf16[64,3072]{1,0:T(8,128)(2,1)S(1)} fusion(bf16[64,1728]{1,0:T(8,128)(2,1)S(1)} %hidden.1, bf16[1,1728,3072]{2,1,0:T(8,128)(2,1)S(1)} %bitcast.10), kind=kOutput, calls=%fused_computation.2 | convolution fusion | flops 679673856 | bytes 11231232 | tf_op jit(solution)/shard_map/dot_general | solution.py:378
  31.4 0.2 collective-permute-start.7
  31.6 1.3 %collective-permute-done.7 = bf16[32,3072]{1,0:T(8,128)(2,1)S(1)} collective-permute-done((bf16[32,3072]{1,0:T(8,128)(2,1)S(1)}, bf16[32,3072]{1,0:T(8,128)(2,1)S(1)}, u32[]{:S(2)}, u32[]{:S(2)}) %collective-permute-start.7) | collective-permute-done | bytes 196640 | tf_op jit(solution)/shard_map/ppermute | solution.py:344
  32.9 0.1 add_convert_fusion
  33.0 1.5 %collective-permute-start.10 = (bf16[8,3072]{1,0:T(8,128)(2,1)S(1)}, bf16[8,3072]{1,0:T(8,128)(2,1)S(1)}, u32[]{:S(2)}, u32[]{:S(2)}) collective-permute-start(bf16[8,3072]{1,0:T(8,128)(2,1)S(1)} %get-tuple-element.18), channel_id=1, source_target_pairs={{0,4},{4,0},{8,12},{12,8},{1,5},{5,1},{9,13},{13,9},{2,6},{6,2},{1... | collective-permute-start | bytes 147464 | tf_op jit(solution)/shard_map/ppermute | solution.py:344
  34.5 1.5 %collective-permute-start.8 = (bf16[8,3072]{1,0:T(8,128)(2,1)S(1)}, bf16[8,3072]{1,0:T(8,128)(2,1)S(1)}, u32[]{:S(2)}, u32[]{:S(2)}) collective-permute-start(bf16[8,3072]{1,0:T(8,128)(2,1)S(1)} %get-tuple-element.17), channel_id=1, source_target_pairs={{0,12},{4,8},{8,4},{12,0},{1,13},{5,9},{9,5},{13,1},{2,14},{6,10},... | collective-permute-start | bytes 147464 | tf_op jit(solution)/shard_map/ppermute | solution.py:344
  36.0 0.5 %collective-permute-start.9 = (bf16[8,3072]{1,0:T(8,128)(2,1)S(1)}, bf16[8,3072]{1,0:T(8,128)(2,1)S(1)}, u32[]{:S(2)}, u32[]{:S(2)}) collective-permute-start(bf16[8,3072]{1,0:T(8,128)(2,1)S(1)} %get-tuple-element.19), channel_id=1, source_target_pairs={{0,8},{4,12},{8,0},{12,4},{1,9},{5,13},{9,1},{13,5},{2,10},{6,14},... | collective-permute-start | bytes 147464 | tf_op jit(solution)/shard_map/ppermute | solution.py:344
  36.6 0.6 %collective-permute-done.10 = bf16[8,3072]{1,0:T(8,128)(2,1)S(1)} collective-permute-done((bf16[8,3072]{1,0:T(8,128)(2,1)S(1)}, bf16[8,3072]{1,0:T(8,128)(2,1)S(1)}, u32[]{:S(2)}, u32[]{:S(2)}) %collective-permute-start.10) | collective-permute-done | bytes 49184 | tf_op jit(solution)/shard_map/ppermute | solution.py:344
  37.2 2.4 %collective-permute-done.8 = bf16[8,3072]{1,0:T(8,128)(2,1)S(1)} collective-permute-done((bf16[8,3072]{1,0:T(8,128)(2,1)S(1)}, bf16[8,3072]{1,0:T(8,128)(2,1)S(1)}, u32[]{:S(2)}, u32[]{:S(2)}) %collective-permute-start.8) | collective-permute-done | bytes 49184 | tf_op jit(solution)/shard_map/ppermute | solution.py:344
  39.6 0.6 %collective-permute-done.9 = bf16[8,3072]{1,0:T(8,128)(2,1)S(1)} collective-permute-done((bf16[8,3072]{1,0:T(8,128)(2,1)S(1)}, bf16[8,3072]{1,0:T(8,128)(2,1)S(1)}, u32[]{:S(2)}, u32[]{:S(2)}) %collective-permute-start.9) | collective-permute-done | bytes 49184 | tf_op jit(solution)/shard_map/ppermute | solution.py:344
  40.2 3.3 %collective-permute-start.11 = (bf16[8,768]{1,0:T(8,128)(2,1)S(1)}, bf16[8,768]{1,0:T(8,128)(2,1)S(1)}, u32[]{:S(2)}, u32[]{:S(2)}) collective-permute-start(bf16[8,768]{1,0:T(8,128)(2,1)S(1)} %get-tuple-element.20), channel_id=1, source_target_pairs={{0,3},{1,2},{2,1},{3,0},{4,7},{5,6},{6,5},{7,4},{8,11},{9,10},{10,... | collective-permute-start | bytes 36872 | tf_op jit(solution)/shard_map/ppermute | solution.py:344
  43.5 1.2 %collective-permute-start.13 = (bf16[8,768]{1,0:T(8,128)(2,1)S(1)}, bf16[8,768]{1,0:T(8,128)(2,1)S(1)}, u32[]{:S(2)}, u32[]{:S(2)}) collective-permute-start(bf16[8,768]{1,0:T(8,128)(2,1)S(1)} %get-tuple-element.21), channel_id=1, source_target_pairs={{0,1},{1,0},{2,3},{3,2},{4,5},{5,4},{6,7},{7,6},{8,9},{9,8},{10,11... | collective-permute-start | bytes 36872 | tf_op jit(solution)/shard_map/ppermute | solution.py:344
  44.7 1.1 %collective-permute-done.11 = bf16[8,768]{1,0:T(8,128)(2,1)S(1)} collective-permute-done((bf16[8,768]{1,0:T(8,128)(2,1)S(1)}, bf16[8,768]{1,0:T(8,128)(2,1)S(1)}, u32[]{:S(2)}, u32[]{:S(2)}) %collective-permute-start.11) | collective-permute-done | bytes 12320 | tf_op jit(solution)/shard_map/ppermute | solution.py:344
  45.8 2.3 %collective-permute-done.12 = bf16[8,768]{1,0:T(8,128)(2,1)S(1)} collective-permute-done((bf16[8,768]{1,0:T(8,128)(2,1)S(1)}, bf16[8,768]{1,0:T(8,128)(2,1)S(1)}, u32[]{:S(2)}, u32[]{:S(2)}) %collective-permute-start.12) | collective-permute-done | bytes 12320 | tf_op jit(solution)/shard_map/ppermute | solution.py:344
  48.1 0.6 %add_convert_fusion.2 = bf16[8,768]{1,0:T(8,128)(2,1)} fusion(bf16[8,768]{1,0:T(8,128)(2,1)S(1)} %collective-permute-done.13, bf16[8,768]{1,0:T(8,128)(2,1)S(1)} %collective-permute-done.12, bf16[8,768]{1,0:T(8,128)(2,1)S(1)} %collective-permute-done.11, bf16[8,1024]{1,0:T(8,128)(2,1)S(1)} %get-tuple-element.11._.refs_3_, ...), kind=kLoop, calls=%fused_computation.5 | loop fusion | flops 61440 | bytes 73732 | tf_op jit(solution)/shard_map/convert_element_type | solution.py:385
  (17 shorter events, 0.1 us)
Async XLA Ops:
  3.3 9.2 %collective-permute-start = (bf16[8,1024]{1,0:T(8,128)(2,1)S(1)}, bf16[8,1024]{1,0:T(8,128)(2,1)S(1)}, u32[]{:S(2)}, u32[]{:S(2)}) collective-permute-start(bf16[8,1024]{1,0:T(8,128)(2,1)S(1)} %get-tuple-element.11._.refs_3_), channel_id=1, source_target_pairs={{0,3},{1,2},{2,1},{3,0},{4,7},{5,6},{6,5},{7,4},{8,11},{9,10},{10,... | collective-permute-start | bytes 49160 | tf_op jit(solution)/shard_map/ppermute | solution.py:344
  8.5 4.6 %collective-permute-start.1 = (bf16[8,1024]{1,0:T(8,128)(2,1)S(1)}, bf16[8,1024]{1,0:T(8,128)(2,1)S(1)}, u32[]{:S(2)}, u32[]{:S(2)}) collective-permute-start(bf16[8,1024]{1,0:T(8,128)(2,1)S(1)} %get-tuple-element.11._.refs_3_), channel_id=1, source_target_pairs={{0,2},{1,3},{2,0},{3,1},{4,6},{5,7},{6,4},{7,5},{8,10},{9,11},{10,... | collective-permute-start | bytes 49160 | tf_op jit(solution)/shard_map/ppermute | solution.py:344
  8.5 4.6 %collective-permute-start.2 = (bf16[8,1024]{1,0:T(8,128)(2,1)S(1)}, bf16[8,1024]{1,0:T(8,128)(2,1)S(1)}, u32[]{:S(2)}, u32[]{:S(2)}) collective-permute-start(bf16[8,1024]{1,0:T(8,128)(2,1)S(1)} %get-tuple-element.11._.refs_3_), channel_id=1, source_target_pairs={{0,1},{1,0},{2,3},{3,2},{4,5},{5,4},{6,7},{7,6},{8,9},{9,8},{10,11... | collective-permute-start | bytes 49160 | tf_op jit(solution)/shard_map/ppermute | solution.py:344
  14.0 7.0 %collective-permute-start.3 = (bf16[8,3200]{1,0:T(8,128)(2,1)S(1)}, bf16[8,3200]{1,0:T(8,128)(2,1)S(1)}, u32[]{:S(2)}, u32[]{:S(2)}) collective-permute-start(bf16[8,3200]{1,0:T(8,128)(2,1)S(1)} %norm.1._.refs_3_), channel_id=1, source_target_pairs={{0,12},{4,8},{8,4},{12,0},{1,13},{5,9},{9,5},{13,1},{2,14},{6,10},... | collective-permute-start | bytes 153608 | tf_op jit(solution)/shard_map/ppermute | solution.py:344
  16.5 4.6 %collective-permute-start.4 = (bf16[8,3200]{1,0:T(8,128)(2,1)S(1)}, bf16[8,3200]{1,0:T(8,128)(2,1)S(1)}, u32[]{:S(2)}, u32[]{:S(2)}) collective-permute-start(bf16[8,3200]{1,0:T(8,128)(2,1)S(1)} %norm.1._.refs_3_), channel_id=1, source_target_pairs={{0,8},{4,12},{8,0},{12,4},{1,9},{5,13},{9,1},{13,5},{2,10},{6,14},... | collective-permute-start | bytes 153608 | tf_op jit(solution)/shard_map/ppermute | solution.py:344
  17.0 4.1 %collective-permute-start.5 = (bf16[8,3200]{1,0:T(8,128)(2,1)S(1)}, bf16[8,3200]{1,0:T(8,128)(2,1)S(1)}, u32[]{:S(2)}, u32[]{:S(2)}) collective-permute-start(bf16[8,3200]{1,0:T(8,128)(2,1)S(1)} %norm.1._.refs_3_), channel_id=1, source_target_pairs={{0,4},{4,0},{8,12},{12,8},{1,5},{5,1},{9,13},{13,9},{2,6},{6,2},{1... | collective-permute-start | bytes 153608 | tf_op jit(solution)/shard_map/ppermute | solution.py:344
  17.5 11.9 %slice-start = ((s8[10616832]{0:T(1024)(128)(4,1)}), s8[4194304]{0:T(1024)(128)(4,1)S(1)}, s32[]{:S(2)}) async-start(s8[10616832]{0:T(1024)(128)(4,1)} %bitcast.9), calls=%async_computation | async-start | bytes 8388608
  21.1 1.5 %collective-permute-start.6 = (bf16[32,3200]{1,0:T(8,128)(2,1)S(1)}, bf16[32,3200]{1,0:T(8,128)(2,1)S(1)}, u32[]{:S(2)}, u32[]{:S(2)}) collective-permute-start(bf16[32,3200]{1,0:T(8,128)(2,1)S(1)} %stack.13.near), channel_id=1, source_target_pairs={{0,16},{16,0},{1,17},{17,1},{2,18},{18,2},{3,19},{19,3},{4,20},{20... | collective-permute-start | bytes 614408 | tf_op jit(solution)/shard_map/ppermute | solution.py:344
  22.6 6.8 %slice-start.1 = ((s8[10616832]{0:T(1024)(128)(4,1)}), s8[4194304]{0:T(1024)(128)(4,1)S(1)}, s32[]{:S(2)}) async-start(s8[10616832]{0:T(1024)(128)(4,1)} %bitcast.9), calls=%async_computation.1 | async-start | bytes 8388608
  22.6 6.8 %slice-start.2 = ((s8[10616832]{0:T(1024)(128)(4,1)}), s8[2228224]{0:T(1024)(128)(4,1)S(1)}, s32[]{:S(2)}) async-start(s8[10616832]{0:T(1024)(128)(4,1)} %bitcast.9), calls=%async_computation.2 | async-start | bytes 4456448
  31.4 1.5 %collective-permute-start.7 = (bf16[32,3072]{1,0:T(8,128)(2,1)S(1)}, bf16[32,3072]{1,0:T(8,128)(2,1)S(1)}, u32[]{:S(2)}, u32[]{:S(2)}) collective-permute-start(bf16[32,3072]{1,0:T(8,128)(2,1)S(1)} %slice.33), channel_id=1, source_target_pairs={{0,16},{16,0},{1,17},{17,1},{2,18},{18,2},{3,19},{19,3},{4,20},{20... | collective-permute-start | bytes 589832 | tf_op jit(solution)/shard_map/ppermute | solution.py:344
  33.0 4.2 %collective-permute-start.10 = (bf16[8,3072]{1,0:T(8,128)(2,1)S(1)}, bf16[8,3072]{1,0:T(8,128)(2,1)S(1)}, u32[]{:S(2)}, u32[]{:S(2)}) collective-permute-start(bf16[8,3072]{1,0:T(8,128)(2,1)S(1)} %get-tuple-element.18), channel_id=1, source_target_pairs={{0,4},{4,0},{8,12},{12,8},{1,5},{5,1},{9,13},{13,9},{2,6},{6,2},{1... | collective-permute-start | bytes 147464 | tf_op jit(solution)/shard_map/ppermute | solution.py:344
  34.5 5.0 %collective-permute-start.8 = (bf16[8,3072]{1,0:T(8,128)(2,1)S(1)}, bf16[8,3072]{1,0:T(8,128)(2,1)S(1)}, u32[]{:S(2)}, u32[]{:S(2)}) collective-permute-start(bf16[8,3072]{1,0:T(8,128)(2,1)S(1)} %get-tuple-element.17), channel_id=1, source_target_pairs={{0,12},{4,8},{8,4},{12,0},{1,13},{5,9},{9,5},{13,1},{2,14},{6,10},... | collective-permute-start | bytes 147464 | tf_op jit(solution)/shard_map/ppermute | solution.py:344
  36.0 4.1 %collective-permute-start.9 = (bf16[8,3072]{1,0:T(8,128)(2,1)S(1)}, bf16[8,3072]{1,0:T(8,128)(2,1)S(1)}, u32[]{:S(2)}, u32[]{:S(2)}) collective-permute-start(bf16[8,3072]{1,0:T(8,128)(2,1)S(1)} %get-tuple-element.19), channel_id=1, source_target_pairs={{0,8},{4,12},{8,0},{12,4},{1,9},{5,13},{9,1},{13,5},{2,10},{6,14},... | collective-permute-start | bytes 147464 | tf_op jit(solution)/shard_map/ppermute | solution.py:344
  40.2 5.6 %collective-permute-start.11 = (bf16[8,768]{1,0:T(8,128)(2,1)S(1)}, bf16[8,768]{1,0:T(8,128)(2,1)S(1)}, u32[]{:S(2)}, u32[]{:S(2)}) collective-permute-start(bf16[8,768]{1,0:T(8,128)(2,1)S(1)} %get-tuple-element.20), channel_id=1, source_target_pairs={{0,3},{1,2},{2,1},{3,0},{4,7},{5,6},{6,5},{7,4},{8,11},{9,10},{10,... | collective-permute-start | bytes 36872 | tf_op jit(solution)/shard_map/ppermute | solution.py:344
  43.5 4.6 %collective-permute-start.12 = (bf16[8,768]{1,0:T(8,128)(2,1)S(1)}, bf16[8,768]{1,0:T(8,128)(2,1)S(1)}, u32[]{:S(2)}, u32[]{:S(2)}) collective-permute-start(bf16[8,768]{1,0:T(8,128)(2,1)S(1)} %get-tuple-element.22), channel_id=1, source_target_pairs={{0,2},{1,3},{2,0},{3,1},{4,6},{5,7},{6,4},{7,5},{8,10},{9,11},{10,... | collective-permute-start | bytes 36872 | tf_op jit(solution)/shard_map/ppermute | solution.py:344
  43.5 4.6 %collective-permute-start.13 = (bf16[8,768]{1,0:T(8,128)(2,1)S(1)}, bf16[8,768]{1,0:T(8,128)(2,1)S(1)}, u32[]{:S(2)}, u32[]{:S(2)}) collective-permute-start(bf16[8,768]{1,0:T(8,128)(2,1)S(1)} %get-tuple-element.21), channel_id=1, source_target_pairs={{0,1},{1,0},{2,3},{3,2},{4,5},{5,4},{6,7},{7,6},{8,9},{9,8},{10,11... | collective-permute-start | bytes 36872 | tf_op jit(solution)/shard_map/ppermute | solution.py:344

commit v4 on v3

--- a/solution.py
+++ b/solution.py
@@ -26,10 +26,11 @@
 
 
 def unit_parts(units):
-    first = max(UNITS, units * 3 // 4 // UNITS * UNITS)
-    if units <= 2 * UNITS:
-        first = units // 32 * 16
-    return pl.ds(0, first), pl.ds(first, units - first)
+    ends = [0, 4 * UNITS, 5 * UNITS, units]
+    if units <= ends[2]:
+        step = units // 64 * 16
+        ends = [0, 2 * step, 3 * step, units]
+    return [pl.ds(a, b - a) for a, b in zip(ends, ends[1:])]
 
 
 def start_load(source, target, part, sems):
@@ -74,15 +75,17 @@
 ):
     slots = kv_hbm.shape[1]
     part = slots // chunks
-    sources = [q_hbm, new_hbm] + [kv_hbm.at[0, pl.ds(c * part, part)] for c in range(chunks)]
-    targets = [q_ref, new_ref] + [kv.at[pl.ds(c * part, part)] for c in range(chunks)]
-    sources += [res_hbm, routes_hbm, router_hbm, gain_hbm]
-    targets += [res_ref, routes_ref, router_ref, gain_ref]
+    sources = [q_hbm, new_hbm, res_hbm, routes_hbm, router_hbm, gain_hbm]
+    targets = [q_ref, new_ref, res_ref, routes_ref, router_ref, gain_ref]
+    small = len(sources)
+    sources += [kv_hbm.at[0, pl.ds(c * part, part)] for c in range(chunks)]
+    targets += [kv.at[pl.ds(c * part, part)] for c in range(chunks)]
     copies = [pltpu.make_async_copy(a, b, sems.at[i]) for i, (a, b) in enumerate(zip(sources, targets))]
     for copy in copies:
         copy.start()
     loads = start_load(weight_hbm, weight_ref, rest, weight_sems)
     tokens, columns = q_ref.shape
+    blocks = range(columns // HEAD_DIM)
     key_heads = new_ref.shape[1] // (2 * HEAD_DIM)
     grouped = columns // HEAD_DIM // key_heads
     rows = grouped * tokens
@@ -103,15 +106,7 @@
         own_key = jnp.concatenate([own_key] * grouped, axis=0)
         selves.append(jnp.sum(q * own_key, axis=1, keepdims=True) * scale)
         queries.append(q.astype(jnp.bfloat16))
-    live = len_ref[0]
-    for c in range(chunks):
-        copies[2 + c].wait()
-        for h in range(key_heads):
-            keys = kv[c * part : (c + 1) * part, 2 * h * HEAD_DIM : (2 * h + 1) * HEAD_DIM]
-            s = lax.dot_general(queries[h], keys, BY_ROW, preferred_element_type=jnp.float32)
-            at = lax.broadcasted_iota(jnp.int32, (rows, part), 1) + c * part
-            scores[h, :, c * part : (c + 1) * part] = jnp.where(at < live, s * scale, -jnp.inf)
-    for copy in copies[2 + chunks :]:
+    for copy in copies[2:small]:
         copy.wait()
 
     experts = router_ref.shape[0]
@@ -122,6 +117,31 @@
         named = jnp.where(expert_at == routes[k : k + 1, :], 1.0, named)
     side = named.T
 
+    lane = lax.broadcasted_iota(jnp.int32, (tokens, LANES), 1)
+    sums = jnp.zeros((tokens, LANES), jnp.float32)
+
+    def put(sums, at, pieces):
+        total = pieces[0]
+        for piece in pieces[1:]:
+            total = total + piece
+        return jnp.where(lane == at, jnp.sum(total, axis=1, keepdims=True), sums)
+
+    gain = gain_ref[...].astype(jnp.float32).reshape(1, -1)
+    gains = [gain[:, b * HEAD_DIM : (b + 1) * HEAD_DIM] for b in blocks]
+    scaled = []
+    for e in range(experts):
+        weights = [router_ref[e : e + 1, b * HEAD_DIM : (b + 1) * HEAD_DIM].astype(jnp.float32) for b in blocks]
+        scaled.append([jnp.broadcast_to(g * w, (tokens, HEAD_DIM)) for g, w in zip(gains, weights)])
+        sums = put(sums, experts + 2 + e, scaled[e])
+
+    live = len_ref[0]
+    for c in range(chunks):
+        copies[small + c].wait()
+        for h in range(key_heads):
+            keys = kv[c * part : (c + 1) * part, 2 * h * HEAD_DIM : (2 * h + 1) * HEAD_DIM]
+            s = lax.dot_general(queries[h], keys, BY_ROW, preferred_element_type=jnp.float32)
+            at = lax.broadcasted_iota(jnp.int32, (rows, part), 1) + c * part
+            scores[h, :, c * part : (c + 1) * part] = jnp.where(at < live, s * scale, -jnp.inf)
     streams = []
     for h in range(key_heads):
         s = scores[h]
@@ -140,26 +160,10 @@
             out_ref[:, at : at + HEAD_DIM] = got
             streams.append(got.astype(jnp.float32))
 
-    lane = lax.broadcasted_iota(jnp.int32, (tokens, LANES), 1)
-    sums = jnp.zeros((tokens, LANES), jnp.float32)
-
-    def put(sums, at, pieces):
-        total = pieces[0]
-        for piece in pieces[1:]:
-            total = total + piece
-        return jnp.where(lane == at, jnp.sum(total, axis=1, keepdims=True), sums)
-
-    blocks = range(len(streams))
     sums = put(sums, experts, streams)
     sums = put(sums, experts + 1, [x * x for x in streams])
-    gain = gain_ref[...].astype(jnp.float32).reshape(1, -1)
-    gains = [gain[:, b * HEAD_DIM : (b + 1) * HEAD_DIM] for b in blocks]
-    scaled = [x * g for x, g in zip(streams, gains)]
     for e in range(experts):
-        weights = [router_ref[e : e + 1, b * HEAD_DIM : (b + 1) * HEAD_DIM].astype(jnp.float32) for b in blocks]
-        sums = put(sums, e, [x * w for x, w in zip(scaled, weights)])
-        plain = [jnp.broadcast_to(g * w, (tokens, HEAD_DIM)) for g, w in zip(gains, weights)]
-        sums = put(sums, experts + 2 + e, plain)
+        sums = put(sums, e, [x * w for x, w in zip(streams, scaled[e])])
     for i, term in enumerate(split_terms(sums)):
         side = side + (pltpu.roll(term, i * SLOT, 1) if i else term)
     out_ref[:, columns : columns + LANES] = side.astype(out_ref.dtype)
@@ -291,8 +295,15 @@
     )(token, *pieces)
 
 
-def hidden_kernel(place_ref, near, far, gate_a, gate_b, up_a, up_hbm, hidden, x, up_b, sems, *, experts, rest):
-    loads = start_load(up_hbm, up_b, rest, sems)
+def hidden_kernel(
+    place_ref, near, far, gate_a, gate_c, up_a, gate_hbm, up_hbm, hidden, x, gate_b, up_b, up_c, sems, *, experts, parts
+):
+    loads = [
+        start_load(source, target, part, sems.at[i])
+        for i, (source, target, part) in enumerate(
+            ((up_hbm, up_c, parts[2]), (gate_hbm, gate_b, parts[1]), (up_hbm, up_b, parts[1]))
+        )
+    ]
     model = gate_a.shape[1]
     step = 2 * LANES
     for at in range(0, model, step):
@@ -303,41 +314,46 @@
     expert = place_ref[1]
     mine = (at == expert) | (at == expert + experts)
     share = jnp.sum(jnp.where(mine, side, 0.0), axis=0, keepdims=True)
-    first = 0
-    for gate, up in ((gate_a, up_a), (gate_b, up_b)):
-        if first:
-            for copy in loads:
-                copy.wait()
-        units = gate.shape[0]
-        for at in range(0, units, UNITS):
-            part = slice(at, min(at + UNITS, units))
-            a = jnp.dot(gate[part], x[...], preferred_element_type=jnp.float32)
-            b = jnp.dot(up[part], x[...], preferred_element_type=jnp.float32)
+    work = (
+        (parts[0], gate_a, up_a, []),
+        (parts[2], gate_c, up_c, loads[0]),
+        (parts[1], gate_b, up_b, loads[1] + loads[2]),
+    )
+    for part, gate, up, copies in work:
+        for copy in copies:
+            copy.wait()
+        for at in range(0, part.size, UNITS):
+            end = min(at + UNITS, part.size)
+            a = jnp.dot(gate[at:end], x[...], preferred_element_type=jnp.float32)
+            b = jnp.dot(up[at:end], x[...], preferred_element_type=jnp.float32)
             out = a / (1.0 + jnp.exp(-a)) * b * share
-            hidden[:, first + part.start : first + part.stop] = out.T.astype(hidden.dtype)
-        first += units
-
-
-def run_hidden(place, near, far, gate_a, gate_b, up_a, up_w, rest, experts):
+            hidden[:, part.start + at : part.start + end] = out.T.astype(hidden.dtype)
+
+
+def run_hidden(place, near, far, gate_a, gate_c, up_a, gate_w, up_w, parts, experts):
     units, model = up_w.shape[1:]
     rows = 2 * near.shape[0]
     vmem = pl.BlockSpec(memory_space=pltpu.VMEM)
     return pl.pallas_call(
-        functools.partial(hidden_kernel, experts=experts, rest=rest),
+        functools.partial(hidden_kernel, experts=experts, parts=parts),
         out_shape=jax.ShapeDtypeStruct((rows, units), jnp.bfloat16),
-        in_specs=[pl.BlockSpec(memory_space=pltpu.SMEM)] + [vmem] * 5 + [pl.BlockSpec(memory_space=pl.ANY)],
+        in_specs=[pl.BlockSpec(memory_space=pltpu.SMEM)]
+        + [vmem] * 5
+        + [pl.BlockSpec(memory_space=pl.ANY)] * 2,
         out_specs=vmem,
         scratch_shapes=[
             pltpu.VMEM((model, rows), jnp.bfloat16),
-            pltpu.VMEM((rest.size, model), up_w.dtype),
-            pltpu.SemaphoreType.DMA((CHUNKS,)),
+            pltpu.VMEM((parts[1].size, model), gate_w.dtype),
+            pltpu.VMEM((parts[1].size, model), up_w.dtype),
+            pltpu.VMEM((parts[2].size, model), up_w.dtype),
+            pltpu.SemaphoreType.DMA((3, CHUNKS)),
         ],
-        compiler_params=pltpu.CompilerParams(vmem_limit_bytes=(8 if rows <= 64 else 24) * MIB),
+        compiler_params=pltpu.CompilerParams(vmem_limit_bytes=(12 if rows <= 64 else 24) * MIB),
         cost_estimate=pl.CostEstimate(
             flops=4 * rows * units * model, bytes_accessed=4 * units * model, transcendentals=rows * units
         ),
         name="hidden",
-    )(place, near, far, gate_a, gate_b, up_a, pltpu.with_memory_space_constraint(up_w, pltpu.HBM))
+    )(place, near, far, gate_a, gate_c, up_a, *[pltpu.with_memory_space_constraint(w, pltpu.HBM) for w in (gate_w, up_w)])
 
 
 def send(x, axis, mask):
@@ -361,27 +377,27 @@
     place = lax.axis_index("tensor")
     where = jnp.stack([place, lax.axis_index("section") * tensors + place]).astype(jnp.int32)
 
-    early, late = unit_parts(gate_w.shape[1])
-
-    fresh, gate_b = attend(
-        cache_len, queries, new_kv, kv_cache, residual, routes, router, norm_gain, gate_w, late
+    parts = unit_parts(gate_w.shape[1])
+
+    fresh, gate_c = attend(
+        cache_len, queries, new_kv, kv_cache, residual, routes, router, norm_gain, gate_w, parts[2]
     )
     blocks = exchange([fresh] * tensors, "tensor") + [fresh]
-    gate_a, token = load(fresh, gate_w, early)
+    gate_a, token = load(fresh, gate_w, parts[0])
     rows = norm_rows(where, token, blocks, experts)
     ranks = exchange([rows] * groups, "group") + [rows]
-    up_a, token = load(rows, up_w, early)
+    up_a, token = load(rows, up_w, parts[0])
     near = stack_rows(token, ranks)
     far = send(near, "section", 1)
 
-    hidden = run_hidden(where, near, far, gate_a, gate_b, up_a, up_w, late, experts)
+    hidden = run_hidden(where, near, far, gate_a, gate_c, up_a, gate_w, up_w, parts, experts)
     out = jnp.dot(hidden, down_w[0], preferred_element_type=jnp.float32).astype(jnp.bfloat16)
     half = out.shape[0] // 2
     both = add(out[:half], send(out[half:], "section", 1)).astype(jnp.bfloat16)
     both = both.reshape(groups, tokens, -1)
     got = add(*exchange(both, "group"), both[0]).astype(jnp.bfloat16)
-    parts = [lax.dynamic_slice_in_dim(got, (place ^ m) * block, block, axis=1) for m in range(tensors)]
-    mixed = add(*exchange(parts, "tensor"), parts[0], fresh[:, :block])
+    pieces = [lax.dynamic_slice_in_dim(got, (place ^ m) * block, block, axis=1) for m in range(tensors)]
+    mixed = add(*exchange(pieces, "tensor"), pieces[0], fresh[:, :block])
     return mixed.astype(jnp.bfloat16)
 
 

time: 48.9 us -> 50.3 us (1.029)
  Pallas kernels: 17.2 us -> 18.1 us
    pallas_call x1, Pallas kernels: 6.73 us -> 8.23 us  [run_hidden(): pl.pallas_call(functools.partial(hidden_kernel, experts=experts, parts=pa...]
    pallas_call x2, Pallas kernels: 6.83 us -> 5.88 us  [load(): pl.pallas_call(functools.partial(load_kernel, part=part), out_shape=(pltp...]
  transfers between devices with their start and end apart: 14 -> 14, of which waited for: 9 -> 9; matrix products, arithmetic and copies ran while one was open for 0% -> 0% of each run, Pallas kernels for 14% -> 12%
where the time goes in v4:
time: 50.3 us; the launch traced here: 50.1 us
  Pallas kernels  18.1 us (36%)
  starting transfers between devices  17.5 us (35%)
  waiting for transfers between devices  10.9 us (22%)
  matrix products  1.97 us (4%)
  between operations  0.8 us (2%)
  other arithmetic  0.77 us (2%)
    ppermute x14, starting transfers between devices, send(): lax.ppermute(x, axis, [(i, i ^ mask) for i in range(lax.axis_size(axis))])  17.5 us
    ppermute x14, waiting for transfers between devices, send(): lax.ppermute(x, axis, [(i, i ^ mask) for i in range(lax.axis_size(axis))])  10.9 us
    pallas_call x1, Pallas kernels, run_hidden(): pl.pallas_call(functools.partial(hidden_kernel, experts=experts, parts=pa...  8.23 us
    pallas_call x2, Pallas kernels, load(): pl.pallas_call(functools.partial(load_kernel, part=part), out_shape=(pltp...  5.88 us
    pallas_call x1, Pallas kernels, attend(): pl.pallas_call(functools.partial(attention_kernel, chunks=chunks, rest=re...  3.04 us
    dot_general x1, matrix products, per_device(): jnp.dot(hidden, down_w[0], preferred_element_type=jnp.float32)  1.97 us
  transfers between devices with their start and end apart: 14, of which 9 were waited for; matrix products, arithmetic and copies ran while one was open for 0% of the time, Pallas kernels for 12%

profile of v4, /device:TPU:0, one launch (start us, length us, event | category | flops | bytes accessed | tf_op | source)
XLA Modules:
  0.0 50.1 jit_solution(9064053647341634343)
XLA Ops:
  0.7 3.0 %attention.1 = (bf16[8,1024]{1,0:T(8,128)(2,1)S(1)}, bf16[448,3072]{1,0:T(8,128)(2,1)S(1)}) custom-call(s32[1]{0:T(128)S(6)} %copy.12.len_ref, bf16[8,768]{1,0:T(8,128)(2,1)} %q_hbm.1, bf16[8,512]{1,0:T(8,128)(2,1)} %new_hbm.1, bf16[1,2048,512]{2,1,0:T(8,128)(2,1)} %kv_hbm.1, bf16[8,768]{1,0:T(8,128)(2,1)} %res_hbm.1, s32[4,8]{1,0:T(4,128)} %bitcast.11, ...), custom_call_target="tpu_custom_call" | custom-call | flops 50331648 | bytes 2097152 | tf_op jit(solution)/shard_map/attention/pallas_call | solution.py:188
  3.7 5.1 %collective-permute-start = (bf16[8,1024]{1,0:T(8,128)(2,1)S(1)}, bf16[8,1024]{1,0:T(8,128)(2,1)S(1)}, u32[]{:S(2)}, u32[]{:S(2)}) collective-permute-start(bf16[8,1024]{1,0:T(8,128)(2,1)S(1)} %get-tuple-element.11._.refs_3_), channel_id=1, source_target_pairs={{0,3},{1,2},{2,1},{3,0},{4,7},{5,6},{6,5},{7,4},{8,11},{9,10},{10,... | collective-permute-start | bytes 49160 | tf_op jit(solution)/shard_map/ppermute | solution.py:360
  8.8 0.0 collective-permute-start.1
  8.8 0.6 %collective-permute-start.2 = (bf16[8,1024]{1,0:T(8,128)(2,1)S(1)}, bf16[8,1024]{1,0:T(8,128)(2,1)S(1)}, u32[]{:S(2)}, u32[]{:S(2)}) collective-permute-start(bf16[8,1024]{1,0:T(8,128)(2,1)S(1)} %get-tuple-element.11._.refs_3_), channel_id=1, source_target_pairs={{0,1},{1,0},{2,3},{3,2},{4,5},{5,4},{6,7},{7,6},{8,9},{9,8},{10,11... | collective-permute-start | bytes 49160 | tf_op jit(solution)/shard_map/ppermute | solution.py:360
  9.5 0.1 pad_add_fusion.place_ref
  9.5 2.9 %load.2 = (bf16[1024,3072]{1,0:T(8,128)(2,1)S(1)}, f32[8,128]{1,0:T(8,128)S(1)}) custom-call(bf16[8,1024]{1,0:T(8,128)(2,1)S(1)} %get-tuple-element.11._.refs_3_, bf16[1,1728,3072]{2,1,0:T(8,128)(2,1)} %gate_hbm.1), custom_call_target="tpu_custom_call" | custom-call | bytes 12582912 | tf_op jit(solution)/shard_map/load/pallas_call | solution.py:222
  12.4 1.0 %collective-permute-done.1.refs_1_ = bf16[8,1024]{1,0:T(8,128)(2,1)S(1)} collective-permute-done((bf16[8,1024]{1,0:T(8,128)(2,1)S(1)}, bf16[8,1024]{1,0:T(8,128)(2,1)S(1)}, u32[]{:S(2)}, u32[]{:S(2)}) %collective-permute-start.1) | collective-permute-done | bytes 16416 | tf_op jit(solution)/shard_map/ppermute | solution.py:360
  13.5 0.9 %norm.1._.refs_3_ = bf16[8,3200]{1,0:T(8,128)(2,1)S(1)} custom-call(s32[2]{0:T(128)S(1)} %pad_add_fusion.place_ref, f32[8,128]{1,0:T(8,128)S(1)} %get-tuple-element.12._, bf16[8,1024]{1,0:T(8,128)(2,1)S(1)} %collective-permute-done.refs_0_, bf16[8,1024]{1,0:T(8,128)(2,1)S(1)} %collective-permute-done.1.refs_1_, ...), custom_call_target="tpu_custom_call" | custom-call | tf_op jit(solution)/shard_map/norm/pallas_call | solution.py:267
  14.4 2.5 %collective-permute-start.3 = (bf16[8,3200]{1,0:T(8,128)(2,1)S(1)}, bf16[8,3200]{1,0:T(8,128)(2,1)S(1)}, u32[]{:S(2)}, u32[]{:S(2)}) collective-permute-start(bf16[8,3200]{1,0:T(8,128)(2,1)S(1)} %norm.1._.refs_3_), channel_id=1, source_target_pairs={{0,12},{4,8},{8,4},{12,0},{1,13},{5,9},{9,5},{13,1},{2,14},{6,10},... | collective-permute-start | bytes 153608 | tf_op jit(solution)/shard_map/ppermute | solution.py:360
  16.8 0.5 %collective-permute-start.4 = (bf16[8,3200]{1,0:T(8,128)(2,1)S(1)}, bf16[8,3200]{1,0:T(8,128)(2,1)S(1)}, u32[]{:S(2)}, u32[]{:S(2)}) collective-permute-start(bf16[8,3200]{1,0:T(8,128)(2,1)S(1)} %norm.1._.refs_3_), channel_id=1, source_target_pairs={{0,8},{4,12},{8,0},{12,4},{1,9},{5,13},{9,1},{13,5},{2,10},{6,14},... | collective-permute-start | bytes 153608 | tf_op jit(solution)/shard_map/ppermute | solution.py:360
  17.3 0.5 %collective-permute-start.5 = (bf16[8,3200]{1,0:T(8,128)(2,1)S(1)}, bf16[8,3200]{1,0:T(8,128)(2,1)S(1)}, u32[]{:S(2)}, u32[]{:S(2)}) collective-permute-start(bf16[8,3200]{1,0:T(8,128)(2,1)S(1)} %norm.1._.refs_3_), channel_id=1, source_target_pairs={{0,4},{4,0},{8,12},{12,8},{1,5},{5,1},{9,13},{13,9},{2,6},{6,2},{1... | collective-permute-start | bytes 153608 | tf_op jit(solution)/shard_map/ppermute | solution.py:360
  17.9 3.0 %load.3 = (bf16[1024,3072]{1,0:T(8,128)(2,1)S(1)}, f32[8,128]{1,0:T(8,128)S(1)}) custom-call(bf16[8,3200]{1,0:T(8,128)(2,1)S(1)} %norm.1._.refs_3_, bf16[1,1728,3072]{2,1,0:T(8,128)(2,1)} %up_hbm.1), custom_call_target="tpu_custom_call" | custom-call | bytes 12582912 | tf_op jit(solution)/shard_map/load/pallas_call | solution.py:222
  20.9 0.0 collective-permute-done.4.refs_1_
  21.0 0.5 %collective-permute-done.5.refs_2_ = bf16[8,3200]{1,0:T(8,128)(2,1)S(1)} collective-permute-done((bf16[8,3200]{1,0:T(8,128)(2,1)S(1)}, bf16[8,3200]{1,0:T(8,128)(2,1)S(1)}, u32[]{:S(2)}, u32[]{:S(2)}) %collective-permute-start.5) | collective-permute-done | bytes 51232 | tf_op jit(solution)/shard_map/ppermute | solution.py:360
  21.5 0.1 collective-permute-start.6
  21.6 1.4 %collective-permute-done.6.far = bf16[32,3200]{1,0:T(8,128)(2,1)S(1)} collective-permute-done((bf16[32,3200]{1,0:T(8,128)(2,1)S(1)}, bf16[32,3200]{1,0:T(8,128)(2,1)S(1)}, u32[]{:S(2)}, u32[]{:S(2)}) %collective-permute-start.6) | collective-permute-done | bytes 204832 | tf_op jit(solution)/shard_map/ppermute | solution.py:360
  23.0 8.2 %hidden.1 = bf16[64,1728]{1,0:T(8,128)(2,1)S(1)} custom-call(s32[2]{0:T(128)S(1)} %pad_add_fusion.place_ref, bf16[32,3200]{1,0:T(8,128)(2,1)S(1)} %stack.13.near, bf16[32,3200]{1,0:T(8,128)(2,1)S(1)} %collective-permute-done.6.far, bf16[1024,3072]{1,0:T(8,128)(2,1)S(1)} %get-tuple-element.14.gate_a, bf16[448,3072]{1,0:T(8,128)(2,1)S(1)} %get-tuple-element.15.gate_c, ...), custom_call_target="tpu_custom_call" | custom-call | flops 1358954496 | bytes 21233664 | tf_op jit(solution)/shard_map/hidden/pallas_call | solution.py:337
  31.3 2.0 %fusion.2 = bf16[64,3072]{1,0:T(8,128)(2,1)S(1)} fusion(bf16[64,1728]{1,0:T(8,128)(2,1)S(1)} %hidden.1, bf16[1,1728,3072]{2,1,0:T(8,128)(2,1)S(1)} %bitcast.10), kind=kOutput, calls=%fused_computation.2 | convolution fusion | flops 679673856 | bytes 11231232 | tf_op jit(solution)/shard_map/dot_general | solution.py:394
  33.3 0.2 collective-permute-start.7
  33.5 1.3 %collective-permute-done.7 = bf16[32,3072]{1,0:T(8,128)(2,1)S(1)} collective-permute-done((bf16[32,3072]{1,0:T(8,128)(2,1)S(1)}, bf16[32,3072]{1,0:T(8,128)(2,1)S(1)}, u32[]{:S(2)}, u32[]{:S(2)}) %collective-permute-start.7) | collective-permute-done | bytes 196640 | tf_op jit(solution)/shard_map/ppermute | solution.py:360
  34.8 0.1 add_convert_fusion
  34.9 1.0 %collective-permute-start.10 = (bf16[8,3072]{1,0:T(8,128)(2,1)S(1)}, bf16[8,3072]{1,0:T(8,128)(2,1)S(1)}, u32[]{:S(2)}, u32[]{:S(2)}) collective-permute-start(bf16[8,3072]{1,0:T(8,128)(2,1)S(1)} %get-tuple-element.18), channel_id=1, source_target_pairs={{0,4},{4,0},{8,12},{12,8},{1,5},{5,1},{9,13},{13,9},{2,6},{6,2},{1... | collective-permute-start | bytes 147464 | tf_op jit(solution)/shard_map/ppermute | solution.py:360
  35.9 2.0 %collective-permute-start.8 = (bf16[8,3072]{1,0:T(8,128)(2,1)S(1)}, bf16[8,3072]{1,0:T(8,128)(2,1)S(1)}, u32[]{:S(2)}, u32[]{:S(2)}) collective-permute-start(bf16[8,3072]{1,0:T(8,128)(2,1)S(1)} %get-tuple-element.17), channel_id=1, source_target_pairs={{0,12},{4,8},{8,4},{12,0},{1,13},{5,9},{9,5},{13,1},{2,14},{6,10},... | collective-permute-start | bytes 147464 | tf_op jit(solution)/shard_map/ppermute | solution.py:360
  37.9 0.5 %collective-permute-start.9 = (bf16[8,3072]{1,0:T(8,128)(2,1)S(1)}, bf16[8,3072]{1,0:T(8,128)(2,1)S(1)}, u32[]{:S(2)}, u32[]{:S(2)}) collective-permute-start(bf16[8,3072]{1,0:T(8,128)(2,1)S(1)} %get-tuple-element.19), channel_id=1, source_target_pairs={{0,8},{4,12},{8,0},{12,4},{1,9},{5,13},{9,1},{13,5},{2,10},{6,14},... | collective-permute-start | bytes 147464 | tf_op jit(solution)/shard_map/ppermute | solution.py:360
  38.4 0.6 %collective-permute-done.10 = bf16[8,3072]{1,0:T(8,128)(2,1)S(1)} collective-permute-done((bf16[8,3072]{1,0:T(8,128)(2,1)S(1)}, bf16[8,3072]{1,0:T(8,128)(2,1)S(1)}, u32[]{:S(2)}, u32[]{:S(2)}) %collective-permute-start.10) | collective-permute-done | bytes 49184 | tf_op jit(solution)/shard_map/ppermute | solution.py:360
  39.0 2.0 %collective-permute-done.8 = bf16[8,3072]{1,0:T(8,128)(2,1)S(1)} collective-permute-done((bf16[8,3072]{1,0:T(8,128)(2,1)S(1)}, bf16[8,3072]{1,0:T(8,128)(2,1)S(1)}, u32[]{:S(2)}, u32[]{:S(2)}) %collective-permute-start.8) | collective-permute-done | bytes 49184 | tf_op jit(solution)/shard_map/ppermute | solution.py:360
  41.0 1.0 %collective-permute-done.9 = bf16[8,3072]{1,0:T(8,128)(2,1)S(1)} collective-permute-done((bf16[8,3072]{1,0:T(8,128)(2,1)S(1)}, bf16[8,3072]{1,0:T(8,128)(2,1)S(1)}, u32[]{:S(2)}, u32[]{:S(2)}) %collective-permute-start.9) | collective-permute-done | bytes 49184 | tf_op jit(solution)/shard_map/ppermute | solution.py:360
  42.1 2.8 %collective-permute-start.11 = (bf16[8,768]{1,0:T(8,128)(2,1)S(1)}, bf16[8,768]{1,0:T(8,128)(2,1)S(1)}, u32[]{:S(2)}, u32[]{:S(2)}) collective-permute-start(bf16[8,768]{1,0:T(8,128)(2,1)S(1)} %get-tuple-element.20), channel_id=1, source_target_pairs={{0,3},{1,2},{2,1},{3,0},{4,7},{5,6},{6,5},{7,4},{8,11},{9,10},{10,... | collective-permute-start | bytes 36872 | tf_op jit(solution)/shard_map/ppermute | solution.py:360
  44.9 1.7 %collective-permute-start.13 = (bf16[8,768]{1,0:T(8,128)(2,1)S(1)}, bf16[8,768]{1,0:T(8,128)(2,1)S(1)}, u32[]{:S(2)}, u32[]{:S(2)}) collective-permute-start(bf16[8,768]{1,0:T(8,128)(2,1)S(1)} %get-tuple-element.21), channel_id=1, source_target_pairs={{0,1},{1,0},{2,3},{3,2},{4,5},{5,4},{6,7},{7,6},{8,9},{9,8},{10,11... | collective-permute-start | bytes 36872 | tf_op jit(solution)/shard_map/ppermute | solution.py:360
  46.5 1.1 %collective-permute-done.11 = bf16[8,768]{1,0:T(8,128)(2,1)S(1)} collective-permute-done((bf16[8,768]{1,0:T(8,128)(2,1)S(1)}, bf16[8,768]{1,0:T(8,128)(2,1)S(1)}, u32[]{:S(2)}, u32[]{:S(2)}) %collective-permute-start.11) | collective-permute-done | bytes 12320 | tf_op jit(solution)/shard_map/ppermute | solution.py:360
  47.6 1.8 %collective-permute-done.12 = bf16[8,768]{1,0:T(8,128)(2,1)S(1)} collective-permute-done((bf16[8,768]{1,0:T(8,128)(2,1)S(1)}, bf16[8,768]{1,0:T(8,128)(2,1)S(1)}, u32[]{:S(2)}, u32[]{:S(2)}) %collective-permute-start.12) | collective-permute-done | bytes 12320 | tf_op jit(solution)/shard_map/ppermute | solution.py:360
  49.4 0.6 %add_convert_fusion.2 = bf16[8,768]{1,0:T(8,128)(2,1)} fusion(bf16[8,768]{1,0:T(8,128)(2,1)S(1)} %collective-permute-done.13, bf16[8,768]{1,0:T(8,128)(2,1)S(1)} %collective-permute-done.12, bf16[8,768]{1,0:T(8,128)(2,1)S(1)} %collective-permute-done.11, bf16[8,1024]{1,0:T(8,128)(2,1)S(1)} %get-tuple-element.11._.refs_3_, ...), kind=kLoop, calls=%fused_computation.5 | loop fusion | flops 61440 | bytes 73732 | tf_op jit(solution)/shard_map/convert_element_type | solution.py:401
  (17 shorter events, 0.1 us)
Async XLA Ops:
  3.7 8.7 %collective-permute-start = (bf16[8,1024]{1,0:T(8,128)(2,1)S(1)}, bf16[8,1024]{1,0:T(8,128)(2,1)S(1)}, u32[]{:S(2)}, u32[]{:S(2)}) collective-permute-start(bf16[8,1024]{1,0:T(8,128)(2,1)S(1)} %get-tuple-element.11._.refs_3_), channel_id=1, source_target_pairs={{0,3},{1,2},{2,1},{3,0},{4,7},{5,6},{6,5},{7,4},{8,11},{9,10},{10,... | collective-permute-start | bytes 49160 | tf_op jit(solution)/shard_map/ppermute | solution.py:360
  8.8 4.6 %collective-permute-start.1 = (bf16[8,1024]{1,0:T(8,128)(2,1)S(1)}, bf16[8,1024]{1,0:T(8,128)(2,1)S(1)}, u32[]{:S(2)}, u32[]{:S(2)}) collective-permute-start(bf16[8,1024]{1,0:T(8,128)(2,1)S(1)} %get-tuple-element.11._.refs_3_), channel_id=1, source_target_pairs={{0,2},{1,3},{2,0},{3,1},{4,6},{5,7},{6,4},{7,5},{8,10},{9,11},{10,... | collective-permute-start | bytes 49160 | tf_op jit(solution)/shard_map/ppermute | solution.py:360
  8.8 4.6 %collective-permute-start.2 = (bf16[8,1024]{1,0:T(8,128)(2,1)S(1)}, bf16[8,1024]{1,0:T(8,128)(2,1)S(1)}, u32[]{:S(2)}, u32[]{:S(2)}) collective-permute-start(bf16[8,1024]{1,0:T(8,128)(2,1)S(1)} %get-tuple-element.11._.refs_3_), channel_id=1, source_target_pairs={{0,1},{1,0},{2,3},{3,2},{4,5},{5,4},{6,7},{7,6},{8,9},{9,8},{10,11... | collective-permute-start | bytes 49160 | tf_op jit(solution)/shard_map/ppermute | solution.py:360
  14.4 6.5 %collective-permute-start.3 = (bf16[8,3200]{1,0:T(8,128)(2,1)S(1)}, bf16[8,3200]{1,0:T(8,128)(2,1)S(1)}, u32[]{:S(2)}, u32[]{:S(2)}) collective-permute-start(bf16[8,3200]{1,0:T(8,128)(2,1)S(1)} %norm.1._.refs_3_), channel_id=1, source_target_pairs={{0,12},{4,8},{8,4},{12,0},{1,13},{5,9},{9,5},{13,1},{2,14},{6,10},... | collective-permute-start | bytes 153608 | tf_op jit(solution)/shard_map/ppermute | solution.py:360
  16.8 4.1 %collective-permute-start.4 = (bf16[8,3200]{1,0:T(8,128)(2,1)S(1)}, bf16[8,3200]{1,0:T(8,128)(2,1)S(1)}, u32[]{:S(2)}, u32[]{:S(2)}) collective-permute-start(bf16[8,3200]{1,0:T(8,128)(2,1)S(1)} %norm.1._.refs_3_), channel_id=1, source_target_pairs={{0,8},{4,12},{8,0},{12,4},{1,9},{5,13},{9,1},{13,5},{2,10},{6,14},... | collective-permute-start | bytes 153608 | tf_op jit(solution)/shard_map/ppermute | solution.py:360
  17.3 4.1 %collective-permute-start.5 = (bf16[8,3200]{1,0:T(8,128)(2,1)S(1)}, bf16[8,3200]{1,0:T(8,128)(2,1)S(1)}, u32[]{:S(2)}, u32[]{:S(2)}) collective-permute-start(bf16[8,3200]{1,0:T(8,128)(2,1)S(1)} %norm.1._.refs_3_), channel_id=1, source_target_pairs={{0,4},{4,0},{8,12},{12,8},{1,5},{5,1},{9,13},{13,9},{2,6},{6,2},{1... | collective-permute-start | bytes 153608 | tf_op jit(solution)/shard_map/ppermute | solution.py:360
  17.9 13.4 %slice-start = ((s8[10616832]{0:T(1024)(128)(4,1)}), s8[4194304]{0:T(1024)(128)(4,1)S(1)}, s32[]{:S(2)}) async-start(s8[10616832]{0:T(1024)(128)(4,1)} %bitcast.9), calls=%async_computation | async-start | bytes 8388608
  21.5 1.5 %collective-permute-start.6 = (bf16[32,3200]{1,0:T(8,128)(2,1)S(1)}, bf16[32,3200]{1,0:T(8,128)(2,1)S(1)}, u32[]{:S(2)}, u32[]{:S(2)}) collective-permute-start(bf16[32,3200]{1,0:T(8,128)(2,1)S(1)} %stack.13.near), channel_id=1, source_target_pairs={{0,16},{16,0},{1,17},{17,1},{2,18},{18,2},{3,19},{19,3},{4,20},{20... | collective-permute-start | bytes 614408 | tf_op jit(solution)/shard_map/ppermute | solution.py:360
  23.0 8.3 %slice-start.1 = ((s8[10616832]{0:T(1024)(128)(4,1)}), s8[4194304]{0:T(1024)(128)(4,1)S(1)}, s32[]{:S(2)}) async-start(s8[10616832]{0:T(1024)(128)(4,1)} %bitcast.9), calls=%async_computation.1 | async-start | bytes 8388608
  23.0 8.3 %slice-start.2 = ((s8[10616832]{0:T(1024)(128)(4,1)}), s8[2228224]{0:T(1024)(128)(4,1)S(1)}, s32[]{:S(2)}) async-start(s8[10616832]{0:T(1024)(128)(4,1)} %bitcast.9), calls=%async_computation.2 | async-start | bytes 4456448
  33.3 1.5 %collective-permute-start.7 = (bf16[32,3072]{1,0:T(8,128)(2,1)S(1)}, bf16[32,3072]{1,0:T(8,128)(2,1)S(1)}, u32[]{:S(2)}, u32[]{:S(2)}) collective-permute-start(bf16[32,3072]{1,0:T(8,128)(2,1)S(1)} %slice.33), channel_id=1, source_target_pairs={{0,16},{16,0},{1,17},{17,1},{2,18},{18,2},{3,19},{19,3},{4,20},{20... | collective-permute-start | bytes 589832 | tf_op jit(solution)/shard_map/ppermute | solution.py:360
  34.9 4.2 %collective-permute-start.10 = (bf16[8,3072]{1,0:T(8,128)(2,1)S(1)}, bf16[8,3072]{1,0:T(8,128)(2,1)S(1)}, u32[]{:S(2)}, u32[]{:S(2)}) collective-permute-start(bf16[8,3072]{1,0:T(8,128)(2,1)S(1)} %get-tuple-element.18), channel_id=1, source_target_pairs={{0,4},{4,0},{8,12},{12,8},{1,5},{5,1},{9,13},{13,9},{2,6},{6,2},{1... | collective-permute-start | bytes 147464 | tf_op jit(solution)/shard_map/ppermute | solution.py:360
  35.9 5.1 %collective-permute-start.8 = (bf16[8,3072]{1,0:T(8,128)(2,1)S(1)}, bf16[8,3072]{1,0:T(8,128)(2,1)S(1)}, u32[]{:S(2)}, u32[]{:S(2)}) collective-permute-start(bf16[8,3072]{1,0:T(8,128)(2,1)S(1)} %get-tuple-element.17), channel_id=1, source_target_pairs={{0,12},{4,8},{8,4},{12,0},{1,13},{5,9},{9,5},{13,1},{2,14},{6,10},... | collective-permute-start | bytes 147464 | tf_op jit(solution)/shard_map/ppermute | solution.py:360
  37.9 4.1 %collective-permute-start.9 = (bf16[8,3072]{1,0:T(8,128)(2,1)S(1)}, bf16[8,3072]{1,0:T(8,128)(2,1)S(1)}, u32[]{:S(2)}, u32[]{:S(2)}) collective-permute-start(bf16[8,3072]{1,0:T(8,128)(2,1)S(1)} %get-tuple-element.19), channel_id=1, source_target_pairs={{0,8},{4,12},{8,0},{12,4},{1,9},{5,13},{9,1},{13,5},{2,10},{6,14},... | collective-permute-start | bytes 147464 | tf_op jit(solution)/shard_map/ppermute | solution.py:360
  42.1 5.6 %collective-permute-start.11 = (bf16[8,768]{1,0:T(8,128)(2,1)S(1)}, bf16[8,768]{1,0:T(8,128)(2,1)S(1)}, u32[]{:S(2)}, u32[]{:S(2)}) collective-permute-start(bf16[8,768]{1,0:T(8,128)(2,1)S(1)} %get-tuple-element.20), channel_id=1, source_target_pairs={{0,3},{1,2},{2,1},{3,0},{4,7},{5,6},{6,5},{7,4},{8,11},{9,10},{10,... | collective-permute-start | bytes 36872 | tf_op jit(solution)/shard_map/ppermute | solution.py:360
  44.8 4.6 %collective-permute-start.12 = (bf16[8,768]{1,0:T(8,128)(2,1)S(1)}, bf16[8,768]{1,0:T(8,128)(2,1)S(1)}, u32[]{:S(2)}, u32[]{:S(2)}) collective-permute-start(bf16[8,768]{1,0:T(8,128)(2,1)S(1)} %get-tuple-element.22), channel_id=1, source_target_pairs={{0,2},{1,3},{2,0},{3,1},{4,6},{5,7},{6,4},{7,5},{8,10},{9,11},{10,... | collective-permute-start | bytes 36872 | tf_op jit(solution)/shard_map/ppermute | solution.py:360
  44.9 4.6 %collective-permute-start.13 = (bf16[8,768]{1,0:T(8,128)(2,1)S(1)}, bf16[8,768]{1,0:T(8,128)(2,1)S(1)}, u32[]{:S(2)}, u32[]{:S(2)}) collective-permute-start(bf16[8,768]{1,0:T(8,128)(2,1)S(1)} %get-tuple-element.21), channel_id=1, source_target_pairs={{0,1},{1,0},{2,3},{3,2},{4,5},{5,4},{6,7},{7,6},{8,9},{9,8},{10,11... | collective-permute-start | bytes 36872 | tf_op jit(solution)/shard_map/ppermute | solution.py:360

commit v5 on v3

--- a/solution.py
+++ b/solution.py
@@ -25,11 +25,14 @@
     return high, middle, rest - middle
 
 
-def unit_parts(units):
-    first = max(UNITS, units * 3 // 4 // UNITS * UNITS)
-    if units <= 2 * UNITS:
-        first = units // 32 * 16
-    return pl.ds(0, first), pl.ds(first, units - first)
+def cut_units(units):
+    if units <= 7 * UNITS // 2:
+        return units // 32 * 16, units // 32 * 16
+    return units * 3 // 4 // UNITS * UNITS, units - UNITS
+
+
+def unit_parts(units, cut):
+    return pl.ds(0, cut), pl.ds(cut, units - cut)
 
 
 def start_load(source, target, part, sems):
@@ -291,53 +294,50 @@
     )(token, *pieces)
 
 
-def hidden_kernel(place_ref, near, far, gate_a, gate_b, up_a, up_hbm, hidden, x, up_b, sems, *, experts, rest):
-    loads = start_load(up_hbm, up_b, rest, sems)
+def hidden_kernel(place_ref, near, far, gate_a, gate_b, up_a, up_b, _, hidden, x, *, experts):
+    half = near.shape[0]
     model = gate_a.shape[1]
-    step = 2 * LANES
-    for at in range(0, model, step):
-        both = [ref[:, at : at + step].astype(jnp.float32) for ref in (near, far)]
-        x[at : at + step] = jnp.concatenate(both, axis=0).T.astype(x.dtype)
+    x[:half] = near[:, :model]
+    x[half:] = far[:, :model]
     side = jnp.concatenate([ref[:, model:].astype(jnp.float32) for ref in (near, far)], axis=0).T
     at = lax.broadcasted_iota(jnp.int32, side.shape, 0)
     expert = place_ref[1]
     mine = (at == expert) | (at == expert + experts)
     share = jnp.sum(jnp.where(mine, side, 0.0), axis=0, keepdims=True)
-    first = 0
-    for gate, up in ((gate_a, up_a), (gate_b, up_b)):
-        if first:
-            for copy in loads:
-                copy.wait()
-        units = gate.shape[0]
-        for at in range(0, units, UNITS):
-            part = slice(at, min(at + UNITS, units))
-            a = jnp.dot(gate[part], x[...], preferred_element_type=jnp.float32)
-            b = jnp.dot(up[part], x[...], preferred_element_type=jnp.float32)
+    units = gate_a.shape[0] + gate_b.shape[0]
+    cuts = sorted({0, gate_a.shape[0], up_a.shape[0], units})
+
+    def times(first, second, start, stop):
+        cut = first.shape[0]
+        block = first[start:stop] if stop <= cut else second[start - cut : stop - cut]
+        return lax.dot_general(block, x[...], BY_ROW, preferred_element_type=jnp.float32)
+
+    for low, high in zip(cuts, cuts[1:]):
+        for start in range(low, high, UNITS):
+            stop = min(start + UNITS, high)
+            a = times(gate_a, gate_b, start, stop)
+            b = times(up_a, up_b, start, stop)
             out = a / (1.0 + jnp.exp(-a)) * b * share
-            hidden[:, first + part.start : first + part.stop] = out.T.astype(hidden.dtype)
-        first += units
-
-
-def run_hidden(place, near, far, gate_a, gate_b, up_a, up_w, rest, experts):
-    units, model = up_w.shape[1:]
+            hidden[:, start:stop] = out.T.astype(hidden.dtype)
+
+
+def run_hidden(place, near, far, weights, token, experts):
+    units = weights[0].shape[0] + weights[1].shape[0]
+    model = weights[0].shape[1]
     rows = 2 * near.shape[0]
     vmem = pl.BlockSpec(memory_space=pltpu.VMEM)
     return pl.pallas_call(
-        functools.partial(hidden_kernel, experts=experts, rest=rest),
+        functools.partial(hidden_kernel, experts=experts),
         out_shape=jax.ShapeDtypeStruct((rows, units), jnp.bfloat16),
-        in_specs=[pl.BlockSpec(memory_space=pltpu.SMEM)] + [vmem] * 5 + [pl.BlockSpec(memory_space=pl.ANY)],
+        in_specs=[pl.BlockSpec(memory_space=pltpu.SMEM)] + [vmem] * 7,
         out_specs=vmem,
-        scratch_shapes=[
-            pltpu.VMEM((model, rows), jnp.bfloat16),
-            pltpu.VMEM((rest.size, model), up_w.dtype),
-            pltpu.SemaphoreType.DMA((CHUNKS,)),
-        ],
-        compiler_params=pltpu.CompilerParams(vmem_limit_bytes=(8 if rows <= 64 else 24) * MIB),
+        scratch_shapes=[pltpu.VMEM((rows, model), jnp.bfloat16)],
+        compiler_params=pltpu.CompilerParams(vmem_limit_bytes=(6 if rows <= 64 else 24) * MIB),
         cost_estimate=pl.CostEstimate(
             flops=4 * rows * units * model, bytes_accessed=4 * units * model, transcendentals=rows * units
         ),
         name="hidden",
-    )(place, near, far, gate_a, gate_b, up_a, pltpu.with_memory_space_constraint(up_w, pltpu.HBM))
+    )(place, near, far, *weights, token)
 
 
 def send(x, axis, mask):
@@ -361,20 +361,22 @@
     place = lax.axis_index("tensor")
     where = jnp.stack([place, lax.axis_index("section") * tensors + place]).astype(jnp.int32)
 
-    early, late = unit_parts(gate_w.shape[1])
+    units = gate_w.shape[1]
+    gate_parts, up_parts = [unit_parts(units, cut) for cut in cut_units(units)]
 
     fresh, gate_b = attend(
-        cache_len, queries, new_kv, kv_cache, residual, routes, router, norm_gain, gate_w, late
+        cache_len, queries, new_kv, kv_cache, residual, routes, router, norm_gain, gate_w, gate_parts[1]
     )
     blocks = exchange([fresh] * tensors, "tensor") + [fresh]
-    gate_a, token = load(fresh, gate_w, early)
+    gate_a, token = load(fresh, gate_w, gate_parts[0])
     rows = norm_rows(where, token, blocks, experts)
     ranks = exchange([rows] * groups, "group") + [rows]
-    up_a, token = load(rows, up_w, early)
+    up_a, token = load(rows, up_w, up_parts[0])
     near = stack_rows(token, ranks)
     far = send(near, "section", 1)
-
-    hidden = run_hidden(where, near, far, gate_a, gate_b, up_a, up_w, late, experts)
+    up_b, token = load(near, up_w, up_parts[1])
+
+    hidden = run_hidden(where, near, far, (gate_a, gate_b, up_a, up_b), token, experts)
     out = jnp.dot(hidden, down_w[0], preferred_element_type=jnp.float32).astype(jnp.bfloat16)
     half = out.shape[0] // 2
     both = add(out[:half], send(out[half:], "section", 1)).astype(jnp.bfloat16)

time: 48.9 us -> 49 us (level)
  waiting for transfers between devices: 10.4 us -> 8.74 us
  Pallas kernels: 17.2 us -> 18.5 us
    pallas_call x2 -> x3, Pallas kernels: 6.83 us -> 8.57 us  [load(): pl.pallas_call(functools.partial(load_kernel, part=part), out_shape=(pltp...]
    ppermute x14, waiting for transfers between devices: 10.4 us -> 8.74 us  [send(): lax.ppermute(x, axis, [(i, i ^ mask) for i in range(lax.axis_size(axis))])]
  transfers between devices with their start and end apart: 14 -> 14, of which waited for: 9 -> 7; matrix products, arithmetic and copies ran while one was open for 0% -> 0% of each run, Pallas kernels for 14% -> 18%
where the time goes in v5:
time: 49 us; the launch traced here: 48.8 us
  Pallas kernels  18.5 us (38%)
  starting transfers between devices  17.9 us (37%)
  waiting for transfers between devices  8.74 us (18%)
  matrix products  1.97 us (4%)
  between operations  0.85 us (2%)
  other arithmetic  0.77 us (2%)
    ppermute x14, starting transfers between devices, send(): lax.ppermute(x, axis, [(i, i ^ mask) for i in range(lax.axis_size(axis))])  17.9 us
    ppermute x14, waiting for transfers between devices, send(): lax.ppermute(x, axis, [(i, i ^ mask) for i in range(lax.axis_size(axis))])  8.74 us
    pallas_call x3, Pallas kernels, load(): pl.pallas_call(functools.partial(load_kernel, part=part), out_shape=(pltp...  8.57 us
    pallas_call x1, Pallas kernels, run_hidden(): pl.pallas_call(functools.partial(hidden_kernel, experts=experts), out_sha...  6.34 us
    pallas_call x1, Pallas kernels, attend(): pl.pallas_call(functools.partial(attention_kernel, chunks=chunks, rest=re...  2.68 us
    dot_general x1, matrix products, per_device(): jnp.dot(hidden, down_w[0], preferred_element_type=jnp.float32)  1.97 us
  transfers between devices with their start and end apart: 14, of which 7 were waited for; matrix products, arithmetic and copies ran while one was open for 0% of the time, Pallas kernels for 18%

profile of v5, /device:TPU:0, one launch (start us, length us, event | category | flops | bytes accessed | tf_op | source)
XLA Modules:
  0.0 48.8 jit_solution(9334463753334619951)
XLA Ops:
  0.7 2.7 %attention.1 = (bf16[8,1024]{1,0:T(8,128)(2,1)S(1)}, bf16[448,3072]{1,0:T(8,128)(2,1)S(1)}) custom-call(s32[1]{0:T(128)S(6)} %copy.12.len_ref, bf16[8,768]{1,0:T(8,128)(2,1)} %q_hbm.1, bf16[8,512]{1,0:T(8,128)(2,1)} %new_hbm.1, bf16[1,2048,512]{2,1,0:T(8,128)(2,1)} %kv_hbm.1, bf16[8,768]{1,0:T(8,128)(2,1)} %res_hbm.1, s32[4,8]{1,0:T(4,128)} %bitcast.11, ...), custom_call_target="tpu_custom_call" | custom-call | flops 50331648 | bytes 2097152 | tf_op jit(solution)/shard_map/attention/pallas_call | solution.py:187
  3.3 5.1 %collective-permute-start = (bf16[8,1024]{1,0:T(8,128)(2,1)S(1)}, bf16[8,1024]{1,0:T(8,128)(2,1)S(1)}, u32[]{:S(2)}, u32[]{:S(2)}) collective-permute-start(bf16[8,1024]{1,0:T(8,128)(2,1)S(1)} %get-tuple-element.13._.refs_3_), channel_id=1, source_target_pairs={{0,3},{1,2},{2,1},{3,0},{4,7},{5,6},{6,5},{7,4},{8,11},{9,10},{10,... | collective-permute-start | bytes 49160 | tf_op jit(solution)/shard_map/ppermute | solution.py:344
  8.5 0.0 collective-permute-start.1
  8.5 0.6 %collective-permute-start.2 = (bf16[8,1024]{1,0:T(8,128)(2,1)S(1)}, bf16[8,1024]{1,0:T(8,128)(2,1)S(1)}, u32[]{:S(2)}, u32[]{:S(2)}) collective-permute-start(bf16[8,1024]{1,0:T(8,128)(2,1)S(1)} %get-tuple-element.13._.refs_3_), channel_id=1, source_target_pairs={{0,1},{1,0},{2,3},{3,2},{4,5},{5,4},{6,7},{7,6},{8,9},{9,8},{10,11... | collective-permute-start | bytes 49160 | tf_op jit(solution)/shard_map/ppermute | solution.py:344
  9.1 0.1 pad_add_fusion.place_ref
  9.2 3.3 %load.3 = (bf16[1280,3072]{1,0:T(8,128)(2,1)S(1)}, f32[8,128]{1,0:T(8,128)S(1)}) custom-call(bf16[8,1024]{1,0:T(8,128)(2,1)S(1)} %get-tuple-element.13._.refs_3_, bf16[1,1728,3072]{2,1,0:T(8,128)(2,1)} %source.3), custom_call_target="tpu_custom_call" | custom-call | bytes 15728640 | tf_op jit(solution)/shard_map/load/pallas_call | solution.py:221
  12.5 0.6 %collective-permute-done.1.refs_1_ = bf16[8,1024]{1,0:T(8,128)(2,1)S(1)} collective-permute-done((bf16[8,1024]{1,0:T(8,128)(2,1)S(1)}, bf16[8,1024]{1,0:T(8,128)(2,1)S(1)}, u32[]{:S(2)}, u32[]{:S(2)}) %collective-permute-start.1) | collective-permute-done | bytes 16416 | tf_op jit(solution)/shard_map/ppermute | solution.py:344
  13.1 0.9 %norm.1._.refs_3_ = bf16[8,3200]{1,0:T(8,128)(2,1)S(1)} custom-call(s32[2]{0:T(128)S(1)} %pad_add_fusion.place_ref, f32[8,128]{1,0:T(8,128)S(1)} %get-tuple-element.14._, bf16[8,1024]{1,0:T(8,128)(2,1)S(1)} %collective-permute-done.refs_0_, bf16[8,1024]{1,0:T(8,128)(2,1)S(1)} %collective-permute-done.1.refs_1_, ...), custom_call_target="tpu_custom_call" | custom-call | tf_op jit(solution)/shard_map/norm/pallas_call | solution.py:266
  14.0 2.5 %collective-permute-start.3 = (bf16[8,3200]{1,0:T(8,128)(2,1)S(1)}, bf16[8,3200]{1,0:T(8,128)(2,1)S(1)}, u32[]{:S(2)}, u32[]{:S(2)}) collective-permute-start(bf16[8,3200]{1,0:T(8,128)(2,1)S(1)} %norm.1._.refs_3_), channel_id=1, source_target_pairs={{0,12},{4,8},{8,4},{12,0},{1,13},{5,9},{9,5},{13,1},{2,14},{6,10},... | collective-permute-start | bytes 153608 | tf_op jit(solution)/shard_map/ppermute | solution.py:344
  16.5 0.5 %collective-permute-start.4 = (bf16[8,3200]{1,0:T(8,128)(2,1)S(1)}, bf16[8,3200]{1,0:T(8,128)(2,1)S(1)}, u32[]{:S(2)}, u32[]{:S(2)}) collective-permute-start(bf16[8,3200]{1,0:T(8,128)(2,1)S(1)} %norm.1._.refs_3_), channel_id=1, source_target_pairs={{0,8},{4,12},{8,0},{12,4},{1,9},{5,13},{9,1},{13,5},{2,10},{6,14},... | collective-permute-start | bytes 153608 | tf_op jit(solution)/shard_map/ppermute | solution.py:344
  17.0 0.5 %collective-permute-start.5 = (bf16[8,3200]{1,0:T(8,128)(2,1)S(1)}, bf16[8,3200]{1,0:T(8,128)(2,1)S(1)}, u32[]{:S(2)}, u32[]{:S(2)}) collective-permute-start(bf16[8,3200]{1,0:T(8,128)(2,1)S(1)} %norm.1._.refs_3_), channel_id=1, source_target_pairs={{0,4},{4,0},{8,12},{12,8},{1,5},{5,1},{9,13},{13,9},{2,6},{6,2},{1... | collective-permute-start | bytes 153608 | tf_op jit(solution)/shard_map/ppermute | solution.py:344
  17.5 3.7 %load.4 = (bf16[1472,3072]{1,0:T(8,128)(2,1)S(1)}, f32[8,128]{1,0:T(8,128)S(1)}) custom-call(bf16[8,3200]{1,0:T(8,128)(2,1)S(1)} %norm.1._.refs_3_, bf16[1,1728,3072]{2,1,0:T(8,128)(2,1)} %source.5), custom_call_target="tpu_custom_call" | custom-call | bytes 18087936 | tf_op jit(solution)/shard_map/load/pallas_call | solution.py:221
  21.3 0.1 collective-permute-start.6
  21.4 0.0 slice-start
  21.4 1.5 %load.5 = (bf16[256,3072]{1,0:T(8,128)(2,1)S(1)}, f32[8,128]{1,0:T(8,128)S(1)}) custom-call(bf16[32,3200]{1,0:T(8,128)(2,1)S(1)} %stack.13._.near, bf16[1,1728,3072]{2,1,0:T(8,128)(2,1)} %source.5), custom_call_target="tpu_custom_call" | custom-call | bytes 3145728 | tf_op jit(solution)/shard_map/load/pallas_call | solution.py:221
  22.9 0.0 slice-start.1
  22.9 6.3 %hidden.1 = bf16[64,1728]{1,0:T(8,128)(2,1)S(1)} custom-call(s32[2]{0:T(128)S(1)} %pad_add_fusion.place_ref, bf16[32,3200]{1,0:T(8,128)(2,1)S(1)} %stack.13._.near, bf16[32,3200]{1,0:T(8,128)(2,1)S(1)} %collective-permute-done.6.far, bf16[1280,3072]{1,0:T(8,128)(2,1)S(1)} %get-tuple-element.16.gate_a, bf16[448,3072]{1,0:T(8,128)(2,1)S(1)} %get-tuple-element.17.gate_b, ...), custom_call_target="tpu_custom_call" | custom-call | flops 1358954496 | bytes 21233664 | tf_op jit(solution)/shard_map/hidden/pallas_call | solution.py:329
  29.3 2.0 %fusion.2 = bf16[64,3072]{1,0:T(8,128)(2,1)S(1)} fusion(bf16[64,1728]{1,0:T(8,128)(2,1)S(1)} %hidden.1, bf16[1,1728,3072]{2,1,0:T(8,128)(2,1)S(1)} %bitcast.10), kind=kOutput, calls=%fused_computation.2 | convolution fusion | flops 679673856 | bytes 11231232 | tf_op jit(solution)/shard_map/dot_general | solution.py:380
  31.3 0.5 %collective-permute-start.7 = (bf16[32,3072]{1,0:T(8,128)(2,1)S(1)}, bf16[32,3072]{1,0:T(8,128)(2,1)S(1)}, u32[]{:S(2)}, u32[]{:S(2)}) collective-permute-start(bf16[32,3072]{1,0:T(8,128)(2,1)S(1)} %slice.33), channel_id=1, source_target_pairs={{0,16},{16,0},{1,17},{17,1},{2,18},{18,2},{3,19},{19,3},{4,20},{20... | collective-permute-start | bytes 589832 | tf_op jit(solution)/shard_map/ppermute | solution.py:344
  31.9 1.1 %collective-permute-done.7 = bf16[32,3072]{1,0:T(8,128)(2,1)S(1)} collective-permute-done((bf16[32,3072]{1,0:T(8,128)(2,1)S(1)}, bf16[32,3072]{1,0:T(8,128)(2,1)S(1)}, u32[]{:S(2)}, u32[]{:S(2)}) %collective-permute-start.7) | collective-permute-done | bytes 196640 | tf_op jit(solution)/shard_map/ppermute | solution.py:344
  33.0 0.1 add_convert_fusion
  33.0 1.6 %collective-permute-start.10 = (bf16[8,3072]{1,0:T(8,128)(2,1)S(1)}, bf16[8,3072]{1,0:T(8,128)(2,1)S(1)}, u32[]{:S(2)}, u32[]{:S(2)}) collective-permute-start(bf16[8,3072]{1,0:T(8,128)(2,1)S(1)} %get-tuple-element.22), channel_id=1, source_target_pairs={{0,4},{4,0},{8,12},{12,8},{1,5},{5,1},{9,13},{13,9},{2,6},{6,2},{1... | collective-permute-start | bytes 147464 | tf_op jit(solution)/shard_map/ppermute | solution.py:344
  34.6 1.5 %collective-permute-start.8 = (bf16[8,3072]{1,0:T(8,128)(2,1)S(1)}, bf16[8,3072]{1,0:T(8,128)(2,1)S(1)}, u32[]{:S(2)}, u32[]{:S(2)}) collective-permute-start(bf16[8,3072]{1,0:T(8,128)(2,1)S(1)} %get-tuple-element.21), channel_id=1, source_target_pairs={{0,12},{4,8},{8,4},{12,0},{1,13},{5,9},{9,5},{13,1},{2,14},{6,10},... | collective-permute-start | bytes 147464 | tf_op jit(solution)/shard_map/ppermute | solution.py:344
  36.1 0.5 %collective-permute-start.9 = (bf16[8,3072]{1,0:T(8,128)(2,1)S(1)}, bf16[8,3072]{1,0:T(8,128)(2,1)S(1)}, u32[]{:S(2)}, u32[]{:S(2)}) collective-permute-start(bf16[8,3072]{1,0:T(8,128)(2,1)S(1)} %get-tuple-element.23), channel_id=1, source_target_pairs={{0,8},{4,12},{8,0},{12,4},{1,9},{5,13},{9,1},{13,5},{2,10},{6,14},... | collective-permute-start | bytes 147464 | tf_op jit(solution)/shard_map/ppermute | solution.py:344
  36.6 0.6 %collective-permute-done.10 = bf16[8,3072]{1,0:T(8,128)(2,1)S(1)} collective-permute-done((bf16[8,3072]{1,0:T(8,128)(2,1)S(1)}, bf16[8,3072]{1,0:T(8,128)(2,1)S(1)}, u32[]{:S(2)}, u32[]{:S(2)}) %collective-permute-start.10) | collective-permute-done | bytes 49184 | tf_op jit(solution)/shard_map/ppermute | solution.py:344
  37.2 2.4 %collective-permute-done.8 = bf16[8,3072]{1,0:T(8,128)(2,1)S(1)} collective-permute-done((bf16[8,3072]{1,0:T(8,128)(2,1)S(1)}, bf16[8,3072]{1,0:T(8,128)(2,1)S(1)}, u32[]{:S(2)}, u32[]{:S(2)}) %collective-permute-start.8) | collective-permute-done | bytes 49184 | tf_op jit(solution)/shard_map/ppermute | solution.py:344
  39.6 0.6 %collective-permute-done.9 = bf16[8,3072]{1,0:T(8,128)(2,1)S(1)} collective-permute-done((bf16[8,3072]{1,0:T(8,128)(2,1)S(1)}, bf16[8,3072]{1,0:T(8,128)(2,1)S(1)}, u32[]{:S(2)}, u32[]{:S(2)}) %collective-permute-start.9) | collective-permute-done | bytes 49184 | tf_op jit(solution)/shard_map/ppermute | solution.py:344
  40.3 3.3 %collective-permute-start.11 = (bf16[8,768]{1,0:T(8,128)(2,1)S(1)}, bf16[8,768]{1,0:T(8,128)(2,1)S(1)}, u32[]{:S(2)}, u32[]{:S(2)}) collective-permute-start(bf16[8,768]{1,0:T(8,128)(2,1)S(1)} %get-tuple-element.24), channel_id=1, source_target_pairs={{0,3},{1,2},{2,1},{3,0},{4,7},{5,6},{6,5},{7,4},{8,11},{9,10},{10,... | collective-permute-start | bytes 36872 | tf_op jit(solution)/shard_map/ppermute | solution.py:344
  43.6 1.2 %collective-permute-start.13 = (bf16[8,768]{1,0:T(8,128)(2,1)S(1)}, bf16[8,768]{1,0:T(8,128)(2,1)S(1)}, u32[]{:S(2)}, u32[]{:S(2)}) collective-permute-start(bf16[8,768]{1,0:T(8,128)(2,1)S(1)} %get-tuple-element.25), channel_id=1, source_target_pairs={{0,1},{1,0},{2,3},{3,2},{4,5},{5,4},{6,7},{7,6},{8,9},{9,8},{10,11... | collective-permute-start | bytes 36872 | tf_op jit(solution)/shard_map/ppermute | solution.py:344
  44.8 1.1 %collective-permute-done.11 = bf16[8,768]{1,0:T(8,128)(2,1)S(1)} collective-permute-done((bf16[8,768]{1,0:T(8,128)(2,1)S(1)}, bf16[8,768]{1,0:T(8,128)(2,1)S(1)}, u32[]{:S(2)}, u32[]{:S(2)}) %collective-permute-start.11) | collective-permute-done | bytes 12320 | tf_op jit(solution)/shard_map/ppermute | solution.py:344
  45.9 2.3 %collective-permute-done.12 = bf16[8,768]{1,0:T(8,128)(2,1)S(1)} collective-permute-done((bf16[8,768]{1,0:T(8,128)(2,1)S(1)}, bf16[8,768]{1,0:T(8,128)(2,1)S(1)}, u32[]{:S(2)}, u32[]{:S(2)}) %collective-permute-start.12) | collective-permute-done | bytes 12320 | tf_op jit(solution)/shard_map/ppermute | solution.py:344
  48.2 0.6 %add_convert_fusion.2 = bf16[8,768]{1,0:T(8,128)(2,1)} fusion(bf16[8,768]{1,0:T(8,128)(2,1)S(1)} %collective-permute-done.13, bf16[8,768]{1,0:T(8,128)(2,1)S(1)} %collective-permute-done.12, bf16[8,768]{1,0:T(8,128)(2,1)S(1)} %collective-permute-done.11, bf16[8,1024]{1,0:T(8,128)(2,1)S(1)} %get-tuple-element.13._.refs_3_, ...), kind=kLoop, calls=%fused_computation.5 | loop fusion | flops 61440 | bytes 73732 | tf_op jit(solution)/shard_map/convert_element_type | solution.py:387
  (18 shorter events, 0.1 us)
Async XLA Ops:
  3.3 9.2 %collective-permute-start = (bf16[8,1024]{1,0:T(8,128)(2,1)S(1)}, bf16[8,1024]{1,0:T(8,128)(2,1)S(1)}, u32[]{:S(2)}, u32[]{:S(2)}) collective-permute-start(bf16[8,1024]{1,0:T(8,128)(2,1)S(1)} %get-tuple-element.13._.refs_3_), channel_id=1, source_target_pairs={{0,3},{1,2},{2,1},{3,0},{4,7},{5,6},{6,5},{7,4},{8,11},{9,10},{10,... | collective-permute-start | bytes 49160 | tf_op jit(solution)/shard_map/ppermute | solution.py:344
  8.5 4.6 %collective-permute-start.1 = (bf16[8,1024]{1,0:T(8,128)(2,1)S(1)}, bf16[8,1024]{1,0:T(8,128)(2,1)S(1)}, u32[]{:S(2)}, u32[]{:S(2)}) collective-permute-start(bf16[8,1024]{1,0:T(8,128)(2,1)S(1)} %get-tuple-element.13._.refs_3_), channel_id=1, source_target_pairs={{0,2},{1,3},{2,0},{3,1},{4,6},{5,7},{6,4},{7,5},{8,10},{9,11},{10,... | collective-permute-start | bytes 49160 | tf_op jit(solution)/shard_map/ppermute | solution.py:344
  8.5 4.6 %collective-permute-start.2 = (bf16[8,1024]{1,0:T(8,128)(2,1)S(1)}, bf16[8,1024]{1,0:T(8,128)(2,1)S(1)}, u32[]{:S(2)}, u32[]{:S(2)}) collective-permute-start(bf16[8,1024]{1,0:T(8,128)(2,1)S(1)} %get-tuple-element.13._.refs_3_), channel_id=1, source_target_pairs={{0,1},{1,0},{2,3},{3,2},{4,5},{5,4},{6,7},{7,6},{8,9},{9,8},{10,11... | collective-permute-start | bytes 49160 | tf_op jit(solution)/shard_map/ppermute | solution.py:344
  14.0 7.2 %collective-permute-start.3 = (bf16[8,3200]{1,0:T(8,128)(2,1)S(1)}, bf16[8,3200]{1,0:T(8,128)(2,1)S(1)}, u32[]{:S(2)}, u32[]{:S(2)}) collective-permute-start(bf16[8,3200]{1,0:T(8,128)(2,1)S(1)} %norm.1._.refs_3_), channel_id=1, source_target_pairs={{0,12},{4,8},{8,4},{12,0},{1,13},{5,9},{9,5},{13,1},{2,14},{6,10},... | collective-permute-start | bytes 153608 | tf_op jit(solution)/shard_map/ppermute | solution.py:344
  16.5 4.8 %collective-permute-start.4 = (bf16[8,3200]{1,0:T(8,128)(2,1)S(1)}, bf16[8,3200]{1,0:T(8,128)(2,1)S(1)}, u32[]{:S(2)}, u32[]{:S(2)}) collective-permute-start(bf16[8,3200]{1,0:T(8,128)(2,1)S(1)} %norm.1._.refs_3_), channel_id=1, source_target_pairs={{0,8},{4,12},{8,0},{12,4},{1,9},{5,13},{9,1},{13,5},{2,10},{6,14},... | collective-permute-start | bytes 153608 | tf_op jit(solution)/shard_map/ppermute | solution.py:344
  17.0 4.3 %collective-permute-start.5 = (bf16[8,3200]{1,0:T(8,128)(2,1)S(1)}, bf16[8,3200]{1,0:T(8,128)(2,1)S(1)}, u32[]{:S(2)}, u32[]{:S(2)}) collective-permute-start(bf16[8,3200]{1,0:T(8,128)(2,1)S(1)} %norm.1._.refs_3_), channel_id=1, source_target_pairs={{0,4},{4,0},{8,12},{12,8},{1,5},{5,1},{9,13},{13,9},{2,6},{6,2},{1... | collective-permute-start | bytes 153608 | tf_op jit(solution)/shard_map/ppermute | solution.py:344
  21.3 1.6 %collective-permute-start.6 = (bf16[32,3200]{1,0:T(8,128)(2,1)S(1)}, bf16[32,3200]{1,0:T(8,128)(2,1)S(1)}, u32[]{:S(2)}, u32[]{:S(2)}) collective-permute-start(bf16[32,3200]{1,0:T(8,128)(2,1)S(1)} %stack.13._.near), channel_id=1, source_target_pairs={{0,16},{16,0},{1,17},{17,1},{2,18},{18,2},{3,19},{19,3},{4,20},{20... | collective-permute-start | bytes 614408 | tf_op jit(solution)/shard_map/ppermute | solution.py:344
  21.4 7.9 %slice-start = ((s8[10616832]{0:T(1024)(128)(4,1)}), s8[4194304]{0:T(1024)(128)(4,1)S(1)}, s32[]{:S(2)}) async-start(s8[10616832]{0:T(1024)(128)(4,1)} %bitcast.9), calls=%async_computation | async-start | bytes 8388608
  22.9 6.4 %slice-start.1 = ((s8[10616832]{0:T(1024)(128)(4,1)}), s8[4194304]{0:T(1024)(128)(4,1)S(1)}, s32[]{:S(2)}) async-start(s8[10616832]{0:T(1024)(128)(4,1)} %bitcast.9), calls=%async_computation.1 | async-start | bytes 8388608
  22.9 6.4 %slice-start.2 = ((s8[10616832]{0:T(1024)(128)(4,1)}), s8[2228224]{0:T(1024)(128)(4,1)S(1)}, s32[]{:S(2)}) async-start(s8[10616832]{0:T(1024)(128)(4,1)} %bitcast.9), calls=%async_computation.2 | async-start | bytes 4456448
  31.3 1.6 %collective-permute-start.7 = (bf16[32,3072]{1,0:T(8,128)(2,1)S(1)}, bf16[32,3072]{1,0:T(8,128)(2,1)S(1)}, u32[]{:S(2)}, u32[]{:S(2)}) collective-permute-start(bf16[32,3072]{1,0:T(8,128)(2,1)S(1)} %slice.33), channel_id=1, source_target_pairs={{0,16},{16,0},{1,17},{17,1},{2,18},{18,2},{3,19},{19,3},{4,20},{20... | collective-permute-start | bytes 589832 | tf_op jit(solution)/shard_map/ppermute | solution.py:344
  33.0 4.2 %collective-permute-start.10 = (bf16[8,3072]{1,0:T(8,128)(2,1)S(1)}, bf16[8,3072]{1,0:T(8,128)(2,1)S(1)}, u32[]{:S(2)}, u32[]{:S(2)}) collective-permute-start(bf16[8,3072]{1,0:T(8,128)(2,1)S(1)} %get-tuple-element.22), channel_id=1, source_target_pairs={{0,4},{4,0},{8,12},{12,8},{1,5},{5,1},{9,13},{13,9},{2,6},{6,2},{1... | collective-permute-start | bytes 147464 | tf_op jit(solution)/shard_map/ppermute | solution.py:344
  34.6 5.0 %collective-permute-start.8 = (bf16[8,3072]{1,0:T(8,128)(2,1)S(1)}, bf16[8,3072]{1,0:T(8,128)(2,1)S(1)}, u32[]{:S(2)}, u32[]{:S(2)}) collective-permute-start(bf16[8,3072]{1,0:T(8,128)(2,1)S(1)} %get-tuple-element.21), channel_id=1, source_target_pairs={{0,12},{4,8},{8,4},{12,0},{1,13},{5,9},{9,5},{13,1},{2,14},{6,10},... | collective-permute-start | bytes 147464 | tf_op jit(solution)/shard_map/ppermute | solution.py:344
  36.1 4.2 %collective-permute-start.9 = (bf16[8,3072]{1,0:T(8,128)(2,1)S(1)}, bf16[8,3072]{1,0:T(8,128)(2,1)S(1)}, u32[]{:S(2)}, u32[]{:S(2)}) collective-permute-start(bf16[8,3072]{1,0:T(8,128)(2,1)S(1)} %get-tuple-element.23), channel_id=1, source_target_pairs={{0,8},{4,12},{8,0},{12,4},{1,9},{5,13},{9,1},{13,5},{2,10},{6,14},... | collective-permute-start | bytes 147464 | tf_op jit(solution)/shard_map/ppermute | solution.py:344
  40.3 5.6 %collective-permute-start.11 = (bf16[8,768]{1,0:T(8,128)(2,1)S(1)}, bf16[8,768]{1,0:T(8,128)(2,1)S(1)}, u32[]{:S(2)}, u32[]{:S(2)}) collective-permute-start(bf16[8,768]{1,0:T(8,128)(2,1)S(1)} %get-tuple-element.24), channel_id=1, source_target_pairs={{0,3},{1,2},{2,1},{3,0},{4,7},{5,6},{6,5},{7,4},{8,11},{9,10},{10,... | collective-permute-start | bytes 36872 | tf_op jit(solution)/shard_map/ppermute | solution.py:344
  43.6 4.6 %collective-permute-start.12 = (bf16[8,768]{1,0:T(8,128)(2,1)S(1)}, bf16[8,768]{1,0:T(8,128)(2,1)S(1)}, u32[]{:S(2)}, u32[]{:S(2)}) collective-permute-start(bf16[8,768]{1,0:T(8,128)(2,1)S(1)} %get-tuple-element.26), channel_id=1, source_target_pairs={{0,2},{1,3},{2,0},{3,1},{4,6},{5,7},{6,4},{7,5},{8,10},{9,11},{10,... | collective-permute-start | bytes 36872 | tf_op jit(solution)/shard_map/ppermute | solution.py:344
  43.6 4.6 %collective-permute-start.13 = (bf16[8,768]{1,0:T(8,128)(2,1)S(1)}, bf16[8,768]{1,0:T(8,128)(2,1)S(1)}, u32[]{:S(2)}, u32[]{:S(2)}) collective-permute-start(bf16[8,768]{1,0:T(8,128)(2,1)S(1)} %get-tuple-element.25), channel_id=1, source_target_pairs={{0,1},{1,0},{2,3},{3,2},{4,5},{5,4},{6,7},{7,6},{8,9},{9,8},{10,11... | collective-permute-start | bytes 36872 | tf_op jit(solution)/shard_map/ppermute | solution.py:344

commit v6 on v5

--- a/solution.py
+++ b/solution.py
@@ -15,6 +15,7 @@
 MIB = 1 << 20
 CHUNKS = 4
 UNITS = 256
+STREAM = 640
 BY_ROW = (((1,), (1,)), ((), ()))
 
 
@@ -251,7 +252,7 @@
     high = share.astype(jnp.bfloat16).astype(jnp.float32)
     side = high + pltpu.roll(share - high, experts, 1)
     out_ref[:, model:] = side.astype(out_ref.dtype)
-    for mask, piece in enumerate(reversed(pieces)):
+    for mask, piece in zip(send_order(len(pieces)) + [0], pieces):
         gain = piece[:, block + LANES :].astype(jnp.float32)
         gain = jnp.concatenate([gain[j : j + 1, :] for j in range(block // LANES)], axis=1)
         x = (piece[:, :block].astype(jnp.float32) - mean) * inv * gain
@@ -274,7 +275,8 @@
 
 
 def stack_kernel(_, *refs):
-    pieces, out_ref = refs[:-1][::-1], refs[-1]
+    masks = send_order(len(refs) - 1) + [0]
+    pieces, out_ref = [refs[masks.index(m)] for m in range(len(masks))], refs[-1]
     rows = 2 * pieces[0].shape[0]
     for i in range(0, len(pieces), 2):
         pair = [piece[...].astype(jnp.float32) for piece in pieces[i : i + 2]]
@@ -313,8 +315,8 @@
         return lax.dot_general(block, x[...], BY_ROW, preferred_element_type=jnp.float32)
 
     for low, high in zip(cuts, cuts[1:]):
-        for start in range(low, high, UNITS):
-            stop = min(start + UNITS, high)
+        for start in range(low, high, STREAM):
+            stop = min(start + STREAM, high)
             a = times(gate_a, gate_b, start, stop)
             b = times(up_a, up_b, start, stop)
             out = a / (1.0 + jnp.exp(-a)) * b * share
@@ -344,8 +346,14 @@
     return lax.ppermute(x, axis, [(i, i ^ mask) for i in range(lax.axis_size(axis))])
 
 
+def send_order(size):
+    order = list(range(size - 1, 0, -1))
+    order[:2] = order[1::-1]
+    return order
+
+
 def exchange(parts, axis):
-    return [send(parts[m], axis, m) for m in reversed(range(1, lax.axis_size(axis)))]
+    return [send(parts[m], axis, m) for m in send_order(lax.axis_size(axis))]
 
 
 def add(*terms):

time: 49 us -> 49.7 us (1.014)
  waiting for transfers between devices: 8.74 us -> 10.3 us
  starting transfers between devices: 17.9 us -> 17.1 us
    ppermute x14, waiting for transfers between devices: 8.74 us -> 10.3 us  [send(): lax.ppermute(x, axis, [(i, i ^ mask) for i in range(lax.axis_size(axis))])]
    ppermute x14, starting transfers between devices: 17.9 us -> 17.1 us  [send(): lax.ppermute(x, axis, [(i, i ^ mask) for i in range(lax.axis_size(axis))])]
  transfers between devices with their start and end apart: 14 -> 14, of which waited for: 7 -> 7; matrix products, arithmetic and copies ran while one was open for 0% -> 0% of each run, Pallas kernels for 18% -> 17%
where the time goes in v6:
time: 49.7 us; the launch traced here: 49.5 us
  Pallas kernels  18.5 us (37%)
  starting transfers between devices  17.1 us (34%)
  waiting for transfers between devices  10.3 us (21%)
  matrix products  1.97 us (4%)
  between operations  0.85 us (2%)
  other arithmetic  0.77 us (2%)
    ppermute x14, starting transfers between devices, send(): lax.ppermute(x, axis, [(i, i ^ mask) for i in range(lax.axis_size(axis))])  17.1 us
    ppermute x14, waiting for transfers between devices, send(): lax.ppermute(x, axis, [(i, i ^ mask) for i in range(lax.axis_size(axis))])  10.3 us
    pallas_call x3, Pallas kernels, load(): pl.pallas_call(functools.partial(load_kernel, part=part), out_shape=(pltp...  8.57 us
    pallas_call x1, Pallas kernels, run_hidden(): pl.pallas_call(functools.partial(hidden_kernel, experts=experts), out_sha...  6.32 us
    pallas_call x1, Pallas kernels, attend(): pl.pallas_call(functools.partial(attention_kernel, chunks=chunks, rest=re...  2.68 us
    dot_general x1, matrix products, per_device(): jnp.dot(hidden, down_w[0], preferred_element_type=jnp.float32)  1.97 us
  transfers between devices with their start and end apart: 14, of which 7 were waited for; matrix products, arithmetic and copies ran while one was open for 0% of the time, Pallas kernels for 17%

profile of v6, /device:TPU:0, one launch (start us, length us, event | category | flops | bytes accessed | tf_op | source)
XLA Modules:
  0.0 49.5 jit_solution(16597597195968532859)
XLA Ops:
  0.7 2.7 %attention.1 = (bf16[8,1024]{1,0:T(8,128)(2,1)S(1)}, bf16[448,3072]{1,0:T(8,128)(2,1)S(1)}) custom-call(s32[1]{0:T(128)S(6)} %copy.12.len_ref, bf16[8,768]{1,0:T(8,128)(2,1)} %q_hbm.1, bf16[8,512]{1,0:T(8,128)(2,1)} %new_hbm.1, bf16[1,2048,512]{2,1,0:T(8,128)(2,1)} %kv_hbm.1, bf16[8,768]{1,0:T(8,128)(2,1)} %res_hbm.1, s32[4,8]{1,0:T(4,128)} %bitcast.11, ...), custom_call_target="tpu_custom_call" | custom-call | flops 50331648 | bytes 2097152 | tf_op jit(solution)/shard_map/attention/pallas_call | solution.py:188
  3.3 4.1 %collective-permute-start = (bf16[8,1024]{1,0:T(8,128)(2,1)S(1)}, bf16[8,1024]{1,0:T(8,128)(2,1)S(1)}, u32[]{:S(2)}, u32[]{:S(2)}) collective-permute-start(bf16[8,1024]{1,0:T(8,128)(2,1)S(1)} %get-tuple-element.13._.refs_3_), channel_id=1, source_target_pairs={{0,2},{1,3},{2,0},{3,1},{4,6},{5,7},{6,4},{7,5},{8,10},{9,11},{10,... | collective-permute-start | bytes 49160 | tf_op jit(solution)/shard_map/ppermute | solution.py:346
  7.4 1.3 %collective-permute-start.1 = (bf16[8,1024]{1,0:T(8,128)(2,1)S(1)}, bf16[8,1024]{1,0:T(8,128)(2,1)S(1)}, u32[]{:S(2)}, u32[]{:S(2)}) collective-permute-start(bf16[8,1024]{1,0:T(8,128)(2,1)S(1)} %get-tuple-element.13._.refs_3_), channel_id=1, source_target_pairs={{0,3},{1,2},{2,1},{3,0},{4,7},{5,6},{6,5},{7,4},{8,11},{9,10},{10,... | collective-permute-start | bytes 49160 | tf_op jit(solution)/shard_map/ppermute | solution.py:346
  8.8 0.2 collective-permute-start.2
  9.0 0.1 pad_add_fusion.place_ref
  9.1 3.3 %load.3 = (bf16[1280,3072]{1,0:T(8,128)(2,1)S(1)}, f32[8,128]{1,0:T(8,128)S(1)}) custom-call(bf16[8,1024]{1,0:T(8,128)(2,1)S(1)} %get-tuple-element.13._.refs_3_, bf16[1,1728,3072]{2,1,0:T(8,128)(2,1)} %source.3), custom_call_target="tpu_custom_call" | custom-call | bytes 15728640 | tf_op jit(solution)/shard_map/load/pallas_call | solution.py:222
  12.5 0.5 %collective-permute-done.1.refs_1_ = bf16[8,1024]{1,0:T(8,128)(2,1)S(1)} collective-permute-done((bf16[8,1024]{1,0:T(8,128)(2,1)S(1)}, bf16[8,1024]{1,0:T(8,128)(2,1)S(1)}, u32[]{:S(2)}, u32[]{:S(2)}) %collective-permute-start.1) | collective-permute-done | bytes 16416 | tf_op jit(solution)/shard_map/ppermute | solution.py:346
  13.0 0.9 %norm.1._.refs_3_ = bf16[8,3200]{1,0:T(8,128)(2,1)S(1)} custom-call(s32[2]{0:T(128)S(1)} %pad_add_fusion.place_ref, f32[8,128]{1,0:T(8,128)S(1)} %get-tuple-element.14._, bf16[8,1024]{1,0:T(8,128)(2,1)S(1)} %collective-permute-done.refs_0_, bf16[8,1024]{1,0:T(8,128)(2,1)S(1)} %collective-permute-done.1.refs_1_, ...), custom_call_target="tpu_custom_call" | custom-call | tf_op jit(solution)/shard_map/norm/pallas_call | solution.py:267
  13.9 1.5 %collective-permute-start.3 = (bf16[8,3200]{1,0:T(8,128)(2,1)S(1)}, bf16[8,3200]{1,0:T(8,128)(2,1)S(1)}, u32[]{:S(2)}, u32[]{:S(2)}) collective-permute-start(bf16[8,3200]{1,0:T(8,128)(2,1)S(1)} %norm.1._.refs_3_), channel_id=1, source_target_pairs={{0,8},{4,12},{8,0},{12,4},{1,9},{5,13},{9,1},{13,5},{2,10},{6,14},... | collective-permute-start | bytes 153608 | tf_op jit(solution)/shard_map/ppermute | solution.py:346
  15.4 1.4 %collective-permute-start.4 = (bf16[8,3200]{1,0:T(8,128)(2,1)S(1)}, bf16[8,3200]{1,0:T(8,128)(2,1)S(1)}, u32[]{:S(2)}, u32[]{:S(2)}) collective-permute-start(bf16[8,3200]{1,0:T(8,128)(2,1)S(1)} %norm.1._.refs_3_), channel_id=1, source_target_pairs={{0,12},{4,8},{8,4},{12,0},{1,13},{5,9},{9,5},{13,1},{2,14},{6,10},... | collective-permute-start | bytes 153608 | tf_op jit(solution)/shard_map/ppermute | solution.py:346
  16.9 0.5 %collective-permute-start.5 = (bf16[8,3200]{1,0:T(8,128)(2,1)S(1)}, bf16[8,3200]{1,0:T(8,128)(2,1)S(1)}, u32[]{:S(2)}, u32[]{:S(2)}) collective-permute-start(bf16[8,3200]{1,0:T(8,128)(2,1)S(1)} %norm.1._.refs_3_), channel_id=1, source_target_pairs={{0,4},{4,0},{8,12},{12,8},{1,5},{5,1},{9,13},{13,9},{2,6},{6,2},{1... | collective-permute-start | bytes 153608 | tf_op jit(solution)/shard_map/ppermute | solution.py:346
  17.4 3.7 %load.4 = (bf16[1472,3072]{1,0:T(8,128)(2,1)S(1)}, f32[8,128]{1,0:T(8,128)S(1)}) custom-call(bf16[8,3200]{1,0:T(8,128)(2,1)S(1)} %norm.1._.refs_3_, bf16[1,1728,3072]{2,1,0:T(8,128)(2,1)} %source.5), custom_call_target="tpu_custom_call" | custom-call | bytes 18087936 | tf_op jit(solution)/shard_map/load/pallas_call | solution.py:222
  21.2 0.1 collective-permute-start.6
  21.2 0.0 slice-start
  21.3 1.5 %load.5 = (bf16[256,3072]{1,0:T(8,128)(2,1)S(1)}, f32[8,128]{1,0:T(8,128)S(1)}) custom-call(bf16[32,3200]{1,0:T(8,128)(2,1)S(1)} %stack.13._.near, bf16[1,1728,3072]{2,1,0:T(8,128)(2,1)} %source.5), custom_call_target="tpu_custom_call" | custom-call | bytes 3145728 | tf_op jit(solution)/shard_map/load/pallas_call | solution.py:222
  22.8 0.0 slice-start.1
  22.8 6.3 %hidden.1 = bf16[64,1728]{1,0:T(8,128)(2,1)S(1)} custom-call(s32[2]{0:T(128)S(1)} %pad_add_fusion.place_ref, bf16[32,3200]{1,0:T(8,128)(2,1)S(1)} %stack.13._.near, bf16[32,3200]{1,0:T(8,128)(2,1)S(1)} %collective-permute-done.6.far, bf16[1280,3072]{1,0:T(8,128)(2,1)S(1)} %get-tuple-element.16.gate_a, bf16[448,3072]{1,0:T(8,128)(2,1)S(1)} %get-tuple-element.17.gate_b, ...), custom_call_target="tpu_custom_call" | custom-call | flops 1358954496 | bytes 21233664 | tf_op jit(solution)/shard_map/hidden/pallas_call | solution.py:331
  29.2 2.0 %fusion.2 = bf16[64,3072]{1,0:T(8,128)(2,1)S(1)} fusion(bf16[64,1728]{1,0:T(8,128)(2,1)S(1)} %hidden.1, bf16[1,1728,3072]{2,1,0:T(8,128)(2,1)S(1)} %bitcast.10), kind=kOutput, calls=%fused_computation.2 | convolution fusion | flops 679673856 | bytes 11231232 | tf_op jit(solution)/shard_map/dot_general | solution.py:388
  31.2 0.6 %collective-permute-start.7 = (bf16[32,3072]{1,0:T(8,128)(2,1)S(1)}, bf16[32,3072]{1,0:T(8,128)(2,1)S(1)}, u32[]{:S(2)}, u32[]{:S(2)}) collective-permute-start(bf16[32,3072]{1,0:T(8,128)(2,1)S(1)} %slice.33), channel_id=1, source_target_pairs={{0,16},{16,0},{1,17},{17,1},{2,18},{18,2},{3,19},{19,3},{4,20},{20... | collective-permute-start | bytes 589832 | tf_op jit(solution)/shard_map/ppermute | solution.py:346
  31.8 1.1 %collective-permute-done.7 = bf16[32,3072]{1,0:T(8,128)(2,1)S(1)} collective-permute-done((bf16[32,3072]{1,0:T(8,128)(2,1)S(1)}, bf16[32,3072]{1,0:T(8,128)(2,1)S(1)}, u32[]{:S(2)}, u32[]{:S(2)}) %collective-permute-start.7) | collective-permute-done | bytes 196640 | tf_op jit(solution)/shard_map/ppermute | solution.py:346
  32.8 0.1 add_convert_fusion
  32.9 1.6 %collective-permute-start.10 = (bf16[8,3072]{1,0:T(8,128)(2,1)S(1)}, bf16[8,3072]{1,0:T(8,128)(2,1)S(1)}, u32[]{:S(2)}, u32[]{:S(2)}) collective-permute-start(bf16[8,3072]{1,0:T(8,128)(2,1)S(1)} %get-tuple-element.22), channel_id=1, source_target_pairs={{0,4},{4,0},{8,12},{12,8},{1,5},{5,1},{9,13},{13,9},{2,6},{6,2},{1... | collective-permute-start | bytes 147464 | tf_op jit(solution)/shard_map/ppermute | solution.py:346
  34.5 1.5 %collective-permute-start.8 = (bf16[8,3072]{1,0:T(8,128)(2,1)S(1)}, bf16[8,3072]{1,0:T(8,128)(2,1)S(1)}, u32[]{:S(2)}, u32[]{:S(2)}) collective-permute-start(bf16[8,3072]{1,0:T(8,128)(2,1)S(1)} %get-tuple-element.21), channel_id=1, source_target_pairs={{0,8},{4,12},{8,0},{12,4},{1,9},{5,13},{9,1},{13,5},{2,10},{6,14},... | collective-permute-start | bytes 147464 | tf_op jit(solution)/shard_map/ppermute | solution.py:346
  36.0 0.5 collective-permute-start.9
  36.5 0.6 %collective-permute-done.10 = bf16[8,3072]{1,0:T(8,128)(2,1)S(1)} collective-permute-done((bf16[8,3072]{1,0:T(8,128)(2,1)S(1)}, bf16[8,3072]{1,0:T(8,128)(2,1)S(1)}, u32[]{:S(2)}, u32[]{:S(2)}) %collective-permute-start.10) | collective-permute-done | bytes 49184 | tf_op jit(solution)/shard_map/ppermute | solution.py:346
  37.1 1.5 %collective-permute-done.8 = bf16[8,3072]{1,0:T(8,128)(2,1)S(1)} collective-permute-done((bf16[8,3072]{1,0:T(8,128)(2,1)S(1)}, bf16[8,3072]{1,0:T(8,128)(2,1)S(1)}, u32[]{:S(2)}, u32[]{:S(2)}) %collective-permute-start.8) | collective-permute-done | bytes 49184 | tf_op jit(solution)/shard_map/ppermute | solution.py:346
  38.6 2.4 %collective-permute-done.9 = bf16[8,3072]{1,0:T(8,128)(2,1)S(1)} collective-permute-done((bf16[8,3072]{1,0:T(8,128)(2,1)S(1)}, bf16[8,3072]{1,0:T(8,128)(2,1)S(1)}, u32[]{:S(2)}, u32[]{:S(2)}) %collective-permute-start.9) | collective-permute-done | bytes 49184 | tf_op jit(solution)/shard_map/ppermute | solution.py:346
  41.0 2.4 %collective-permute-start.11 = (bf16[8,768]{1,0:T(8,128)(2,1)S(1)}, bf16[8,768]{1,0:T(8,128)(2,1)S(1)}, u32[]{:S(2)}, u32[]{:S(2)}) collective-permute-start(bf16[8,768]{1,0:T(8,128)(2,1)S(1)} %get-tuple-element.24), channel_id=1, source_target_pairs={{0,2},{1,3},{2,0},{3,1},{4,6},{5,7},{6,4},{7,5},{8,10},{9,11},{10,... | collective-permute-start | bytes 36872 | tf_op jit(solution)/shard_map/ppermute | solution.py:346
  43.4 1.4 %collective-permute-start.12 = (bf16[8,768]{1,0:T(8,128)(2,1)S(1)}, bf16[8,768]{1,0:T(8,128)(2,1)S(1)}, u32[]{:S(2)}, u32[]{:S(2)}) collective-permute-start(bf16[8,768]{1,0:T(8,128)(2,1)S(1)} %get-tuple-element.26), channel_id=1, source_target_pairs={{0,3},{1,2},{2,1},{3,0},{4,7},{5,6},{6,5},{7,4},{8,11},{9,10},{10,... | collective-permute-start | bytes 36872 | tf_op jit(solution)/shard_map/ppermute | solution.py:346
  44.8 0.9 %collective-permute-done.11 = bf16[8,768]{1,0:T(8,128)(2,1)S(1)} collective-permute-done((bf16[8,768]{1,0:T(8,128)(2,1)S(1)}, bf16[8,768]{1,0:T(8,128)(2,1)S(1)}, u32[]{:S(2)}, u32[]{:S(2)}) %collective-permute-start.11) | collective-permute-done | bytes 12320 | tf_op jit(solution)/shard_map/ppermute | solution.py:346
  45.7 3.2 %collective-permute-done.12 = bf16[8,768]{1,0:T(8,128)(2,1)S(1)} collective-permute-done((bf16[8,768]{1,0:T(8,128)(2,1)S(1)}, bf16[8,768]{1,0:T(8,128)(2,1)S(1)}, u32[]{:S(2)}, u32[]{:S(2)}) %collective-permute-start.12) | collective-permute-done | bytes 12320 | tf_op jit(solution)/shard_map/ppermute | solution.py:346
  48.9 0.6 %add_convert_fusion.2 = bf16[8,768]{1,0:T(8,128)(2,1)} fusion(bf16[8,768]{1,0:T(8,128)(2,1)S(1)} %collective-permute-done.13, bf16[8,768]{1,0:T(8,128)(2,1)S(1)} %collective-permute-done.12, bf16[8,768]{1,0:T(8,128)(2,1)S(1)} %collective-permute-done.11, bf16[8,1024]{1,0:T(8,128)(2,1)S(1)} %get-tuple-element.13._.refs_3_, ...), kind=kLoop, calls=%fused_computation.5 | loop fusion | flops 61440 | bytes 73732 | tf_op jit(solution)/shard_map/convert_element_type | solution.py:395
  (18 shorter events, 0.1 us)
Async XLA Ops:
  3.3 9.1 %collective-permute-start = (bf16[8,1024]{1,0:T(8,128)(2,1)S(1)}, bf16[8,1024]{1,0:T(8,128)(2,1)S(1)}, u32[]{:S(2)}, u32[]{:S(2)}) collective-permute-start(bf16[8,1024]{1,0:T(8,128)(2,1)S(1)} %get-tuple-element.13._.refs_3_), channel_id=1, source_target_pairs={{0,2},{1,3},{2,0},{3,1},{4,6},{5,7},{6,4},{7,5},{8,10},{9,11},{10,... | collective-permute-start | bytes 49160 | tf_op jit(solution)/shard_map/ppermute | solution.py:346
  7.4 5.5 %collective-permute-start.1 = (bf16[8,1024]{1,0:T(8,128)(2,1)S(1)}, bf16[8,1024]{1,0:T(8,128)(2,1)S(1)}, u32[]{:S(2)}, u32[]{:S(2)}) collective-permute-start(bf16[8,1024]{1,0:T(8,128)(2,1)S(1)} %get-tuple-element.13._.refs_3_), channel_id=1, source_target_pairs={{0,3},{1,2},{2,1},{3,0},{4,7},{5,6},{6,5},{7,4},{8,11},{9,10},{10,... | collective-permute-start | bytes 49160 | tf_op jit(solution)/shard_map/ppermute | solution.py:346
  8.8 4.2 %collective-permute-start.2 = (bf16[8,1024]{1,0:T(8,128)(2,1)S(1)}, bf16[8,1024]{1,0:T(8,128)(2,1)S(1)}, u32[]{:S(2)}, u32[]{:S(2)}) collective-permute-start(bf16[8,1024]{1,0:T(8,128)(2,1)S(1)} %get-tuple-element.13._.refs_3_), channel_id=1, source_target_pairs={{0,1},{1,0},{2,3},{3,2},{4,5},{5,4},{6,7},{7,6},{8,9},{9,8},{10,11... | collective-permute-start | bytes 49160 | tf_op jit(solution)/shard_map/ppermute | solution.py:346
  13.9 7.2 %collective-permute-start.3 = (bf16[8,3200]{1,0:T(8,128)(2,1)S(1)}, bf16[8,3200]{1,0:T(8,128)(2,1)S(1)}, u32[]{:S(2)}, u32[]{:S(2)}) collective-permute-start(bf16[8,3200]{1,0:T(8,128)(2,1)S(1)} %norm.1._.refs_3_), channel_id=1, source_target_pairs={{0,8},{4,12},{8,0},{12,4},{1,9},{5,13},{9,1},{13,5},{2,10},{6,14},... | collective-permute-start | bytes 153608 | tf_op jit(solution)/shard_map/ppermute | solution.py:346
  15.4 5.7 %collective-permute-start.4 = (bf16[8,3200]{1,0:T(8,128)(2,1)S(1)}, bf16[8,3200]{1,0:T(8,128)(2,1)S(1)}, u32[]{:S(2)}, u32[]{:S(2)}) collective-permute-start(bf16[8,3200]{1,0:T(8,128)(2,1)S(1)} %norm.1._.refs_3_), channel_id=1, source_target_pairs={{0,12},{4,8},{8,4},{12,0},{1,13},{5,9},{9,5},{13,1},{2,14},{6,10},... | collective-permute-start | bytes 153608 | tf_op jit(solution)/shard_map/ppermute | solution.py:346
  16.9 4.3 %collective-permute-start.5 = (bf16[8,3200]{1,0:T(8,128)(2,1)S(1)}, bf16[8,3200]{1,0:T(8,128)(2,1)S(1)}, u32[]{:S(2)}, u32[]{:S(2)}) collective-permute-start(bf16[8,3200]{1,0:T(8,128)(2,1)S(1)} %norm.1._.refs_3_), channel_id=1, source_target_pairs={{0,4},{4,0},{8,12},{12,8},{1,5},{5,1},{9,13},{13,9},{2,6},{6,2},{1... | collective-permute-start | bytes 153608 | tf_op jit(solution)/shard_map/ppermute | solution.py:346
  21.2 1.6 %collective-permute-start.6 = (bf16[32,3200]{1,0:T(8,128)(2,1)S(1)}, bf16[32,3200]{1,0:T(8,128)(2,1)S(1)}, u32[]{:S(2)}, u32[]{:S(2)}) collective-permute-start(bf16[32,3200]{1,0:T(8,128)(2,1)S(1)} %stack.13._.near), channel_id=1, source_target_pairs={{0,16},{16,0},{1,17},{17,1},{2,18},{18,2},{3,19},{19,3},{4,20},{20... | collective-permute-start | bytes 614408 | tf_op jit(solution)/shard_map/ppermute | solution.py:346
  21.2 7.9 %slice-start = ((s8[10616832]{0:T(1024)(128)(4,1)}), s8[4194304]{0:T(1024)(128)(4,1)S(1)}, s32[]{:S(2)}) async-start(s8[10616832]{0:T(1024)(128)(4,1)} %bitcast.9), calls=%async_computation | async-start | bytes 8388608
  22.8 6.4 %slice-start.1 = ((s8[10616832]{0:T(1024)(128)(4,1)}), s8[4194304]{0:T(1024)(128)(4,1)S(1)}, s32[]{:S(2)}) async-start(s8[10616832]{0:T(1024)(128)(4,1)} %bitcast.9), calls=%async_computation.1 | async-start | bytes 8388608
  22.8 6.4 %slice-start.2 = ((s8[10616832]{0:T(1024)(128)(4,1)}), s8[2228224]{0:T(1024)(128)(4,1)S(1)}, s32[]{:S(2)}) async-start(s8[10616832]{0:T(1024)(128)(4,1)} %bitcast.9), calls=%async_computation.2 | async-start | bytes 4456448
  31.2 1.6 %collective-permute-start.7 = (bf16[32,3072]{1,0:T(8,128)(2,1)S(1)}, bf16[32,3072]{1,0:T(8,128)(2,1)S(1)}, u32[]{:S(2)}, u32[]{:S(2)}) collective-permute-start(bf16[32,3072]{1,0:T(8,128)(2,1)S(1)} %slice.33), channel_id=1, source_target_pairs={{0,16},{16,0},{1,17},{17,1},{2,18},{18,2},{3,19},{19,3},{4,20},{20... | collective-permute-start | bytes 589832 | tf_op jit(solution)/shard_map/ppermute | solution.py:346
  32.9 4.2 %collective-permute-start.10 = (bf16[8,3072]{1,0:T(8,128)(2,1)S(1)}, bf16[8,3072]{1,0:T(8,128)(2,1)S(1)}, u32[]{:S(2)}, u32[]{:S(2)}) collective-permute-start(bf16[8,3072]{1,0:T(8,128)(2,1)S(1)} %get-tuple-element.22), channel_id=1, source_target_pairs={{0,4},{4,0},{8,12},{12,8},{1,5},{5,1},{9,13},{13,9},{2,6},{6,2},{1... | collective-permute-start | bytes 147464 | tf_op jit(solution)/shard_map/ppermute | solution.py:346
  34.5 4.1 %collective-permute-start.8 = (bf16[8,3072]{1,0:T(8,128)(2,1)S(1)}, bf16[8,3072]{1,0:T(8,128)(2,1)S(1)}, u32[]{:S(2)}, u32[]{:S(2)}) collective-permute-start(bf16[8,3072]{1,0:T(8,128)(2,1)S(1)} %get-tuple-element.21), channel_id=1, source_target_pairs={{0,8},{4,12},{8,0},{12,4},{1,9},{5,13},{9,1},{13,5},{2,10},{6,14},... | collective-permute-start | bytes 147464 | tf_op jit(solution)/shard_map/ppermute | solution.py:346
  36.0 5.0 %collective-permute-start.9 = (bf16[8,3072]{1,0:T(8,128)(2,1)S(1)}, bf16[8,3072]{1,0:T(8,128)(2,1)S(1)}, u32[]{:S(2)}, u32[]{:S(2)}) collective-permute-start(bf16[8,3072]{1,0:T(8,128)(2,1)S(1)} %get-tuple-element.23), channel_id=1, source_target_pairs={{0,12},{4,8},{8,4},{12,0},{1,13},{5,9},{9,5},{13,1},{2,14},{6,10},... | collective-permute-start | bytes 147464 | tf_op jit(solution)/shard_map/ppermute | solution.py:346
  41.0 4.7 %collective-permute-start.11 = (bf16[8,768]{1,0:T(8,128)(2,1)S(1)}, bf16[8,768]{1,0:T(8,128)(2,1)S(1)}, u32[]{:S(2)}, u32[]{:S(2)}) collective-permute-start(bf16[8,768]{1,0:T(8,128)(2,1)S(1)} %get-tuple-element.24), channel_id=1, source_target_pairs={{0,2},{1,3},{2,0},{3,1},{4,6},{5,7},{6,4},{7,5},{8,10},{9,11},{10,... | collective-permute-start | bytes 36872 | tf_op jit(solution)/shard_map/ppermute | solution.py:346
  43.4 5.5 %collective-permute-start.12 = (bf16[8,768]{1,0:T(8,128)(2,1)S(1)}, bf16[8,768]{1,0:T(8,128)(2,1)S(1)}, u32[]{:S(2)}, u32[]{:S(2)}) collective-permute-start(bf16[8,768]{1,0:T(8,128)(2,1)S(1)} %get-tuple-element.26), channel_id=1, source_target_pairs={{0,3},{1,2},{2,1},{3,0},{4,7},{5,6},{6,5},{7,4},{8,11},{9,10},{10,... | collective-permute-start | bytes 36872 | tf_op jit(solution)/shard_map/ppermute | solution.py:346
  44.8 4.1 %collective-permute-start.13 = (bf16[8,768]{1,0:T(8,128)(2,1)S(1)}, bf16[8,768]{1,0:T(8,128)(2,1)S(1)}, u32[]{:S(2)}, u32[]{:S(2)}) collective-permute-start(bf16[8,768]{1,0:T(8,128)(2,1)S(1)} %get-tuple-element.25), channel_id=1, source_target_pairs={{0,1},{1,0},{2,3},{3,2},{4,5},{5,4},{6,7},{7,6},{8,9},{9,8},{10,11... | collective-permute-start | bytes 36872 | tf_op jit(solution)/shard_map/ppermute | solution.py:346

commit v7 on v6

--- a/solution.py
+++ b/solution.py
@@ -15,7 +15,6 @@
 MIB = 1 << 20
 CHUNKS = 4
 UNITS = 256
-STREAM = 640
 BY_ROW = (((1,), (1,)), ((), ()))
 
 
@@ -301,26 +300,26 @@
     model = gate_a.shape[1]
     x[:half] = near[:, :model]
     x[half:] = far[:, :model]
-    side = jnp.concatenate([ref[:, model:].astype(jnp.float32) for ref in (near, far)], axis=0).T
-    at = lax.broadcasted_iota(jnp.int32, side.shape, 0)
+    side = jnp.concatenate([ref[:, model:].astype(jnp.float32) for ref in (near, far)], axis=0)
+    lane = lax.broadcasted_iota(jnp.int32, side.shape, 1)
     expert = place_ref[1]
-    mine = (at == expert) | (at == expert + experts)
-    share = jnp.sum(jnp.where(mine, side, 0.0), axis=0, keepdims=True)
+    mine = (lane == expert) | (lane == expert + experts)
+    share = jnp.sum(jnp.where(mine, side, 0.0), axis=1, keepdims=True)
     units = gate_a.shape[0] + gate_b.shape[0]
     cuts = sorted({0, gate_a.shape[0], up_a.shape[0], units})
 
-    def times(first, second, start, stop):
+    def rows(first, second, start, stop):
         cut = first.shape[0]
-        block = first[start:stop] if stop <= cut else second[start - cut : stop - cut]
-        return lax.dot_general(block, x[...], BY_ROW, preferred_element_type=jnp.float32)
+        return first[start:stop] if stop <= cut else second[start - cut : stop - cut]
 
     for low, high in zip(cuts, cuts[1:]):
-        for start in range(low, high, STREAM):
-            stop = min(start + STREAM, high)
-            a = times(gate_a, gate_b, start, stop)
-            b = times(up_a, up_b, start, stop)
-            out = a / (1.0 + jnp.exp(-a)) * b * share
-            hidden[:, start:stop] = out.T.astype(hidden.dtype)
+        for start in range(low, high, UNITS):
+            stop = min(start + UNITS, high)
+            gate, up = rows(gate_a, gate_b, start, stop), rows(up_a, up_b, start, stop)
+            a = lax.dot_general(x[...], gate, BY_ROW, preferred_element_type=jnp.float32)
+            b = lax.dot_general(up, x[...], BY_ROW, preferred_element_type=jnp.float32)
+            out = a / (1.0 + jnp.exp(-a)) * share * b.T
+            hidden[:, start:stop] = out.astype(hidden.dtype)
 
 
 def run_hidden(place, near, far, weights, token, experts):

time: 49.7 us -> 49.7 us (level)
  no operation moved by 1% of the time
where the time goes in v7:
time: 49.7 us; the launch traced here: 49.5 us
  Pallas kernels  18.5 us (37%)
  starting transfers between devices  17.1 us (34%)
  waiting for transfers between devices  10.2 us (21%)
  matrix products  1.97 us (4%)
  between operations  0.85 us (2%)
  other arithmetic  0.77 us (2%)
    ppermute x14, starting transfers between devices, send(): lax.ppermute(x, axis, [(i, i ^ mask) for i in range(lax.axis_size(axis))])  17.1 us
    ppermute x14, waiting for transfers between devices, send(): lax.ppermute(x, axis, [(i, i ^ mask) for i in range(lax.axis_size(axis))])  10.2 us
    pallas_call x3, Pallas kernels, load(): pl.pallas_call(functools.partial(load_kernel, part=part), out_shape=(pltp...  8.57 us
    pallas_call x1, Pallas kernels, run_hidden(): pl.pallas_call(functools.partial(hidden_kernel, experts=experts), out_sha...  6.3 us
    pallas_call x1, Pallas kernels, attend(): pl.pallas_call(functools.partial(attention_kernel, chunks=chunks, rest=re...  2.68 us
    dot_general x1, matrix products, per_device(): jnp.dot(hidden, down_w[0], preferred_element_type=jnp.float32)  1.97 us
  transfers between devices with their start and end apart: 14, of which 7 were waited for; matrix products, arithmetic and copies ran while one was open for 0% of the time, Pallas kernels for 17%

profile of v7, /device:TPU:0, one launch (start us, length us, event | category | flops | bytes accessed | tf_op | source)
XLA Modules:
  0.0 49.5 jit_solution(16218842198147017906)
XLA Ops:
  0.7 2.7 %attention.1 = (bf16[8,1024]{1,0:T(8,128)(2,1)S(1)}, bf16[448,3072]{1,0:T(8,128)(2,1)S(1)}) custom-call(s32[1]{0:T(128)S(6)} %copy.12.len_ref, bf16[8,768]{1,0:T(8,128)(2,1)} %q_hbm.1, bf16[8,512]{1,0:T(8,128)(2,1)} %new_hbm.1, bf16[1,2048,512]{2,1,0:T(8,128)(2,1)} %kv_hbm.1, bf16[8,768]{1,0:T(8,128)(2,1)} %res_hbm.1, s32[4,8]{1,0:T(4,128)} %bitcast.11, ...), custom_call_target="tpu_custom_call" | custom-call | flops 50331648 | bytes 2097152 | tf_op jit(solution)/shard_map/attention/pallas_call | solution.py:187
  3.3 4.1 %collective-permute-start = (bf16[8,1024]{1,0:T(8,128)(2,1)S(1)}, bf16[8,1024]{1,0:T(8,128)(2,1)S(1)}, u32[]{:S(2)}, u32[]{:S(2)}) collective-permute-start(bf16[8,1024]{1,0:T(8,128)(2,1)S(1)} %get-tuple-element.13._.refs_3_), channel_id=1, source_target_pairs={{0,2},{1,3},{2,0},{3,1},{4,6},{5,7},{6,4},{7,5},{8,10},{9,11},{10,... | collective-permute-start | bytes 49160 | tf_op jit(solution)/shard_map/ppermute | solution.py:345
  7.4 1.3 %collective-permute-start.1 = (bf16[8,1024]{1,0:T(8,128)(2,1)S(1)}, bf16[8,1024]{1,0:T(8,128)(2,1)S(1)}, u32[]{:S(2)}, u32[]{:S(2)}) collective-permute-start(bf16[8,1024]{1,0:T(8,128)(2,1)S(1)} %get-tuple-element.13._.refs_3_), channel_id=1, source_target_pairs={{0,3},{1,2},{2,1},{3,0},{4,7},{5,6},{6,5},{7,4},{8,11},{9,10},{10,... | collective-permute-start | bytes 49160 | tf_op jit(solution)/shard_map/ppermute | solution.py:345
  8.8 0.2 collective-permute-start.2
  9.0 0.1 pad_add_fusion.place_ref
  9.1 3.3 %load.3 = (bf16[1280,3072]{1,0:T(8,128)(2,1)S(1)}, f32[8,128]{1,0:T(8,128)S(1)}) custom-call(bf16[8,1024]{1,0:T(8,128)(2,1)S(1)} %get-tuple-element.13._.refs_3_, bf16[1,1728,3072]{2,1,0:T(8,128)(2,1)} %source.3), custom_call_target="tpu_custom_call" | custom-call | bytes 15728640 | tf_op jit(solution)/shard_map/load/pallas_call | solution.py:221
  12.5 0.5 %collective-permute-done.1.refs_1_ = bf16[8,1024]{1,0:T(8,128)(2,1)S(1)} collective-permute-done((bf16[8,1024]{1,0:T(8,128)(2,1)S(1)}, bf16[8,1024]{1,0:T(8,128)(2,1)S(1)}, u32[]{:S(2)}, u32[]{:S(2)}) %collective-permute-start.1) | collective-permute-done | bytes 16416 | tf_op jit(solution)/shard_map/ppermute | solution.py:345
  13.0 0.9 %norm.1._.refs_3_ = bf16[8,3200]{1,0:T(8,128)(2,1)S(1)} custom-call(s32[2]{0:T(128)S(1)} %pad_add_fusion.place_ref, f32[8,128]{1,0:T(8,128)S(1)} %get-tuple-element.14._, bf16[8,1024]{1,0:T(8,128)(2,1)S(1)} %collective-permute-done.refs_0_, bf16[8,1024]{1,0:T(8,128)(2,1)S(1)} %collective-permute-done.1.refs_1_, ...), custom_call_target="tpu_custom_call" | custom-call | tf_op jit(solution)/shard_map/norm/pallas_call | solution.py:266
  13.9 1.5 %collective-permute-start.3 = (bf16[8,3200]{1,0:T(8,128)(2,1)S(1)}, bf16[8,3200]{1,0:T(8,128)(2,1)S(1)}, u32[]{:S(2)}, u32[]{:S(2)}) collective-permute-start(bf16[8,3200]{1,0:T(8,128)(2,1)S(1)} %norm.1._.refs_3_), channel_id=1, source_target_pairs={{0,8},{4,12},{8,0},{12,4},{1,9},{5,13},{9,1},{13,5},{2,10},{6,14},... | collective-permute-start | bytes 153608 | tf_op jit(solution)/shard_map/ppermute | solution.py:345
  15.4 1.4 %collective-permute-start.4 = (bf16[8,3200]{1,0:T(8,128)(2,1)S(1)}, bf16[8,3200]{1,0:T(8,128)(2,1)S(1)}, u32[]{:S(2)}, u32[]{:S(2)}) collective-permute-start(bf16[8,3200]{1,0:T(8,128)(2,1)S(1)} %norm.1._.refs_3_), channel_id=1, source_target_pairs={{0,12},{4,8},{8,4},{12,0},{1,13},{5,9},{9,5},{13,1},{2,14},{6,10},... | collective-permute-start | bytes 153608 | tf_op jit(solution)/shard_map/ppermute | solution.py:345
  16.9 0.5 %collective-permute-start.5 = (bf16[8,3200]{1,0:T(8,128)(2,1)S(1)}, bf16[8,3200]{1,0:T(8,128)(2,1)S(1)}, u32[]{:S(2)}, u32[]{:S(2)}) collective-permute-start(bf16[8,3200]{1,0:T(8,128)(2,1)S(1)} %norm.1._.refs_3_), channel_id=1, source_target_pairs={{0,4},{4,0},{8,12},{12,8},{1,5},{5,1},{9,13},{13,9},{2,6},{6,2},{1... | collective-permute-start | bytes 153608 | tf_op jit(solution)/shard_map/ppermute | solution.py:345
  17.4 3.7 %load.4 = (bf16[1472,3072]{1,0:T(8,128)(2,1)S(1)}, f32[8,128]{1,0:T(8,128)S(1)}) custom-call(bf16[8,3200]{1,0:T(8,128)(2,1)S(1)} %norm.1._.refs_3_, bf16[1,1728,3072]{2,1,0:T(8,128)(2,1)} %source.5), custom_call_target="tpu_custom_call" | custom-call | bytes 18087936 | tf_op jit(solution)/shard_map/load/pallas_call | solution.py:221
  21.2 0.1 collective-permute-start.6
  21.2 0.0 slice-start
  21.3 1.5 %load.5 = (bf16[256,3072]{1,0:T(8,128)(2,1)S(1)}, f32[8,128]{1,0:T(8,128)S(1)}) custom-call(bf16[32,3200]{1,0:T(8,128)(2,1)S(1)} %stack.13._.near, bf16[1,1728,3072]{2,1,0:T(8,128)(2,1)} %source.5), custom_call_target="tpu_custom_call" | custom-call | bytes 3145728 | tf_op jit(solution)/shard_map/load/pallas_call | solution.py:221
  22.8 0.0 slice-start.1
  22.8 6.3 %hidden.1 = bf16[64,1728]{1,0:T(8,128)(2,1)S(1)} custom-call(s32[2]{0:T(128)S(1)} %pad_add_fusion.place_ref, bf16[32,3200]{1,0:T(8,128)(2,1)S(1)} %stack.13._.near, bf16[32,3200]{1,0:T(8,128)(2,1)S(1)} %collective-permute-done.6.far, bf16[1280,3072]{1,0:T(8,128)(2,1)S(1)} %get-tuple-element.16.gate_a, bf16[448,3072]{1,0:T(8,128)(2,1)S(1)} %get-tuple-element.17.gate_b, ...), custom_call_target="tpu_custom_call" | custom-call | flops 1358954496 | bytes 21233664 | tf_op jit(solution)/shard_map/hidden/pallas_call | solution.py:330
  29.2 2.0 %fusion.2 = bf16[64,3072]{1,0:T(8,128)(2,1)S(1)} fusion(bf16[64,1728]{1,0:T(8,128)(2,1)S(1)} %hidden.1, bf16[1,1728,3072]{2,1,0:T(8,128)(2,1)S(1)} %bitcast.10), kind=kOutput, calls=%fused_computation.2 | convolution fusion | flops 679673856 | bytes 11231232 | tf_op jit(solution)/shard_map/dot_general | solution.py:387
  31.2 0.6 %collective-permute-start.7 = (bf16[32,3072]{1,0:T(8,128)(2,1)S(1)}, bf16[32,3072]{1,0:T(8,128)(2,1)S(1)}, u32[]{:S(2)}, u32[]{:S(2)}) collective-permute-start(bf16[32,3072]{1,0:T(8,128)(2,1)S(1)} %slice.33), channel_id=1, source_target_pairs={{0,16},{16,0},{1,17},{17,1},{2,18},{18,2},{3,19},{19,3},{4,20},{20... | collective-permute-start | bytes 589832 | tf_op jit(solution)/shard_map/ppermute | solution.py:345
  31.7 1.1 %collective-permute-done.7 = bf16[32,3072]{1,0:T(8,128)(2,1)S(1)} collective-permute-done((bf16[32,3072]{1,0:T(8,128)(2,1)S(1)}, bf16[32,3072]{1,0:T(8,128)(2,1)S(1)}, u32[]{:S(2)}, u32[]{:S(2)}) %collective-permute-start.7) | collective-permute-done | bytes 196640 | tf_op jit(solution)/shard_map/ppermute | solution.py:345
  32.8 0.1 add_convert_fusion
  32.9 1.6 %collective-permute-start.10 = (bf16[8,3072]{1,0:T(8,128)(2,1)S(1)}, bf16[8,3072]{1,0:T(8,128)(2,1)S(1)}, u32[]{:S(2)}, u32[]{:S(2)}) collective-permute-start(bf16[8,3072]{1,0:T(8,128)(2,1)S(1)} %get-tuple-element.22), channel_id=1, source_target_pairs={{0,4},{4,0},{8,12},{12,8},{1,5},{5,1},{9,13},{13,9},{2,6},{6,2},{1... | collective-permute-start | bytes 147464 | tf_op jit(solution)/shard_map/ppermute | solution.py:345
  34.4 1.5 %collective-permute-start.8 = (bf16[8,3072]{1,0:T(8,128)(2,1)S(1)}, bf16[8,3072]{1,0:T(8,128)(2,1)S(1)}, u32[]{:S(2)}, u32[]{:S(2)}) collective-permute-start(bf16[8,3072]{1,0:T(8,128)(2,1)S(1)} %get-tuple-element.21), channel_id=1, source_target_pairs={{0,8},{4,12},{8,0},{12,4},{1,9},{5,13},{9,1},{13,5},{2,10},{6,14},... | collective-permute-start | bytes 147464 | tf_op jit(solution)/shard_map/ppermute | solution.py:345
  36.0 0.5 collective-permute-start.9
  36.4 0.6 %collective-permute-done.10 = bf16[8,3072]{1,0:T(8,128)(2,1)S(1)} collective-permute-done((bf16[8,3072]{1,0:T(8,128)(2,1)S(1)}, bf16[8,3072]{1,0:T(8,128)(2,1)S(1)}, u32[]{:S(2)}, u32[]{:S(2)}) %collective-permute-start.10) | collective-permute-done | bytes 49184 | tf_op jit(solution)/shard_map/ppermute | solution.py:345
  37.0 1.5 %collective-permute-done.8 = bf16[8,3072]{1,0:T(8,128)(2,1)S(1)} collective-permute-done((bf16[8,3072]{1,0:T(8,128)(2,1)S(1)}, bf16[8,3072]{1,0:T(8,128)(2,1)S(1)}, u32[]{:S(2)}, u32[]{:S(2)}) %collective-permute-start.8) | collective-permute-done | bytes 49184 | tf_op jit(solution)/shard_map/ppermute | solution.py:345
  38.5 2.4 %collective-permute-done.9 = bf16[8,3072]{1,0:T(8,128)(2,1)S(1)} collective-permute-done((bf16[8,3072]{1,0:T(8,128)(2,1)S(1)}, bf16[8,3072]{1,0:T(8,128)(2,1)S(1)}, u32[]{:S(2)}, u32[]{:S(2)}) %collective-permute-start.9) | collective-permute-done | bytes 49184 | tf_op jit(solution)/shard_map/ppermute | solution.py:345
  41.0 2.4 %collective-permute-start.11 = (bf16[8,768]{1,0:T(8,128)(2,1)S(1)}, bf16[8,768]{1,0:T(8,128)(2,1)S(1)}, u32[]{:S(2)}, u32[]{:S(2)}) collective-permute-start(bf16[8,768]{1,0:T(8,128)(2,1)S(1)} %get-tuple-element.24), channel_id=1, source_target_pairs={{0,2},{1,3},{2,0},{3,1},{4,6},{5,7},{6,4},{7,5},{8,10},{9,11},{10,... | collective-permute-start | bytes 36872 | tf_op jit(solution)/shard_map/ppermute | solution.py:345
  43.4 1.4 %collective-permute-start.12 = (bf16[8,768]{1,0:T(8,128)(2,1)S(1)}, bf16[8,768]{1,0:T(8,128)(2,1)S(1)}, u32[]{:S(2)}, u32[]{:S(2)}) collective-permute-start(bf16[8,768]{1,0:T(8,128)(2,1)S(1)} %get-tuple-element.26), channel_id=1, source_target_pairs={{0,3},{1,2},{2,1},{3,0},{4,7},{5,6},{6,5},{7,4},{8,11},{9,10},{10,... | collective-permute-start | bytes 36872 | tf_op jit(solution)/shard_map/ppermute | solution.py:345
  44.7 0.9 %collective-permute-done.11 = bf16[8,768]{1,0:T(8,128)(2,1)S(1)} collective-permute-done((bf16[8,768]{1,0:T(8,128)(2,1)S(1)}, bf16[8,768]{1,0:T(8,128)(2,1)S(1)}, u32[]{:S(2)}, u32[]{:S(2)}) %collective-permute-start.11) | collective-permute-done | bytes 12320 | tf_op jit(solution)/shard_map/ppermute | solution.py:345
  45.7 3.2 %collective-permute-done.12 = bf16[8,768]{1,0:T(8,128)(2,1)S(1)} collective-permute-done((bf16[8,768]{1,0:T(8,128)(2,1)S(1)}, bf16[8,768]{1,0:T(8,128)(2,1)S(1)}, u32[]{:S(2)}, u32[]{:S(2)}) %collective-permute-start.12) | collective-permute-done | bytes 12320 | tf_op jit(solution)/shard_map/ppermute | solution.py:345
  48.9 0.6 %add_convert_fusion.2 = bf16[8,768]{1,0:T(8,128)(2,1)} fusion(bf16[8,768]{1,0:T(8,128)(2,1)S(1)} %collective-permute-done.13, bf16[8,768]{1,0:T(8,128)(2,1)S(1)} %collective-permute-done.12, bf16[8,768]{1,0:T(8,128)(2,1)S(1)} %collective-permute-done.11, bf16[8,1024]{1,0:T(8,128)(2,1)S(1)} %get-tuple-element.13._.refs_3_, ...), kind=kLoop, calls=%fused_computation.5 | loop fusion | flops 61440 | bytes 73732 | tf_op jit(solution)/shard_map/convert_element_type | solution.py:394
  (18 shorter events, 0.1 us)
Async XLA Ops:
  3.3 9.1 %collective-permute-start = (bf16[8,1024]{1,0:T(8,128)(2,1)S(1)}, bf16[8,1024]{1,0:T(8,128)(2,1)S(1)}, u32[]{:S(2)}, u32[]{:S(2)}) collective-permute-start(bf16[8,1024]{1,0:T(8,128)(2,1)S(1)} %get-tuple-element.13._.refs_3_), channel_id=1, source_target_pairs={{0,2},{1,3},{2,0},{3,1},{4,6},{5,7},{6,4},{7,5},{8,10},{9,11},{10,... | collective-permute-start | bytes 49160 | tf_op jit(solution)/shard_map/ppermute | solution.py:345
  7.4 5.5 %collective-permute-start.1 = (bf16[8,1024]{1,0:T(8,128)(2,1)S(1)}, bf16[8,1024]{1,0:T(8,128)(2,1)S(1)}, u32[]{:S(2)}, u32[]{:S(2)}) collective-permute-start(bf16[8,1024]{1,0:T(8,128)(2,1)S(1)} %get-tuple-element.13._.refs_3_), channel_id=1, source_target_pairs={{0,3},{1,2},{2,1},{3,0},{4,7},{5,6},{6,5},{7,4},{8,11},{9,10},{10,... | collective-permute-start | bytes 49160 | tf_op jit(solution)/shard_map/ppermute | solution.py:345
  8.8 4.2 %collective-permute-start.2 = (bf16[8,1024]{1,0:T(8,128)(2,1)S(1)}, bf16[8,1024]{1,0:T(8,128)(2,1)S(1)}, u32[]{:S(2)}, u32[]{:S(2)}) collective-permute-start(bf16[8,1024]{1,0:T(8,128)(2,1)S(1)} %get-tuple-element.13._.refs_3_), channel_id=1, source_target_pairs={{0,1},{1,0},{2,3},{3,2},{4,5},{5,4},{6,7},{7,6},{8,9},{9,8},{10,11... | collective-permute-start | bytes 49160 | tf_op jit(solution)/shard_map/ppermute | solution.py:345
  13.9 7.2 %collective-permute-start.3 = (bf16[8,3200]{1,0:T(8,128)(2,1)S(1)}, bf16[8,3200]{1,0:T(8,128)(2,1)S(1)}, u32[]{:S(2)}, u32[]{:S(2)}) collective-permute-start(bf16[8,3200]{1,0:T(8,128)(2,1)S(1)} %norm.1._.refs_3_), channel_id=1, source_target_pairs={{0,8},{4,12},{8,0},{12,4},{1,9},{5,13},{9,1},{13,5},{2,10},{6,14},... | collective-permute-start | bytes 153608 | tf_op jit(solution)/shard_map/ppermute | solution.py:345
  15.4 5.7 %collective-permute-start.4 = (bf16[8,3200]{1,0:T(8,128)(2,1)S(1)}, bf16[8,3200]{1,0:T(8,128)(2,1)S(1)}, u32[]{:S(2)}, u32[]{:S(2)}) collective-permute-start(bf16[8,3200]{1,0:T(8,128)(2,1)S(1)} %norm.1._.refs_3_), channel_id=1, source_target_pairs={{0,12},{4,8},{8,4},{12,0},{1,13},{5,9},{9,5},{13,1},{2,14},{6,10},... | collective-permute-start | bytes 153608 | tf_op jit(solution)/shard_map/ppermute | solution.py:345
  16.9 4.3 %collective-permute-start.5 = (bf16[8,3200]{1,0:T(8,128)(2,1)S(1)}, bf16[8,3200]{1,0:T(8,128)(2,1)S(1)}, u32[]{:S(2)}, u32[]{:S(2)}) collective-permute-start(bf16[8,3200]{1,0:T(8,128)(2,1)S(1)} %norm.1._.refs_3_), channel_id=1, source_target_pairs={{0,4},{4,0},{8,12},{12,8},{1,5},{5,1},{9,13},{13,9},{2,6},{6,2},{1... | collective-permute-start | bytes 153608 | tf_op jit(solution)/shard_map/ppermute | solution.py:345
  21.2 1.6 %collective-permute-start.6 = (bf16[32,3200]{1,0:T(8,128)(2,1)S(1)}, bf16[32,3200]{1,0:T(8,128)(2,1)S(1)}, u32[]{:S(2)}, u32[]{:S(2)}) collective-permute-start(bf16[32,3200]{1,0:T(8,128)(2,1)S(1)} %stack.13._.near), channel_id=1, source_target_pairs={{0,16},{16,0},{1,17},{17,1},{2,18},{18,2},{3,19},{19,3},{4,20},{20... | collective-permute-start | bytes 614408 | tf_op jit(solution)/shard_map/ppermute | solution.py:345
  21.2 7.9 %slice-start = ((s8[10616832]{0:T(1024)(128)(4,1)}), s8[4194304]{0:T(1024)(128)(4,1)S(1)}, s32[]{:S(2)}) async-start(s8[10616832]{0:T(1024)(128)(4,1)} %bitcast.9), calls=%async_computation | async-start | bytes 8388608
  22.8 6.3 %slice-start.1 = ((s8[10616832]{0:T(1024)(128)(4,1)}), s8[4194304]{0:T(1024)(128)(4,1)S(1)}, s32[]{:S(2)}) async-start(s8[10616832]{0:T(1024)(128)(4,1)} %bitcast.9), calls=%async_computation.1 | async-start | bytes 8388608
  22.8 6.3 %slice-start.2 = ((s8[10616832]{0:T(1024)(128)(4,1)}), s8[2228224]{0:T(1024)(128)(4,1)S(1)}, s32[]{:S(2)}) async-start(s8[10616832]{0:T(1024)(128)(4,1)} %bitcast.9), calls=%async_computation.2 | async-start | bytes 4456448
  31.2 1.6 %collective-permute-start.7 = (bf16[32,3072]{1,0:T(8,128)(2,1)S(1)}, bf16[32,3072]{1,0:T(8,128)(2,1)S(1)}, u32[]{:S(2)}, u32[]{:S(2)}) collective-permute-start(bf16[32,3072]{1,0:T(8,128)(2,1)S(1)} %slice.33), channel_id=1, source_target_pairs={{0,16},{16,0},{1,17},{17,1},{2,18},{18,2},{3,19},{19,3},{4,20},{20... | collective-permute-start | bytes 589832 | tf_op jit(solution)/shard_map/ppermute | solution.py:345
  32.9 4.2 %collective-permute-start.10 = (bf16[8,3072]{1,0:T(8,128)(2,1)S(1)}, bf16[8,3072]{1,0:T(8,128)(2,1)S(1)}, u32[]{:S(2)}, u32[]{:S(2)}) collective-permute-start(bf16[8,3072]{1,0:T(8,128)(2,1)S(1)} %get-tuple-element.22), channel_id=1, source_target_pairs={{0,4},{4,0},{8,12},{12,8},{1,5},{5,1},{9,13},{13,9},{2,6},{6,2},{1... | collective-permute-start | bytes 147464 | tf_op jit(solution)/shard_map/ppermute | solution.py:345
  34.4 4.1 %collective-permute-start.8 = (bf16[8,3072]{1,0:T(8,128)(2,1)S(1)}, bf16[8,3072]{1,0:T(8,128)(2,1)S(1)}, u32[]{:S(2)}, u32[]{:S(2)}) collective-permute-start(bf16[8,3072]{1,0:T(8,128)(2,1)S(1)} %get-tuple-element.21), channel_id=1, source_target_pairs={{0,8},{4,12},{8,0},{12,4},{1,9},{5,13},{9,1},{13,5},{2,10},{6,14},... | collective-permute-start | bytes 147464 | tf_op jit(solution)/shard_map/ppermute | solution.py:345
  36.0 5.0 %collective-permute-start.9 = (bf16[8,3072]{1,0:T(8,128)(2,1)S(1)}, bf16[8,3072]{1,0:T(8,128)(2,1)S(1)}, u32[]{:S(2)}, u32[]{:S(2)}) collective-permute-start(bf16[8,3072]{1,0:T(8,128)(2,1)S(1)} %get-tuple-element.23), channel_id=1, source_target_pairs={{0,12},{4,8},{8,4},{12,0},{1,13},{5,9},{9,5},{13,1},{2,14},{6,10},... | collective-permute-start | bytes 147464 | tf_op jit(solution)/shard_map/ppermute | solution.py:345
  41.0 4.7 %collective-permute-start.11 = (bf16[8,768]{1,0:T(8,128)(2,1)S(1)}, bf16[8,768]{1,0:T(8,128)(2,1)S(1)}, u32[]{:S(2)}, u32[]{:S(2)}) collective-permute-start(bf16[8,768]{1,0:T(8,128)(2,1)S(1)} %get-tuple-element.24), channel_id=1, source_target_pairs={{0,2},{1,3},{2,0},{3,1},{4,6},{5,7},{6,4},{7,5},{8,10},{9,11},{10,... | collective-permute-start | bytes 36872 | tf_op jit(solution)/shard_map/ppermute | solution.py:345
  43.4 5.5 %collective-permute-start.12 = (bf16[8,768]{1,0:T(8,128)(2,1)S(1)}, bf16[8,768]{1,0:T(8,128)(2,1)S(1)}, u32[]{:S(2)}, u32[]{:S(2)}) collective-permute-start(bf16[8,768]{1,0:T(8,128)(2,1)S(1)} %get-tuple-element.26), channel_id=1, source_target_pairs={{0,3},{1,2},{2,1},{3,0},{4,7},{5,6},{6,5},{7,4},{8,11},{9,10},{10,... | collective-permute-start | bytes 36872 | tf_op jit(solution)/shard_map/ppermute | solution.py:345
  44.7 4.1 %collective-permute-start.13 = (bf16[8,768]{1,0:T(8,128)(2,1)S(1)}, bf16[8,768]{1,0:T(8,128)(2,1)S(1)}, u32[]{:S(2)}, u32[]{:S(2)}) collective-permute-start(bf16[8,768]{1,0:T(8,128)(2,1)S(1)} %get-tuple-element.25), channel_id=1, source_target_pairs={{0,1},{1,0},{2,3},{3,2},{4,5},{5,4},{6,7},{7,6},{8,9},{9,8},{10,11... | collective-permute-start | bytes 36872 | tf_op jit(solution)/shard_map/ppermute | solution.py:345

commit v8 on v7

--- a/solution.py
+++ b/solution.py
@@ -13,7 +13,7 @@
 SLOT = 36
 MASK_AT = 3 * SLOT
 MIB = 1 << 20
-CHUNKS = 4
+CHUNKS = 16
 UNITS = 256
 BY_ROW = (((1,), (1,)), ((), ()))
 
@@ -388,7 +388,8 @@
     half = out.shape[0] // 2
     both = add(out[:half], send(out[half:], "section", 1)).astype(jnp.bfloat16)
     both = both.reshape(groups, tokens, -1)
-    got = add(*exchange(both, "group"), both[0]).astype(jnp.bfloat16)
+    others = [send(both[m], "group", m) for m in reversed(range(1, groups))]
+    got = add(*others[1:], others[0], both[0]).astype(jnp.bfloat16)
     parts = [lax.dynamic_slice_in_dim(got, (place ^ m) * block, block, axis=1) for m in range(tensors)]
     mixed = add(*exchange(parts, "tensor"), parts[0], fresh[:, :block])
     return mixed.astype(jnp.bfloat16)

time: 49.7 us -> 49.5 us (level)
  waiting for transfers between devices: 10.2 us -> 9.29 us
  Pallas kernels: 18.5 us -> 19.3 us
    ppermute x14, waiting for transfers between devices: 10.2 us -> 9.29 us  [send(): lax.ppermute(x, axis, [(i, i ^ mask) for i in range(lax.axis_size(axis))])]
    pallas_call x1, Pallas kernels: 2.68 us -> 3.22 us  [attend(): pl.pallas_call(functools.partial(attention_kernel, chunks=chunks, rest=re...]
  transfers between devices with their start and end apart: 14 -> 14, of which waited for: 7 -> 7; matrix products, arithmetic and copies ran while one was open for 0% -> 0% of each run, Pallas kernels for 17% -> 18%
where the time goes in v8:
time: 49.5 us; the launch traced here: 49.4 us
  Pallas kernels  19.3 us (39%)
  starting transfers between devices  17.1 us (35%)
  waiting for transfers between devices  9.29 us (19%)
  matrix products  1.97 us (4%)
  between operations  0.85 us (2%)
  other arithmetic  0.77 us (2%)
    ppermute x14, starting transfers between devices, send(): lax.ppermute(x, axis, [(i, i ^ mask) for i in range(lax.axis_size(axis))])  17.1 us
    ppermute x14, waiting for transfers between devices, send(): lax.ppermute(x, axis, [(i, i ^ mask) for i in range(lax.axis_size(axis))])  9.29 us
    pallas_call x3, Pallas kernels, load(): pl.pallas_call(functools.partial(load_kernel, part=part), out_shape=(pltp...  8.89 us
    pallas_call x1, Pallas kernels, run_hidden(): pl.pallas_call(functools.partial(hidden_kernel, experts=experts), out_sha...  6.3 us
    pallas_call x1, Pallas kernels, attend(): pl.pallas_call(functools.partial(attention_kernel, chunks=chunks, rest=re...  3.22 us
    dot_general x1, matrix products, per_device(): jnp.dot(hidden, down_w[0], preferred_element_type=jnp.float32)  1.97 us
  transfers between devices with their start and end apart: 14, of which 7 were waited for; matrix products, arithmetic and copies ran while one was open for 0% of the time, Pallas kernels for 18%

profile of v8, /device:TPU:0, one launch (start us, length us, event | category | flops | bytes accessed | tf_op | source)
XLA Modules:
  0.0 49.4 jit_solution(7502352106531246166)
XLA Ops:
  0.7 3.2 %attention.1 = (bf16[8,1024]{1,0:T(8,128)(2,1)S(1)}, bf16[448,3072]{1,0:T(8,128)(2,1)S(1)}) custom-call(s32[1]{0:T(128)S(6)} %copy.12.len_ref, bf16[8,768]{1,0:T(8,128)(2,1)} %q_hbm.1, bf16[8,512]{1,0:T(8,128)(2,1)} %new_hbm.1, bf16[1,2048,512]{2,1,0:T(8,128)(2,1)} %kv_hbm.1, bf16[8,768]{1,0:T(8,128)(2,1)} %res_hbm.1, s32[4,8]{1,0:T(4,128)} %bitcast.11, ...), custom_call_target="tpu_custom_call" | custom-call | flops 50331648 | bytes 2097152 | tf_op jit(solution)/shard_map/attention/pallas_call | solution.py:187
  3.9 4.1 %collective-permute-start = (bf16[8,1024]{1,0:T(8,128)(2,1)S(1)}, bf16[8,1024]{1,0:T(8,128)(2,1)S(1)}, u32[]{:S(2)}, u32[]{:S(2)}) collective-permute-start(bf16[8,1024]{1,0:T(8,128)(2,1)S(1)} %get-tuple-element.13._.refs_3_), channel_id=1, source_target_pairs={{0,2},{1,3},{2,0},{3,1},{4,6},{5,7},{6,4},{7,5},{8,10},{9,11},{10,... | collective-permute-start | bytes 49160 | tf_op jit(solution)/shard_map/ppermute | solution.py:345
  8.0 1.3 %collective-permute-start.1 = (bf16[8,1024]{1,0:T(8,128)(2,1)S(1)}, bf16[8,1024]{1,0:T(8,128)(2,1)S(1)}, u32[]{:S(2)}, u32[]{:S(2)}) collective-permute-start(bf16[8,1024]{1,0:T(8,128)(2,1)S(1)} %get-tuple-element.13._.refs_3_), channel_id=1, source_target_pairs={{0,3},{1,2},{2,1},{3,0},{4,7},{5,6},{6,5},{7,4},{8,11},{9,10},{10,... | collective-permute-start | bytes 49160 | tf_op jit(solution)/shard_map/ppermute | solution.py:345
  9.3 0.2 collective-permute-start.2
  9.6 0.1 pad_add_fusion.place_ref
  9.6 3.4 %load.3 = (bf16[1280,3072]{1,0:T(8,128)(2,1)S(1)}, f32[8,128]{1,0:T(8,128)S(1)}) custom-call(bf16[8,1024]{1,0:T(8,128)(2,1)S(1)} %get-tuple-element.13._.refs_3_, bf16[1,1728,3072]{2,1,0:T(8,128)(2,1)} %source.3), custom_call_target="tpu_custom_call" | custom-call | bytes 15728640 | tf_op jit(solution)/shard_map/load/pallas_call | solution.py:221
  13.0 0.5 %collective-permute-done.1.refs_1_ = bf16[8,1024]{1,0:T(8,128)(2,1)S(1)} collective-permute-done((bf16[8,1024]{1,0:T(8,128)(2,1)S(1)}, bf16[8,1024]{1,0:T(8,128)(2,1)S(1)}, u32[]{:S(2)}, u32[]{:S(2)}) %collective-permute-start.1) | collective-permute-done | bytes 16416 | tf_op jit(solution)/shard_map/ppermute | solution.py:345
  13.5 0.9 %norm.1._.refs_3_ = bf16[8,3200]{1,0:T(8,128)(2,1)S(1)} custom-call(s32[2]{0:T(128)S(1)} %pad_add_fusion.place_ref, f32[8,128]{1,0:T(8,128)S(1)} %get-tuple-element.14._, bf16[8,1024]{1,0:T(8,128)(2,1)S(1)} %collective-permute-done.refs_0_, bf16[8,1024]{1,0:T(8,128)(2,1)S(1)} %collective-permute-done.1.refs_1_, ...), custom_call_target="tpu_custom_call" | custom-call | tf_op jit(solution)/shard_map/norm/pallas_call | solution.py:266
  14.4 1.5 %collective-permute-start.3 = (bf16[8,3200]{1,0:T(8,128)(2,1)S(1)}, bf16[8,3200]{1,0:T(8,128)(2,1)S(1)}, u32[]{:S(2)}, u32[]{:S(2)}) collective-permute-start(bf16[8,3200]{1,0:T(8,128)(2,1)S(1)} %norm.1._.refs_3_), channel_id=1, source_target_pairs={{0,8},{4,12},{8,0},{12,4},{1,9},{5,13},{9,1},{13,5},{2,10},{6,14},... | collective-permute-start | bytes 153608 | tf_op jit(solution)/shard_map/ppermute | solution.py:345
  16.0 1.4 %collective-permute-start.4 = (bf16[8,3200]{1,0:T(8,128)(2,1)S(1)}, bf16[8,3200]{1,0:T(8,128)(2,1)S(1)}, u32[]{:S(2)}, u32[]{:S(2)}) collective-permute-start(bf16[8,3200]{1,0:T(8,128)(2,1)S(1)} %norm.1._.refs_3_), channel_id=1, source_target_pairs={{0,12},{4,8},{8,4},{12,0},{1,13},{5,9},{9,5},{13,1},{2,14},{6,10},... | collective-permute-start | bytes 153608 | tf_op jit(solution)/shard_map/ppermute | solution.py:345
  17.4 0.5 %collective-permute-start.5 = (bf16[8,3200]{1,0:T(8,128)(2,1)S(1)}, bf16[8,3200]{1,0:T(8,128)(2,1)S(1)}, u32[]{:S(2)}, u32[]{:S(2)}) collective-permute-start(bf16[8,3200]{1,0:T(8,128)(2,1)S(1)} %norm.1._.refs_3_), channel_id=1, source_target_pairs={{0,4},{4,0},{8,12},{12,8},{1,5},{5,1},{9,13},{13,9},{2,6},{6,2},{1... | collective-permute-start | bytes 153608 | tf_op jit(solution)/shard_map/ppermute | solution.py:345
  18.0 3.8 %load.4 = (bf16[1472,3072]{1,0:T(8,128)(2,1)S(1)}, f32[8,128]{1,0:T(8,128)S(1)}) custom-call(bf16[8,3200]{1,0:T(8,128)(2,1)S(1)} %norm.1._.refs_3_, bf16[1,1728,3072]{2,1,0:T(8,128)(2,1)} %source.5), custom_call_target="tpu_custom_call" | custom-call | bytes 18087936 | tf_op jit(solution)/shard_map/load/pallas_call | solution.py:221
  21.8 0.1 collective-permute-start.6
  21.9 0.0 slice-start
  21.9 1.7 %load.5 = (bf16[256,3072]{1,0:T(8,128)(2,1)S(1)}, f32[8,128]{1,0:T(8,128)S(1)}) custom-call(bf16[32,3200]{1,0:T(8,128)(2,1)S(1)} %stack.13._.near, bf16[1,1728,3072]{2,1,0:T(8,128)(2,1)} %source.5), custom_call_target="tpu_custom_call" | custom-call | bytes 3145728 | tf_op jit(solution)/shard_map/load/pallas_call | solution.py:221
  23.7 0.0 slice-start.1
  23.7 6.3 %hidden.1 = bf16[64,1728]{1,0:T(8,128)(2,1)S(1)} custom-call(s32[2]{0:T(128)S(1)} %pad_add_fusion.place_ref, bf16[32,3200]{1,0:T(8,128)(2,1)S(1)} %stack.13._.near, bf16[32,3200]{1,0:T(8,128)(2,1)S(1)} %collective-permute-done.6.far, bf16[1280,3072]{1,0:T(8,128)(2,1)S(1)} %get-tuple-element.16.gate_a, bf16[448,3072]{1,0:T(8,128)(2,1)S(1)} %get-tuple-element.17.gate_b, ...), custom_call_target="tpu_custom_call" | custom-call | flops 1358954496 | bytes 21233664 | tf_op jit(solution)/shard_map/hidden/pallas_call | solution.py:330
  30.0 2.0 %fusion.2 = bf16[64,3072]{1,0:T(8,128)(2,1)S(1)} fusion(bf16[64,1728]{1,0:T(8,128)(2,1)S(1)} %hidden.1, bf16[1,1728,3072]{2,1,0:T(8,128)(2,1)S(1)} %bitcast.10), kind=kOutput, calls=%fused_computation.2 | convolution fusion | flops 679673856 | bytes 11231232 | tf_op jit(solution)/shard_map/dot_general | solution.py:387
  32.0 0.6 %collective-permute-start.7 = (bf16[32,3072]{1,0:T(8,128)(2,1)S(1)}, bf16[32,3072]{1,0:T(8,128)(2,1)S(1)}, u32[]{:S(2)}, u32[]{:S(2)}) collective-permute-start(bf16[32,3072]{1,0:T(8,128)(2,1)S(1)} %slice.33), channel_id=1, source_target_pairs={{0,16},{16,0},{1,17},{17,1},{2,18},{18,2},{3,19},{19,3},{4,20},{20... | collective-permute-start | bytes 589832 | tf_op jit(solution)/shard_map/ppermute | solution.py:345
  32.6 1.1 %collective-permute-done.7 = bf16[32,3072]{1,0:T(8,128)(2,1)S(1)} collective-permute-done((bf16[32,3072]{1,0:T(8,128)(2,1)S(1)}, bf16[32,3072]{1,0:T(8,128)(2,1)S(1)}, u32[]{:S(2)}, u32[]{:S(2)}) %collective-permute-start.7) | collective-permute-done | bytes 196640 | tf_op jit(solution)/shard_map/ppermute | solution.py:345
  33.6 0.1 add_convert_fusion
  33.7 2.5 %collective-permute-start.10 = (bf16[8,3072]{1,0:T(8,128)(2,1)S(1)}, bf16[8,3072]{1,0:T(8,128)(2,1)S(1)}, u32[]{:S(2)}, u32[]{:S(2)}) collective-permute-start(bf16[8,3072]{1,0:T(8,128)(2,1)S(1)} %get-tuple-element.22), channel_id=1, source_target_pairs={{0,12},{4,8},{8,4},{12,0},{1,13},{5,9},{9,5},{13,1},{2,14},{6,10},... | collective-permute-start | bytes 147464 | tf_op jit(solution)/shard_map/ppermute | solution.py:345
  36.2 0.5 %collective-permute-start.8 = (bf16[8,3072]{1,0:T(8,128)(2,1)S(1)}, bf16[8,3072]{1,0:T(8,128)(2,1)S(1)}, u32[]{:S(2)}, u32[]{:S(2)}) collective-permute-start(bf16[8,3072]{1,0:T(8,128)(2,1)S(1)} %get-tuple-element.21), channel_id=1, source_target_pairs={{0,8},{4,12},{8,0},{12,4},{1,9},{5,13},{9,1},{13,5},{2,10},{6,14},... | collective-permute-start | bytes 147464 | tf_op jit(solution)/shard_map/ppermute | solution.py:345
  36.8 0.5 %collective-permute-start.9 = (bf16[8,3072]{1,0:T(8,128)(2,1)S(1)}, bf16[8,3072]{1,0:T(8,128)(2,1)S(1)}, u32[]{:S(2)}, u32[]{:S(2)}) collective-permute-start(bf16[8,3072]{1,0:T(8,128)(2,1)S(1)} %get-tuple-element.23), channel_id=1, source_target_pairs={{0,4},{4,0},{8,12},{12,8},{1,5},{5,1},{9,13},{13,9},{2,6},{6,2},{1... | collective-permute-start | bytes 147464 | tf_op jit(solution)/shard_map/ppermute | solution.py:345
  37.3 1.5 %collective-permute-done.10 = bf16[8,3072]{1,0:T(8,128)(2,1)S(1)} collective-permute-done((bf16[8,3072]{1,0:T(8,128)(2,1)S(1)}, bf16[8,3072]{1,0:T(8,128)(2,1)S(1)}, u32[]{:S(2)}, u32[]{:S(2)}) %collective-permute-start.10) | collective-permute-done | bytes 49184 | tf_op jit(solution)/shard_map/ppermute | solution.py:345
  38.8 1.5 %collective-permute-done.8 = bf16[8,3072]{1,0:T(8,128)(2,1)S(1)} collective-permute-done((bf16[8,3072]{1,0:T(8,128)(2,1)S(1)}, bf16[8,3072]{1,0:T(8,128)(2,1)S(1)}, u32[]{:S(2)}, u32[]{:S(2)}) %collective-permute-start.8) | collective-permute-done | bytes 49184 | tf_op jit(solution)/shard_map/ppermute | solution.py:345
  40.3 0.5 %collective-permute-done.9 = bf16[8,3072]{1,0:T(8,128)(2,1)S(1)} collective-permute-done((bf16[8,3072]{1,0:T(8,128)(2,1)S(1)}, bf16[8,3072]{1,0:T(8,128)(2,1)S(1)}, u32[]{:S(2)}, u32[]{:S(2)}) %collective-permute-start.9) | collective-permute-done | bytes 49184 | tf_op jit(solution)/shard_map/ppermute | solution.py:345
  40.9 2.4 %collective-permute-start.11 = (bf16[8,768]{1,0:T(8,128)(2,1)S(1)}, bf16[8,768]{1,0:T(8,128)(2,1)S(1)}, u32[]{:S(2)}, u32[]{:S(2)}) collective-permute-start(bf16[8,768]{1,0:T(8,128)(2,1)S(1)} %get-tuple-element.24), channel_id=1, source_target_pairs={{0,2},{1,3},{2,0},{3,1},{4,6},{5,7},{6,4},{7,5},{8,10},{9,11},{10,... | collective-permute-start | bytes 36872 | tf_op jit(solution)/shard_map/ppermute | solution.py:345
  43.3 1.3 %collective-permute-start.12 = (bf16[8,768]{1,0:T(8,128)(2,1)S(1)}, bf16[8,768]{1,0:T(8,128)(2,1)S(1)}, u32[]{:S(2)}, u32[]{:S(2)}) collective-permute-start(bf16[8,768]{1,0:T(8,128)(2,1)S(1)} %get-tuple-element.26), channel_id=1, source_target_pairs={{0,3},{1,2},{2,1},{3,0},{4,7},{5,6},{6,5},{7,4},{8,11},{9,10},{10,... | collective-permute-start | bytes 36872 | tf_op jit(solution)/shard_map/ppermute | solution.py:345
  44.6 0.9 %collective-permute-done.11 = bf16[8,768]{1,0:T(8,128)(2,1)S(1)} collective-permute-done((bf16[8,768]{1,0:T(8,128)(2,1)S(1)}, bf16[8,768]{1,0:T(8,128)(2,1)S(1)}, u32[]{:S(2)}, u32[]{:S(2)}) %collective-permute-start.11) | collective-permute-done | bytes 12320 | tf_op jit(solution)/shard_map/ppermute | solution.py:345
  45.6 3.2 %collective-permute-done.12 = bf16[8,768]{1,0:T(8,128)(2,1)S(1)} collective-permute-done((bf16[8,768]{1,0:T(8,128)(2,1)S(1)}, bf16[8,768]{1,0:T(8,128)(2,1)S(1)}, u32[]{:S(2)}, u32[]{:S(2)}) %collective-permute-start.12) | collective-permute-done | bytes 12320 | tf_op jit(solution)/shard_map/ppermute | solution.py:345
  48.8 0.6 %add_convert_fusion.2 = bf16[8,768]{1,0:T(8,128)(2,1)} fusion(bf16[8,768]{1,0:T(8,128)(2,1)S(1)} %collective-permute-done.13, bf16[8,768]{1,0:T(8,128)(2,1)S(1)} %collective-permute-done.12, bf16[8,768]{1,0:T(8,128)(2,1)S(1)} %collective-permute-done.11, bf16[8,1024]{1,0:T(8,128)(2,1)S(1)} %get-tuple-element.13._.refs_3_, ...), kind=kLoop, calls=%fused_computation.5 | loop fusion | flops 61440 | bytes 73732 | tf_op jit(solution)/shard_map/convert_element_type | solution.py:395
  (18 shorter events, 0.1 us)
Async XLA Ops:
  3.9 9.1 %collective-permute-start = (bf16[8,1024]{1,0:T(8,128)(2,1)S(1)}, bf16[8,1024]{1,0:T(8,128)(2,1)S(1)}, u32[]{:S(2)}, u32[]{:S(2)}) collective-permute-start(bf16[8,1024]{1,0:T(8,128)(2,1)S(1)} %get-tuple-element.13._.refs_3_), channel_id=1, source_target_pairs={{0,2},{1,3},{2,0},{3,1},{4,6},{5,7},{6,4},{7,5},{8,10},{9,11},{10,... | collective-permute-start | bytes 49160 | tf_op jit(solution)/shard_map/ppermute | solution.py:345
  8.0 5.5 %collective-permute-start.1 = (bf16[8,1024]{1,0:T(8,128)(2,1)S(1)}, bf16[8,1024]{1,0:T(8,128)(2,1)S(1)}, u32[]{:S(2)}, u32[]{:S(2)}) collective-permute-start(bf16[8,1024]{1,0:T(8,128)(2,1)S(1)} %get-tuple-element.13._.refs_3_), channel_id=1, source_target_pairs={{0,3},{1,2},{2,1},{3,0},{4,7},{5,6},{6,5},{7,4},{8,11},{9,10},{10,... | collective-permute-start | bytes 49160 | tf_op jit(solution)/shard_map/ppermute | solution.py:345
  9.3 4.2 %collective-permute-start.2 = (bf16[8,1024]{1,0:T(8,128)(2,1)S(1)}, bf16[8,1024]{1,0:T(8,128)(2,1)S(1)}, u32[]{:S(2)}, u32[]{:S(2)}) collective-permute-start(bf16[8,1024]{1,0:T(8,128)(2,1)S(1)} %get-tuple-element.13._.refs_3_), channel_id=1, source_target_pairs={{0,1},{1,0},{2,3},{3,2},{4,5},{5,4},{6,7},{7,6},{8,9},{9,8},{10,11... | collective-permute-start | bytes 49160 | tf_op jit(solution)/shard_map/ppermute | solution.py:345
  14.4 7.3 %collective-permute-start.3 = (bf16[8,3200]{1,0:T(8,128)(2,1)S(1)}, bf16[8,3200]{1,0:T(8,128)(2,1)S(1)}, u32[]{:S(2)}, u32[]{:S(2)}) collective-permute-start(bf16[8,3200]{1,0:T(8,128)(2,1)S(1)} %norm.1._.refs_3_), channel_id=1, source_target_pairs={{0,8},{4,12},{8,0},{12,4},{1,9},{5,13},{9,1},{13,5},{2,10},{6,14},... | collective-permute-start | bytes 153608 | tf_op jit(solution)/shard_map/ppermute | solution.py:345
  16.0 5.8 %collective-permute-start.4 = (bf16[8,3200]{1,0:T(8,128)(2,1)S(1)}, bf16[8,3200]{1,0:T(8,128)(2,1)S(1)}, u32[]{:S(2)}, u32[]{:S(2)}) collective-permute-start(bf16[8,3200]{1,0:T(8,128)(2,1)S(1)} %norm.1._.refs_3_), channel_id=1, source_target_pairs={{0,12},{4,8},{8,4},{12,0},{1,13},{5,9},{9,5},{13,1},{2,14},{6,10},... | collective-permute-start | bytes 153608 | tf_op jit(solution)/shard_map/ppermute | solution.py:345
  17.4 4.4 %collective-permute-start.5 = (bf16[8,3200]{1,0:T(8,128)(2,1)S(1)}, bf16[8,3200]{1,0:T(8,128)(2,1)S(1)}, u32[]{:S(2)}, u32[]{:S(2)}) collective-permute-start(bf16[8,3200]{1,0:T(8,128)(2,1)S(1)} %norm.1._.refs_3_), channel_id=1, source_target_pairs={{0,4},{4,0},{8,12},{12,8},{1,5},{5,1},{9,13},{13,9},{2,6},{6,2},{1... | collective-permute-start | bytes 153608 | tf_op jit(solution)/shard_map/ppermute | solution.py:345
  21.8 1.8 %collective-permute-start.6 = (bf16[32,3200]{1,0:T(8,128)(2,1)S(1)}, bf16[32,3200]{1,0:T(8,128)(2,1)S(1)}, u32[]{:S(2)}, u32[]{:S(2)}) collective-permute-start(bf16[32,3200]{1,0:T(8,128)(2,1)S(1)} %stack.13._.near), channel_id=1, source_target_pairs={{0,16},{16,0},{1,17},{17,1},{2,18},{18,2},{3,19},{19,3},{4,20},{20... | collective-permute-start | bytes 614408 | tf_op jit(solution)/shard_map/ppermute | solution.py:345
  21.9 8.1 %slice-start = ((s8[10616832]{0:T(1024)(128)(4,1)}), s8[4194304]{0:T(1024)(128)(4,1)S(1)}, s32[]{:S(2)}) async-start(s8[10616832]{0:T(1024)(128)(4,1)} %bitcast.9), calls=%async_computation | async-start | bytes 8388608
  23.7 6.3 %slice-start.1 = ((s8[10616832]{0:T(1024)(128)(4,1)}), s8[4194304]{0:T(1024)(128)(4,1)S(1)}, s32[]{:S(2)}) async-start(s8[10616832]{0:T(1024)(128)(4,1)} %bitcast.9), calls=%async_computation.1 | async-start | bytes 8388608
  23.7 6.3 %slice-start.2 = ((s8[10616832]{0:T(1024)(128)(4,1)}), s8[2228224]{0:T(1024)(128)(4,1)S(1)}, s32[]{:S(2)}) async-start(s8[10616832]{0:T(1024)(128)(4,1)} %bitcast.9), calls=%async_computation.2 | async-start | bytes 4456448
  32.0 1.6 %collective-permute-start.7 = (bf16[32,3072]{1,0:T(8,128)(2,1)S(1)}, bf16[32,3072]{1,0:T(8,128)(2,1)S(1)}, u32[]{:S(2)}, u32[]{:S(2)}) collective-permute-start(bf16[32,3072]{1,0:T(8,128)(2,1)S(1)} %slice.33), channel_id=1, source_target_pairs={{0,16},{16,0},{1,17},{17,1},{2,18},{18,2},{3,19},{19,3},{4,20},{20... | collective-permute-start | bytes 589832 | tf_op jit(solution)/shard_map/ppermute | solution.py:345
  33.7 5.1 %collective-permute-start.10 = (bf16[8,3072]{1,0:T(8,128)(2,1)S(1)}, bf16[8,3072]{1,0:T(8,128)(2,1)S(1)}, u32[]{:S(2)}, u32[]{:S(2)}) collective-permute-start(bf16[8,3072]{1,0:T(8,128)(2,1)S(1)} %get-tuple-element.22), channel_id=1, source_target_pairs={{0,12},{4,8},{8,4},{12,0},{1,13},{5,9},{9,5},{13,1},{2,14},{6,10},... | collective-permute-start | bytes 147464 | tf_op jit(solution)/shard_map/ppermute | solution.py:345
  36.2 4.1 %collective-permute-start.8 = (bf16[8,3072]{1,0:T(8,128)(2,1)S(1)}, bf16[8,3072]{1,0:T(8,128)(2,1)S(1)}, u32[]{:S(2)}, u32[]{:S(2)}) collective-permute-start(bf16[8,3072]{1,0:T(8,128)(2,1)S(1)} %get-tuple-element.21), channel_id=1, source_target_pairs={{0,8},{4,12},{8,0},{12,4},{1,9},{5,13},{9,1},{13,5},{2,10},{6,14},... | collective-permute-start | bytes 147464 | tf_op jit(solution)/shard_map/ppermute | solution.py:345
  36.8 4.1 %collective-permute-start.9 = (bf16[8,3072]{1,0:T(8,128)(2,1)S(1)}, bf16[8,3072]{1,0:T(8,128)(2,1)S(1)}, u32[]{:S(2)}, u32[]{:S(2)}) collective-permute-start(bf16[8,3072]{1,0:T(8,128)(2,1)S(1)} %get-tuple-element.23), channel_id=1, source_target_pairs={{0,4},{4,0},{8,12},{12,8},{1,5},{5,1},{9,13},{13,9},{2,6},{6,2},{1... | collective-permute-start | bytes 147464 | tf_op jit(solution)/shard_map/ppermute | solution.py:345
  40.9 4.7 %collective-permute-start.11 = (bf16[8,768]{1,0:T(8,128)(2,1)S(1)}, bf16[8,768]{1,0:T(8,128)(2,1)S(1)}, u32[]{:S(2)}, u32[]{:S(2)}) collective-permute-start(bf16[8,768]{1,0:T(8,128)(2,1)S(1)} %get-tuple-element.24), channel_id=1, source_target_pairs={{0,2},{1,3},{2,0},{3,1},{4,6},{5,7},{6,4},{7,5},{8,10},{9,11},{10,... | collective-permute-start | bytes 36872 | tf_op jit(solution)/shard_map/ppermute | solution.py:345
  43.3 5.5 %collective-permute-start.12 = (bf16[8,768]{1,0:T(8,128)(2,1)S(1)}, bf16[8,768]{1,0:T(8,128)(2,1)S(1)}, u32[]{:S(2)}, u32[]{:S(2)}) collective-permute-start(bf16[8,768]{1,0:T(8,128)(2,1)S(1)} %get-tuple-element.26), channel_id=1, source_target_pairs={{0,3},{1,2},{2,1},{3,0},{4,7},{5,6},{6,5},{7,4},{8,11},{9,10},{10,... | collective-permute-start | bytes 36872 | tf_op jit(solution)/shard_map/ppermute | solution.py:345
  44.6 4.1 %collective-permute-start.13 = (bf16[8,768]{1,0:T(8,128)(2,1)S(1)}, bf16[8,768]{1,0:T(8,128)(2,1)S(1)}, u32[]{:S(2)}, u32[]{:S(2)}) collective-permute-start(bf16[8,768]{1,0:T(8,128)(2,1)S(1)} %get-tuple-element.25), channel_id=1, source_target_pairs={{0,1},{1,0},{2,3},{3,2},{4,5},{5,4},{6,7},{7,6},{8,9},{9,8},{10,11... | collective-permute-start | bytes 36872 | tf_op jit(solution)/shard_map/ppermute | solution.py:345

commit v9 on v8

--- a/solution.py
+++ b/solution.py
@@ -13,7 +13,6 @@
 SLOT = 36
 MASK_AT = 3 * SLOT
 MIB = 1 << 20
-CHUNKS = 16
 UNITS = 256
 BY_ROW = (((1,), (1,)), ((), ()))
 
@@ -35,18 +34,10 @@
     return pl.ds(0, cut), pl.ds(cut, units - cut)
 
 
-def start_load(source, target, part, sems):
-    count = max(c for c in range(1, CHUNKS + 1) if part.size % (16 * c) == 0 or c == 1)
-    step = part.size // count
-    copies = [
-        pltpu.make_async_copy(
-            source.at[0, pl.ds(part.start + i * step, step)], target.at[pl.ds(i * step, step)], sems.at[i]
-        )
-        for i in range(count)
-    ]
-    for copy in copies:
-        copy.start()
-    return copies
+def start_load(source, target, part, sem):
+    copy = pltpu.make_async_copy(source.at[0, part], target, sem)
+    copy.start()
+    return copy
 
 
 def attention_kernel(
@@ -70,7 +61,7 @@
     gain_ref,
     scores,
     sems,
-    weight_sems,
+    weight_sem,
     *,
     chunks,
     rest,
@@ -84,7 +75,7 @@
     copies = [pltpu.make_async_copy(a, b, sems.at[i]) for i, (a, b) in enumerate(zip(sources, targets))]
     for copy in copies:
         copy.start()
-    loads = start_load(weight_hbm, weight_ref, rest, weight_sems)
+    load = start_load(weight_hbm, weight_ref, rest, weight_sem)
     tokens, columns = q_ref.shape
     key_heads = new_ref.shape[1] // (2 * HEAD_DIM)
     grouped = columns // HEAD_DIM // key_heads
@@ -170,8 +161,7 @@
         gains + [jnp.zeros((1, LANES), jnp.float32)] * (tokens - len(gains)), axis=0
     )
     out_ref[:, columns + LANES :] = gain_rows.astype(out_ref.dtype)
-    for copy in loads:
-        copy.wait()
+    load.wait()
 
 
 def attend(cache_len, queries, new_kv, kv_cache, residual, routes, router, norm_gain, weight, rest):
@@ -197,7 +187,7 @@
         + [
             pltpu.VMEM((key_heads, rows, slots), jnp.float32),
             pltpu.SemaphoreType.DMA((chunks + len(operands) - 2,)),
-            pltpu.SemaphoreType.DMA((CHUNKS,)),
+            pltpu.SemaphoreType.DMA,
         ],
         compiler_params=pltpu.CompilerParams(vmem_limit_bytes=8 * MIB),
         cost_estimate=pl.CostEstimate(
@@ -209,11 +199,10 @@
     )(cache_len, *operands)
 
 
-def load_kernel(_, source, out_ref, token_ref, sems, *, part):
-    copies = start_load(source, out_ref, part, sems)
+def load_kernel(_, source, out_ref, token_ref, sem, *, part):
+    copy = start_load(source, out_ref, part, sem)
     token_ref[...] = jnp.zeros_like(token_ref)
-    for copy in copies:
-        copy.wait()
+    copy.wait()
 
 
 def load(after, weight, part):
@@ -223,7 +212,7 @@
         out_shape=(pltpu.VMEM(shape, weight.dtype), jax.ShapeDtypeStruct((8, LANES), jnp.float32)),
         in_specs=[pl.BlockSpec(memory_space=pl.ANY)] * 2,
         out_specs=(pl.BlockSpec(memory_space=pltpu.VMEM),) * 2,
-        scratch_shapes=[pltpu.SemaphoreType.DMA((CHUNKS,))],
+        scratch_shapes=[pltpu.SemaphoreType.DMA],
         compiler_params=pltpu.CompilerParams(vmem_limit_bytes=MIB),
         cost_estimate=pl.CostEstimate(flops=0, bytes_accessed=4 * shape[0] * shape[1], transcendentals=0),
         name="load",

time: 49.5 us -> 48.5 us (0.980)
  Pallas kernels: 19.3 us -> 18.2 us
    pallas_call x1, Pallas kernels: 3.22 us -> 2.59 us  [attend(): pl.pallas_call(functools.partial(attention_kernel, chunks=chunks, rest=re...]
    pallas_call x3, Pallas kernels: 8.89 us -> 8.39 us  [load(): pl.pallas_call(functools.partial(load_kernel, part=part), out_shape=(pltp...]
  transfers between devices with their start and end apart: 14 -> 14, of which waited for: 7 -> 7; matrix products, arithmetic and copies ran while one was open for 0% -> 0% of each run, Pallas kernels for 18% -> 17%
where the time goes in v9:
time: 48.5 us; the launch traced here: 48.3 us
  Pallas kernels  18.2 us (38%)
  starting transfers between devices  17 us (35%)
  waiting for transfers between devices  9.4 us (19%)
  matrix products  1.97 us (4%)
  between operations  0.85 us (2%)
  other arithmetic  0.77 us (2%)
    ppermute x14, starting transfers between devices, send(): lax.ppermute(x, axis, [(i, i ^ mask) for i in range(lax.axis_size(axis))])  17 us
    ppermute x14, waiting for transfers between devices, send(): lax.ppermute(x, axis, [(i, i ^ mask) for i in range(lax.axis_size(axis))])  9.4 us
    pallas_call x3, Pallas kernels, load(): pl.pallas_call(functools.partial(load_kernel, part=part), out_shape=(pltp...  8.39 us
    pallas_call x1, Pallas kernels, run_hidden(): pl.pallas_call(functools.partial(hidden_kernel, experts=experts), out_sha...  6.3 us
    pallas_call x1, Pallas kernels, attend(): pl.pallas_call(functools.partial(attention_kernel, chunks=chunks, rest=re...  2.59 us
    dot_general x1, matrix products, per_device(): jnp.dot(hidden, down_w[0], preferred_element_type=jnp.float32)  1.97 us
  transfers between devices with their start and end apart: 14, of which 7 were waited for; matrix products, arithmetic and copies ran while one was open for 0% of the time, Pallas kernels for 17%

profile of v9, /device:TPU:0, one launch (start us, length us, event | category | flops | bytes accessed | tf_op | source)
XLA Modules:
  0.0 48.3 jit_solution(9682796640320490398)
XLA Ops:
  0.7 2.6 %attention.1 = (bf16[8,1024]{1,0:T(8,128)(2,1)S(1)}, bf16[448,3072]{1,0:T(8,128)(2,1)S(1)}) custom-call(s32[1]{0:T(128)S(6)} %copy.12.len_ref, bf16[8,768]{1,0:T(8,128)(2,1)} %q_hbm.1, bf16[8,512]{1,0:T(8,128)(2,1)} %new_hbm.1, bf16[1,2048,512]{2,1,0:T(8,128)(2,1)} %kv_hbm.1, bf16[8,768]{1,0:T(8,128)(2,1)} %res_hbm.1, s32[4,8]{1,0:T(4,128)} %bitcast.11, ...), custom_call_target="tpu_custom_call" | custom-call | flops 50331648 | bytes 2097152 | tf_op jit(solution)/shard_map/attention/pallas_call | solution.py:177
  3.2 4.1 %collective-permute-start = (bf16[8,1024]{1,0:T(8,128)(2,1)S(1)}, bf16[8,1024]{1,0:T(8,128)(2,1)S(1)}, u32[]{:S(2)}, u32[]{:S(2)}) collective-permute-start(bf16[8,1024]{1,0:T(8,128)(2,1)S(1)} %get-tuple-element.13._.refs_3_), channel_id=1, source_target_pairs={{0,2},{1,3},{2,0},{3,1},{4,6},{5,7},{6,4},{7,5},{8,10},{9,11},{10,... | collective-permute-start | bytes 49160 | tf_op jit(solution)/shard_map/ppermute | solution.py:334
  7.4 1.3 %collective-permute-start.1 = (bf16[8,1024]{1,0:T(8,128)(2,1)S(1)}, bf16[8,1024]{1,0:T(8,128)(2,1)S(1)}, u32[]{:S(2)}, u32[]{:S(2)}) collective-permute-start(bf16[8,1024]{1,0:T(8,128)(2,1)S(1)} %get-tuple-element.13._.refs_3_), channel_id=1, source_target_pairs={{0,3},{1,2},{2,1},{3,0},{4,7},{5,6},{6,5},{7,4},{8,11},{9,10},{10,... | collective-permute-start | bytes 49160 | tf_op jit(solution)/shard_map/ppermute | solution.py:334
  8.7 0.2 collective-permute-start.2
  8.9 0.1 pad_add_fusion.place_ref
  9.0 3.2 %load.3 = (bf16[1280,3072]{1,0:T(8,128)(2,1)S(1)}, f32[8,128]{1,0:T(8,128)S(1)}) custom-call(bf16[8,1024]{1,0:T(8,128)(2,1)S(1)} %get-tuple-element.13._.refs_3_, bf16[1,1728,3072]{2,1,0:T(8,128)(2,1)} %source.3), custom_call_target="tpu_custom_call" | custom-call | bytes 15728640 | tf_op jit(solution)/shard_map/load/pallas_call | solution.py:210
  12.3 0.6 %collective-permute-done.1.refs_1_ = bf16[8,1024]{1,0:T(8,128)(2,1)S(1)} collective-permute-done((bf16[8,1024]{1,0:T(8,128)(2,1)S(1)}, bf16[8,1024]{1,0:T(8,128)(2,1)S(1)}, u32[]{:S(2)}, u32[]{:S(2)}) %collective-permute-start.1) | collective-permute-done | bytes 16416 | tf_op jit(solution)/shard_map/ppermute | solution.py:334
  12.9 0.9 %norm.1._.refs_3_ = bf16[8,3200]{1,0:T(8,128)(2,1)S(1)} custom-call(s32[2]{0:T(128)S(1)} %pad_add_fusion.place_ref, f32[8,128]{1,0:T(8,128)S(1)} %get-tuple-element.14._, bf16[8,1024]{1,0:T(8,128)(2,1)S(1)} %collective-permute-done.refs_0_, bf16[8,1024]{1,0:T(8,128)(2,1)S(1)} %collective-permute-done.1.refs_1_, ...), custom_call_target="tpu_custom_call" | custom-call | tf_op jit(solution)/shard_map/norm/pallas_call | solution.py:255
  13.8 1.5 %collective-permute-start.3 = (bf16[8,3200]{1,0:T(8,128)(2,1)S(1)}, bf16[8,3200]{1,0:T(8,128)(2,1)S(1)}, u32[]{:S(2)}, u32[]{:S(2)}) collective-permute-start(bf16[8,3200]{1,0:T(8,128)(2,1)S(1)} %norm.1._.refs_3_), channel_id=1, source_target_pairs={{0,8},{4,12},{8,0},{12,4},{1,9},{5,13},{9,1},{13,5},{2,10},{6,14},... | collective-permute-start | bytes 153608 | tf_op jit(solution)/shard_map/ppermute | solution.py:334
  15.3 1.4 %collective-permute-start.4 = (bf16[8,3200]{1,0:T(8,128)(2,1)S(1)}, bf16[8,3200]{1,0:T(8,128)(2,1)S(1)}, u32[]{:S(2)}, u32[]{:S(2)}) collective-permute-start(bf16[8,3200]{1,0:T(8,128)(2,1)S(1)} %norm.1._.refs_3_), channel_id=1, source_target_pairs={{0,12},{4,8},{8,4},{12,0},{1,13},{5,9},{9,5},{13,1},{2,14},{6,10},... | collective-permute-start | bytes 153608 | tf_op jit(solution)/shard_map/ppermute | solution.py:334
  16.8 0.5 %collective-permute-start.5 = (bf16[8,3200]{1,0:T(8,128)(2,1)S(1)}, bf16[8,3200]{1,0:T(8,128)(2,1)S(1)}, u32[]{:S(2)}, u32[]{:S(2)}) collective-permute-start(bf16[8,3200]{1,0:T(8,128)(2,1)S(1)} %norm.1._.refs_3_), channel_id=1, source_target_pairs={{0,4},{4,0},{8,12},{12,8},{1,5},{5,1},{9,13},{13,9},{2,6},{6,2},{1... | collective-permute-start | bytes 153608 | tf_op jit(solution)/shard_map/ppermute | solution.py:334
  17.3 3.6 %load.4 = (bf16[1472,3072]{1,0:T(8,128)(2,1)S(1)}, f32[8,128]{1,0:T(8,128)S(1)}) custom-call(bf16[8,3200]{1,0:T(8,128)(2,1)S(1)} %norm.1._.refs_3_, bf16[1,1728,3072]{2,1,0:T(8,128)(2,1)} %source.5), custom_call_target="tpu_custom_call" | custom-call | bytes 18087936 | tf_op jit(solution)/shard_map/load/pallas_call | solution.py:210
  21.0 0.1 collective-permute-start.6
  21.0 0.0 slice-start
  21.1 1.6 %load.5 = (bf16[256,3072]{1,0:T(8,128)(2,1)S(1)}, f32[8,128]{1,0:T(8,128)S(1)}) custom-call(bf16[32,3200]{1,0:T(8,128)(2,1)S(1)} %stack.13._.near, bf16[1,1728,3072]{2,1,0:T(8,128)(2,1)} %source.5), custom_call_target="tpu_custom_call" | custom-call | bytes 3145728 | tf_op jit(solution)/shard_map/load/pallas_call | solution.py:210
  22.6 0.0 slice-start.1
  22.7 6.3 %hidden.1 = bf16[64,1728]{1,0:T(8,128)(2,1)S(1)} custom-call(s32[2]{0:T(128)S(1)} %pad_add_fusion.place_ref, bf16[32,3200]{1,0:T(8,128)(2,1)S(1)} %stack.13._.near, bf16[32,3200]{1,0:T(8,128)(2,1)S(1)} %collective-permute-done.6.far, bf16[1280,3072]{1,0:T(8,128)(2,1)S(1)} %get-tuple-element.16.gate_a, bf16[448,3072]{1,0:T(8,128)(2,1)S(1)} %get-tuple-element.17.gate_b, ...), custom_call_target="tpu_custom_call" | custom-call | flops 1358954496 | bytes 21233664 | tf_op jit(solution)/shard_map/hidden/pallas_call | solution.py:319
  29.0 2.0 %fusion.2 = bf16[64,3072]{1,0:T(8,128)(2,1)S(1)} fusion(bf16[64,1728]{1,0:T(8,128)(2,1)S(1)} %hidden.1, bf16[1,1728,3072]{2,1,0:T(8,128)(2,1)S(1)} %bitcast.10), kind=kOutput, calls=%fused_computation.2 | convolution fusion | flops 679673856 | bytes 11231232 | tf_op jit(solution)/shard_map/dot_general | solution.py:376
  31.0 0.6 %collective-permute-start.7 = (bf16[32,3072]{1,0:T(8,128)(2,1)S(1)}, bf16[32,3072]{1,0:T(8,128)(2,1)S(1)}, u32[]{:S(2)}, u32[]{:S(2)}) collective-permute-start(bf16[32,3072]{1,0:T(8,128)(2,1)S(1)} %slice.33), channel_id=1, source_target_pairs={{0,16},{16,0},{1,17},{17,1},{2,18},{18,2},{3,19},{19,3},{4,20},{20... | collective-permute-start | bytes 589832 | tf_op jit(solution)/shard_map/ppermute | solution.py:334
  31.6 1.1 %collective-permute-done.7 = bf16[32,3072]{1,0:T(8,128)(2,1)S(1)} collective-permute-done((bf16[32,3072]{1,0:T(8,128)(2,1)S(1)}, bf16[32,3072]{1,0:T(8,128)(2,1)S(1)}, u32[]{:S(2)}, u32[]{:S(2)}) %collective-permute-start.7) | collective-permute-done | bytes 196640 | tf_op jit(solution)/shard_map/ppermute | solution.py:334
  32.6 0.1 add_convert_fusion
  32.7 2.5 %collective-permute-start.10 = (bf16[8,3072]{1,0:T(8,128)(2,1)S(1)}, bf16[8,3072]{1,0:T(8,128)(2,1)S(1)}, u32[]{:S(2)}, u32[]{:S(2)}) collective-permute-start(bf16[8,3072]{1,0:T(8,128)(2,1)S(1)} %get-tuple-element.22), channel_id=1, source_target_pairs={{0,12},{4,8},{8,4},{12,0},{1,13},{5,9},{9,5},{13,1},{2,14},{6,10},... | collective-permute-start | bytes 147464 | tf_op jit(solution)/shard_map/ppermute | solution.py:334
  35.2 0.5 %collective-permute-start.8 = (bf16[8,3072]{1,0:T(8,128)(2,1)S(1)}, bf16[8,3072]{1,0:T(8,128)(2,1)S(1)}, u32[]{:S(2)}, u32[]{:S(2)}) collective-permute-start(bf16[8,3072]{1,0:T(8,128)(2,1)S(1)} %get-tuple-element.21), channel_id=1, source_target_pairs={{0,8},{4,12},{8,0},{12,4},{1,9},{5,13},{9,1},{13,5},{2,10},{6,14},... | collective-permute-start | bytes 147464 | tf_op jit(solution)/shard_map/ppermute | solution.py:334
  35.7 0.5 %collective-permute-start.9 = (bf16[8,3072]{1,0:T(8,128)(2,1)S(1)}, bf16[8,3072]{1,0:T(8,128)(2,1)S(1)}, u32[]{:S(2)}, u32[]{:S(2)}) collective-permute-start(bf16[8,3072]{1,0:T(8,128)(2,1)S(1)} %get-tuple-element.23), channel_id=1, source_target_pairs={{0,4},{4,0},{8,12},{12,8},{1,5},{5,1},{9,13},{13,9},{2,6},{6,2},{1... | collective-permute-start | bytes 147464 | tf_op jit(solution)/shard_map/ppermute | solution.py:334
  36.3 1.5 %collective-permute-done.10 = bf16[8,3072]{1,0:T(8,128)(2,1)S(1)} collective-permute-done((bf16[8,3072]{1,0:T(8,128)(2,1)S(1)}, bf16[8,3072]{1,0:T(8,128)(2,1)S(1)}, u32[]{:S(2)}, u32[]{:S(2)}) %collective-permute-start.10) | collective-permute-done | bytes 49184 | tf_op jit(solution)/shard_map/ppermute | solution.py:334
  37.8 1.5 %collective-permute-done.8 = bf16[8,3072]{1,0:T(8,128)(2,1)S(1)} collective-permute-done((bf16[8,3072]{1,0:T(8,128)(2,1)S(1)}, bf16[8,3072]{1,0:T(8,128)(2,1)S(1)}, u32[]{:S(2)}, u32[]{:S(2)}) %collective-permute-start.8) | collective-permute-done | bytes 49184 | tf_op jit(solution)/shard_map/ppermute | solution.py:334
  39.3 0.5 %collective-permute-done.9 = bf16[8,3072]{1,0:T(8,128)(2,1)S(1)} collective-permute-done((bf16[8,3072]{1,0:T(8,128)(2,1)S(1)}, bf16[8,3072]{1,0:T(8,128)(2,1)S(1)}, u32[]{:S(2)}, u32[]{:S(2)}) %collective-permute-start.9) | collective-permute-done | bytes 49184 | tf_op jit(solution)/shard_map/ppermute | solution.py:334
  39.9 2.3 %collective-permute-start.11 = (bf16[8,768]{1,0:T(8,128)(2,1)S(1)}, bf16[8,768]{1,0:T(8,128)(2,1)S(1)}, u32[]{:S(2)}, u32[]{:S(2)}) collective-permute-start(bf16[8,768]{1,0:T(8,128)(2,1)S(1)} %get-tuple-element.24), channel_id=1, source_target_pairs={{0,2},{1,3},{2,0},{3,1},{4,6},{5,7},{6,4},{7,5},{8,10},{9,11},{10,... | collective-permute-start | bytes 36872 | tf_op jit(solution)/shard_map/ppermute | solution.py:334
  42.2 1.3 %collective-permute-start.12 = (bf16[8,768]{1,0:T(8,128)(2,1)S(1)}, bf16[8,768]{1,0:T(8,128)(2,1)S(1)}, u32[]{:S(2)}, u32[]{:S(2)}) collective-permute-start(bf16[8,768]{1,0:T(8,128)(2,1)S(1)} %get-tuple-element.26), channel_id=1, source_target_pairs={{0,3},{1,2},{2,1},{3,0},{4,7},{5,6},{6,5},{7,4},{8,11},{9,10},{10,... | collective-permute-start | bytes 36872 | tf_op jit(solution)/shard_map/ppermute | solution.py:334
  43.5 1.0 %collective-permute-done.11 = bf16[8,768]{1,0:T(8,128)(2,1)S(1)} collective-permute-done((bf16[8,768]{1,0:T(8,128)(2,1)S(1)}, bf16[8,768]{1,0:T(8,128)(2,1)S(1)}, u32[]{:S(2)}, u32[]{:S(2)}) %collective-permute-start.11) | collective-permute-done | bytes 12320 | tf_op jit(solution)/shard_map/ppermute | solution.py:334
  44.5 3.1 %collective-permute-done.12 = bf16[8,768]{1,0:T(8,128)(2,1)S(1)} collective-permute-done((bf16[8,768]{1,0:T(8,128)(2,1)S(1)}, bf16[8,768]{1,0:T(8,128)(2,1)S(1)}, u32[]{:S(2)}, u32[]{:S(2)}) %collective-permute-start.12) | collective-permute-done | bytes 12320 | tf_op jit(solution)/shard_map/ppermute | solution.py:334
  47.7 0.6 %add_convert_fusion.2 = bf16[8,768]{1,0:T(8,128)(2,1)} fusion(bf16[8,768]{1,0:T(8,128)(2,1)S(1)} %collective-permute-done.13, bf16[8,768]{1,0:T(8,128)(2,1)S(1)} %collective-permute-done.12, bf16[8,768]{1,0:T(8,128)(2,1)S(1)} %collective-permute-done.11, bf16[8,1024]{1,0:T(8,128)(2,1)S(1)} %get-tuple-element.13._.refs_3_, ...), kind=kLoop, calls=%fused_computation.5 | loop fusion | flops 61440 | bytes 73732 | tf_op jit(solution)/shard_map/convert_element_type | solution.py:384
  (18 shorter events, 0.1 us)
Async XLA Ops:
  3.2 9.0 %collective-permute-start = (bf16[8,1024]{1,0:T(8,128)(2,1)S(1)}, bf16[8,1024]{1,0:T(8,128)(2,1)S(1)}, u32[]{:S(2)}, u32[]{:S(2)}) collective-permute-start(bf16[8,1024]{1,0:T(8,128)(2,1)S(1)} %get-tuple-element.13._.refs_3_), channel_id=1, source_target_pairs={{0,2},{1,3},{2,0},{3,1},{4,6},{5,7},{6,4},{7,5},{8,10},{9,11},{10,... | collective-permute-start | bytes 49160 | tf_op jit(solution)/shard_map/ppermute | solution.py:334
  7.4 5.5 %collective-permute-start.1 = (bf16[8,1024]{1,0:T(8,128)(2,1)S(1)}, bf16[8,1024]{1,0:T(8,128)(2,1)S(1)}, u32[]{:S(2)}, u32[]{:S(2)}) collective-permute-start(bf16[8,1024]{1,0:T(8,128)(2,1)S(1)} %get-tuple-element.13._.refs_3_), channel_id=1, source_target_pairs={{0,3},{1,2},{2,1},{3,0},{4,7},{5,6},{6,5},{7,4},{8,11},{9,10},{10,... | collective-permute-start | bytes 49160 | tf_op jit(solution)/shard_map/ppermute | solution.py:334
  8.7 4.2 %collective-permute-start.2 = (bf16[8,1024]{1,0:T(8,128)(2,1)S(1)}, bf16[8,1024]{1,0:T(8,128)(2,1)S(1)}, u32[]{:S(2)}, u32[]{:S(2)}) collective-permute-start(bf16[8,1024]{1,0:T(8,128)(2,1)S(1)} %get-tuple-element.13._.refs_3_), channel_id=1, source_target_pairs={{0,1},{1,0},{2,3},{3,2},{4,5},{5,4},{6,7},{7,6},{8,9},{9,8},{10,11... | collective-permute-start | bytes 49160 | tf_op jit(solution)/shard_map/ppermute | solution.py:334
  13.8 7.1 %collective-permute-start.3 = (bf16[8,3200]{1,0:T(8,128)(2,1)S(1)}, bf16[8,3200]{1,0:T(8,128)(2,1)S(1)}, u32[]{:S(2)}, u32[]{:S(2)}) collective-permute-start(bf16[8,3200]{1,0:T(8,128)(2,1)S(1)} %norm.1._.refs_3_), channel_id=1, source_target_pairs={{0,8},{4,12},{8,0},{12,4},{1,9},{5,13},{9,1},{13,5},{2,10},{6,14},... | collective-permute-start | bytes 153608 | tf_op jit(solution)/shard_map/ppermute | solution.py:334
  15.3 5.6 %collective-permute-start.4 = (bf16[8,3200]{1,0:T(8,128)(2,1)S(1)}, bf16[8,3200]{1,0:T(8,128)(2,1)S(1)}, u32[]{:S(2)}, u32[]{:S(2)}) collective-permute-start(bf16[8,3200]{1,0:T(8,128)(2,1)S(1)} %norm.1._.refs_3_), channel_id=1, source_target_pairs={{0,12},{4,8},{8,4},{12,0},{1,13},{5,9},{9,5},{13,1},{2,14},{6,10},... | collective-permute-start | bytes 153608 | tf_op jit(solution)/shard_map/ppermute | solution.py:334
  16.8 4.1 %collective-permute-start.5 = (bf16[8,3200]{1,0:T(8,128)(2,1)S(1)}, bf16[8,3200]{1,0:T(8,128)(2,1)S(1)}, u32[]{:S(2)}, u32[]{:S(2)}) collective-permute-start(bf16[8,3200]{1,0:T(8,128)(2,1)S(1)} %norm.1._.refs_3_), channel_id=1, source_target_pairs={{0,4},{4,0},{8,12},{12,8},{1,5},{5,1},{9,13},{13,9},{2,6},{6,2},{1... | collective-permute-start | bytes 153608 | tf_op jit(solution)/shard_map/ppermute | solution.py:334
  21.0 1.7 %collective-permute-start.6 = (bf16[32,3200]{1,0:T(8,128)(2,1)S(1)}, bf16[32,3200]{1,0:T(8,128)(2,1)S(1)}, u32[]{:S(2)}, u32[]{:S(2)}) collective-permute-start(bf16[32,3200]{1,0:T(8,128)(2,1)S(1)} %stack.13._.near), channel_id=1, source_target_pairs={{0,16},{16,0},{1,17},{17,1},{2,18},{18,2},{3,19},{19,3},{4,20},{20... | collective-permute-start | bytes 614408 | tf_op jit(solution)/shard_map/ppermute | solution.py:334
  21.0 7.9 %slice-start = ((s8[10616832]{0:T(1024)(128)(4,1)}), s8[4194304]{0:T(1024)(128)(4,1)S(1)}, s32[]{:S(2)}) async-start(s8[10616832]{0:T(1024)(128)(4,1)} %bitcast.9), calls=%async_computation | async-start | bytes 8388608
  22.6 6.3 %slice-start.1 = ((s8[10616832]{0:T(1024)(128)(4,1)}), s8[4194304]{0:T(1024)(128)(4,1)S(1)}, s32[]{:S(2)}) async-start(s8[10616832]{0:T(1024)(128)(4,1)} %bitcast.9), calls=%async_computation.1 | async-start | bytes 8388608
  22.7 6.3 %slice-start.2 = ((s8[10616832]{0:T(1024)(128)(4,1)}), s8[2228224]{0:T(1024)(128)(4,1)S(1)}, s32[]{:S(2)}) async-start(s8[10616832]{0:T(1024)(128)(4,1)} %bitcast.9), calls=%async_computation.2 | async-start | bytes 4456448
  31.0 1.6 %collective-permute-start.7 = (bf16[32,3072]{1,0:T(8,128)(2,1)S(1)}, bf16[32,3072]{1,0:T(8,128)(2,1)S(1)}, u32[]{:S(2)}, u32[]{:S(2)}) collective-permute-start(bf16[32,3072]{1,0:T(8,128)(2,1)S(1)} %slice.33), channel_id=1, source_target_pairs={{0,16},{16,0},{1,17},{17,1},{2,18},{18,2},{3,19},{19,3},{4,20},{20... | collective-permute-start | bytes 589832 | tf_op jit(solution)/shard_map/ppermute | solution.py:334
  32.7 5.1 %collective-permute-start.10 = (bf16[8,3072]{1,0:T(8,128)(2,1)S(1)}, bf16[8,3072]{1,0:T(8,128)(2,1)S(1)}, u32[]{:S(2)}, u32[]{:S(2)}) collective-permute-start(bf16[8,3072]{1,0:T(8,128)(2,1)S(1)} %get-tuple-element.22), channel_id=1, source_target_pairs={{0,12},{4,8},{8,4},{12,0},{1,13},{5,9},{9,5},{13,1},{2,14},{6,10},... | collective-permute-start | bytes 147464 | tf_op jit(solution)/shard_map/ppermute | solution.py:334
  35.2 4.1 %collective-permute-start.8 = (bf16[8,3072]{1,0:T(8,128)(2,1)S(1)}, bf16[8,3072]{1,0:T(8,128)(2,1)S(1)}, u32[]{:S(2)}, u32[]{:S(2)}) collective-permute-start(bf16[8,3072]{1,0:T(8,128)(2,1)S(1)} %get-tuple-element.21), channel_id=1, source_target_pairs={{0,8},{4,12},{8,0},{12,4},{1,9},{5,13},{9,1},{13,5},{2,10},{6,14},... | collective-permute-start | bytes 147464 | tf_op jit(solution)/shard_map/ppermute | solution.py:334
  35.7 4.1 %collective-permute-start.9 = (bf16[8,3072]{1,0:T(8,128)(2,1)S(1)}, bf16[8,3072]{1,0:T(8,128)(2,1)S(1)}, u32[]{:S(2)}, u32[]{:S(2)}) collective-permute-start(bf16[8,3072]{1,0:T(8,128)(2,1)S(1)} %get-tuple-element.23), channel_id=1, source_target_pairs={{0,4},{4,0},{8,12},{12,8},{1,5},{5,1},{9,13},{13,9},{2,6},{6,2},{1... | collective-permute-start | bytes 147464 | tf_op jit(solution)/shard_map/ppermute | solution.py:334
  39.9 4.7 %collective-permute-start.11 = (bf16[8,768]{1,0:T(8,128)(2,1)S(1)}, bf16[8,768]{1,0:T(8,128)(2,1)S(1)}, u32[]{:S(2)}, u32[]{:S(2)}) collective-permute-start(bf16[8,768]{1,0:T(8,128)(2,1)S(1)} %get-tuple-element.24), channel_id=1, source_target_pairs={{0,2},{1,3},{2,0},{3,1},{4,6},{5,7},{6,4},{7,5},{8,10},{9,11},{10,... | collective-permute-start | bytes 36872 | tf_op jit(solution)/shard_map/ppermute | solution.py:334
  42.2 5.5 %collective-permute-start.12 = (bf16[8,768]{1,0:T(8,128)(2,1)S(1)}, bf16[8,768]{1,0:T(8,128)(2,1)S(1)}, u32[]{:S(2)}, u32[]{:S(2)}) collective-permute-start(bf16[8,768]{1,0:T(8,128)(2,1)S(1)} %get-tuple-element.26), channel_id=1, source_target_pairs={{0,3},{1,2},{2,1},{3,0},{4,7},{5,6},{6,5},{7,4},{8,11},{9,10},{10,... | collective-permute-start | bytes 36872 | tf_op jit(solution)/shard_map/ppermute | solution.py:334
  43.5 4.1 %collective-permute-start.13 = (bf16[8,768]{1,0:T(8,128)(2,1)S(1)}, bf16[8,768]{1,0:T(8,128)(2,1)S(1)}, u32[]{:S(2)}, u32[]{:S(2)}) collective-permute-start(bf16[8,768]{1,0:T(8,128)(2,1)S(1)} %get-tuple-element.25), channel_id=1, source_target_pairs={{0,1},{1,0},{2,3},{3,2},{4,5},{5,4},{6,7},{7,6},{8,9},{9,8},{10,11... | collective-permute-start | bytes 36872 | tf_op jit(solution)/shard_map/ppermute | solution.py:334

commit v10 on v9

--- a/solution.py
+++ b/solution.py
@@ -24,13 +24,8 @@
     return high, middle, rest - middle
 
 
-def cut_units(units):
-    if units <= 7 * UNITS // 2:
-        return units // 32 * 16, units // 32 * 16
-    return units * 3 // 4 // UNITS * UNITS, units - UNITS
-
-
-def unit_parts(units, cut):
+def unit_parts(units):
+    cut = units * 3 // 4 // UNITS * UNITS or units // 32 * 16
     return pl.ds(0, cut), pl.ds(cut, units - cut)
 
 
@@ -262,7 +257,7 @@
     )(place, token, *blocks)
 
 
-def stack_kernel(_, *refs):
+def stack_kernel(*refs):
     masks = send_order(len(refs) - 1) + [0]
     pieces, out_ref = [refs[masks.index(m)] for m in range(len(masks))], refs[-1]
     rows = 2 * pieces[0].shape[0]
@@ -271,20 +266,20 @@
         out_ref[i // 2 * rows : (i // 2 + 1) * rows] = jnp.concatenate(pair, axis=0).astype(out_ref.dtype)
 
 
-def stack_rows(token, pieces):
+def stack_rows(pieces):
     rows, wide = pieces[0].shape
     vmem = pl.BlockSpec(memory_space=pltpu.VMEM)
     return pl.pallas_call(
         stack_kernel,
         out_shape=jax.ShapeDtypeStruct((rows * len(pieces), wide), pieces[0].dtype),
-        in_specs=[vmem] * (1 + len(pieces)),
+        in_specs=[vmem] * len(pieces),
         out_specs=vmem,
         compiler_params=pltpu.CompilerParams(vmem_limit_bytes=4 * MIB),
         name="stack",
-    )(token, *pieces)
-
-
-def hidden_kernel(place_ref, near, far, gate_a, gate_b, up_a, up_b, _, hidden, x, *, experts):
+    )(*pieces)
+
+
+def hidden_kernel(place_ref, near, far, gate_a, gate_b, up, hidden, x, *, experts):
     half = near.shape[0]
     model = gate_a.shape[1]
     x[:half] = near[:, :model]
@@ -294,24 +289,21 @@
     expert = place_ref[1]
     mine = (lane == expert) | (lane == expert + experts)
     share = jnp.sum(jnp.where(mine, side, 0.0), axis=1, keepdims=True)
-    units = gate_a.shape[0] + gate_b.shape[0]
-    cuts = sorted({0, gate_a.shape[0], up_a.shape[0], units})
-
-    def rows(first, second, start, stop):
-        cut = first.shape[0]
-        return first[start:stop] if stop <= cut else second[start - cut : stop - cut]
-
-    for low, high in zip(cuts, cuts[1:]):
-        for start in range(low, high, UNITS):
-            stop = min(start + UNITS, high)
-            gate, up = rows(gate_a, gate_b, start, stop), rows(up_a, up_b, start, stop)
-            a = lax.dot_general(x[...], gate, BY_ROW, preferred_element_type=jnp.float32)
-            b = lax.dot_general(up, x[...], BY_ROW, preferred_element_type=jnp.float32)
+    first = 0
+    for gate in (gate_a, gate_b):
+        units = gate.shape[0]
+        for start in range(0, units, UNITS):
+            stop = min(start + UNITS, units)
+            a = lax.dot_general(x[...], gate[start:stop], BY_ROW, preferred_element_type=jnp.float32)
+            b = lax.dot_general(
+                up[first + start : first + stop], x[...], BY_ROW, preferred_element_type=jnp.float32
+            )
             out = a / (1.0 + jnp.exp(-a)) * share * b.T
-            hidden[:, start:stop] = out.astype(hidden.dtype)
-
-
-def run_hidden(place, near, far, weights, token, experts):
+            hidden[:, first + start : first + stop] = out.astype(hidden.dtype)
+        first += units
+
+
+def run_hidden(place, near, far, weights, experts):
     units = weights[0].shape[0] + weights[1].shape[0]
     model = weights[0].shape[1]
     rows = 2 * near.shape[0]
@@ -319,15 +311,15 @@
     return pl.pallas_call(
         functools.partial(hidden_kernel, experts=experts),
         out_shape=jax.ShapeDtypeStruct((rows, units), jnp.bfloat16),
-        in_specs=[pl.BlockSpec(memory_space=pltpu.SMEM)] + [vmem] * 7,
+        in_specs=[pl.BlockSpec(memory_space=pltpu.SMEM)] + [vmem] * 5,
         out_specs=vmem,
         scratch_shapes=[pltpu.VMEM((rows, model), jnp.bfloat16)],
-        compiler_params=pltpu.CompilerParams(vmem_limit_bytes=(6 if rows <= 64 else 24) * MIB),
+        compiler_params=pltpu.CompilerParams(vmem_limit_bytes=(18 if rows <= 64 else 24) * MIB),
         cost_estimate=pl.CostEstimate(
             flops=4 * rows * units * model, bytes_accessed=4 * units * model, transcendentals=rows * units
         ),
         name="hidden",
-    )(place, near, far, *weights, token)
+    )(place, near, far, *weights)
 
 
 def send(x, axis, mask):
@@ -357,8 +349,7 @@
     place = lax.axis_index("tensor")
     where = jnp.stack([place, lax.axis_index("section") * tensors + place]).astype(jnp.int32)
 
-    units = gate_w.shape[1]
-    gate_parts, up_parts = [unit_parts(units, cut) for cut in cut_units(units)]
+    gate_parts = unit_parts(gate_w.shape[1])
 
     fresh, gate_b = attend(
         cache_len, queries, new_kv, kv_cache, residual, routes, router, norm_gain, gate_w, gate_parts[1]
@@ -367,12 +358,10 @@
     gate_a, token = load(fresh, gate_w, gate_parts[0])
     rows = norm_rows(where, token, blocks, experts)
     ranks = exchange([rows] * groups, "group") + [rows]
-    up_a, token = load(rows, up_w, up_parts[0])
-    near = stack_rows(token, ranks)
+    near = stack_rows(ranks)
     far = send(near, "section", 1)
-    up_b, token = load(near, up_w, up_parts[1])
-
-    hidden = run_hidden(where, near, far, (gate_a, gate_b, up_a, up_b), token, experts)
+
+    hidden = run_hidden(where, near, far, (gate_a, gate_b, up_w[0]), experts)
     out = jnp.dot(hidden, down_w[0], preferred_element_type=jnp.float32).astype(jnp.bfloat16)
     half = out.shape[0] // 2
     both = add(out[:half], send(out[half:], "section", 1)).astype(jnp.bfloat16)

time: 48.5 us -> 51.6 us (1.064)
  Pallas kernels: 18.2 us -> 13.1 us
  waiting for transfers between devices: 9.4 us -> 14.1 us
  local copies, waits for them, and re-layouts: 0.06 us -> 4.06 us
    pallas_call x3 -> x1, Pallas kernels: 8.39 us -> 3.24 us  [load(): pl.pallas_call(functools.partial(load_kernel, part=part), out_shape=(pltp...]
    ppermute x14, waiting for transfers between devices: 9.4 us -> 14.1 us  [send(): lax.ppermute(x, axis, [(i, i ^ mask) for i in range(lax.axis_size(axis))])]
    unnamed x6 -> x4, local copies, waits for them, and re-layouts: 0.02 us -> 4.02 us
  transfers between devices with their start and end apart: 14 -> 14, of which waited for: 7 -> 11; matrix products, arithmetic and copies ran while one was open for 0% -> 0% of each run, Pallas kernels for 17% -> 6%
where the time goes in v10:
time: 51.6 us; the launch traced here: 51.4 us
  starting transfers between devices  16.6 us (32%)
  waiting for transfers between devices  14.1 us (27%)
  Pallas kernels  13.1 us (25%)
  local copies, waits for them, and re-layouts  4.06 us (8%)
  matrix products  1.97 us (4%)
  other arithmetic  0.77 us (1%)
  between operations  0.75 us (1%)
    ppermute x14, starting transfers between devices, send(): lax.ppermute(x, axis, [(i, i ^ mask) for i in range(lax.axis_size(axis))])  16.6 us
    ppermute x14, waiting for transfers between devices, send(): lax.ppermute(x, axis, [(i, i ^ mask) for i in range(lax.axis_size(axis))])  14.1 us
    pallas_call x1, Pallas kernels, run_hidden(): pl.pallas_call(functools.partial(hidden_kernel, experts=experts), out_sha...  6.29 us
    unnamed x4, local copies, waits for them, and re-layouts  4.02 us
    pallas_call x1, Pallas kernels, load(): pl.pallas_call(functools.partial(load_kernel, part=part), out_shape=(pltp...  3.24 us
    pallas_call x1, Pallas kernels, attend(): pl.pallas_call(functools.partial(attention_kernel, chunks=chunks, rest=re...  2.59 us
    dot_general x1, matrix products, per_device(): jnp.dot(hidden, down_w[0], preferred_element_type=jnp.float32)  1.97 us
  transfers between devices with their start and end apart: 14, of which 11 were waited for; matrix products, arithmetic and copies ran while one was open for 0% of the time, Pallas kernels for 6%

profile of v10, /device:TPU:0, one launch (start us, length us, event | category | flops | bytes accessed | tf_op | source)
XLA Modules:
  0.0 51.4 jit_solution(16428565951314721288)
XLA Ops:
  0.7 2.6 %attention.1 = (bf16[8,1024]{1,0:T(8,128)(2,1)S(1)}, bf16[448,3072]{1,0:T(8,128)(2,1)S(1)}) custom-call(s32[1]{0:T(128)S(6)} %copy.12.len_ref, bf16[8,768]{1,0:T(8,128)(2,1)} %q_hbm.1, bf16[8,512]{1,0:T(8,128)(2,1)} %new_hbm.1, bf16[1,2048,512]{2,1,0:T(8,128)(2,1)} %kv_hbm.1, bf16[8,768]{1,0:T(8,128)(2,1)} %res_hbm.1, s32[4,8]{1,0:T(4,128)} %bitcast.11, ...), custom_call_target="tpu_custom_call" | custom-call | flops 50331648 | bytes 2097152 | tf_op jit(solution)/shard_map/attention/pallas_call | solution.py:172
  3.2 4.1 %collective-permute-start = (bf16[8,1024]{1,0:T(8,128)(2,1)S(1)}, bf16[8,1024]{1,0:T(8,128)(2,1)S(1)}, u32[]{:S(2)}, u32[]{:S(2)}) collective-permute-start(bf16[8,1024]{1,0:T(8,128)(2,1)S(1)} %get-tuple-element.9._.refs_3_), channel_id=1, source_target_pairs={{0,2},{1,3},{2,0},{3,1},{4,6},{5,7},{6,4},{7,5},{8,10},{9,11},{10,... | collective-permute-start | bytes 49160 | tf_op jit(solution)/shard_map/ppermute | solution.py:326
  7.4 1.3 %collective-permute-start.1 = (bf16[8,1024]{1,0:T(8,128)(2,1)S(1)}, bf16[8,1024]{1,0:T(8,128)(2,1)S(1)}, u32[]{:S(2)}, u32[]{:S(2)}) collective-permute-start(bf16[8,1024]{1,0:T(8,128)(2,1)S(1)} %get-tuple-element.9._.refs_3_), channel_id=1, source_target_pairs={{0,3},{1,2},{2,1},{3,0},{4,7},{5,6},{6,5},{7,4},{8,11},{9,10},{10,... | collective-permute-start | bytes 49160 | tf_op jit(solution)/shard_map/ppermute | solution.py:326
  8.7 0.2 collective-permute-start.2
  8.9 0.1 pad_add_fusion.place_ref
  9.0 3.2 %load.1 = (bf16[1280,3072]{1,0:T(8,128)(2,1)S(1)}, f32[8,128]{1,0:T(8,128)S(1)}) custom-call(bf16[8,1024]{1,0:T(8,128)(2,1)S(1)} %get-tuple-element.9._.refs_3_, bf16[1,1728,3072]{2,1,0:T(8,128)(2,1)} %source.1), custom_call_target="tpu_custom_call" | custom-call | bytes 15728640 | tf_op jit(solution)/shard_map/load/pallas_call | solution.py:205
  12.3 0.6 %collective-permute-done.1.refs_1_ = bf16[8,1024]{1,0:T(8,128)(2,1)S(1)} collective-permute-done((bf16[8,1024]{1,0:T(8,128)(2,1)S(1)}, bf16[8,1024]{1,0:T(8,128)(2,1)S(1)}, u32[]{:S(2)}, u32[]{:S(2)}) %collective-permute-start.1) | collective-permute-done | bytes 16416 | tf_op jit(solution)/shard_map/ppermute | solution.py:326
  12.9 0.9 %norm.1.refs_3_ = bf16[8,3200]{1,0:T(8,128)(2,1)S(1)} custom-call(s32[2]{0:T(128)S(1)} %pad_add_fusion.place_ref, f32[8,128]{1,0:T(8,128)S(1)} %get-tuple-element.10._, bf16[8,1024]{1,0:T(8,128)(2,1)S(1)} %collective-permute-done.refs_0_, bf16[8,1024]{1,0:T(8,128)(2,1)S(1)} %collective-permute-done.1.refs_1_, ...), custom_call_target="tpu_custom_call" | custom-call | tf_op jit(solution)/shard_map/norm/pallas_call | solution.py:250
  13.8 1.5 %collective-permute-start.3 = (bf16[8,3200]{1,0:T(8,128)(2,1)S(1)}, bf16[8,3200]{1,0:T(8,128)(2,1)S(1)}, u32[]{:S(2)}, u32[]{:S(2)}) collective-permute-start(bf16[8,3200]{1,0:T(8,128)(2,1)S(1)} %norm.1.refs_3_), channel_id=1, source_target_pairs={{0,8},{4,12},{8,0},{12,4},{1,9},{5,13},{9,1},{13,5},{2,10},{6,14},... | collective-permute-start | bytes 153608 | tf_op jit(solution)/shard_map/ppermute | solution.py:326
  15.3 1.4 %collective-permute-start.4 = (bf16[8,3200]{1,0:T(8,128)(2,1)S(1)}, bf16[8,3200]{1,0:T(8,128)(2,1)S(1)}, u32[]{:S(2)}, u32[]{:S(2)}) collective-permute-start(bf16[8,3200]{1,0:T(8,128)(2,1)S(1)} %norm.1.refs_3_), channel_id=1, source_target_pairs={{0,12},{4,8},{8,4},{12,0},{1,13},{5,9},{9,5},{13,1},{2,14},{6,10},... | collective-permute-start | bytes 153608 | tf_op jit(solution)/shard_map/ppermute | solution.py:326
  16.8 0.5 %collective-permute-start.5 = (bf16[8,3200]{1,0:T(8,128)(2,1)S(1)}, bf16[8,3200]{1,0:T(8,128)(2,1)S(1)}, u32[]{:S(2)}, u32[]{:S(2)}) collective-permute-start(bf16[8,3200]{1,0:T(8,128)(2,1)S(1)} %norm.1.refs_3_), channel_id=1, source_target_pairs={{0,4},{4,0},{8,12},{12,8},{1,5},{5,1},{9,13},{13,9},{2,6},{6,2},{1... | collective-permute-start | bytes 153608 | tf_op jit(solution)/shard_map/ppermute | solution.py:326
  17.3 1.0 %collective-permute-done.3.refs_0_ = bf16[8,3200]{1,0:T(8,128)(2,1)S(1)} collective-permute-done((bf16[8,3200]{1,0:T(8,128)(2,1)S(1)}, bf16[8,3200]{1,0:T(8,128)(2,1)S(1)}, u32[]{:S(2)}, u32[]{:S(2)}) %collective-permute-start.3) | collective-permute-done | bytes 51232 | tf_op jit(solution)/shard_map/ppermute | solution.py:326
  18.3 2.0 %collective-permute-done.4.refs_1_ = bf16[8,3200]{1,0:T(8,128)(2,1)S(1)} collective-permute-done((bf16[8,3200]{1,0:T(8,128)(2,1)S(1)}, bf16[8,3200]{1,0:T(8,128)(2,1)S(1)}, u32[]{:S(2)}, u32[]{:S(2)}) %collective-permute-start.4) | collective-permute-done | bytes 51232 | tf_op jit(solution)/shard_map/ppermute | solution.py:326
  20.4 0.5 %collective-permute-done.5.refs_2_ = bf16[8,3200]{1,0:T(8,128)(2,1)S(1)} collective-permute-done((bf16[8,3200]{1,0:T(8,128)(2,1)S(1)}, bf16[8,3200]{1,0:T(8,128)(2,1)S(1)}, u32[]{:S(2)}, u32[]{:S(2)}) %collective-permute-start.5) | collective-permute-done | bytes 51232 | tf_op jit(solution)/shard_map/ppermute | solution.py:326
  20.9 0.1 collective-permute-start.6
  21.0 1.4 %collective-permute-done.6.far = bf16[32,3200]{1,0:T(8,128)(2,1)S(1)} collective-permute-done((bf16[32,3200]{1,0:T(8,128)(2,1)S(1)}, bf16[32,3200]{1,0:T(8,128)(2,1)S(1)}, u32[]{:S(2)}, u32[]{:S(2)}) %collective-permute-start.6) | collective-permute-done | bytes 204832 | tf_op jit(solution)/shard_map/ppermute | solution.py:326
  22.4 4.0 %copy-done = bf16[1,1728,3072]{2,1,0:T(8,128)(2,1)S(1)} copy-done((bf16[1,1728,3072]{2,1,0:T(8,128)(2,1)S(1)}, bf16[1,1728,3072]{2,1,0:T(8,128)(2,1)}, u32[]{:S(2)}) %copy-start) | copy-done | bytes 10616856
  26.5 6.3 %hidden.1 = bf16[64,1728]{1,0:T(8,128)(2,1)S(1)} custom-call(s32[2]{0:T(128)S(1)} %pad_add_fusion.place_ref, bf16[32,3200]{1,0:T(8,128)(2,1)S(1)} %stack.13.near, bf16[32,3200]{1,0:T(8,128)(2,1)S(1)} %collective-permute-done.6.far, bf16[1280,3072]{1,0:T(8,128)(2,1)S(1)} %get-tuple-element.11.gate_a, bf16[448,3072]{1,0:T(8,128)(2,1)S(1)} %get-tuple-element.12.gate_b, ...), custom_call_target="tpu_custom_call" | custom-call | flops 1358954496 | bytes 21233664 | tf_op jit(solution)/shard_map/hidden/pallas_call | solution.py:311
  32.8 2.0 %fusion.2 = bf16[64,3072]{1,0:T(8,128)(2,1)S(1)} fusion(bf16[64,1728]{1,0:T(8,128)(2,1)S(1)} %hidden.1, bf16[1,1728,3072]{2,1,0:T(8,128)(2,1)S(1)} %copy-done.1), kind=kOutput, calls=%fused_computation.2 | convolution fusion | flops 679673856 | bytes 11231232 | tf_op jit(solution)/shard_map/dot_general | solution.py:365
  34.8 0.2 collective-permute-start.7
  35.0 1.3 %collective-permute-done.7 = bf16[32,3072]{1,0:T(8,128)(2,1)S(1)} collective-permute-done((bf16[32,3072]{1,0:T(8,128)(2,1)S(1)}, bf16[32,3072]{1,0:T(8,128)(2,1)S(1)}, u32[]{:S(2)}, u32[]{:S(2)}) %collective-permute-start.7) | collective-permute-done | bytes 196640 | tf_op jit(solution)/shard_map/ppermute | solution.py:326
  36.3 1.6 %collective-permute-start.10 = (bf16[8,3072]{1,0:T(8,128)(2,1)S(1)}, bf16[8,3072]{1,0:T(8,128)(2,1)S(1)}, u32[]{:S(2)}, u32[]{:S(2)}) collective-permute-start(bf16[8,3072]{1,0:T(8,128)(2,1)S(1)} %get-tuple-element.14), channel_id=1, source_target_pairs={{0,12},{4,8},{8,4},{12,0},{1,13},{5,9},{9,5},{13,1},{2,14},{6,10},... | collective-permute-start | bytes 147464 | tf_op jit(solution)/shard_map/ppermute | solution.py:326
  37.9 0.9 %collective-permute-start.8 = (bf16[8,3072]{1,0:T(8,128)(2,1)S(1)}, bf16[8,3072]{1,0:T(8,128)(2,1)S(1)}, u32[]{:S(2)}, u32[]{:S(2)}) collective-permute-start(bf16[8,3072]{1,0:T(8,128)(2,1)S(1)} %get-tuple-element.13), channel_id=1, source_target_pairs={{0,8},{4,12},{8,0},{12,4},{1,9},{5,13},{9,1},{13,5},{2,10},{6,14},... | collective-permute-start | bytes 147464 | tf_op jit(solution)/shard_map/ppermute | solution.py:326
  38.8 1.1 %collective-permute-start.9 = (bf16[8,3072]{1,0:T(8,128)(2,1)S(1)}, bf16[8,3072]{1,0:T(8,128)(2,1)S(1)}, u32[]{:S(2)}, u32[]{:S(2)}) collective-permute-start(bf16[8,3072]{1,0:T(8,128)(2,1)S(1)} %get-tuple-element.15), channel_id=1, source_target_pairs={{0,4},{4,0},{8,12},{12,8},{1,5},{5,1},{9,13},{13,9},{2,6},{6,2},{1... | collective-permute-start | bytes 147464 | tf_op jit(solution)/shard_map/ppermute | solution.py:326
  39.9 1.6 %collective-permute-done.10 = bf16[8,3072]{1,0:T(8,128)(2,1)S(1)} collective-permute-done((bf16[8,3072]{1,0:T(8,128)(2,1)S(1)}, bf16[8,3072]{1,0:T(8,128)(2,1)S(1)}, u32[]{:S(2)}, u32[]{:S(2)}) %collective-permute-start.10) | collective-permute-done | bytes 49184 | tf_op jit(solution)/shard_map/ppermute | solution.py:326
  41.5 0.7 %collective-permute-done.8 = bf16[8,3072]{1,0:T(8,128)(2,1)S(1)} collective-permute-done((bf16[8,3072]{1,0:T(8,128)(2,1)S(1)}, bf16[8,3072]{1,0:T(8,128)(2,1)S(1)}, u32[]{:S(2)}, u32[]{:S(2)}) %collective-permute-start.8) | collective-permute-done | bytes 49184 | tf_op jit(solution)/shard_map/ppermute | solution.py:326
  42.1 0.8 %collective-permute-done.9 = bf16[8,3072]{1,0:T(8,128)(2,1)S(1)} collective-permute-done((bf16[8,3072]{1,0:T(8,128)(2,1)S(1)}, bf16[8,3072]{1,0:T(8,128)(2,1)S(1)}, u32[]{:S(2)}, u32[]{:S(2)}) %collective-permute-start.9) | collective-permute-done | bytes 49184 | tf_op jit(solution)/shard_map/ppermute | solution.py:326
  43.0 2.3 %collective-permute-start.11 = (bf16[8,768]{1,0:T(8,128)(2,1)S(1)}, bf16[8,768]{1,0:T(8,128)(2,1)S(1)}, u32[]{:S(2)}, u32[]{:S(2)}) collective-permute-start(bf16[8,768]{1,0:T(8,128)(2,1)S(1)} %get-tuple-element.16), channel_id=1, source_target_pairs={{0,2},{1,3},{2,0},{3,1},{4,6},{5,7},{6,4},{7,5},{8,10},{9,11},{10,... | collective-permute-start | bytes 36872 | tf_op jit(solution)/shard_map/ppermute | solution.py:326
  45.2 1.3 %collective-permute-start.12 = (bf16[8,768]{1,0:T(8,128)(2,1)S(1)}, bf16[8,768]{1,0:T(8,128)(2,1)S(1)}, u32[]{:S(2)}, u32[]{:S(2)}) collective-permute-start(bf16[8,768]{1,0:T(8,128)(2,1)S(1)} %get-tuple-element.18), channel_id=1, source_target_pairs={{0,3},{1,2},{2,1},{3,0},{4,7},{5,6},{6,5},{7,4},{8,11},{9,10},{10,... | collective-permute-start | bytes 36872 | tf_op jit(solution)/shard_map/ppermute | solution.py:326
  46.6 1.0 %collective-permute-done.11 = bf16[8,768]{1,0:T(8,128)(2,1)S(1)} collective-permute-done((bf16[8,768]{1,0:T(8,128)(2,1)S(1)}, bf16[8,768]{1,0:T(8,128)(2,1)S(1)}, u32[]{:S(2)}, u32[]{:S(2)}) %collective-permute-start.11) | collective-permute-done | bytes 12320 | tf_op jit(solution)/shard_map/ppermute | solution.py:326
  47.6 3.1 %collective-permute-done.12 = bf16[8,768]{1,0:T(8,128)(2,1)S(1)} collective-permute-done((bf16[8,768]{1,0:T(8,128)(2,1)S(1)}, bf16[8,768]{1,0:T(8,128)(2,1)S(1)}, u32[]{:S(2)}, u32[]{:S(2)}) %collective-permute-start.12) | collective-permute-done | bytes 12320 | tf_op jit(solution)/shard_map/ppermute | solution.py:326
  50.7 0.6 %add_convert_fusion.2 = bf16[8,768]{1,0:T(8,128)(2,1)} fusion(bf16[8,768]{1,0:T(8,128)(2,1)S(1)} %collective-permute-done.13, bf16[8,768]{1,0:T(8,128)(2,1)S(1)} %collective-permute-done.12, bf16[8,768]{1,0:T(8,128)(2,1)S(1)} %collective-permute-done.11, bf16[8,1024]{1,0:T(8,128)(2,1)S(1)} %get-tuple-element.9._.refs_3_, ...), kind=kLoop, calls=%fused_computation.5 | loop fusion | flops 61440 | bytes 73732 | tf_op jit(solution)/shard_map/convert_element_type | solution.py:373
  (13 shorter events, 0.2 us)
Async XLA Ops:
  3.2 9.0 %collective-permute-start = (bf16[8,1024]{1,0:T(8,128)(2,1)S(1)}, bf16[8,1024]{1,0:T(8,128)(2,1)S(1)}, u32[]{:S(2)}, u32[]{:S(2)}) collective-permute-start(bf16[8,1024]{1,0:T(8,128)(2,1)S(1)} %get-tuple-element.9._.refs_3_), channel_id=1, source_target_pairs={{0,2},{1,3},{2,0},{3,1},{4,6},{5,7},{6,4},{7,5},{8,10},{9,11},{10,... | collective-permute-start | bytes 49160 | tf_op jit(solution)/shard_map/ppermute | solution.py:326
  7.4 5.5 %collective-permute-start.1 = (bf16[8,1024]{1,0:T(8,128)(2,1)S(1)}, bf16[8,1024]{1,0:T(8,128)(2,1)S(1)}, u32[]{:S(2)}, u32[]{:S(2)}) collective-permute-start(bf16[8,1024]{1,0:T(8,128)(2,1)S(1)} %get-tuple-element.9._.refs_3_), channel_id=1, source_target_pairs={{0,3},{1,2},{2,1},{3,0},{4,7},{5,6},{6,5},{7,4},{8,11},{9,10},{10,... | collective-permute-start | bytes 49160 | tf_op jit(solution)/shard_map/ppermute | solution.py:326
  8.7 4.2 %collective-permute-start.2 = (bf16[8,1024]{1,0:T(8,128)(2,1)S(1)}, bf16[8,1024]{1,0:T(8,128)(2,1)S(1)}, u32[]{:S(2)}, u32[]{:S(2)}) collective-permute-start(bf16[8,1024]{1,0:T(8,128)(2,1)S(1)} %get-tuple-element.9._.refs_3_), channel_id=1, source_target_pairs={{0,1},{1,0},{2,3},{3,2},{4,5},{5,4},{6,7},{7,6},{8,9},{9,8},{10,11... | collective-permute-start | bytes 49160 | tf_op jit(solution)/shard_map/ppermute | solution.py:326
  13.8 4.5 %collective-permute-start.3 = (bf16[8,3200]{1,0:T(8,128)(2,1)S(1)}, bf16[8,3200]{1,0:T(8,128)(2,1)S(1)}, u32[]{:S(2)}, u32[]{:S(2)}) collective-permute-start(bf16[8,3200]{1,0:T(8,128)(2,1)S(1)} %norm.1.refs_3_), channel_id=1, source_target_pairs={{0,8},{4,12},{8,0},{12,4},{1,9},{5,13},{9,1},{13,5},{2,10},{6,14},... | collective-permute-start | bytes 153608 | tf_op jit(solution)/shard_map/ppermute | solution.py:326
  15.3 5.0 %collective-permute-start.4 = (bf16[8,3200]{1,0:T(8,128)(2,1)S(1)}, bf16[8,3200]{1,0:T(8,128)(2,1)S(1)}, u32[]{:S(2)}, u32[]{:S(2)}) collective-permute-start(bf16[8,3200]{1,0:T(8,128)(2,1)S(1)} %norm.1.refs_3_), channel_id=1, source_target_pairs={{0,12},{4,8},{8,4},{12,0},{1,13},{5,9},{9,5},{13,1},{2,14},{6,10},... | collective-permute-start | bytes 153608 | tf_op jit(solution)/shard_map/ppermute | solution.py:326
  16.8 4.1 %collective-permute-start.5 = (bf16[8,3200]{1,0:T(8,128)(2,1)S(1)}, bf16[8,3200]{1,0:T(8,128)(2,1)S(1)}, u32[]{:S(2)}, u32[]{:S(2)}) collective-permute-start(bf16[8,3200]{1,0:T(8,128)(2,1)S(1)} %norm.1.refs_3_), channel_id=1, source_target_pairs={{0,4},{4,0},{8,12},{12,8},{1,5},{5,1},{9,13},{13,9},{2,6},{6,2},{1... | collective-permute-start | bytes 153608 | tf_op jit(solution)/shard_map/ppermute | solution.py:326
  20.9 1.5 %collective-permute-start.6 = (bf16[32,3200]{1,0:T(8,128)(2,1)S(1)}, bf16[32,3200]{1,0:T(8,128)(2,1)S(1)}, u32[]{:S(2)}, u32[]{:S(2)}) collective-permute-start(bf16[32,3200]{1,0:T(8,128)(2,1)S(1)} %stack.13.near), channel_id=1, source_target_pairs={{0,16},{16,0},{1,17},{17,1},{2,18},{18,2},{3,19},{19,3},{4,20},{20... | collective-permute-start | bytes 614408 | tf_op jit(solution)/shard_map/ppermute | solution.py:326
  22.4 4.0 %copy-start = (bf16[1,1728,3072]{2,1,0:T(8,128)(2,1)S(1)}, bf16[1,1728,3072]{2,1,0:T(8,128)(2,1)}, u32[]{:S(2)}) copy-start(bf16[1,1728,3072]{2,1,0:T(8,128)(2,1)} %param.20) | copy-start | bytes 31850500
  26.4 6.3 %copy-start.1 = (bf16[1,1728,3072]{2,1,0:T(8,128)(2,1)S(1)}, bf16[1,1728,3072]{2,1,0:T(8,128)(2,1)}, u32[]{:S(2)}) copy-start(bf16[1,1728,3072]{2,1,0:T(8,128)(2,1)} %param.21) | copy-start | bytes 31850500
  34.8 1.5 %collective-permute-start.7 = (bf16[32,3072]{1,0:T(8,128)(2,1)S(1)}, bf16[32,3072]{1,0:T(8,128)(2,1)S(1)}, u32[]{:S(2)}, u32[]{:S(2)}) collective-permute-start(bf16[32,3072]{1,0:T(8,128)(2,1)S(1)} %slice.33), channel_id=1, source_target_pairs={{0,16},{16,0},{1,17},{17,1},{2,18},{18,2},{3,19},{19,3},{4,20},{20... | collective-permute-start | bytes 589832 | tf_op jit(solution)/shard_map/ppermute | solution.py:326
  36.3 5.1 %collective-permute-start.10 = (bf16[8,3072]{1,0:T(8,128)(2,1)S(1)}, bf16[8,3072]{1,0:T(8,128)(2,1)S(1)}, u32[]{:S(2)}, u32[]{:S(2)}) collective-permute-start(bf16[8,3072]{1,0:T(8,128)(2,1)S(1)} %get-tuple-element.14), channel_id=1, source_target_pairs={{0,12},{4,8},{8,4},{12,0},{1,13},{5,9},{9,5},{13,1},{2,14},{6,10},... | collective-permute-start | bytes 147464 | tf_op jit(solution)/shard_map/ppermute | solution.py:326
  37.9 4.2 %collective-permute-start.8 = (bf16[8,3072]{1,0:T(8,128)(2,1)S(1)}, bf16[8,3072]{1,0:T(8,128)(2,1)S(1)}, u32[]{:S(2)}, u32[]{:S(2)}) collective-permute-start(bf16[8,3072]{1,0:T(8,128)(2,1)S(1)} %get-tuple-element.13), channel_id=1, source_target_pairs={{0,8},{4,12},{8,0},{12,4},{1,9},{5,13},{9,1},{13,5},{2,10},{6,14},... | collective-permute-start | bytes 147464 | tf_op jit(solution)/shard_map/ppermute | solution.py:326
  38.8 4.1 %collective-permute-start.9 = (bf16[8,3072]{1,0:T(8,128)(2,1)S(1)}, bf16[8,3072]{1,0:T(8,128)(2,1)S(1)}, u32[]{:S(2)}, u32[]{:S(2)}) collective-permute-start(bf16[8,3072]{1,0:T(8,128)(2,1)S(1)} %get-tuple-element.15), channel_id=1, source_target_pairs={{0,4},{4,0},{8,12},{12,8},{1,5},{5,1},{9,13},{13,9},{2,6},{6,2},{1... | collective-permute-start | bytes 147464 | tf_op jit(solution)/shard_map/ppermute | solution.py:326
  43.0 4.7 %collective-permute-start.11 = (bf16[8,768]{1,0:T(8,128)(2,1)S(1)}, bf16[8,768]{1,0:T(8,128)(2,1)S(1)}, u32[]{:S(2)}, u32[]{:S(2)}) collective-permute-start(bf16[8,768]{1,0:T(8,128)(2,1)S(1)} %get-tuple-element.16), channel_id=1, source_target_pairs={{0,2},{1,3},{2,0},{3,1},{4,6},{5,7},{6,4},{7,5},{8,10},{9,11},{10,... | collective-permute-start | bytes 36872 | tf_op jit(solution)/shard_map/ppermute | solution.py:326
  45.2 5.5 %collective-permute-start.12 = (bf16[8,768]{1,0:T(8,128)(2,1)S(1)}, bf16[8,768]{1,0:T(8,128)(2,1)S(1)}, u32[]{:S(2)}, u32[]{:S(2)}) collective-permute-start(bf16[8,768]{1,0:T(8,128)(2,1)S(1)} %get-tuple-element.18), channel_id=1, source_target_pairs={{0,3},{1,2},{2,1},{3,0},{4,7},{5,6},{6,5},{7,4},{8,11},{9,10},{10,... | collective-permute-start | bytes 36872 | tf_op jit(solution)/shard_map/ppermute | solution.py:326
  46.6 4.1 %collective-permute-start.13 = (bf16[8,768]{1,0:T(8,128)(2,1)S(1)}, bf16[8,768]{1,0:T(8,128)(2,1)S(1)}, u32[]{:S(2)}, u32[]{:S(2)}) collective-permute-start(bf16[8,768]{1,0:T(8,128)(2,1)S(1)} %get-tuple-element.17), channel_id=1, source_target_pairs={{0,1},{1,0},{2,3},{3,2},{4,5},{5,4},{6,7},{7,6},{8,9},{9,8},{10,11... | collective-permute-start | bytes 36872 | tf_op jit(solution)/shard_map/ppermute | solution.py:326

commit v11 on v9

--- a/solution.py
+++ b/solution.py
@@ -24,13 +24,8 @@
     return high, middle, rest - middle
 
 
-def cut_units(units):
-    if units <= 7 * UNITS // 2:
-        return units // 32 * 16, units // 32 * 16
-    return units * 3 // 4 // UNITS * UNITS, units - UNITS
-
-
-def unit_parts(units, cut):
+def unit_parts(units):
+    cut = units * 3 // 4 // UNITS * UNITS or units // 32 * 16
     return pl.ds(0, cut), pl.ds(cut, units - cut)
 
 
@@ -49,9 +44,11 @@
     routes_hbm,
     router_hbm,
     gain_hbm,
-    weight_hbm,
+    gate_hbm,
+    up_hbm,
     out_ref,
-    weight_ref,
+    gate_ref,
+    up_ref,
     q_ref,
     new_ref,
     kv,
@@ -61,7 +58,7 @@
     gain_ref,
     scores,
     sems,
-    weight_sem,
+    weight_sems,
     *,
     chunks,
     rest,
@@ -75,7 +72,10 @@
     copies = [pltpu.make_async_copy(a, b, sems.at[i]) for i, (a, b) in enumerate(zip(sources, targets))]
     for copy in copies:
         copy.start()
-    load = start_load(weight_hbm, weight_ref, rest, weight_sem)
+    loads = [
+        start_load(gate_hbm, gate_ref, rest, weight_sems.at[0]),
+        start_load(up_hbm, up_ref, rest, weight_sems.at[1]),
+    ]
     tokens, columns = q_ref.shape
     key_heads = new_ref.shape[1] // (2 * HEAD_DIM)
     grouped = columns // HEAD_DIM // key_heads
@@ -161,33 +161,34 @@
         gains + [jnp.zeros((1, LANES), jnp.float32)] * (tokens - len(gains)), axis=0
     )
     out_ref[:, columns + LANES :] = gain_rows.astype(out_ref.dtype)
-    load.wait()
-
-
-def attend(cache_len, queries, new_kv, kv_cache, residual, routes, router, norm_gain, weight, rest):
+    for copy in loads:
+        copy.wait()
+
+
+def attend(cache_len, queries, new_kv, kv_cache, residual, routes, router, norm_gain, gate_w, up_w, rest):
     tokens, columns = queries.shape
     slots, width = kv_cache.shape[1:]
     key_heads = new_kv.shape[1] // (2 * HEAD_DIM)
     rows = columns // HEAD_DIM // key_heads * tokens
     chunks = 4
-    operands = [queries, new_kv, kv_cache, residual, routes.T, router, norm_gain, weight]
+    operands = [queries, new_kv, kv_cache, residual, routes.T, router, norm_gain, gate_w, up_w]
     operands = [pltpu.with_memory_space_constraint(x, pltpu.HBM) for x in operands]
-    kept = [pltpu.VMEM(x.shape, x.dtype) for x in operands[:-1]]
+    kept = [pltpu.VMEM(x.shape, x.dtype) for x in operands[:-2]]
     kept[2] = pltpu.VMEM((slots, width), kv_cache.dtype)
     return pl.pallas_call(
         functools.partial(attention_kernel, chunks=chunks, rest=rest),
         out_shape=(
             jax.ShapeDtypeStruct((tokens, columns + 2 * LANES), jnp.bfloat16),
-            pltpu.VMEM((rest.size, weight.shape[2]), weight.dtype),
+            *[pltpu.VMEM((rest.size, w.shape[2]), w.dtype) for w in (gate_w, up_w)],
         ),
         in_specs=[pl.BlockSpec(memory_space=pltpu.SMEM)]
         + [pl.BlockSpec(memory_space=pl.ANY)] * len(operands),
-        out_specs=(pl.BlockSpec(memory_space=pltpu.VMEM),) * 2,
+        out_specs=(pl.BlockSpec(memory_space=pltpu.VMEM),) * 3,
         scratch_shapes=kept
         + [
             pltpu.VMEM((key_heads, rows, slots), jnp.float32),
-            pltpu.SemaphoreType.DMA((chunks + len(operands) - 2,)),
-            pltpu.SemaphoreType.DMA,
+            pltpu.SemaphoreType.DMA((chunks + len(operands) - 3,)),
+            pltpu.SemaphoreType.DMA((2,)),
         ],
         compiler_params=pltpu.CompilerParams(vmem_limit_bytes=8 * MIB),
         cost_estimate=pl.CostEstimate(
@@ -284,7 +285,7 @@
     )(token, *pieces)
 
 
-def hidden_kernel(place_ref, near, far, gate_a, gate_b, up_a, up_b, _, hidden, x, *, experts):
+def hidden_kernel(place_ref, near, far, gate_a, gate_b, up_a, up_b, hidden, x, *, experts):
     half = near.shape[0]
     model = gate_a.shape[1]
     x[:half] = near[:, :model]
@@ -311,7 +312,7 @@
             hidden[:, start:stop] = out.astype(hidden.dtype)
 
 
-def run_hidden(place, near, far, weights, token, experts):
+def run_hidden(place, near, far, weights, experts):
     units = weights[0].shape[0] + weights[1].shape[0]
     model = weights[0].shape[1]
     rows = 2 * near.shape[0]
@@ -319,7 +320,7 @@
     return pl.pallas_call(
         functools.partial(hidden_kernel, experts=experts),
         out_shape=jax.ShapeDtypeStruct((rows, units), jnp.bfloat16),
-        in_specs=[pl.BlockSpec(memory_space=pltpu.SMEM)] + [vmem] * 7,
+        in_specs=[pl.BlockSpec(memory_space=pltpu.SMEM)] + [vmem] * 6,
         out_specs=vmem,
         scratch_shapes=[pltpu.VMEM((rows, model), jnp.bfloat16)],
         compiler_params=pltpu.CompilerParams(vmem_limit_bytes=(6 if rows <= 64 else 24) * MIB),
@@ -327,7 +328,7 @@
             flops=4 * rows * units * model, bytes_accessed=4 * units * model, transcendentals=rows * units
         ),
         name="hidden",
-    )(place, near, far, *weights, token)
+    )(place, near, far, *weights)
 
 
 def send(x, axis, mask):
@@ -357,22 +358,20 @@
     place = lax.axis_index("tensor")
     where = jnp.stack([place, lax.axis_index("section") * tensors + place]).astype(jnp.int32)
 
-    units = gate_w.shape[1]
-    gate_parts, up_parts = [unit_parts(units, cut) for cut in cut_units(units)]
-
-    fresh, gate_b = attend(
-        cache_len, queries, new_kv, kv_cache, residual, routes, router, norm_gain, gate_w, gate_parts[1]
+    later, beside = unit_parts(gate_w.shape[1])
+
+    fresh, gate_b, up_b = attend(
+        cache_len, queries, new_kv, kv_cache, residual, routes, router, norm_gain, gate_w, up_w, beside
     )
     blocks = exchange([fresh] * tensors, "tensor") + [fresh]
-    gate_a, token = load(fresh, gate_w, gate_parts[0])
+    gate_a, token = load(fresh, gate_w, later)
     rows = norm_rows(where, token, blocks, experts)
     ranks = exchange([rows] * groups, "group") + [rows]
-    up_a, token = load(rows, up_w, up_parts[0])
+    up_a, token = load(rows, up_w, later)
     near = stack_rows(token, ranks)
     far = send(near, "section", 1)
-    up_b, token = load(near, up_w, up_parts[1])
-
-    hidden = run_hidden(where, near, far, (gate_a, gate_b, up_a, up_b), token, experts)
+
+    hidden = run_hidden(where, near, far, (gate_a, gate_b, up_a, up_b), experts)
     out = jnp.dot(hidden, down_w[0], preferred_element_type=jnp.float32).astype(jnp.bfloat16)
     half = out.shape[0] // 2
     both = add(out[:half], send(out[half:], "section", 1)).astype(jnp.bfloat16)

time: 48.5 us -> 50.5 us (1.041)
  local copies, waits for them, and re-layouts: 0.06 us -> 1.58 us
  waiting for transfers between devices: 9.4 us -> 10.9 us
  Pallas kernels: 18.2 us -> 17.4 us
    pallas_call x3 -> x2, Pallas kernels: 8.39 us -> 6.78 us  [load(): pl.pallas_call(functools.partial(load_kernel, part=part), out_shape=(pltp...]
    ppermute x14, waiting for transfers between devices: 9.4 us -> 10.9 us  [send(): lax.ppermute(x, axis, [(i, i ^ mask) for i in range(lax.axis_size(axis))])]
    unnamed x6 -> x10, local copies, waits for them, and re-layouts: 0.02 us -> 1.54 us
    pallas_call x1, Pallas kernels: 2.59 us -> 3.43 us  [attend(): pl.pallas_call(functools.partial(attention_kernel, chunks=chunks, rest=re...]
  transfers between devices with their start and end apart: 14 -> 14, of which waited for: 7 -> 9; matrix products, arithmetic and copies ran while one was open for 0% -> 0% of each run, Pallas kernels for 17% -> 14%
where the time goes in v11:
time: 50.5 us; the launch traced here: 50.2 us
  Pallas kernels  17.4 us (34%)
  starting transfers between devices  16.7 us (33%)
  waiting for transfers between devices  10.9 us (22%)
  matrix products  1.97 us (4%)
  local copies, waits for them, and re-layouts  1.58 us (3%)
  between operations  0.81 us (2%)
  other arithmetic  0.77 us (2%)
    ppermute x14, starting transfers between devices, send(): lax.ppermute(x, axis, [(i, i ^ mask) for i in range(lax.axis_size(axis))])  16.7 us
    ppermute x14, waiting for transfers between devices, send(): lax.ppermute(x, axis, [(i, i ^ mask) for i in range(lax.axis_size(axis))])  10.9 us
    pallas_call x2, Pallas kernels, load(): pl.pallas_call(functools.partial(load_kernel, part=part), out_shape=(pltp...  6.78 us
    pallas_call x1, Pallas kernels, run_hidden(): pl.pallas_call(functools.partial(hidden_kernel, experts=experts), out_sha...  6.29 us
    pallas_call x1, Pallas kernels, attend(): pl.pallas_call(functools.partial(attention_kernel, chunks=chunks, rest=re...  3.43 us
    dot_general x1, matrix products, per_device(): jnp.dot(hidden, down_w[0], preferred_element_type=jnp.float32)  1.97 us
    unnamed x10, local copies, waits for them, and re-layouts  1.54 us
  transfers between devices with their start and end apart: 14, of which 9 were waited for; matrix products, arithmetic and copies ran while one was open for 0% of the time, Pallas kernels for 14%

profile of v11, /device:TPU:0, one launch (start us, length us, event | category | flops | bytes accessed | tf_op | source)
XLA Modules:
  0.0 50.2 jit_solution(7219436608865110628)
XLA Ops:
  0.7 3.4 %attention.1 = (bf16[8,1024]{1,0:T(8,128)(2,1)S(1)}, bf16[448,3072]{1,0:T(8,128)(2,1)S(1)}, bf16[448,3072]{1,0:T(8,128)(2,1)S(1)}) custom-call(s32[1]{0:T(128)S(6)} %copy.12.len_ref, bf16[8,768]{1,0:T(8,128)(2,1)} %q_hbm.1, bf16[8,512]{1,0:T(8,128)(2,1)} %new_hbm.1, bf16[1,2048,512]{2,1,0:T(8,128)(2,1)} %kv_hbm.1, bf16[8,768]{1,0:T(8,128)(2,1)} %res_hbm.1, ...), custom_call_target="tpu_custom_call" | custom-call | flops 50331648 | bytes 2097152 | tf_op jit(solution)/shard_map/attention/pallas_call | solution.py:178
  4.1 1.5 %copy-done = bf16[448,3072]{1,0:T(8,128)(2,1)} copy-done((bf16[448,3072]{1,0:T(8,128)(2,1)}, bf16[448,3072]{1,0:T(8,128)(2,1)S(1)}, u32[]{:S(2)}) %copy-start) | copy-done | bytes 2752536
  5.6 4.0 %collective-permute-start = (bf16[8,1024]{1,0:T(8,128)(2,1)S(1)}, bf16[8,1024]{1,0:T(8,128)(2,1)S(1)}, u32[]{:S(2)}, u32[]{:S(2)}) collective-permute-start(bf16[8,1024]{1,0:T(8,128)(2,1)S(1)} %get-tuple-element.12._.refs_3_), channel_id=1, source_target_pairs={{0,2},{1,3},{2,0},{3,1},{4,6},{5,7},{6,4},{7,5},{8,10},{9,11},{10,... | collective-permute-start | bytes 49160 | tf_op jit(solution)/shard_map/ppermute | solution.py:335
  9.7 1.3 %collective-permute-start.1 = (bf16[8,1024]{1,0:T(8,128)(2,1)S(1)}, bf16[8,1024]{1,0:T(8,128)(2,1)S(1)}, u32[]{:S(2)}, u32[]{:S(2)}) collective-permute-start(bf16[8,1024]{1,0:T(8,128)(2,1)S(1)} %get-tuple-element.12._.refs_3_), channel_id=1, source_target_pairs={{0,3},{1,2},{2,1},{3,0},{4,7},{5,6},{6,5},{7,4},{8,11},{9,10},{10,... | collective-permute-start | bytes 49160 | tf_op jit(solution)/shard_map/ppermute | solution.py:335
  11.0 0.2 collective-permute-start.2
  11.2 0.1 pad_add_fusion.place_ref
  11.3 3.4 %load.2 = (bf16[1280,3072]{1,0:T(8,128)(2,1)S(1)}, f32[8,128]{1,0:T(8,128)S(1)}) custom-call(bf16[8,1024]{1,0:T(8,128)(2,1)S(1)} %get-tuple-element.12._.refs_3_, bf16[1,1728,3072]{2,1,0:T(8,128)(2,1)} %source.2), custom_call_target="tpu_custom_call" | custom-call | bytes 15728640 | tf_op jit(solution)/shard_map/load/pallas_call | solution.py:211
  14.7 0.5 collective-permute-done.1.refs_1_
  15.2 0.9 %norm.1._.refs_3_ = bf16[8,3200]{1,0:T(8,128)(2,1)S(1)} custom-call(s32[2]{0:T(128)S(1)} %pad_add_fusion.place_ref, f32[8,128]{1,0:T(8,128)S(1)} %get-tuple-element.13._, bf16[8,1024]{1,0:T(8,128)(2,1)S(1)} %collective-permute-done.refs_0_, bf16[8,1024]{1,0:T(8,128)(2,1)S(1)} %collective-permute-done.1.refs_1_, ...), custom_call_target="tpu_custom_call" | custom-call | tf_op jit(solution)/shard_map/norm/pallas_call | solution.py:256
  16.1 1.5 %collective-permute-start.3 = (bf16[8,3200]{1,0:T(8,128)(2,1)S(1)}, bf16[8,3200]{1,0:T(8,128)(2,1)S(1)}, u32[]{:S(2)}, u32[]{:S(2)}) collective-permute-start(bf16[8,3200]{1,0:T(8,128)(2,1)S(1)} %norm.1._.refs_3_), channel_id=1, source_target_pairs={{0,8},{4,12},{8,0},{12,4},{1,9},{5,13},{9,1},{13,5},{2,10},{6,14},... | collective-permute-start | bytes 153608 | tf_op jit(solution)/shard_map/ppermute | solution.py:335
  17.7 1.4 %collective-permute-start.4 = (bf16[8,3200]{1,0:T(8,128)(2,1)S(1)}, bf16[8,3200]{1,0:T(8,128)(2,1)S(1)}, u32[]{:S(2)}, u32[]{:S(2)}) collective-permute-start(bf16[8,3200]{1,0:T(8,128)(2,1)S(1)} %norm.1._.refs_3_), channel_id=1, source_target_pairs={{0,12},{4,8},{8,4},{12,0},{1,13},{5,9},{9,5},{13,1},{2,14},{6,10},... | collective-permute-start | bytes 153608 | tf_op jit(solution)/shard_map/ppermute | solution.py:335
  19.1 0.5 %collective-permute-start.5 = (bf16[8,3200]{1,0:T(8,128)(2,1)S(1)}, bf16[8,3200]{1,0:T(8,128)(2,1)S(1)}, u32[]{:S(2)}, u32[]{:S(2)}) collective-permute-start(bf16[8,3200]{1,0:T(8,128)(2,1)S(1)} %norm.1._.refs_3_), channel_id=1, source_target_pairs={{0,4},{4,0},{8,12},{12,8},{1,5},{5,1},{9,13},{13,9},{2,6},{6,2},{1... | collective-permute-start | bytes 153608 | tf_op jit(solution)/shard_map/ppermute | solution.py:335
  19.6 3.4 %load.3 = (bf16[1280,3072]{1,0:T(8,128)(2,1)S(1)}, f32[8,128]{1,0:T(8,128)S(1)}) custom-call(bf16[8,3200]{1,0:T(8,128)(2,1)S(1)} %norm.1._.refs_3_, bf16[1,1728,3072]{2,1,0:T(8,128)(2,1)} %source.3), custom_call_target="tpu_custom_call" | custom-call | bytes 15728640 | tf_op jit(solution)/shard_map/load/pallas_call | solution.py:211
  23.1 0.2 collective-permute-done.5.refs_2_
  23.2 0.1 collective-permute-start.6
  23.3 1.4 %collective-permute-done.6.far = bf16[32,3200]{1,0:T(8,128)(2,1)S(1)} collective-permute-done((bf16[32,3200]{1,0:T(8,128)(2,1)S(1)}, bf16[32,3200]{1,0:T(8,128)(2,1)S(1)}, u32[]{:S(2)}, u32[]{:S(2)}) %collective-permute-start.6) | collective-permute-done | bytes 204832 | tf_op jit(solution)/shard_map/ppermute | solution.py:335
  24.8 6.3 %hidden.1 = bf16[64,1728]{1,0:T(8,128)(2,1)S(1)} custom-call(s32[2]{0:T(128)S(1)} %pad_add_fusion.place_ref, bf16[32,3200]{1,0:T(8,128)(2,1)S(1)} %stack.13.near, bf16[32,3200]{1,0:T(8,128)(2,1)S(1)} %collective-permute-done.6.far, bf16[1280,3072]{1,0:T(8,128)(2,1)S(1)} %get-tuple-element.15.gate_a, bf16[448,3072]{1,0:T(8,128)(2,1)S(1)} %get-tuple-element.16.gate_b, ...), custom_call_target="tpu_custom_call" | custom-call | flops 1358954496 | bytes 21233664 | tf_op jit(solution)/shard_map/hidden/pallas_call | solution.py:320
  31.1 2.0 %fusion.2 = bf16[64,3072]{1,0:T(8,128)(2,1)S(1)} fusion(bf16[64,1728]{1,0:T(8,128)(2,1)S(1)} %hidden.1, bf16[1,1728,3072]{2,1,0:T(8,128)(2,1)S(1)} %bitcast.10), kind=kOutput, calls=%fused_computation.2 | convolution fusion | flops 679673856 | bytes 11231232 | tf_op jit(solution)/shard_map/dot_general | solution.py:375
  33.1 0.2 collective-permute-start.7
  33.3 1.3 %collective-permute-done.7 = bf16[32,3072]{1,0:T(8,128)(2,1)S(1)} collective-permute-done((bf16[32,3072]{1,0:T(8,128)(2,1)S(1)}, bf16[32,3072]{1,0:T(8,128)(2,1)S(1)}, u32[]{:S(2)}, u32[]{:S(2)}) %collective-permute-start.7) | collective-permute-done | bytes 196640 | tf_op jit(solution)/shard_map/ppermute | solution.py:335
  34.6 0.1 add_convert_fusion
  34.7 2.4 %collective-permute-start.10 = (bf16[8,3072]{1,0:T(8,128)(2,1)S(1)}, bf16[8,3072]{1,0:T(8,128)(2,1)S(1)}, u32[]{:S(2)}, u32[]{:S(2)}) collective-permute-start(bf16[8,3072]{1,0:T(8,128)(2,1)S(1)} %get-tuple-element.20), channel_id=1, source_target_pairs={{0,12},{4,8},{8,4},{12,0},{1,13},{5,9},{9,5},{13,1},{2,14},{6,10},... | collective-permute-start | bytes 147464 | tf_op jit(solution)/shard_map/ppermute | solution.py:335
  37.1 0.5 %collective-permute-start.8 = (bf16[8,3072]{1,0:T(8,128)(2,1)S(1)}, bf16[8,3072]{1,0:T(8,128)(2,1)S(1)}, u32[]{:S(2)}, u32[]{:S(2)}) collective-permute-start(bf16[8,3072]{1,0:T(8,128)(2,1)S(1)} %get-tuple-element.19), channel_id=1, source_target_pairs={{0,8},{4,12},{8,0},{12,4},{1,9},{5,13},{9,1},{13,5},{2,10},{6,14},... | collective-permute-start | bytes 147464 | tf_op jit(solution)/shard_map/ppermute | solution.py:335
  37.6 0.7 %collective-permute-start.9 = (bf16[8,3072]{1,0:T(8,128)(2,1)S(1)}, bf16[8,3072]{1,0:T(8,128)(2,1)S(1)}, u32[]{:S(2)}, u32[]{:S(2)}) collective-permute-start(bf16[8,3072]{1,0:T(8,128)(2,1)S(1)} %get-tuple-element.21), channel_id=1, source_target_pairs={{0,4},{4,0},{8,12},{12,8},{1,5},{5,1},{9,13},{13,9},{2,6},{6,2},{1... | collective-permute-start | bytes 147464 | tf_op jit(solution)/shard_map/ppermute | solution.py:335
  38.2 1.5 %collective-permute-done.10 = bf16[8,3072]{1,0:T(8,128)(2,1)S(1)} collective-permute-done((bf16[8,3072]{1,0:T(8,128)(2,1)S(1)}, bf16[8,3072]{1,0:T(8,128)(2,1)S(1)}, u32[]{:S(2)}, u32[]{:S(2)}) %collective-permute-start.10) | collective-permute-done | bytes 49184 | tf_op jit(solution)/shard_map/ppermute | solution.py:335
  39.8 1.4 %collective-permute-done.8 = bf16[8,3072]{1,0:T(8,128)(2,1)S(1)} collective-permute-done((bf16[8,3072]{1,0:T(8,128)(2,1)S(1)}, bf16[8,3072]{1,0:T(8,128)(2,1)S(1)}, u32[]{:S(2)}, u32[]{:S(2)}) %collective-permute-start.8) | collective-permute-done | bytes 49184 | tf_op jit(solution)/shard_map/ppermute | solution.py:335
  41.1 0.5 %collective-permute-done.9 = bf16[8,3072]{1,0:T(8,128)(2,1)S(1)} collective-permute-done((bf16[8,3072]{1,0:T(8,128)(2,1)S(1)}, bf16[8,3072]{1,0:T(8,128)(2,1)S(1)}, u32[]{:S(2)}, u32[]{:S(2)}) %collective-permute-start.9) | collective-permute-done | bytes 49184 | tf_op jit(solution)/shard_map/ppermute | solution.py:335
  41.7 2.4 %collective-permute-start.11 = (bf16[8,768]{1,0:T(8,128)(2,1)S(1)}, bf16[8,768]{1,0:T(8,128)(2,1)S(1)}, u32[]{:S(2)}, u32[]{:S(2)}) collective-permute-start(bf16[8,768]{1,0:T(8,128)(2,1)S(1)} %get-tuple-element.22), channel_id=1, source_target_pairs={{0,2},{1,3},{2,0},{3,1},{4,6},{5,7},{6,4},{7,5},{8,10},{9,11},{10,... | collective-permute-start | bytes 36872 | tf_op jit(solution)/shard_map/ppermute | solution.py:335
  44.1 1.3 %collective-permute-start.12 = (bf16[8,768]{1,0:T(8,128)(2,1)S(1)}, bf16[8,768]{1,0:T(8,128)(2,1)S(1)}, u32[]{:S(2)}, u32[]{:S(2)}) collective-permute-start(bf16[8,768]{1,0:T(8,128)(2,1)S(1)} %get-tuple-element.24), channel_id=1, source_target_pairs={{0,3},{1,2},{2,1},{3,0},{4,7},{5,6},{6,5},{7,4},{8,11},{9,10},{10,... | collective-permute-start | bytes 36872 | tf_op jit(solution)/shard_map/ppermute | solution.py:335
  45.5 0.9 %collective-permute-done.11 = bf16[8,768]{1,0:T(8,128)(2,1)S(1)} collective-permute-done((bf16[8,768]{1,0:T(8,128)(2,1)S(1)}, bf16[8,768]{1,0:T(8,128)(2,1)S(1)}, u32[]{:S(2)}, u32[]{:S(2)}) %collective-permute-start.11) | collective-permute-done | bytes 12320 | tf_op jit(solution)/shard_map/ppermute | solution.py:335
  46.4 3.3 %collective-permute-done.12 = bf16[8,768]{1,0:T(8,128)(2,1)S(1)} collective-permute-done((bf16[8,768]{1,0:T(8,128)(2,1)S(1)}, bf16[8,768]{1,0:T(8,128)(2,1)S(1)}, u32[]{:S(2)}, u32[]{:S(2)}) %collective-permute-start.12) | collective-permute-done | bytes 12320 | tf_op jit(solution)/shard_map/ppermute | solution.py:335
  49.6 0.6 %add_convert_fusion.2 = bf16[8,768]{1,0:T(8,128)(2,1)} fusion(bf16[8,768]{1,0:T(8,128)(2,1)S(1)} %collective-permute-done.13, bf16[8,768]{1,0:T(8,128)(2,1)S(1)} %collective-permute-done.12, bf16[8,768]{1,0:T(8,128)(2,1)S(1)} %collective-permute-done.11, bf16[8,1024]{1,0:T(8,128)(2,1)S(1)} %get-tuple-element.12._.refs_3_, ...), kind=kLoop, calls=%fused_computation.5 | loop fusion | flops 61440 | bytes 73732 | tf_op jit(solution)/shard_map/convert_element_type | solution.py:383
  (21 shorter events, 0.1 us)
Async XLA Ops:
  4.1 1.5 %copy-start = (bf16[448,3072]{1,0:T(8,128)(2,1)}, bf16[448,3072]{1,0:T(8,128)(2,1)S(1)}, u32[]{:S(2)}) copy-start(bf16[448,3072]{1,0:T(8,128)(2,1)S(1)} %get-tuple-element.18.up_b) | copy-start | bytes 8257540
  5.6 9.1 %collective-permute-start = (bf16[8,1024]{1,0:T(8,128)(2,1)S(1)}, bf16[8,1024]{1,0:T(8,128)(2,1)S(1)}, u32[]{:S(2)}, u32[]{:S(2)}) collective-permute-start(bf16[8,1024]{1,0:T(8,128)(2,1)S(1)} %get-tuple-element.12._.refs_3_), channel_id=1, source_target_pairs={{0,2},{1,3},{2,0},{3,1},{4,6},{5,7},{6,4},{7,5},{8,10},{9,11},{10,... | collective-permute-start | bytes 49160 | tf_op jit(solution)/shard_map/ppermute | solution.py:335
  9.7 5.5 %collective-permute-start.1 = (bf16[8,1024]{1,0:T(8,128)(2,1)S(1)}, bf16[8,1024]{1,0:T(8,128)(2,1)S(1)}, u32[]{:S(2)}, u32[]{:S(2)}) collective-permute-start(bf16[8,1024]{1,0:T(8,128)(2,1)S(1)} %get-tuple-element.12._.refs_3_), channel_id=1, source_target_pairs={{0,3},{1,2},{2,1},{3,0},{4,7},{5,6},{6,5},{7,4},{8,11},{9,10},{10,... | collective-permute-start | bytes 49160 | tf_op jit(solution)/shard_map/ppermute | solution.py:335
  11.0 4.2 %collective-permute-start.2 = (bf16[8,1024]{1,0:T(8,128)(2,1)S(1)}, bf16[8,1024]{1,0:T(8,128)(2,1)S(1)}, u32[]{:S(2)}, u32[]{:S(2)}) collective-permute-start(bf16[8,1024]{1,0:T(8,128)(2,1)S(1)} %get-tuple-element.12._.refs_3_), channel_id=1, source_target_pairs={{0,1},{1,0},{2,3},{3,2},{4,5},{5,4},{6,7},{7,6},{8,9},{9,8},{10,11... | collective-permute-start | bytes 49160 | tf_op jit(solution)/shard_map/ppermute | solution.py:335
  11.3 13.4 %copy-start.1 = (bf16[448,3072]{1,0:T(8,128)(2,1)S(1)}, bf16[448,3072]{1,0:T(8,128)(2,1)}, u32[]{:S(2)}) copy-start(bf16[448,3072]{1,0:T(8,128)(2,1)} %copy-done) | copy-start | bytes 8257540
  16.1 6.9 %collective-permute-start.3 = (bf16[8,3200]{1,0:T(8,128)(2,1)S(1)}, bf16[8,3200]{1,0:T(8,128)(2,1)S(1)}, u32[]{:S(2)}, u32[]{:S(2)}) collective-permute-start(bf16[8,3200]{1,0:T(8,128)(2,1)S(1)} %norm.1._.refs_3_), channel_id=1, source_target_pairs={{0,8},{4,12},{8,0},{12,4},{1,9},{5,13},{9,1},{13,5},{2,10},{6,14},... | collective-permute-start | bytes 153608 | tf_op jit(solution)/shard_map/ppermute | solution.py:335
  17.7 5.4 %collective-permute-start.4 = (bf16[8,3200]{1,0:T(8,128)(2,1)S(1)}, bf16[8,3200]{1,0:T(8,128)(2,1)S(1)}, u32[]{:S(2)}, u32[]{:S(2)}) collective-permute-start(bf16[8,3200]{1,0:T(8,128)(2,1)S(1)} %norm.1._.refs_3_), channel_id=1, source_target_pairs={{0,12},{4,8},{8,4},{12,0},{1,13},{5,9},{9,5},{13,1},{2,14},{6,10},... | collective-permute-start | bytes 153608 | tf_op jit(solution)/shard_map/ppermute | solution.py:335
  19.1 4.1 %collective-permute-start.5 = (bf16[8,3200]{1,0:T(8,128)(2,1)S(1)}, bf16[8,3200]{1,0:T(8,128)(2,1)S(1)}, u32[]{:S(2)}, u32[]{:S(2)}) collective-permute-start(bf16[8,3200]{1,0:T(8,128)(2,1)S(1)} %norm.1._.refs_3_), channel_id=1, source_target_pairs={{0,4},{4,0},{8,12},{12,8},{1,5},{5,1},{9,13},{13,9},{2,6},{6,2},{1... | collective-permute-start | bytes 153608 | tf_op jit(solution)/shard_map/ppermute | solution.py:335
  19.6 11.4 %slice-start = ((s8[10616832]{0:T(1024)(128)(4,1)}), s8[4194304]{0:T(1024)(128)(4,1)S(1)}, s32[]{:S(2)}) async-start(s8[10616832]{0:T(1024)(128)(4,1)} %bitcast.9), calls=%async_computation | async-start | bytes 8388608
  23.2 7.9 %slice-start.1 = ((s8[10616832]{0:T(1024)(128)(4,1)}), s8[4194304]{0:T(1024)(128)(4,1)S(1)}, s32[]{:S(2)}) async-start(s8[10616832]{0:T(1024)(128)(4,1)} %bitcast.9), calls=%async_computation.1 | async-start | bytes 8388608
  23.2 1.5 %collective-permute-start.6 = (bf16[32,3200]{1,0:T(8,128)(2,1)S(1)}, bf16[32,3200]{1,0:T(8,128)(2,1)S(1)}, u32[]{:S(2)}, u32[]{:S(2)}) collective-permute-start(bf16[32,3200]{1,0:T(8,128)(2,1)S(1)} %stack.13.near), channel_id=1, source_target_pairs={{0,16},{16,0},{1,17},{17,1},{2,18},{18,2},{3,19},{19,3},{4,20},{20... | collective-permute-start | bytes 614408 | tf_op jit(solution)/shard_map/ppermute | solution.py:335
  24.8 6.3 %slice-start.2 = ((s8[10616832]{0:T(1024)(128)(4,1)}), s8[2228224]{0:T(1024)(128)(4,1)S(1)}, s32[]{:S(2)}) async-start(s8[10616832]{0:T(1024)(128)(4,1)} %bitcast.9), calls=%async_computation.2 | async-start | bytes 4456448
  33.1 1.5 %collective-permute-start.7 = (bf16[32,3072]{1,0:T(8,128)(2,1)S(1)}, bf16[32,3072]{1,0:T(8,128)(2,1)S(1)}, u32[]{:S(2)}, u32[]{:S(2)}) collective-permute-start(bf16[32,3072]{1,0:T(8,128)(2,1)S(1)} %slice.33), channel_id=1, source_target_pairs={{0,16},{16,0},{1,17},{17,1},{2,18},{18,2},{3,19},{19,3},{4,20},{20... | collective-permute-start | bytes 589832 | tf_op jit(solution)/shard_map/ppermute | solution.py:335
  34.7 5.1 %collective-permute-start.10 = (bf16[8,3072]{1,0:T(8,128)(2,1)S(1)}, bf16[8,3072]{1,0:T(8,128)(2,1)S(1)}, u32[]{:S(2)}, u32[]{:S(2)}) collective-permute-start(bf16[8,3072]{1,0:T(8,128)(2,1)S(1)} %get-tuple-element.20), channel_id=1, source_target_pairs={{0,12},{4,8},{8,4},{12,0},{1,13},{5,9},{9,5},{13,1},{2,14},{6,10},... | collective-permute-start | bytes 147464 | tf_op jit(solution)/shard_map/ppermute | solution.py:335
  37.1 4.1 %collective-permute-start.8 = (bf16[8,3072]{1,0:T(8,128)(2,1)S(1)}, bf16[8,3072]{1,0:T(8,128)(2,1)S(1)}, u32[]{:S(2)}, u32[]{:S(2)}) collective-permute-start(bf16[8,3072]{1,0:T(8,128)(2,1)S(1)} %get-tuple-element.19), channel_id=1, source_target_pairs={{0,8},{4,12},{8,0},{12,4},{1,9},{5,13},{9,1},{13,5},{2,10},{6,14},... | collective-permute-start | bytes 147464 | tf_op jit(solution)/shard_map/ppermute | solution.py:335
  37.6 4.1 %collective-permute-start.9 = (bf16[8,3072]{1,0:T(8,128)(2,1)S(1)}, bf16[8,3072]{1,0:T(8,128)(2,1)S(1)}, u32[]{:S(2)}, u32[]{:S(2)}) collective-permute-start(bf16[8,3072]{1,0:T(8,128)(2,1)S(1)} %get-tuple-element.21), channel_id=1, source_target_pairs={{0,4},{4,0},{8,12},{12,8},{1,5},{5,1},{9,13},{13,9},{2,6},{6,2},{1... | collective-permute-start | bytes 147464 | tf_op jit(solution)/shard_map/ppermute | solution.py:335
  41.7 4.7 %collective-permute-start.11 = (bf16[8,768]{1,0:T(8,128)(2,1)S(1)}, bf16[8,768]{1,0:T(8,128)(2,1)S(1)}, u32[]{:S(2)}, u32[]{:S(2)}) collective-permute-start(bf16[8,768]{1,0:T(8,128)(2,1)S(1)} %get-tuple-element.22), channel_id=1, source_target_pairs={{0,2},{1,3},{2,0},{3,1},{4,6},{5,7},{6,4},{7,5},{8,10},{9,11},{10,... | collective-permute-start | bytes 36872 | tf_op jit(solution)/shard_map/ppermute | solution.py:335
  44.1 5.5 %collective-permute-start.12 = (bf16[8,768]{1,0:T(8,128)(2,1)S(1)}, bf16[8,768]{1,0:T(8,128)(2,1)S(1)}, u32[]{:S(2)}, u32[]{:S(2)}) collective-permute-start(bf16[8,768]{1,0:T(8,128)(2,1)S(1)} %get-tuple-element.24), channel_id=1, source_target_pairs={{0,3},{1,2},{2,1},{3,0},{4,7},{5,6},{6,5},{7,4},{8,11},{9,10},{10,... | collective-permute-start | bytes 36872 | tf_op jit(solution)/shard_map/ppermute | solution.py:335
  45.5 4.1 %collective-permute-start.13 = (bf16[8,768]{1,0:T(8,128)(2,1)S(1)}, bf16[8,768]{1,0:T(8,128)(2,1)S(1)}, u32[]{:S(2)}, u32[]{:S(2)}) collective-permute-start(bf16[8,768]{1,0:T(8,128)(2,1)S(1)} %get-tuple-element.23), channel_id=1, source_target_pairs={{0,1},{1,0},{2,3},{3,2},{4,5},{5,4},{6,7},{7,6},{8,9},{9,8},{10,11... | collective-permute-start | bytes 36872 | tf_op jit(solution)/shard_map/ppermute | solution.py:335
